TPU v7x, 32 devices: a whole 2x2x4 slice. The times are simulated.
32 devices in a mesh: dp: 2 (over x), row: 4 (over y, core), col: 4 (over z).
Axes of the slice: x: 2, y: 2, z: 4, core: 2. Of those that a mesh axis runs over, the one named last changes fastest.
Arguments:
- residual_in: bfloat16 [1576, 768], P(('dp', 'col'), 'row'), may hold values from -12 to 12
- cotangent: float32 [1576, 768], P(('dp', 'col'), 'row'), may hold values from -6 to 6
- qkv_weight: float32 [2, 768, 2304], P(None, 'row', 'col'), may hold values from -0.21875 to 0.21875
- proj_weight: float32 [2, 768, 768], P(None, 'col', 'row'), may hold values from -1.25 to 1.25
- up_weight: float32 [2, 768, 3072], P(None, 'row', 'col'), may hold values from -0.21875 to 0.21875
- down_weight: float32 [2, 3072, 768], P(None, 'col', 'row'), may hold values from -0.109375 to 0.109375
- norm_params: float32 [2, 4, 768], P(None, None, 'row')
- qkv_moment: float32 [2, 768, 2304], P(None, 'row', 'col')
- proj_moment: float32 [2, 768, 768], P(None, 'col', 'row')
- up_moment: float32 [2, 768, 3072], P(None, 'row', 'col')
- down_moment: float32 [2, 3072, 768], P(None, 'col', 'row')
- norm_moment: float32 [2, 4, 768], P(None, None, 'row')
Outputs:
- block_output: float32 [1576, 768], P(('dp', 'col'), 'row')
- input_grad: float32 [1576, 768], P(('dp', 'col'), 'row')
- qkv_grad: float32 [2, 768, 2304], P(None, 'row', 'col')
- proj_grad: float32 [2, 768, 768], P(None, 'col', 'row')
- up_grad: float32 [2, 768, 3072], P(None, 'row', 'col')
- down_grad: float32 [2, 3072, 768], P(None, 'col', 'row')
- norm_grad: float32 [2, 4, 768], P(None, None, 'row')
- qkv_moment_new: float32 [2, 768, 2304], P(None, 'row', 'col')
- proj_moment_new: float32 [2, 768, 768], P(None, 'col', 'row')
- up_moment_new: float32 [2, 768, 3072], P(None, 'row', 'col')
- down_moment_new: float32 [2, 3072, 768], P(None, 'col', 'row')
- norm_moment_new: float32 [2, 4, 768], P(None, None, 'row')
- qkv_new: float32 [2, 768, 2304], P(None, 'row', 'col')
- proj_new: float32 [2, 768, 768], P(None, 'col', 'row')
- up_new: float32 [2, 768, 3072], P(None, 'row', 'col')
- down_new: float32 [2, 3072, 768], P(None, 'col', 'row')
- norm_new: float32 [2, 4, 768], P(None, None, 'row')
All inputs are finite; a program needn't handle non-finite values.
Results may differ from a plain program's by a relative error of at most 0.015.
Values may be sent and summed in bfloat16 or wider, within the bound.
No kernel may reach another device: no remote copies, remote signals or barrier semaphores. Data moves between devices by JAX's collectives and lax.ppermute only.
A program may use at most 256 MiB of HBM per device.

v0:
```python
import math

import jax
import jax.numpy as jnp
from jax import lax
from jax.sharding import PartitionSpec as P

HD = 64

norm_epsilon = 1e-06
moment_decay = 0.9
norm_rate = 0.05
step_rates = (1.7, 5.6, 2.0, 1.0)
schulz_first = 3.4445
schulz_second = -4.775
schulz_third = 2.0315
high = lax.Precision.HIGH
kinds = 4


def product(left_side, right_side):
    return lax.dot_general(
        left_side, right_side, (((1,), (0,)), ((), ())), preferred_element_type=jnp.float32
    )


def product_flipped(left_side, right_side):
    return lax.dot_general(
        left_side, right_side, (((1,), (1,)), ((), ())), preferred_element_type=jnp.float32
    )


def outer_grad(left_side, right_side):
    return lax.dot_general(
        left_side, right_side, (((0,), (0,)), ((), ())), preferred_element_type=jnp.float32
    )


def dot_high(left_side, right_side):
    return jnp.dot(left_side, right_side, precision=high)


def pad_rows(values, rows):
    return jnp.pad(values, ((0, rows - values.shape[0]), (0, 0)))


def pad_columns(values, columns):
    return jnp.pad(values, ((0, 0), (0, columns - values.shape[1])))


def norm_parts_of(values):
    average = jnp.mean(values, axis=1, keepdims=True)
    square = jnp.mean(values * values, axis=1, keepdims=True)
    inverse = lax.rsqrt(square - average * average + norm_epsilon)
    return ((values - average) * inverse, inverse)


def norm_backward(grad_out, plain, inverse, gain_row):
    scaled = grad_out * gain_row
    first = jnp.mean(scaled, axis=1, keepdims=True)
    second = jnp.mean(scaled * plain, axis=1, keepdims=True)
    return inverse * (scaled - first - plain * second)


def split_heads(mixed_low):
    token_count = mixed_low.shape[0]
    heads_here = mixed_low.shape[1] // (3 * HD)
    grouped = mixed_low.reshape(token_count, heads_here, 3, HD)
    return (grouped[:, :, 0, :], grouped[:, :, 1, :], grouped[:, :, 2, :])


def score_block(query_rows, key_rows):
    return jnp.einsum(
        "qhd,khd->hqk", query_rows, key_rows, preferred_element_type=jnp.float32
    ) * HD ** (-0.5)


def attend_forward(mixed_low):
    query_rows, key_rows, value_rows = split_heads(mixed_low)
    scores = score_block(query_rows, key_rows)
    row_top = jnp.max(scores, axis=-1, keepdims=True)
    log_total = jnp.log(jnp.sum(jnp.exp(scores - row_top), axis=-1, keepdims=True)) + row_top
    weights = jnp.exp(scores - log_total).astype(jnp.bfloat16)
    attended = jnp.einsum("hqk,khd->qhd", weights, value_rows, preferred_element_type=jnp.float32)
    return (attended.reshape(mixed_low.shape[0], -1).astype(jnp.bfloat16), log_total)


def attend_backward(mixed_low, log_total, grad_att):
    query_rows, key_rows, value_rows = split_heads(mixed_low)
    scores = score_block(query_rows, key_rows)
    probs = jnp.exp(scores - log_total)
    grad_out = grad_att.reshape(query_rows.shape)
    grad_probs = jnp.einsum(
        "qhd,khd->hqk", grad_out, value_rows, preferred_element_type=jnp.float32
    )
    grad_scores = (
        probs * (grad_probs - jnp.sum(probs * grad_probs, axis=-1, keepdims=True))
    ).astype(jnp.bfloat16)
    scaling = HD ** (-0.5)
    grad_query = (
        jnp.einsum("hqk,khd->qhd", grad_scores, key_rows, preferred_element_type=jnp.float32)
        * scaling
    )
    grad_key = (
        jnp.einsum("hqk,qhd->khd", grad_scores, query_rows, preferred_element_type=jnp.float32)
        * scaling
    )
    grad_value = jnp.einsum(
        "hqk,qhd->khd", probs.astype(jnp.bfloat16), grad_out, preferred_element_type=jnp.float32
    )
    stacked = jnp.stack((grad_query, grad_key, grad_value), axis=2)
    return stacked.reshape(mixed_low.shape[0], -1).astype(jnp.bfloat16)


def swap_row_col(values):
    size = lax.axis_size("row")
    pairs = [(i * size + j, j * size + i) for i in range(size) for j in range(size)]
    return lax.ppermute(values, ("row", "col"), pairs)


def from_partner(values, step, axes=("dp", "row"), wanted=None):
    count = math.prod(lax.axis_size(a) for a in axes)
    pairs = [(i, i ^ step) for i in range(count) if wanted is None or wanted(i ^ step)]
    return lax.ppermute(values, axes, pairs)


def pick(stacked, index):
    return lax.dynamic_index_in_dim(stacked, index, 0, keepdims=False)


def placed_blocks(blocks, places):
    result = jnp.zeros((len(blocks),) + blocks[0].shape, blocks[0].dtype)
    for block, place in zip(blocks, places):
        result = lax.dynamic_update_index_in_dim(result, block, place, 0)
    return result


def gather_by_pairs(values, axis):
    step = lax.axis_size(axis) // 2
    me = lax.axis_index(axis)
    blocks, places = [values], [me]
    while step:
        sent = blocks[0][None] if len(blocks) == 1 else jnp.stack(blocks)
        received = from_partner(sent, step, (axis,))
        blocks = blocks + [received[i] for i in range(len(blocks))]
        places = places + [p ^ step for p in places]
        step //= 2
    return placed_blocks(blocks, places)


def sum_by_pairs(values, axis):
    step = 1
    while step < lax.axis_size(axis):
        values = values + from_partner(values, step, (axis,))
        step *= 2
    return values


def to_all(block, axis):
    size = lax.axis_size(axis)
    return lax.all_to_all(jnp.broadcast_to(block[None], (size,) + block.shape), axis, 0, 0)


def gather_tokens(chunk):
    blocks = to_all(chunk, "col")
    return blocks.reshape(-1, chunk.shape[1])


def sum_tokens(partial, padded):
    size = lax.axis_size("col")
    blocks = pad_rows(partial.astype(jnp.bfloat16), padded)
    blocks = blocks.reshape(size, padded // size, partial.shape[1])
    blocks = lax.all_to_all(blocks, "col", 0, 0)
    return jnp.sum(blocks.astype(jnp.float32), axis=0)


def schulz(raw):
    size = lax.axis_size("col")
    height = raw.shape[0]
    third = height // 3
    strips = [
        lax.dot_general(
            raw[i * third : (i + 1) * third],
            raw[i * third :],
            (((1,), (1,)), ((), ())),
            precision=high,
            preferred_element_type=jnp.float32,
        )
        for i in range(3)
    ]
    packed = jnp.concatenate(strips, axis=1)
    blocks = lax.all_to_all(packed.reshape(size, third // size, -1), "col", 0, 0)
    packed = to_all(jnp.sum(blocks, axis=0), "col").reshape(third, -1)
    first = packed[:, :height]
    second = packed[:, height : 2 * height - third]
    last = packed[:, 2 * height - third :]
    gram = jnp.concatenate(
        [
            first,
            jnp.concatenate([first[:, third : 2 * third].T, second], axis=1),
            jnp.concatenate([first[:, 2 * third :].T, second[:, third:].T, last], axis=1),
        ],
        axis=0,
    )
    eye = jnp.eye(height, dtype=jnp.float32)
    scale = 1.0 / (jnp.sqrt(jnp.sum(gram * eye)) + 1e-07)
    current = raw * scale
    gram = gram * (scale * scale)
    for sweep_index in range(5):
        square = schulz_second * gram + schulz_third * dot_high(gram, gram)
        if sweep_index < 4:
            both = jnp.concatenate([gram, current], axis=1)
            both = schulz_first * both + dot_high(square, both)
            half = both[:, :height]
            current = both[:, height:]
            gram = schulz_first * half + dot_high(half, square)
        else:
            current = schulz_first * current + dot_high(square, current)
    return current


def on_device(
    residual_in,
    cotangent,
    qkv_weight,
    proj_weight,
    up_weight,
    down_weight,
    norm_params,
    qkv_moment,
    proj_moment,
    up_moment,
    down_moment,
    norm_moment,
):
    tokens, width_row = residual_in.shape
    row_size = lax.axis_size("row")
    col_size = lax.axis_size("col")
    dp_size = lax.axis_size("dp")
    model_width = width_row * row_size
    levels = qkv_weight.shape[0]
    jobs = levels * kinds
    chunk = -(-tokens // (8 * col_size)) * 8
    padded = chunk * col_size
    sent_rows = -(-tokens // 16) * 16
    me = (lax.axis_index("dp") * row_size + lax.axis_index("row")) % jobs
    my_row = lax.axis_index("row")
    my_chunk = lax.axis_index("col") * chunk

    weights = (qkv_weight, proj_weight, up_weight, down_weight)
    moments = (qkv_moment, proj_moment, up_moment, down_moment)
    flipped = (False, True, False, True)

    def upright(array, kind_index, level_index):
        block = array[level_index]
        return block.T if flipped[kind_index] else block

    widths = [
        w.shape[1] if flipped[k] else w.shape[2] for k, w in enumerate(weights)
    ]
    widest = max(widths)

    def gathered_weights(level_index, which):
        parts = [upright(weights[k], k, level_index).astype(jnp.bfloat16) for k in which]
        whole = gather_by_pairs(jnp.concatenate(parts, axis=1), "row")
        whole = whole.reshape(model_width, -1)
        result = []
        start = 0
        for k in which:
            result.append(whole[:, start : start + widths[k]])
            start += widths[k]
        return result

    def features_first(blocks):
        return blocks.transpose(1, 0, 2).reshape(blocks.shape[1], model_width)

    def own_chunk(values):
        return lax.dynamic_slice_in_dim(pad_rows(values, padded), my_chunk, chunk, 0)

    all_norms = gather_by_pairs(norm_params, "row")
    all_norms = all_norms.transpose(1, 2, 0, 3).reshape(levels, kinds, model_width)
    image = features_first(to_all(swap_row_col(residual_in), "col")).astype(jnp.float32)
    weight_sets = []
    for level_index in range(levels):
        attention = gathered_weights(level_index, (0, 1))
        perceptron = gathered_weights(level_index, (2, 3))
        weight_sets.append(attention + perceptron)
    upstream_image = features_first(gather_by_pairs(swap_row_col(cotangent), "col"))

    stacked_moment = jnp.stack(
        [
            pad_columns(upright(moments[j // levels], j // levels, j % levels), widest)
            for j in range(jobs)
        ]
    )
    moment_parts = [pick(stacked_moment, me)]
    for step in range(1, row_size):
        moment_parts.append(from_partner(pick(stacked_moment, me ^ step), step))
    own_moment = placed_blocks(moment_parts, [my_row ^ i for i in range(row_size)])
    own_moment = own_moment.reshape(model_width, widest)

    stream = own_chunk(image)
    saved = []
    early = []
    for level_index in range(levels):
        weight_qkv, weight_proj, weight_up, weight_down = weight_sets[level_index]
        gains = all_norms[level_index]
        plain_one, inverse_one = norm_parts_of(stream)
        if level_index == 0:
            normed_one = (norm_parts_of(image)[0] * gains[0] + gains[1]).astype(jnp.bfloat16)
        else:
            normed_one = gather_tokens(
                (plain_one * gains[0] + gains[1]).astype(jnp.bfloat16)
            )[:tokens]
        mixed_low = product(normed_one, weight_qkv).astype(jnp.bfloat16)
        attended, log_total = attend_forward(mixed_low)
        stream = stream + sum_tokens(product_flipped(attended, weight_proj), padded)
        plain_two, inverse_two = norm_parts_of(stream)
        normed_two = gather_tokens((plain_two * gains[2] + gains[3]).astype(jnp.bfloat16))[:tokens]
        hidden = product(normed_two, weight_up)
        activated = jax.nn.gelu(hidden, approximate=False).astype(jnp.bfloat16)
        stream = stream + sum_tokens(product_flipped(activated, weight_down), padded)
        saved.append((plain_one, inverse_one, mixed_low, log_total, plain_two, inverse_two, hidden))
        early.append((normed_one, attended, normed_two, activated))

    def sent_form(values):
        return pad_rows(pad_columns(values, widest), sent_rows)

    early_stack = jnp.stack([sent_form(early[j % levels][j // levels]) for j in range(jobs)])
    early_all = [pick(early_stack, me)]
    for step in range(1, jobs):
        early_all.append(from_partner(pick(early_stack, me ^ step), step))

    def send_late(parts, level_index):
        stack = jnp.stack([sent_form(part) for part in parts])
        received = [pick(stack, me // levels)]
        for step in range(1, jobs):
            received.append(
                from_partner(
                    pick(stack, (me ^ step) // levels),
                    step,
                    wanted=lambda i: i % levels == level_index,
                )
            )
        return received

    upstream = own_chunk(upstream_image)
    back_two = upstream_image.astype(jnp.bfloat16)
    upstream, own_moment = lax.optimization_barrier((upstream, own_moment))
    late = [None] * levels
    norm_sums = [None] * levels
    for level_index in reversed(range(levels)):
        weight_qkv, weight_proj, weight_up, weight_down = weight_sets[level_index]
        plain_one, inverse_one, mixed_low, log_total, plain_two, inverse_two, hidden = saved[
            level_index
        ]
        gains = all_norms[level_index]
        if level_index < levels - 1:
            back_two = gather_tokens(upstream.astype(jnp.bfloat16))[:tokens]
        act_grad = product(back_two, weight_down)
        hidden_grad = jax.vjp(lambda inner: jax.nn.gelu(inner, approximate=False), hidden)[1](
            act_grad
        )[0].astype(jnp.bfloat16)
        normed_grad_two = sum_tokens(product_flipped(hidden_grad, weight_up), padded)
        upstream = upstream + norm_backward(normed_grad_two, plain_two, inverse_two, gains[2])
        if level_index == levels - 1:
            upstream, early_all = lax.optimization_barrier((upstream, early_all))
        else:
            upstream, late[level_index + 1] = lax.optimization_barrier(
                (upstream, late[level_index + 1])
            )
        back_one = gather_tokens(upstream.astype(jnp.bfloat16))[:tokens]
        att_grad = product(back_one, weight_proj).astype(jnp.bfloat16)
        mixed_grad = attend_backward(mixed_low, log_total, att_grad)
        normed_grad_one = sum_tokens(product_flipped(mixed_grad, weight_qkv), padded)
        upstream = upstream + norm_backward(normed_grad_one, plain_one, inverse_one, gains[0])
        norm_sums[level_index] = jnp.stack(
            (
                jnp.sum(normed_grad_one * plain_one, axis=0),
                jnp.sum(normed_grad_one, axis=0),
                jnp.sum(normed_grad_two * plain_two, axis=0),
                jnp.sum(normed_grad_two, axis=0),
            )
        )
        late[level_index] = send_late(
            (mixed_grad, back_one, hidden_grad, back_two), level_index
        )

    norm_whole = jnp.stack(norm_sums)
    for axis in ("row", "col", "dp"):
        norm_whole = sum_by_pairs(norm_whole, axis)
    norm_grad = lax.dynamic_slice_in_dim(norm_whole, my_row * width_row, width_row, 2)
    norm_moment_new = moment_decay * norm_moment + norm_grad

    early_all = jnp.concatenate(early_all, axis=0)
    late_all = jnp.concatenate(late[0], axis=0)
    for level_index in range(1, levels):
        late_all = jnp.where(
            me % levels == level_index, jnp.concatenate(late[level_index], axis=0), late_all
        )
    turned = (me // levels) % 2 == 1
    model_side = jnp.where(turned, late_all, early_all)
    hidden_side = jnp.where(turned, early_all, late_all)
    own_grad = outer_grad(model_side, hidden_side)
    step = jobs // row_size
    while step < dp_size:
        pairs = [(i, i ^ step) for i in range(dp_size)]
        own_grad = own_grad + lax.ppermute(own_grad, "dp", pairs)
        step *= 2

    def returned(whole):
        blocks = whole.astype(jnp.bfloat16).reshape(row_size, width_row, widest)
        received = [pick(blocks, my_row)]
        for step in range(1, jobs):
            received.append(from_partner(pick(blocks, (me ^ step) % row_size), step))
        received = placed_blocks(received, [me ^ j for j in range(jobs)])
        return [received[j].astype(jnp.float32) for j in range(jobs)]

    grads = returned(own_grad)
    orths = returned(schulz(moment_decay * own_moment + own_grad))

    grad_outs = []
    moment_outs = []
    new_outs = []
    for kind_index in range(kinds):
        grad_levels = []
        orth_levels = []
        for level_index in range(levels):
            job = kind_index * levels + level_index
            grad_here = grads[job][:, : widths[kind_index]]
            orth_here = orths[job][:, : widths[kind_index]]
            if flipped[kind_index]:
                grad_here = grad_here.T
                orth_here = orth_here.T
            grad_levels.append(grad_here)
            orth_levels.append(orth_here)
        grad_out = jnp.stack(grad_levels)
        grad_outs.append(grad_out)
        moment_outs.append(moment_decay * moments[kind_index] + grad_out)
        new_outs.append(weights[kind_index] - step_rates[kind_index] * jnp.stack(orth_levels))

    def placed(chunk_values):
        blocks = chunk_values.reshape(chunk, col_size, width_row).transpose(1, 0, 2)
        blocks = lax.all_to_all(blocks, "col", 0, 0)
        return swap_row_col(blocks.reshape(padded, width_row)[:tokens])

    tokens_all = tokens * col_size * dp_size
    norm_new = norm_params - norm_rate / math.sqrt(tokens_all) * norm_moment_new
    return (
        placed(stream),
        placed(upstream),
        *grad_outs,
        norm_grad,
        *moment_outs,
        norm_moment_new,
        *new_outs,
        norm_new,
    )


def solution(mesh):
    tokens_spec = P(("dp", "col"), "row")
    wide = P(None, "row", "col")
    tall = P(None, "col", "row")
    norms = P(None, None, "row")
    return jax.shard_map(
        on_device,
        mesh=mesh,
        in_specs=(tokens_spec, tokens_spec) + (wide, tall, wide, tall, norms) * 2,
        out_specs=(tokens_spec, tokens_spec) + (wide, tall, wide, tall, norms) * 3,
        check_vma=False,
    )
```

profile of v0, /device:TPU:15, one launch (start us, length us, event | category | flops | bytes accessed | tf_op | source)
XLA Modules:
  0.0 670.4 jit_solution(2936411174013528455)
XLA Ops:
  0.7 4.3 collective-permute-start.12
  14.4 3.1 dynamic-slice_bitcast_fusion
  17.6 3.2 collective-permute-start
  39.1 5.2 all-to-all-start
  46.8 5.7 dynamic_update_slice.158
  66.1 5.7 dynamic_update_slice.159
  86.1 5.4 all-to-all-start.1
  91.6 10.3 %collective-permute-done.5 = bf16[1,192,1536]{2,1,0:T(8,128)(2,1)S(1)} collective-permute-done((bf16[1,192,1536]{2,1,0:T(8,128)(2,1)}, bf16[1,192,1536]{2,1,0:T(8,128)(2,1)S(1)}, u32[]{:S(2)}, u32[]{:S(2)}) %collective-permute-start.5) | collective-permute-done | bytes 589856 | tf_op jit(solution)/shard_map/ppermute | solution.py:124
  110.0 5.4 all-to-all-start.2
  119.8 4.0 all-to-all-done.2
  123.8 3.9 multiply_convert_fusion.3
  131.0 5.2 all-to-all-start.3
  144.4 5.6 all-to-all-start.4
  154.9 5.7 dynamic_update_slice.160
  160.6 5.7 dynamic_update_slice.161
  177.9 4.5 all-to-all-start.5
  190.6 4.3 all-to-all-start.6
  201.1 3.7 multiply_convert_fusion.2
  209.9 3.7 all-to-all-start.9
  218.8 3.2 dynamic-slice_bitcast_fusion.18
  222.0 6.3 collective-permute-start.18
  235.1 4.5 all-to-all-start.7
  244.1 3.9 all-to-all-done.7
  253.5 7.1 %collective-permute-done.24 = bf16[208,768]{1,0:T(8,128)(2,1)} collective-permute-done((bf16[208,768]{1,0:T(8,128)(2,1)}, bf16[208,768]{1,0:T(8,128)(2,1)}, u32[]{:S(2)}, u32[]{:S(2)}) %collective-permute-start.24) | collective-permute-done | bytes 319520 | tf_op jit(solution)/shard_map/ppermute | solution.py:124
  261.4 4.6 all-to-all-start.10
  274.3 6.1 all-to-all-start.8
  285.8 4.9 all-to-all-start.11
  300.3 4.8 collective-permute-start.11
  306.9 7.1 %all-to-all-start.12 = ((bf16[4,56,768]{2,1,0:T(8,128)(2,1)}), bf16[4,56,768]{2,1,0:T(8,128)(2,1)S(1)}, u32[]{:S(2)}, u32[]{:S(2)}) async-start(bf16[4,56,768]{2,1,0:T(8,128)(2,1)} %broadcast_in_dim.200), calls=%async_computation.12 | async-start | bytes 688128 | tf_op jit(solution)/shard_map/all_to_all | solution.py:161
  328.1 6.1 all-to-all-start.13
  347.4 4.3 collective-permute-start.30
  354.1 3.6 collective-permute-done.30
  357.7 3.4 collective-permute-done.31
  362.6 4.5 all-to-all-start.14
  390.2 4.5 all-to-all-start.15
  398.5 3.6 collective-permute-start.37
  404.0 4.8 collective-permute-start.39
  410.0 4.4 collective-permute-done.39
  414.4 6.0 multiply_add_fusion.12
  430.0 4.5 all-to-all-start.17
  446.1 15.2 %collective-permute-done.49 = f32[2,4,768]{2,1,0:T(4,128)} collective-permute-done((f32[2,4,768]{2,1,0:T(4,128)}, f32[2,4,768]{2,1,0:T(4,128)}, u32[]{:S(2)}, u32[]{:S(2)}) %collective-permute-start.49) | collective-permute-done | bytes 24608 | tf_op jit(solution)/shard_map/ppermute | solution.py:124
  474.5 3.8 collective-permute-done.45
  479.0 4.8 collective-permute-done.46
  487.5 4.9 all-to-all-start.18
  501.9 23.2 %all-to-all-done.18 = f32[4,64,1536]{2,1,0:T(8,128)} async-done(((f32[4,64,1536]{2,1,0:T(8,128)}), f32[4,64,1536]{2,1,0:T(8,128)}, u32[]{:S(2)}, u32[]{:S(2)}) %all-to-all-start.18) | async-done | bytes 1572896 | tf_op jit(solution)/shard_map/all_to_all | solution.py:161
  525.1 9.4 %all-to-all-start.16 = ((f32[4,56,192]{2,1,0:T(8,128)}), f32[4,56,192]{2,1,0:T(8,128)}, u32[]{:S(2)}, u32[]{:S(2)}) async-start(f32[4,56,192]{2,1,0:T(8,128)} %bitcast.451), calls=%async_computation.16 | async-start | bytes 458752 | tf_op jit(solution)/shard_map/all_to_all | solution.py:444
  553.1 5.9 multiply_add_fusion.3
  561.2 3.6 multiply_add_fusion.10
  567.8 5.9 multiply_add_fusion.2
  575.9 3.2 multiply_add_fusion.8
  579.1 3.2 fusion.175
  582.3 5.9 multiply_add_fusion.1
  590.3 3.2 multiply_add_fusion.6
  593.5 3.3 fusion.176
  596.8 5.9 multiply_add_fusion
  602.6 3.2 multiply_add_fusion.4
  605.8 3.3 fusion.177
  609.1 3.2 add_convert_fusion
  617.7 4.7 collective-permute-start.32
  623.8 7.4 %collective-permute-done.32 = f32[197,192]{1,0:T(8,128)S(1)} collective-permute-done((f32[197,192]{1,0:T(8,128)S(1)}, f32[197,192]{1,0:T(8,128)S(1)}, u32[]{:S(2)}, u32[]{:S(2)}) %collective-permute-start.32) | collective-permute-done | bytes 151328 | tf_op jit(solution)/shard_map/ppermute | solution.py:118
  638.1 3.6 collective-permute-done.54
  641.8 7.0 %collective-permute-done.56 = bf16[192,768]{1,0:T(8,128)(2,1)S(1)} collective-permute-done((bf16[192,768]{1,0:T(8,128)(2,1)}, bf16[192,768]{1,0:T(8,128)(2,1)S(1)}, u32[]{:S(2)}, u32[]{:S(2)}) %collective-permute-start.56) | collective-permute-done | bytes 294944 | tf_op jit(solution)/shard_map/ppermute | solution.py:124
  648.8 7.1 %collective-permute-done.57 = bf16[192,768]{1,0:T(8,128)(2,1)S(1)} collective-permute-done((bf16[192,768]{1,0:T(8,128)(2,1)}, bf16[192,768]{1,0:T(8,128)(2,1)S(1)}, u32[]{:S(2)}, u32[]{:S(2)}) %collective-permute-start.57) | collective-permute-done | bytes 294944 | tf_op jit(solution)/shard_map/ppermute | solution.py:124
  655.9 6.3 collective-permute-done.58
  (557 shorter events, 322.9 us)
Async XLA Ops:
  0.7 43.7 %collective-permute-start.12 = (f32[197,192]{0,1:T(8,128)}, f32[197,192]{0,1:T(8,128)}, u32[]{:S(2)}, u32[]{:S(2)}) collective-permute-start(f32[197,192]{0,1:T(8,128)} %param.13), channel_id=1, source_target_pairs={{0,0},{1,4},{2,8},{3,12},{4,1},{5,5},{6,9},{7,13},{8,2},{9,6},{10,... | collective-permute-start | bytes 453896 | tf_op jit(solution)/shard_map/ppermute | solution.py:118
  17.6 120.3 %collective-permute-start.15 = (f32[192,768]{1,0:T(8,128)}, f32[192,768]{1,0:T(8,128)}, u32[]{:S(2)}, u32[]{:S(2)}) collective-permute-start(f32[192,768]{1,0:T(8,128)} %get-tuple-element.170), channel_id=1, source_target_pairs={{0,4},{4,0},{8,12},{12,8},{16,20},{20,16},{24,28},{28,24},{1,5},{5... | collective-permute-start | bytes 1769480 | tf_op jit(solution)/shard_map/ppermute | solution.py:124
  17.6 18.6 %collective-permute-start = (bf16[197,192]{0,1:T(8,128)(2,1)}, bf16[197,192]{0,1:T(8,128)(2,1)}, u32[]{:S(2)}, u32[]{:S(2)}) collective-permute-start(bf16[197,192]{0,1:T(8,128)(2,1)} %param.12), channel_id=1, source_target_pairs={{0,0},{1,4},{2,8},{3,12},{4,1},{5,5},{6,9},{7,13},{8,2},{9,6},{10,... | collective-permute-start | bytes 226952 | tf_op jit(solution)/shard_map/ppermute | solution.py:118
  20.8 12.9 %collective-permute-start.1 = (f32[1,2,4,192]{3,2,1,0:T(4,128)S(1)}, f32[1,2,4,192]{3,2,1,0:T(4,128)S(1)}, u32[]{:S(2)}, u32[]{:S(2)}) collective-permute-start(f32[1,2,4,192]{3,2,1,0:T(4,128)S(1)} %bitcast.498), channel_id=1, source_target_pairs={{0,8},{4,12},{8,0},{12,4},{1,9},{5,13},{9,1},{13,5},{2,10},{6,14},... | collective-permute-start | bytes 18440 | tf_op jit(solution)/shard_map/ppermute | solution.py:124
  23.9 28.7 %collective-permute-start.7 = (bf16[1,192,768]{2,1,0:T(8,128)(2,1)}, bf16[1,192,768]{2,1,0:T(8,128)(2,1)}, u32[]{:S(2)}, u32[]{:S(2)}) collective-permute-start(bf16[1,192,768]{2,1,0:T(8,128)(2,1)} %get-tuple-element.162), channel_id=1, source_target_pairs={{0,8},{4,12},{8,0},{12,4},{1,9},{5,13},{9,1},{13,5},{2,10},{6,14},... | collective-permute-start | bytes 884744 | tf_op jit(solution)/shard_map/ppermute | solution.py:124
  35.3 23.0 %collective-permute-start.3 = (bf16[1,192,768]{2,1,0:T(8,128)(2,1)S(1)}, bf16[1,192,768]{2,1,0:T(8,128)(2,1)}, u32[]{:S(2)}, u32[]{:S(2)}) collective-permute-start(bf16[1,192,768]{2,1,0:T(8,128)(2,1)S(1)} %get-tuple-element.167), channel_id=1, source_target_pairs={{0,8},{4,12},{8,0},{12,4},{1,9},{5,13},{9,1},{13,5},{2,10},{6,14},... | collective-permute-start | bytes 884744 | tf_op jit(solution)/shard_map/ppermute | solution.py:124
  36.1 103.7 %collective-permute-start.16 = (f32[192,768]{1,0:T(8,128)}, f32[192,768]{1,0:T(8,128)}, u32[]{:S(2)}, u32[]{:S(2)}) collective-permute-start(f32[192,768]{1,0:T(8,128)} %get-tuple-element.169), channel_id=1, source_target_pairs={{0,8},{4,12},{8,0},{12,4},{16,24},{20,28},{24,16},{28,20},{1,9},{5... | collective-permute-start | bytes 1769480 | tf_op jit(solution)/shard_map/ppermute | solution.py:124
  39.1 34.5 %all-to-all-start = ((bf16[4,197,192]{1,2,0:T(8,128)(2,1)}), bf16[4,197,192]{1,2,0:T(8,128)(2,1)S(1)}, u32[]{:S(2)}, u32[]{:S(2)}) async-start(bf16[4,197,192]{1,2,0:T(8,128)(2,1)} %broadcast_in_dim.183), calls=%async_computation | async-start | bytes 786432 | tf_op jit(solution)/shard_map/all_to_all | solution.py:161
  44.4 30.0 %collective-permute-start.9 = (bf16[1,192,1536]{2,1,0:T(8,128)(2,1)}, bf16[1,192,1536]{2,1,0:T(8,128)(2,1)}, u32[]{:S(2)}, u32[]{:S(2)}) collective-permute-start(bf16[1,192,1536]{2,1,0:T(8,128)(2,1)} %maximum_bitcast_fusion.1), channel_id=1, source_target_pairs={{0,8},{4,12},{8,0},{12,4},{1,9},{5,13},{9,1},{13,5},{2,10},{6,14},... | collective-permute-start | bytes 1769480 | tf_op jit(solution)/shard_map/ppermute | solution.py:124
  58.3 18.6 %collective-permute-start.8 = (bf16[2,192,768]{2,1,0:T(8,128)(2,1)}, bf16[2,192,768]{2,1,0:T(8,128)(2,1)}, u32[]{:S(2)}, u32[]{:S(2)}) collective-permute-start(bf16[2,192,768]{2,1,0:T(8,128)(2,1)} %pad_maximum_fusion.22), channel_id=1, source_target_pairs={{0,4},{4,0},{8,12},{12,8},{1,5},{5,1},{9,13},{13,9},{2,6},{6,2},{1... | collective-permute-start | bytes 1769480 | tf_op jit(solution)/shard_map/ppermute | solution.py:124
  64.5 13.6 %collective-permute-start.4 = (bf16[2,192,768]{2,1,0:T(8,128)(2,1)}, bf16[2,192,768]{2,1,0:T(8,128)(2,1)}, u32[]{:S(2)}, u32[]{:S(2)}) collective-permute-start(bf16[2,192,768]{2,1,0:T(8,128)(2,1)} %pad_maximum_fusion.21), channel_id=1, source_target_pairs={{0,4},{4,0},{8,12},{12,8},{1,5},{5,1},{9,13},{13,9},{2,6},{6,2},{1... | collective-permute-start | bytes 1769480 | tf_op jit(solution)/shard_map/ppermute | solution.py:124
  74.3 75.7 %collective-permute-start.17 = (f32[192,768]{1,0:T(8,128)}, f32[192,768]{1,0:T(8,128)}, u32[]{:S(2)}, u32[]{:S(2)}) collective-permute-start(f32[192,768]{1,0:T(8,128)} %get-tuple-element.168), channel_id=1, source_target_pairs={{0,12},{4,8},{8,4},{12,0},{16,28},{20,24},{24,20},{28,16},{1,13},{... | collective-permute-start | bytes 1769480 | tf_op jit(solution)/shard_map/ppermute | solution.py:124
  76.9 24.9 %collective-permute-start.5 = (bf16[1,192,1536]{2,1,0:T(8,128)(2,1)}, bf16[1,192,1536]{2,1,0:T(8,128)(2,1)S(1)}, u32[]{:S(2)}, u32[]{:S(2)}) collective-permute-start(bf16[1,192,1536]{2,1,0:T(8,128)(2,1)} %maximum_bitcast_fusion), channel_id=1, source_target_pairs={{0,8},{4,12},{8,0},{12,4},{1,9},{5,13},{9,1},{13,5},{2,10},{6,14},... | collective-permute-start | bytes 1769480 | tf_op jit(solution)/shard_map/ppermute | solution.py:124
  78.1 37.3 %collective-permute-start.10 = (bf16[2,192,1536]{2,1,0:T(8,128)(2,1)}, bf16[2,192,1536]{2,1,0:T(8,128)(2,1)}, u32[]{:S(2)}, u32[]{:S(2)}) collective-permute-start(bf16[2,192,1536]{2,1,0:T(8,128)(2,1)} %pad_maximum_fusion.20), channel_id=1, source_target_pairs={{0,4},{4,0},{8,12},{12,8},{1,5},{5,1},{9,13},{13,9},{2,6},{6,2},{1... | collective-permute-start | bytes 3538952 | tf_op jit(solution)/shard_map/ppermute | solution.py:124
  86.1 21.7 %all-to-all-start.1 = ((bf16[4,56,768]{2,1,0:T(8,128)(2,1)}), bf16[4,56,768]{2,1,0:T(8,128)(2,1)}, u32[]{:S(2)}, u32[]{:S(2)}) async-start(bf16[4,56,768]{2,1,0:T(8,128)(2,1)} %bitcast.477), calls=%async_computation.1 | async-start | bytes 688128 | tf_op jit(solution)/shard_map/all_to_all | solution.py:173
  104.0 11.4 %collective-permute-start.6 = (bf16[2,192,1536]{2,1,0:T(8,128)(2,1)}, bf16[2,192,1536]{2,1,0:T(8,128)(2,1)}, u32[]{:S(2)}, u32[]{:S(2)}) collective-permute-start(bf16[2,192,1536]{2,1,0:T(8,128)(2,1)} %pad_maximum_fusion.19), channel_id=1, source_target_pairs={{0,4},{4,0},{8,12},{12,8},{1,5},{5,1},{9,13},{13,9},{2,6},{6,2},{1... | collective-permute-start | bytes 3538952 | tf_op jit(solution)/shard_map/ppermute | solution.py:124
  110.0 13.8 %all-to-all-start.2 = ((bf16[4,56,768]{2,1,0:T(8,128)(2,1)}), bf16[4,56,768]{2,1,0:T(8,128)(2,1)S(1)}, u32[]{:S(2)}, u32[]{:S(2)}) async-start(bf16[4,56,768]{2,1,0:T(8,128)(2,1)} %broadcast_in_dim.187), calls=%async_computation.2 | async-start | bytes 688128 | tf_op jit(solution)/shard_map/all_to_all | solution.py:161
  115.4 36.5 %collective-permute-start.14 = (f32[2,197,192]{1,2,0:T(8,128)}, f32[2,197,192]{1,2,0:T(8,128)}, u32[]{:S(2)}, u32[]{:S(2)}) collective-permute-start(f32[2,197,192]{1,2,0:T(8,128)} %pad_maximum_fusion.23), channel_id=1, source_target_pairs={{0,1},{1,0},{2,3},{3,2},{4,5},{5,4},{6,7},{7,6},{8,9},{9,8},{10,11... | collective-permute-start | bytes 907784 | tf_op jit(solution)/shard_map/ppermute | solution.py:124
  131.0 12.4 %all-to-all-start.3 = ((bf16[4,56,768]{2,1,0:T(8,128)(2,1)}), bf16[4,56,768]{2,1,0:T(8,128)(2,1)S(1)}, u32[]{:S(2)}, u32[]{:S(2)}) async-start(bf16[4,56,768]{2,1,0:T(8,128)(2,1)} %bitcast.476), calls=%async_computation.3 | async-start | bytes 688128 | tf_op jit(solution)/shard_map/all_to_all | solution.py:173
  144.4 26.2 %all-to-all-start.4 = ((bf16[4,56,768]{2,1,0:T(8,128)(2,1)}), bf16[4,56,768]{2,1,0:T(8,128)(2,1)}, u32[]{:S(2)}, u32[]{:S(2)}) async-start(bf16[4,56,768]{2,1,0:T(8,128)(2,1)} %broadcast_in_dim.189), calls=%async_computation.4 | async-start | bytes 688128 | tf_op jit(solution)/shard_map/all_to_all | solution.py:161
  209.9 24.4 %all-to-all-start.9 = ((bf16[4,56,768]{2,1,0:T(8,128)(2,1)}), bf16[4,56,768]{2,1,0:T(8,128)(2,1)S(1)}, u32[]{:S(2)}, u32[]{:S(2)}) async-start(bf16[4,56,768]{2,1,0:T(8,128)(2,1)} %bitcast.474), calls=%async_computation.9 | async-start | bytes 688128 | tf_op jit(solution)/shard_map/all_to_all | solution.py:173
  222.0 18.9 %collective-permute-start.18 = (bf16[208,768]{1,0:T(8,128)(2,1)}, bf16[208,768]{1,0:T(8,128)(2,1)}, u32[]{:S(2)}, u32[]{:S(2)}) collective-permute-start(bf16[208,768]{1,0:T(8,128)(2,1)} %get-tuple-element.178), channel_id=1, source_target_pairs={{0,4},{4,0},{8,12},{12,8},{16,20},{20,16},{24,28},{28,24},{1,5},{5... | collective-permute-start | bytes 958472 | tf_op jit(solution)/shard_map/ppermute | solution.py:124
  228.3 13.5 %collective-permute-start.19 = (bf16[208,768]{1,0:T(8,128)(2,1)}, bf16[208,768]{1,0:T(8,128)(2,1)}, u32[]{:S(2)}, u32[]{:S(2)}) collective-permute-start(bf16[208,768]{1,0:T(8,128)(2,1)} %get-tuple-element.177), channel_id=1, source_target_pairs={{0,8},{4,12},{8,0},{12,4},{16,24},{20,28},{24,16},{28,20},{1,9},{5... | collective-permute-start | bytes 958472 | tf_op jit(solution)/shard_map/ppermute | solution.py:124
  229.1 21.6 %collective-permute-start.20 = (bf16[208,768]{1,0:T(8,128)(2,1)}, bf16[208,768]{1,0:T(8,128)(2,1)}, u32[]{:S(2)}, u32[]{:S(2)}) collective-permute-start(bf16[208,768]{1,0:T(8,128)(2,1)} %get-tuple-element.176), channel_id=1, source_target_pairs={{0,12},{4,8},{8,4},{12,0},{16,28},{20,24},{24,20},{28,16},{1,13},{... | collective-permute-start | bytes 958472 | tf_op jit(solution)/shard_map/ppermute | solution.py:124
  230.0 20.7 %collective-permute-start.21 = (bf16[208,768]{1,0:T(8,128)(2,1)}, bf16[208,768]{1,0:T(8,128)(2,1)}, u32[]{:S(2)}, u32[]{:S(2)}) collective-permute-start(bf16[208,768]{1,0:T(8,128)(2,1)} %get-tuple-element.175), channel_id=1, source_target_pairs={{0,16},{4,20},{8,24},{12,28},{16,0},{20,4},{24,8},{28,12},{1,17},{... | collective-permute-start | bytes 958472 | tf_op jit(solution)/shard_map/ppermute | solution.py:124
  230.2 20.5 %collective-permute-start.22 = (bf16[208,768]{1,0:T(8,128)(2,1)}, bf16[208,768]{1,0:T(8,128)(2,1)}, u32[]{:S(2)}, u32[]{:S(2)}) collective-permute-start(bf16[208,768]{1,0:T(8,128)(2,1)} %get-tuple-element.174), channel_id=1, source_target_pairs={{0,20},{4,16},{8,28},{12,24},{16,4},{20,0},{24,12},{28,8},{1,21},{... | collective-permute-start | bytes 958472 | tf_op jit(solution)/shard_map/ppermute | solution.py:124
  235.1 13.0 %all-to-all-start.7 = ((bf16[4,56,768]{2,1,0:T(8,128)(2,1)}), bf16[4,56,768]{2,1,0:T(8,128)(2,1)}, u32[]{:S(2)}, u32[]{:S(2)}) async-start(bf16[4,56,768]{2,1,0:T(8,128)(2,1)} %bitcast.475), calls=%async_computation.7 | async-start | bytes 688128 | tf_op jit(solution)/shard_map/all_to_all | solution.py:173
  240.9 12.5 %collective-permute-start.23 = (bf16[208,768]{1,0:T(8,128)(2,1)}, bf16[208,768]{1,0:T(8,128)(2,1)}, u32[]{:S(2)}, u32[]{:S(2)}) collective-permute-start(bf16[208,768]{1,0:T(8,128)(2,1)} %get-tuple-element.173), channel_id=1, source_target_pairs={{0,24},{4,28},{8,16},{12,20},{16,8},{20,12},{24,0},{28,4},{1,25},{... | collective-permute-start | bytes 958472 | tf_op jit(solution)/shard_map/ppermute | solution.py:124
  241.8 18.8 %collective-permute-start.24 = (bf16[208,768]{1,0:T(8,128)(2,1)}, bf16[208,768]{1,0:T(8,128)(2,1)}, u32[]{:S(2)}, u32[]{:S(2)}) collective-permute-start(bf16[208,768]{1,0:T(8,128)(2,1)} %get-tuple-element.172), channel_id=1, source_target_pairs={{0,28},{4,24},{8,20},{12,16},{16,12},{20,8},{24,4},{28,0},{1,29},{... | collective-permute-start | bytes 958472 | tf_op jit(solution)/shard_map/ppermute | solution.py:124
  261.4 13.0 %all-to-all-start.10 = ((bf16[4,56,768]{2,1,0:T(8,128)(2,1)}), bf16[4,56,768]{2,1,0:T(8,128)(2,1)}, u32[]{:S(2)}, u32[]{:S(2)}) async-start(bf16[4,56,768]{2,1,0:T(8,128)(2,1)} %broadcast_in_dim.199), calls=%async_computation.10 | async-start | bytes 688128 | tf_op jit(solution)/shard_map/all_to_all | solution.py:161
  274.3 11.5 %all-to-all-start.8 = ((f32[4,56,192]{2,1,0:T(8,128)}), f32[4,56,192]{2,1,0:T(8,128)}, u32[]{:S(2)}, u32[]{:S(2)}) async-start(f32[4,56,192]{2,1,0:T(8,128)} %bitcast.452), calls=%async_computation.8 | async-start | bytes 458752 | tf_op jit(solution)/shard_map/all_to_all | solution.py:444
  285.8 19.2 %all-to-all-start.11 = ((bf16[4,56,768]{2,1,0:T(8,128)(2,1)}), bf16[4,56,768]{2,1,0:T(8,128)(2,1)S(1)}, u32[]{:S(2)}, u32[]{:S(2)}) async-start(bf16[4,56,768]{2,1,0:T(8,128)(2,1)} %bitcast.99), calls=%async_computation.11 | async-start | bytes 688128 | tf_op jit(solution)/shard_map/all_to_all | solution.py:173
  300.3 17.3 %collective-permute-start.11 = (f32[197,192]{1,0:T(8,128)S(1)}, f32[197,192]{1,0:T(8,128)S(1)}, u32[]{:S(2)}, u32[]{:S(2)}) collective-permute-start(f32[197,192]{1,0:T(8,128)S(1)} %slice.504), channel_id=1, source_target_pairs={{0,0},{1,4},{2,8},{3,12},{4,1},{5,5},{6,9},{7,13},{8,2},{9,6},{10,... | collective-permute-start | bytes 453896 | tf_op jit(solution)/shard_map/ppermute | solution.py:118
  306.9 16.2 %all-to-all-start.12 = ((bf16[4,56,768]{2,1,0:T(8,128)(2,1)}), bf16[4,56,768]{2,1,0:T(8,128)(2,1)S(1)}, u32[]{:S(2)}, u32[]{:S(2)}) async-start(bf16[4,56,768]{2,1,0:T(8,128)(2,1)} %broadcast_in_dim.200), calls=%async_computation.12 | async-start | bytes 688128 | tf_op jit(solution)/shard_map/all_to_all | solution.py:161
  328.1 18.0 %all-to-all-start.13 = ((bf16[4,56,768]{2,1,0:T(8,128)(2,1)}), bf16[4,56,768]{2,1,0:T(8,128)(2,1)}, u32[]{:S(2)}, u32[]{:S(2)}) async-start(bf16[4,56,768]{2,1,0:T(8,128)(2,1)} %bitcast.101), calls=%async_computation.13 | async-start | bytes 688128 | tf_op jit(solution)/shard_map/all_to_all | solution.py:173
  338.5 13.1 %collective-permute-start.26 = (bf16[208,768]{1,0:T(8,128)(2,1)}, bf16[208,768]{1,0:T(8,128)(2,1)}, u32[]{:S(2)}, u32[]{:S(2)}) collective-permute-start(bf16[208,768]{1,0:T(8,128)(2,1)} %get-tuple-element.210), channel_id=1, source_target_pairs={{4,12},{12,4},{20,28},{28,20},{5,13},{13,5},{21,29},{29,21},{6,14}... | collective-permute-start | bytes 958472 | tf_op jit(solution)/shard_map/ppermute | solution.py:124
  340.5 13.6 %collective-permute-start.27 = (bf16[208,768]{1,0:T(8,128)(2,1)}, bf16[208,768]{1,0:T(8,128)(2,1)}, u32[]{:S(2)}, u32[]{:S(2)}) collective-permute-start(bf16[208,768]{1,0:T(8,128)(2,1)} %get-tuple-element.209), channel_id=1, source_target_pairs={{0,12},{8,4},{16,28},{24,20},{1,13},{9,5},{17,29},{25,21},{2,14},{... | collective-permute-start | bytes 958472 | tf_op jit(solution)/shard_map/ppermute | solution.py:124
  341.8 12.3 %collective-permute-start.28 = (bf16[208,768]{1,0:T(8,128)(2,1)}, bf16[208,768]{1,0:T(8,128)(2,1)S(1)}, u32[]{:S(2)}, u32[]{:S(2)}) collective-permute-start(bf16[208,768]{1,0:T(8,128)(2,1)} %get-tuple-element.208), channel_id=1, source_target_pairs={{4,20},{12,28},{20,4},{28,12},{5,21},{13,29},{21,5},{29,13},{6,22}... | collective-permute-start | bytes 958472 | tf_op jit(solution)/shard_map/ppermute | solution.py:124
  362.6 15.7 %all-to-all-start.14 = ((bf16[4,56,768]{2,1,0:T(8,128)(2,1)}), bf16[4,56,768]{2,1,0:T(8,128)(2,1)S(1)}, u32[]{:S(2)}, u32[]{:S(2)}) async-start(bf16[4,56,768]{2,1,0:T(8,128)(2,1)} %broadcast_in_dim.201), calls=%async_computation.14 | async-start | bytes 688128 | tf_op jit(solution)/shard_map/all_to_all | solution.py:161
  385.5 16.7 %collective-permute-start.33 = (bf16[208,768]{1,0:T(8,128)(2,1)}, bf16[208,768]{1,0:T(8,128)(2,1)}, u32[]{:S(2)}, u32[]{:S(2)}) collective-permute-start(bf16[208,768]{1,0:T(8,128)(2,1)} %get-tuple-element.204), channel_id=1, source_target_pairs={{4,0},{12,8},{20,16},{28,24},{5,1},{13,9},{21,17},{29,25},{6,2},{1... | collective-permute-start | bytes 958472 | tf_op jit(solution)/shard_map/ppermute | solution.py:124
  387.5 16.5 %collective-permute-start.34 = (bf16[208,768]{1,0:T(8,128)(2,1)}, bf16[208,768]{1,0:T(8,128)(2,1)}, u32[]{:S(2)}, u32[]{:S(2)}) collective-permute-start(bf16[208,768]{1,0:T(8,128)(2,1)} %get-tuple-element.203), channel_id=1, source_target_pairs={{0,8},{8,0},{16,24},{24,16},{1,9},{9,1},{17,25},{25,17},{2,10},{10... | collective-permute-start | bytes 958472 | tf_op jit(solution)/shard_map/ppermute | solution.py:124
  390.2 39.8 %all-to-all-start.15 = ((bf16[4,56,768]{2,1,0:T(8,128)(2,1)}), bf16[4,56,768]{2,1,0:T(8,128)(2,1)}, u32[]{:S(2)}, u32[]{:S(2)}) async-start(bf16[4,56,768]{2,1,0:T(8,128)(2,1)} %bitcast.123), calls=%async_computation.15 | async-start | bytes 688128 | tf_op jit(solution)/shard_map/all_to_all | solution.py:173
  394.7 15.1 %collective-permute-start.35 = (bf16[208,768]{1,0:T(8,128)(2,1)}, bf16[208,768]{1,0:T(8,128)(2,1)S(1)}, u32[]{:S(2)}, u32[]{:S(2)}) collective-permute-start(bf16[208,768]{1,0:T(8,128)(2,1)} %get-tuple-element.202), channel_id=1, source_target_pairs={{4,8},{12,0},{20,24},{28,16},{5,9},{13,1},{21,25},{29,17},{6,10},{... | collective-permute-start | bytes 958472 | tf_op jit(solution)/shard_map/ppermute | solution.py:124
  397.8 12.1 %collective-permute-start.36 = (bf16[208,768]{1,0:T(8,128)(2,1)}, bf16[208,768]{1,0:T(8,128)(2,1)S(1)}, u32[]{:S(2)}, u32[]{:S(2)}) collective-permute-start(bf16[208,768]{1,0:T(8,128)(2,1)} %get-tuple-element.201), channel_id=1, source_target_pairs={{0,16},{8,24},{16,0},{24,8},{1,17},{9,25},{17,1},{25,9},{2,18},{10... | collective-permute-start | bytes 958472 | tf_op jit(solution)/shard_map/ppermute | solution.py:124
  398.5 11.4 %collective-permute-start.37 = (bf16[208,768]{1,0:T(8,128)(2,1)}, bf16[208,768]{1,0:T(8,128)(2,1)S(1)}, u32[]{:S(2)}, u32[]{:S(2)}) collective-permute-start(bf16[208,768]{1,0:T(8,128)(2,1)} %get-tuple-element.200), channel_id=1, source_target_pairs={{4,16},{12,24},{20,0},{28,8},{5,17},{13,25},{21,1},{29,9},{6,18},{... | collective-permute-start | bytes 958472 | tf_op jit(solution)/shard_map/ppermute | solution.py:124
  425.4 38.5 %collective-permute-start.40 = (bf16[192,768]{1,0:T(8,128)(2,1)}, bf16[192,768]{1,0:T(8,128)(2,1)}, u32[]{:S(2)}, u32[]{:S(2)}) collective-permute-start(bf16[192,768]{1,0:T(8,128)(2,1)} %get-tuple-element.227), channel_id=1, source_target_pairs={{0,4},{4,0},{8,12},{12,8},{16,20},{20,16},{24,28},{28,24},{1,5},{5... | collective-permute-start | bytes 884744 | tf_op jit(solution)/shard_map/ppermute | solution.py:124
  425.9 41.2 %collective-permute-start.41 = (bf16[192,768]{1,0:T(8,128)(2,1)}, bf16[192,768]{1,0:T(8,128)(2,1)}, u32[]{:S(2)}, u32[]{:S(2)}) collective-permute-start(bf16[192,768]{1,0:T(8,128)(2,1)} %get-tuple-element.226), channel_id=1, source_target_pairs={{0,8},{4,12},{8,0},{12,4},{16,24},{20,28},{24,16},{28,20},{1,9},{5... | collective-permute-start | bytes 884744 | tf_op jit(solution)/shard_map/ppermute | solution.py:124
  426.7 42.3 %collective-permute-start.42 = (bf16[192,768]{1,0:T(8,128)(2,1)}, bf16[192,768]{1,0:T(8,128)(2,1)}, u32[]{:S(2)}, u32[]{:S(2)}) collective-permute-start(bf16[192,768]{1,0:T(8,128)(2,1)} %get-tuple-element.225), channel_id=1, source_target_pairs={{0,12},{4,8},{8,4},{12,0},{16,28},{20,24},{24,20},{28,16},{1,13},{... | collective-permute-start | bytes 884744 | tf_op jit(solution)/shard_map/ppermute | solution.py:124
  427.6 44.5 %collective-permute-start.43 = (bf16[192,768]{1,0:T(8,128)(2,1)}, bf16[192,768]{1,0:T(8,128)(2,1)}, u32[]{:S(2)}, u32[]{:S(2)}) collective-permute-start(bf16[192,768]{1,0:T(8,128)(2,1)} %get-tuple-element.224), channel_id=1, source_target_pairs={{0,16},{4,20},{8,24},{12,28},{16,0},{20,4},{24,8},{28,12},{1,17},{... | collective-permute-start | bytes 884744 | tf_op jit(solution)/shard_map/ppermute | solution.py:124
  430.0 54.6 %all-to-all-start.17 = ((f32[4,64,1536]{2,1,0:T(8,128)}), f32[4,64,1536]{2,1,0:T(8,128)}, u32[]{:S(2)}, u32[]{:S(2)}) async-start(f32[4,64,1536]{2,1,0:T(8,128)} %bitcast.454), calls=%async_computation.17 | async-start | bytes 3145728 | tf_op jit(solution)/shard_map/all_to_all | solution.py:192
  442.8 18.5 %collective-permute-start.49 = (f32[2,4,768]{2,1,0:T(4,128)}, f32[2,4,768]{2,1,0:T(4,128)}, u32[]{:S(2)}, u32[]{:S(2)}) collective-permute-start(f32[2,4,768]{2,1,0:T(4,128)} %fusion.207), channel_id=1, source_target_pairs={{0,1},{1,0},{2,3},{3,2},{4,5},{5,4},{6,7},{7,6},{8,9},{9,8},{10,11... | collective-permute-start | bytes 73736 | tf_op jit(solution)/shard_map/ppermute | solution.py:124
  461.2 12.5 %collective-permute-start.44 = (bf16[192,768]{1,0:T(8,128)(2,1)}, bf16[192,768]{1,0:T(8,128)(2,1)S(1)}, u32[]{:S(2)}, u32[]{:S(2)}) collective-permute-start(bf16[192,768]{1,0:T(8,128)(2,1)} %get-tuple-element.223), channel_id=1, source_target_pairs={{0,20},{4,16},{8,28},{12,24},{16,4},{20,0},{24,12},{28,8},{1,21},{... | collective-permute-start | bytes 884744 | tf_op jit(solution)/shard_map/ppermute | solution.py:124
  463.9 14.4 %collective-permute-start.45 = (bf16[192,768]{1,0:T(8,128)(2,1)}, bf16[192,768]{1,0:T(8,128)(2,1)S(1)}, u32[]{:S(2)}, u32[]{:S(2)}) collective-permute-start(bf16[192,768]{1,0:T(8,128)(2,1)} %get-tuple-element.222), channel_id=1, source_target_pairs={{0,24},{4,28},{8,16},{12,20},{16,8},{20,12},{24,0},{28,4},{1,25},{... | collective-permute-start | bytes 884744 | tf_op jit(solution)/shard_map/ppermute | solution.py:124
  467.1 16.7 %collective-permute-start.46 = (bf16[192,768]{1,0:T(8,128)(2,1)}, bf16[192,768]{1,0:T(8,128)(2,1)S(1)}, u32[]{:S(2)}, u32[]{:S(2)}) collective-permute-start(bf16[192,768]{1,0:T(8,128)(2,1)} %get-tuple-element.221), channel_id=1, source_target_pairs={{0,28},{4,24},{8,20},{12,16},{16,12},{20,8},{24,4},{28,0},{1,29},{... | collective-permute-start | bytes 884744 | tf_op jit(solution)/shard_map/ppermute | solution.py:124
  469.1 31.6 %collective-permute-start.50 = (f32[2,4,768]{2,1,0:T(4,128)S(1)}, f32[2,4,768]{2,1,0:T(4,128)S(1)}, u32[]{:S(2)}, u32[]{:S(2)}) collective-permute-start(f32[2,4,768]{2,1,0:T(4,128)S(1)} %add.549), channel_id=1, source_target_pairs={{0,2},{1,3},{2,0},{3,1},{4,6},{5,7},{6,4},{7,5},{8,10},{9,11},{10,... | collective-permute-start | bytes 73736 | tf_op jit(solution)/shard_map/ppermute | solution.py:124
  487.5 37.6 %all-to-all-start.18 = ((f32[4,64,1536]{2,1,0:T(8,128)}), f32[4,64,1536]{2,1,0:T(8,128)}, u32[]{:S(2)}, u32[]{:S(2)}) async-start(f32[4,64,1536]{2,1,0:T(8,128)} %broadcast_in_dim.209), calls=%async_computation.18 | async-start | bytes 3145728 | tf_op jit(solution)/shard_map/all_to_all | solution.py:161
  500.7 121.7 %collective-permute-start.51 = (f32[2,4,768]{2,1,0:T(4,128)S(1)}, f32[2,4,768]{2,1,0:T(4,128)}, u32[]{:S(2)}, u32[]{:S(2)}) collective-permute-start(f32[2,4,768]{2,1,0:T(4,128)S(1)} %add.550), channel_id=1, source_target_pairs={{0,16},{16,0},{1,17},{17,1},{2,18},{18,2},{3,19},{19,3},{4,20},{20... | collective-permute-start | bytes 73736 | tf_op jit(solution)/shard_map/ppermute | solution.py:124
  525.1 91.6 %all-to-all-start.16 = ((f32[4,56,192]{2,1,0:T(8,128)}), f32[4,56,192]{2,1,0:T(8,128)}, u32[]{:S(2)}, u32[]{:S(2)}) async-start(f32[4,56,192]{2,1,0:T(8,128)} %bitcast.451), calls=%async_computation.16 | async-start | bytes 458752 | tf_op jit(solution)/shard_map/all_to_all | solution.py:444
  613.8 20.8 %collective-permute-start.52 = (bf16[192,768]{1,0:T(8,128)(2,1)}, bf16[192,768]{1,0:T(8,128)(2,1)}, u32[]{:S(2)}, u32[]{:S(2)}) collective-permute-start(bf16[192,768]{1,0:T(8,128)(2,1)} %get-tuple-element.219), channel_id=1, source_target_pairs={{0,4},{4,0},{8,12},{12,8},{16,20},{20,16},{24,28},{28,24},{1,5},{5... | collective-permute-start | bytes 884744 | tf_op jit(solution)/shard_map/ppermute | solution.py:124
  617.7 13.6 %collective-permute-start.32 = (f32[197,192]{1,0:T(8,128)S(1)}, f32[197,192]{1,0:T(8,128)S(1)}, u32[]{:S(2)}, u32[]{:S(2)}) collective-permute-start(f32[197,192]{1,0:T(8,128)S(1)} %slice.516), channel_id=1, source_target_pairs={{0,0},{1,4},{2,8},{3,12},{4,1},{5,5},{6,9},{7,13},{8,2},{9,6},{10,... | collective-permute-start | bytes 453896 | tf_op jit(solution)/shard_map/ppermute | solution.py:118
  622.3 14.2 %collective-permute-start.53 = (bf16[192,768]{1,0:T(8,128)(2,1)}, bf16[192,768]{1,0:T(8,128)(2,1)S(1)}, u32[]{:S(2)}, u32[]{:S(2)}) collective-permute-start(bf16[192,768]{1,0:T(8,128)(2,1)} %get-tuple-element.218), channel_id=1, source_target_pairs={{0,8},{4,12},{8,0},{12,4},{16,24},{20,28},{24,16},{28,20},{1,9},{5... | collective-permute-start | bytes 884744 | tf_op jit(solution)/shard_map/ppermute | solution.py:124
  632.3 16.4 %collective-permute-start.56 = (bf16[192,768]{1,0:T(8,128)(2,1)}, bf16[192,768]{1,0:T(8,128)(2,1)S(1)}, u32[]{:S(2)}, u32[]{:S(2)}) collective-permute-start(bf16[192,768]{1,0:T(8,128)(2,1)} %get-tuple-element.215), channel_id=1, source_target_pairs={{0,20},{4,16},{8,28},{12,24},{16,4},{20,0},{24,12},{28,8},{1,21},{... | collective-permute-start | bytes 884744 | tf_op jit(solution)/shard_map/ppermute | solution.py:124
  634.6 21.3 %collective-permute-start.57 = (bf16[192,768]{1,0:T(8,128)(2,1)}, bf16[192,768]{1,0:T(8,128)(2,1)S(1)}, u32[]{:S(2)}, u32[]{:S(2)}) collective-permute-start(bf16[192,768]{1,0:T(8,128)(2,1)} %get-tuple-element.214), channel_id=1, source_target_pairs={{0,24},{4,28},{8,16},{12,20},{16,8},{20,12},{24,0},{28,4},{1,25},{... | collective-permute-start | bytes 884744 | tf_op jit(solution)/shard_map/ppermute | solution.py:124
  636.5 25.7 %collective-permute-start.58 = (bf16[192,768]{1,0:T(8,128)(2,1)S(1)}, bf16[192,768]{1,0:T(8,128)(2,1)S(1)}, u32[]{:S(2)}, u32[]{:S(2)}) collective-permute-start(bf16[192,768]{1,0:T(8,128)(2,1)S(1)} %copy-done.59), channel_id=1, source_target_pairs={{0,28},{4,24},{8,20},{12,16},{16,12},{20,8},{24,4},{28,0},{1,29},{... | collective-permute-start | bytes 884744 | tf_op jit(solution)/shard_map/ppermute | solution.py:124
  (88 other events, 646.5 us)
where the time goes:
time: 684 us; the launch traced here: 670 us
  starting transfers between devices  191 us (28%)
  local copies, waits for them, and re-layouts  184 us (27%)
  waiting for transfers between devices  131 us (19%)
  matrix products  98.5 us (14%)
  other arithmetic  63.2 us (9%)
    ppermute x55, waiting for transfers between devices, from_partner(): return lax.ppermute(values, axes, pairs)  83.1 us
    ppermute x55, starting transfers between devices, from_partner(): return lax.ppermute(values, axes, pairs)  73.1 us
    dot_general x14, matrix products, dot_high(): return jnp.dot(left_side, right_side, precision=high)  55.5 us
    dynamic_update_slice x35, local copies, waits for them, and re-layouts, placed_blocks(): result = lax.dynamic_update_index_in_dim(result, block, place, 0)  55 us
    unnamed x181, local copies, waits for them, and re-layouts  54.2 us
    all_to_all x8, starting transfers between devices, to_all(): lax.all_to_all(jnp.broadcast_to(block[None], (size,) + block.shape), axis...  41.6 us
    all_to_all x8, starting transfers between devices, sum_tokens(): blocks = lax.all_to_all(blocks, 'col', 0, 0)  38.9 us
    all_to_all x8, waiting for transfers between devices, to_all(): lax.all_to_all(jnp.broadcast_to(block[None], (size,) + block.shape), axis...  31.9 us
  transfers between devices with their start and end apart: 78, of which 26 were waited for; matrix products, arithmetic and copies ran while one was open for 44% of the time, Pallas kernels for 0%

commit v1 on v0

--- a/solution.py
+++ b/solution.py
@@ -174,7 +174,7 @@
     return jnp.sum(blocks.astype(jnp.float32), axis=0)
 
 
-def schulz(raw):
+def gram_of(raw):
     size = lax.axis_size("col")
     height = raw.shape[0]
     third = height // 3
@@ -194,7 +194,7 @@
     first = packed[:, :height]
     second = packed[:, height : 2 * height - third]
     last = packed[:, 2 * height - third :]
-    gram = jnp.concatenate(
+    return jnp.concatenate(
         [
             first,
             jnp.concatenate([first[:, third : 2 * third].T, second], axis=1),
@@ -202,6 +202,10 @@
         ],
         axis=0,
     )
+
+
+def schulz(raw, gram):
+    height = raw.shape[0]
     eye = jnp.eye(height, dtype=jnp.float32)
     scale = 1.0 / (jnp.sqrt(jnp.sum(gram * eye)) + 1e-07)
     current = raw * scale
@@ -285,17 +289,23 @@
         attention = gathered_weights(level_index, (0, 1))
         perceptron = gathered_weights(level_index, (2, 3))
         weight_sets.append(attention + perceptron)
-    upstream_image = features_first(gather_by_pairs(swap_row_col(cotangent), "col"))
-
-    stacked_moment = jnp.stack(
-        [
-            pad_columns(upright(moments[j // levels], j // levels, j % levels), widest)
-            for j in range(jobs)
+    cotangent_blocks = pad_rows(swap_row_col(cotangent), padded)
+    cotangent_blocks = cotangent_blocks.reshape(col_size, chunk, width_row)
+    upstream = features_first(lax.all_to_all(cotangent_blocks, "col", 0, 0))
+
+    upper = (me // row_size) % 2 == 1
+    half = jobs // 2
+    near_moments = []
+    for j in range(half):
+        low_job, high_job = [
+            pad_columns(upright(moments[i // levels], i // levels, i % levels), widest)
+            for i in (j, j + half)
         ]
-    )
-    moment_parts = [pick(stacked_moment, me)]
+        near_moments.append(jnp.where(upper, high_job, low_job))
+    stacked_moment = jnp.stack(near_moments)
+    moment_parts = [pick(stacked_moment, me % half)]
     for step in range(1, row_size):
-        moment_parts.append(from_partner(pick(stacked_moment, me ^ step), step))
+        moment_parts.append(from_partner(pick(stacked_moment, (me ^ step) % half), step))
     own_moment = placed_blocks(moment_parts, [my_row ^ i for i in range(row_size)])
     own_moment = own_moment.reshape(model_width, widest)
 
@@ -344,8 +354,6 @@
             )
         return received
 
-    upstream = own_chunk(upstream_image)
-    back_two = upstream_image.astype(jnp.bfloat16)
     upstream, own_moment = lax.optimization_barrier((upstream, own_moment))
     late = [None] * levels
     norm_sums = [None] * levels
@@ -355,8 +363,7 @@
             level_index
         ]
         gains = all_norms[level_index]
-        if level_index < levels - 1:
-            back_two = gather_tokens(upstream.astype(jnp.bfloat16))[:tokens]
+        back_two = gather_tokens(upstream.astype(jnp.bfloat16))[:tokens]
         act_grad = product(back_two, weight_down)
         hidden_grad = jax.vjp(lambda inner: jax.nn.gelu(inner, approximate=False), hidden)[1](
             act_grad
@@ -386,12 +393,6 @@
             (mixed_grad, back_one, hidden_grad, back_two), level_index
         )
 
-    norm_whole = jnp.stack(norm_sums)
-    for axis in ("row", "col", "dp"):
-        norm_whole = sum_by_pairs(norm_whole, axis)
-    norm_grad = lax.dynamic_slice_in_dim(norm_whole, my_row * width_row, width_row, 2)
-    norm_moment_new = moment_decay * norm_moment + norm_grad
-
     early_all = jnp.concatenate(early_all, axis=0)
     late_all = jnp.concatenate(late[0], axis=0)
     for level_index in range(1, levels):
@@ -416,8 +417,18 @@
         received = placed_blocks(received, [me ^ j for j in range(jobs)])
         return [received[j].astype(jnp.float32) for j in range(jobs)]
 
+    own_raw = moment_decay * own_moment + own_grad
+    gram, own_grad, stream, upstream, norm_sums = lax.optimization_barrier(
+        (gram_of(own_raw), own_grad, stream, upstream, norm_sums)
+    )
     grads = returned(own_grad)
-    orths = returned(schulz(moment_decay * own_moment + own_grad))
+    norm_whole = jnp.stack(norm_sums)
+    for axis in ("row", "col", "dp"):
+        norm_whole = sum_by_pairs(norm_whole, axis)
+    norm_grad = lax.dynamic_slice_in_dim(norm_whole, my_row * width_row, width_row, 2)
+    norm_moment_new = moment_decay * norm_moment + norm_grad
+
+    orths = returned(schulz(own_raw, gram))
 
     grad_outs = []
     moment_outs = []

time: 684 us -> 674 us (0.985)
  the two profiles are of different devices: /device:TPU:15 before, /device:TPU:16 now
where the time goes in v1:
time: 674 us; the launch traced here: 661 us
  starting transfers between devices  203 us (30%)
  local copies, waits for them, and re-layouts  152 us (23%)
  waiting for transfers between devices  131 us (19%)
  matrix products  114 us (17%)
  other arithmetic  56.8 us (8%)
    dot_general x14, matrix products, dot_high(): return jnp.dot(left_side, right_side, precision=high)  68.4 us
    ppermute x53, starting transfers between devices, from_partner(): return lax.ppermute(values, axes, pairs)  56.7 us
    all_to_all x9, starting transfers between devices, to_all(): lax.all_to_all(jnp.broadcast_to(block[None], (size,) + block.shape), axis...  55.4 us
    unnamed x200, local copies, waits for them, and re-layouts  52.8 us
    ppermute x53, waiting for transfers between devices, from_partner(): return lax.ppermute(values, axes, pairs)  50 us
    all_to_all x8, starting transfers between devices, sum_tokens(): blocks = lax.all_to_all(blocks, 'col', 0, 0)  49.6 us
    all_to_all x9, waiting for transfers between devices, to_all(): lax.all_to_all(jnp.broadcast_to(block[None], (size,) + block.shape), axis...  37.5 us
    dynamic_update_slice x31, local copies, waits for them, and re-layouts, placed_blocks(): result = lax.dynamic_update_index_in_dim(result, block, place, 0)  32.7 us
  transfers between devices with their start and end apart: 78, of which 26 were waited for; matrix products, arithmetic and copies ran while one was open for 32% of the time, Pallas kernels for 0%

profile of v1, /device:TPU:16, one launch (start us, length us, event | category | flops | bytes accessed | tf_op | source)
XLA Modules:
  0.0 660.7 jit_solution(10553165605652474412)
XLA Ops:
  2.4 3.2 collective-permute-start
  5.6 4.4 collective-permute-start.4
  32.9 5.8 all-to-all-start.1
  48.7 2.6 pad_maximum_fusion.21
  58.7 5.9 all-to-all-start.2
  74.5 6.7 %all-to-all-start.3 = ((bf16[4,56,768]{2,1,0:T(8,128)(2,1)}), bf16[4,56,768]{2,1,0:T(8,128)(2,1)S(1)}, u32[]{:S(2)}, u32[]{:S(2)}) async-start(bf16[4,56,768]{2,1,0:T(8,128)(2,1)} %broadcast_in_dim.186), calls=%async_computation.3 | async-start | bytes 688128 | tf_op jit(solution)/shard_map/all_to_all | solution.py:161
  85.4 3.3 all-to-all-done.3
  88.7 6.6 %all-to-all-start = ((f32[4,56,192]{2,1,0:T(8,128)}), f32[4,56,192]{2,1,0:T(8,128)S(1)}, u32[]{:S(2)}, u32[]{:S(2)}) async-start(f32[4,56,192]{2,1,0:T(8,128)} %bitcast), calls=%async_computation | async-start | bytes 458752 | tf_op jit(solution)/shard_map/all_to_all | solution.py:294
  95.4 3.8 multiply_convert_fusion.3
  101.9 5.1 all-to-all-start.4
  107.0 2.9 fusion.103
  120.9 5.3 all-to-all-start.5
  143.0 6.7 %all-to-all-start.6 = ((bf16[4,56,768]{2,1,0:T(8,128)(2,1)}), bf16[4,56,768]{2,1,0:T(8,128)(2,1)S(1)}, u32[]{:S(2)}, u32[]{:S(2)}) async-start(bf16[4,56,768]{2,1,0:T(8,128)(2,1)} %bitcast.61), calls=%async_computation.6 | async-start | bytes 688128 | tf_op jit(solution)/shard_map/all_to_all | solution.py:173
  156.6 6.7 %all-to-all-start.7 = ((bf16[4,56,768]{2,1,0:T(8,128)(2,1)}), bf16[4,56,768]{2,1,0:T(8,128)(2,1)S(1)}, u32[]{:S(2)}, u32[]{:S(2)}) async-start(bf16[4,56,768]{2,1,0:T(8,128)(2,1)} %broadcast_in_dim.190), calls=%async_computation.7 | async-start | bytes 688128 | tf_op jit(solution)/shard_map/all_to_all | solution.py:161
  169.4 6.7 %all-to-all-start.8 = ((bf16[4,56,768]{2,1,0:T(8,128)(2,1)}), bf16[4,56,768]{2,1,0:T(8,128)(2,1)S(1)}, u32[]{:S(2)}, u32[]{:S(2)}) async-start(bf16[4,56,768]{2,1,0:T(8,128)(2,1)} %broadcast_in_dim.192), calls=%async_computation.8 | async-start | bytes 688128 | tf_op jit(solution)/shard_map/all_to_all | solution.py:161
  176.1 3.8 multiply_convert_fusion.2
  186.1 6.0 all-to-all-start.9
  195.5 3.1 dynamic-slice_bitcast_fusion.18
  204.7 5.1 all-to-all-start.17
  211.2 2.7 collective-permute-start.20
  213.9 3.9 all-to-all-done.17
  218.6 7.3 %collective-permute-done.20 = bf16[208,768]{1,0:T(8,128)(2,1)S(1)} collective-permute-done((bf16[208,768]{1,0:T(8,128)(2,1)}, bf16[208,768]{1,0:T(8,128)(2,1)S(1)}, u32[]{:S(2)}, u32[]{:S(2)}) %collective-permute-start.20) | collective-permute-done | bytes 319520 | tf_op jit(solution)/shard_map/ppermute | solution.py:124
  225.9 5.7 collective-permute-done.21
  232.4 5.1 all-to-all-start.10
  237.5 3.1 copy.205
  241.4 4.1 all-to-all-done.10
  250.9 6.7 %all-to-all-start.11 = ((bf16[4,56,768]{2,1,0:T(8,128)(2,1)}), bf16[4,56,768]{2,1,0:T(8,128)(2,1)S(1)}, u32[]{:S(2)}, u32[]{:S(2)}) async-start(bf16[4,56,768]{2,1,0:T(8,128)(2,1)} %bitcast.97), calls=%async_computation.11 | async-start | bytes 688128 | tf_op jit(solution)/shard_map/all_to_all | solution.py:173
  268.2 6.2 all-to-all-start.12
  284.9 6.7 %all-to-all-start.13 = ((bf16[4,56,768]{2,1,0:T(8,128)(2,1)}), bf16[4,56,768]{2,1,0:T(8,128)(2,1)S(1)}, u32[]{:S(2)}, u32[]{:S(2)}) async-start(bf16[4,56,768]{2,1,0:T(8,128)(2,1)} %bitcast.99), calls=%async_computation.13 | async-start | bytes 688128 | tf_op jit(solution)/shard_map/all_to_all | solution.py:173
  304.3 2.7 collective-permute-start.28
  307.9 4.9 collective-permute-done.28
  315.0 5.1 all-to-all-start.14
  333.9 3.3 collective-permute-start.30
  342.5 3.5 collective-permute-start.34
  348.9 3.8 collective-permute-done.33
  352.8 3.1 collective-permute-done.34
  357.8 5.8 multiply_add_fusion.12
  368.1 7.3 %all-to-all-start.15 = ((f32[4,64,1536]{2,1,0:T(8,128)}), f32[4,64,1536]{2,1,0:T(8,128)}, u32[]{:S(2)}, u32[]{:S(2)}) async-start(f32[4,64,1536]{2,1,0:T(8,128)} %bitcast.463), calls=%async_computation.15 | async-start | bytes 3145728 | tf_op jit(solution)/shard_map/all_to_all | solution.py:192
  377.9 29.8 %all-to-all-done.15 = f32[4,64,1536]{2,1,0:T(8,128)} async-done(((f32[4,64,1536]{2,1,0:T(8,128)}), f32[4,64,1536]{2,1,0:T(8,128)}, u32[]{:S(2)}, u32[]{:S(2)}) %all-to-all-start.15) | async-done | bytes 1572896 | tf_op jit(solution)/shard_map/all_to_all | solution.py:192
  407.7 7.4 %all-to-all-start.18 = ((bf16[4,56,768]{2,1,0:T(8,128)(2,1)}), bf16[4,56,768]{2,1,0:T(8,128)(2,1)}, u32[]{:S(2)}, u32[]{:S(2)}) async-start(bf16[4,56,768]{2,1,0:T(8,128)(2,1)} %bitcast.139), calls=%async_computation.18 | async-start | bytes 688128 | tf_op jit(solution)/shard_map/all_to_all | solution.py:173
  416.7 5.4 all-to-all-done.18
  423.5 7.9 %all-to-all-start.16 = ((f32[4,64,1536]{2,1,0:T(8,128)}), f32[4,64,1536]{2,1,0:T(8,128)}, u32[]{:S(2)}, u32[]{:S(2)}) async-start(f32[4,64,1536]{2,1,0:T(8,128)} %broadcast_in_dim.196), calls=%async_computation.16 | async-start | bytes 3145728 | tf_op jit(solution)/shard_map/all_to_all | solution.py:161
  437.9 25.2 %all-to-all-done.16 = f32[4,64,1536]{2,1,0:T(8,128)} async-done(((f32[4,64,1536]{2,1,0:T(8,128)}), f32[4,64,1536]{2,1,0:T(8,128)}, u32[]{:S(2)}, u32[]{:S(2)}) %all-to-all-start.16) | async-done | bytes 1572896 | tf_op jit(solution)/shard_map/all_to_all | solution.py:161
  479.6 3.3 fusion.173
  482.9 7.3 %multiply_add_fusion.3 = f32[768,1536]{0,1:T(8,128)S(1)} fusion(f32[768,768]{0,1:T(8,128)S(1)} %copy-done.30, f32[768,768]{0,1:T(8,128)S(1)} %broadcast_multiply_fusion.1, f32[768,768]{0,1:T(8,128)S(1)} %fusion.173), kind=kOutput, calls=%fused_computation.7 | convolution fusion | flops 5442306048 | bytes 11796480 | tf_op jit(solution)/shard_map/dot_general | solution.py:40
  492.4 3.8 multiply_add_fusion.10
  496.2 3.3 fusion.174
  499.5 7.7 %multiply_add_fusion.2 = f32[768,1536]{0,1:T(8,128)S(1)} fusion(f32[768,768]{0,1:T(8,128)S(1)} %slice-done, f32[768,768]{0,1:T(8,128)S(1)} %multiply_add_fusion.10, f32[768,768]{0,1:T(8,128)S(1)} %fusion.174), kind=kOutput, calls=%fused_computation.6 | convolution fusion | flops 5442306048 | bytes 11796480 | tf_op jit(solution)/shard_map/dot_general | solution.py:40
  509.4 3.6 multiply_add_fusion.8
  513.0 3.3 fusion.175
  516.3 7.4 %multiply_add_fusion.1 = f32[768,1536]{0,1:T(8,128)S(1)} fusion(f32[768,768]{0,1:T(8,128)S(1)} %slice-done.1, f32[768,768]{0,1:T(8,128)S(1)} %multiply_add_fusion.8, f32[768,768]{0,1:T(8,128)S(1)} %fusion.175), kind=kOutput, calls=%fused_computation.5 | convolution fusion | flops 5442306048 | bytes 11796480 | tf_op jit(solution)/shard_map/dot_general | solution.py:40
  525.9 3.6 multiply_add_fusion.6
  530.4 6.7 %all-to-all-start.19 = ((f32[4,56,192]{2,1,0:T(8,128)}), f32[4,56,192]{2,1,0:T(8,128)S(1)}, u32[]{:S(2)}, u32[]{:S(2)}) async-start(f32[4,56,192]{2,1,0:T(8,128)} %bitcast.459), calls=%async_computation.19 | async-start | bytes 458752 | tf_op jit(solution)/shard_map/all_to_all | solution.py:455
  544.3 3.3 fusion.176
  547.6 7.3 %multiply_add_fusion = f32[768,1536]{0,1:T(8,128)S(1)} fusion(f32[768,768]{0,1:T(8,128)S(1)} %slice-done.2, f32[768,768]{0,1:T(8,128)S(1)} %multiply_add_fusion.6, f32[768,768]{0,1:T(8,128)S(1)} %fusion.176), kind=kOutput, calls=%fused_computation.4 | convolution fusion | flops 5442306048 | bytes 11796480 | tf_op jit(solution)/shard_map/dot_general | solution.py:40
  556.3 3.8 multiply_add_fusion.4
  561.7 3.3 fusion.177
  567.3 7.5 %add_convert_fusion = bf16[768,768]{0,1:T(8,128)(2,1)} fusion(f32[768,1536]{0,1:T(8,128)} %copy-done.16, f32[768,768]{0,1:T(8,128)S(1)} %fusion.177, f32[768,768]{0,1:T(8,128)} %copy-done), kind=kOutput, calls=%fused_computation.20 | convolution fusion | flops 2721447936 | bytes 10616832 | tf_op jit(solution)/shard_map/dot_general | solution.py:40
  578.0 5.7 all-to-all-start.20
  604.4 4.4 collective-permute-done.44
  611.0 4.1 collective-permute-done.51
  623.8 5.2 collective-permute-start.37
  629.9 2.7 multiply_add_fusion.22
  632.6 7.2 %collective-permute-done.56 = bf16[192,768]{1,0:T(8,128)(2,1)S(1)} collective-permute-done((bf16[192,768]{1,0:T(8,128)(2,1)S(1)}, bf16[192,768]{1,0:T(8,128)(2,1)S(1)}, u32[]{:S(2)}, u32[]{:S(2)}) %collective-permute-start.56) | collective-permute-done | bytes 294944 | tf_op jit(solution)/shard_map/ppermute | solution.py:124
  (569 shorter events, 291.9 us)
Async XLA Ops:
  2.4 36.3 %collective-permute-start = (f32[197,192]{1,0:T(8,128)}, f32[197,192]{1,0:T(8,128)}, u32[]{:S(2)}, u32[]{:S(2)}) collective-permute-start(f32[197,192]{1,0:T(8,128)} %copy.201), channel_id=1, source_target_pairs={{0,0},{1,4},{2,8},{3,12},{4,1},{5,5},{6,9},{7,13},{8,2},{9,6},{10,... | collective-permute-start | bytes 453896 | tf_op jit(solution)/shard_map/ppermute | solution.py:118
  5.6 25.6 %collective-permute-start.4 = (bf16[197,192]{0,1:T(8,128)(2,1)}, bf16[197,192]{0,1:T(8,128)(2,1)}, u32[]{:S(2)}, u32[]{:S(2)}) collective-permute-start(bf16[197,192]{0,1:T(8,128)(2,1)} %param.12), channel_id=1, source_target_pairs={{0,0},{1,4},{2,8},{3,12},{4,1},{5,5},{6,9},{7,13},{8,2},{9,6},{10,... | collective-permute-start | bytes 226952 | tf_op jit(solution)/shard_map/ppermute | solution.py:118
  10.0 17.4 %collective-permute-start.5 = (f32[1,2,4,192]{3,2,1,0:T(4,128)}, f32[1,2,4,192]{3,2,1,0:T(4,128)S(1)}, u32[]{:S(2)}, u32[]{:S(2)}) collective-permute-start(f32[1,2,4,192]{3,2,1,0:T(4,128)} %bitcast.513), channel_id=1, source_target_pairs={{0,8},{4,12},{8,0},{12,4},{1,9},{5,13},{9,1},{13,5},{2,10},{6,14},... | collective-permute-start | bytes 18440 | tf_op jit(solution)/shard_map/ppermute | solution.py:124
  14.5 25.8 %collective-permute-start.11 = (bf16[1,192,768]{2,1,0:T(8,128)(2,1)S(1)}, bf16[1,192,768]{2,1,0:T(8,128)(2,1)}, u32[]{:S(2)}, u32[]{:S(2)}) collective-permute-start(bf16[1,192,768]{2,1,0:T(8,128)(2,1)S(1)} %get-tuple-element.191), channel_id=1, source_target_pairs={{0,8},{4,12},{8,0},{12,4},{1,9},{5,13},{9,1},{13,5},{2,10},{6,14},... | collective-permute-start | bytes 884744 | tf_op jit(solution)/shard_map/ppermute | solution.py:124
  18.5 23.6 %collective-permute-start.7 = (bf16[1,192,768]{2,1,0:T(8,128)(2,1)}, bf16[1,192,768]{2,1,0:T(8,128)(2,1)}, u32[]{:S(2)}, u32[]{:S(2)}) collective-permute-start(bf16[1,192,768]{2,1,0:T(8,128)(2,1)} %get-tuple-element.196), channel_id=1, source_target_pairs={{0,8},{4,12},{8,0},{12,4},{1,9},{5,13},{9,1},{13,5},{2,10},{6,14},... | collective-permute-start | bytes 884744 | tf_op jit(solution)/shard_map/ppermute | solution.py:124
  28.7 20.0 %collective-permute-start.13 = (bf16[1,192,1536]{2,1,0:T(8,128)(2,1)S(1)}, bf16[1,192,1536]{2,1,0:T(8,128)(2,1)}, u32[]{:S(2)}, u32[]{:S(2)}) collective-permute-start(bf16[1,192,1536]{2,1,0:T(8,128)(2,1)S(1)} %maximum_bitcast_fusion.1), channel_id=1, source_target_pairs={{0,8},{4,12},{8,0},{12,4},{1,9},{5,13},{9,1},{13,5},{2,10},{6,14},... | collective-permute-start | bytes 1769480 | tf_op jit(solution)/shard_map/ppermute | solution.py:124
  31.2 33.4 %collective-permute-start.9 = (bf16[1,192,1536]{2,1,0:T(8,128)(2,1)S(1)}, bf16[1,192,1536]{2,1,0:T(8,128)(2,1)}, u32[]{:S(2)}, u32[]{:S(2)}) collective-permute-start(bf16[1,192,1536]{2,1,0:T(8,128)(2,1)S(1)} %maximum_bitcast_fusion), channel_id=1, source_target_pairs={{0,8},{4,12},{8,0},{12,4},{1,9},{5,13},{9,1},{13,5},{2,10},{6,14},... | collective-permute-start | bytes 1769480 | tf_op jit(solution)/shard_map/ppermute | solution.py:124
  32.9 15.1 %all-to-all-start.1 = ((bf16[4,197,192]{1,2,0:T(8,128)(2,1)}), bf16[4,197,192]{1,2,0:T(8,128)(2,1)S(1)}, u32[]{:S(2)}, u32[]{:S(2)}) async-start(bf16[4,197,192]{1,2,0:T(8,128)(2,1)} %broadcast_in_dim.182), calls=%async_computation.1 | async-start | bytes 786432 | tf_op jit(solution)/shard_map/all_to_all | solution.py:161
  51.3 29.9 %collective-permute-start.14 = (bf16[2,192,1536]{2,1,0:T(8,128)(2,1)}, bf16[2,192,1536]{2,1,0:T(8,128)(2,1)}, u32[]{:S(2)}, u32[]{:S(2)}) collective-permute-start(bf16[2,192,1536]{2,1,0:T(8,128)(2,1)} %pad_maximum_fusion.21), channel_id=1, source_target_pairs={{0,4},{4,0},{8,12},{12,8},{1,5},{5,1},{9,13},{13,9},{2,6},{6,2},{1... | collective-permute-start | bytes 3538952 | tf_op jit(solution)/shard_map/ppermute | solution.py:124
  58.7 14.2 %all-to-all-start.2 = ((bf16[4,56,768]{2,1,0:T(8,128)(2,1)}), bf16[4,56,768]{2,1,0:T(8,128)(2,1)S(1)}, u32[]{:S(2)}, u32[]{:S(2)}) async-start(bf16[4,56,768]{2,1,0:T(8,128)(2,1)} %bitcast.41), calls=%async_computation.2 | async-start | bytes 688128 | tf_op jit(solution)/shard_map/all_to_all | solution.py:173
  66.7 14.5 %collective-permute-start.10 = (bf16[2,192,1536]{2,1,0:T(8,128)(2,1)}, bf16[2,192,1536]{2,1,0:T(8,128)(2,1)}, u32[]{:S(2)}, u32[]{:S(2)}) collective-permute-start(bf16[2,192,1536]{2,1,0:T(8,128)(2,1)} %pad_maximum_fusion.20), channel_id=1, source_target_pairs={{0,4},{4,0},{8,12},{12,8},{1,5},{5,1},{9,13},{13,9},{2,6},{6,2},{1... | collective-permute-start | bytes 3538952 | tf_op jit(solution)/shard_map/ppermute | solution.py:124
  74.5 14.3 %all-to-all-start.3 = ((bf16[4,56,768]{2,1,0:T(8,128)(2,1)}), bf16[4,56,768]{2,1,0:T(8,128)(2,1)S(1)}, u32[]{:S(2)}, u32[]{:S(2)}) async-start(bf16[4,56,768]{2,1,0:T(8,128)(2,1)} %broadcast_in_dim.186), calls=%async_computation.3 | async-start | bytes 688128 | tf_op jit(solution)/shard_map/all_to_all | solution.py:161
  88.7 13.1 %all-to-all-start = ((f32[4,56,192]{2,1,0:T(8,128)}), f32[4,56,192]{2,1,0:T(8,128)S(1)}, u32[]{:S(2)}, u32[]{:S(2)}) async-start(f32[4,56,192]{2,1,0:T(8,128)} %bitcast), calls=%async_computation | async-start | bytes 458752 | tf_op jit(solution)/shard_map/all_to_all | solution.py:294
  101.9 16.9 %all-to-all-start.4 = ((bf16[4,56,768]{2,1,0:T(8,128)(2,1)}), bf16[4,56,768]{2,1,0:T(8,128)(2,1)}, u32[]{:S(2)}, u32[]{:S(2)}) async-start(bf16[4,56,768]{2,1,0:T(8,128)(2,1)} %bitcast.48), calls=%async_computation.4 | async-start | bytes 688128 | tf_op jit(solution)/shard_map/all_to_all | solution.py:173
  113.1 13.2 %collective-permute-start.1 = (f32[192,768]{1,0:T(8,128)}, f32[192,768]{1,0:T(8,128)}, u32[]{:S(2)}, u32[]{:S(2)}) collective-permute-start(f32[192,768]{1,0:T(8,128)} %get-tuple-element.219), channel_id=1, source_target_pairs={{0,4},{4,0},{8,12},{12,8},{16,20},{20,16},{24,28},{28,24},{1,5},{5... | collective-permute-start | bytes 1769480 | tf_op jit(solution)/shard_map/ppermute | solution.py:124
  113.1 16.4 %collective-permute-start.2 = (f32[192,768]{1,0:T(8,128)}, f32[192,768]{1,0:T(8,128)}, u32[]{:S(2)}, u32[]{:S(2)}) collective-permute-start(f32[192,768]{1,0:T(8,128)} %get-tuple-element.218), channel_id=1, source_target_pairs={{0,8},{4,12},{8,0},{12,4},{16,24},{20,28},{24,16},{28,20},{1,9},{5... | collective-permute-start | bytes 1769480 | tf_op jit(solution)/shard_map/ppermute | solution.py:124
  114.8 35.0 %collective-permute-start.3 = (f32[192,768]{1,0:T(8,128)}, f32[192,768]{1,0:T(8,128)}, u32[]{:S(2)}, u32[]{:S(2)}) collective-permute-start(f32[192,768]{1,0:T(8,128)} %get-tuple-element.217), channel_id=1, source_target_pairs={{0,12},{4,8},{8,4},{12,0},{16,28},{20,24},{24,20},{28,16},{1,13},{... | collective-permute-start | bytes 1769480 | tf_op jit(solution)/shard_map/ppermute | solution.py:124
  120.9 13.2 %all-to-all-start.5 = ((bf16[4,56,768]{2,1,0:T(8,128)(2,1)}), bf16[4,56,768]{2,1,0:T(8,128)(2,1)}, u32[]{:S(2)}, u32[]{:S(2)}) async-start(bf16[4,56,768]{2,1,0:T(8,128)(2,1)} %broadcast_in_dim.188), calls=%async_computation.5 | async-start | bytes 688128 | tf_op jit(solution)/shard_map/all_to_all | solution.py:161
  143.0 12.5 %all-to-all-start.6 = ((bf16[4,56,768]{2,1,0:T(8,128)(2,1)}), bf16[4,56,768]{2,1,0:T(8,128)(2,1)S(1)}, u32[]{:S(2)}, u32[]{:S(2)}) async-start(bf16[4,56,768]{2,1,0:T(8,128)(2,1)} %bitcast.61), calls=%async_computation.6 | async-start | bytes 688128 | tf_op jit(solution)/shard_map/all_to_all | solution.py:173
  156.6 12.1 %all-to-all-start.7 = ((bf16[4,56,768]{2,1,0:T(8,128)(2,1)}), bf16[4,56,768]{2,1,0:T(8,128)(2,1)S(1)}, u32[]{:S(2)}, u32[]{:S(2)}) async-start(bf16[4,56,768]{2,1,0:T(8,128)(2,1)} %broadcast_in_dim.190), calls=%async_computation.7 | async-start | bytes 688128 | tf_op jit(solution)/shard_map/all_to_all | solution.py:161
  169.4 11.7 %all-to-all-start.8 = ((bf16[4,56,768]{2,1,0:T(8,128)(2,1)}), bf16[4,56,768]{2,1,0:T(8,128)(2,1)S(1)}, u32[]{:S(2)}, u32[]{:S(2)}) async-start(bf16[4,56,768]{2,1,0:T(8,128)(2,1)} %broadcast_in_dim.192), calls=%async_computation.8 | async-start | bytes 688128 | tf_op jit(solution)/shard_map/all_to_all | solution.py:161
  186.1 18.6 %all-to-all-start.9 = ((bf16[4,56,768]{2,1,0:T(8,128)(2,1)}), bf16[4,56,768]{2,1,0:T(8,128)(2,1)S(1)}, u32[]{:S(2)}, u32[]{:S(2)}) async-start(bf16[4,56,768]{2,1,0:T(8,128)(2,1)} %bitcast.69), calls=%async_computation.9 | async-start | bytes 688128 | tf_op jit(solution)/shard_map/all_to_all | solution.py:173
  198.6 12.6 %collective-permute-start.15 = (bf16[208,768]{1,0:T(8,128)(2,1)}, bf16[208,768]{1,0:T(8,128)(2,1)}, u32[]{:S(2)}, u32[]{:S(2)}) collective-permute-start(bf16[208,768]{1,0:T(8,128)(2,1)} %get-tuple-element.203), channel_id=1, source_target_pairs={{0,4},{4,0},{8,12},{12,8},{16,20},{20,16},{24,28},{28,24},{1,5},{5... | collective-permute-start | bytes 958472 | tf_op jit(solution)/shard_map/ppermute | solution.py:124
  198.6 15.4 %collective-permute-start.16 = (bf16[208,768]{1,0:T(8,128)(2,1)}, bf16[208,768]{1,0:T(8,128)(2,1)}, u32[]{:S(2)}, u32[]{:S(2)}) collective-permute-start(bf16[208,768]{1,0:T(8,128)(2,1)} %get-tuple-element.202), channel_id=1, source_target_pairs={{0,8},{4,12},{8,0},{12,4},{16,24},{20,28},{24,16},{28,20},{1,9},{5... | collective-permute-start | bytes 958472 | tf_op jit(solution)/shard_map/ppermute | solution.py:124
  200.3 18.2 %collective-permute-start.17 = (bf16[208,768]{1,0:T(8,128)(2,1)}, bf16[208,768]{1,0:T(8,128)(2,1)}, u32[]{:S(2)}, u32[]{:S(2)}) collective-permute-start(bf16[208,768]{1,0:T(8,128)(2,1)} %get-tuple-element.201), channel_id=1, source_target_pairs={{0,12},{4,8},{8,4},{12,0},{16,28},{20,24},{24,20},{28,16},{1,13},{... | collective-permute-start | bytes 958472 | tf_op jit(solution)/shard_map/ppermute | solution.py:124
  200.5 18.1 %collective-permute-start.18 = (bf16[208,768]{1,0:T(8,128)(2,1)}, bf16[208,768]{1,0:T(8,128)(2,1)}, u32[]{:S(2)}, u32[]{:S(2)}) collective-permute-start(bf16[208,768]{1,0:T(8,128)(2,1)} %get-tuple-element.200), channel_id=1, source_target_pairs={{0,16},{4,20},{8,24},{12,28},{16,0},{20,4},{24,8},{28,12},{1,17},{... | collective-permute-start | bytes 958472 | tf_op jit(solution)/shard_map/ppermute | solution.py:124
  202.0 16.6 %collective-permute-start.19 = (bf16[208,768]{1,0:T(8,128)(2,1)}, bf16[208,768]{1,0:T(8,128)(2,1)}, u32[]{:S(2)}, u32[]{:S(2)}) collective-permute-start(bf16[208,768]{1,0:T(8,128)(2,1)} %get-tuple-element.199), channel_id=1, source_target_pairs={{0,20},{4,16},{8,28},{12,24},{16,4},{20,0},{24,12},{28,8},{1,21},{... | collective-permute-start | bytes 958472 | tf_op jit(solution)/shard_map/ppermute | solution.py:124
  204.7 13.1 %all-to-all-start.17 = ((bf16[4,56,768]{2,1,0:T(8,128)(2,1)}), bf16[4,56,768]{2,1,0:T(8,128)(2,1)S(1)}, u32[]{:S(2)}, u32[]{:S(2)}) async-start(bf16[4,56,768]{2,1,0:T(8,128)(2,1)} %bitcast.138), calls=%async_computation.17 | async-start | bytes 688128 | tf_op jit(solution)/shard_map/all_to_all | solution.py:173
  211.2 14.7 %collective-permute-start.20 = (bf16[208,768]{1,0:T(8,128)(2,1)}, bf16[208,768]{1,0:T(8,128)(2,1)S(1)}, u32[]{:S(2)}, u32[]{:S(2)}) collective-permute-start(bf16[208,768]{1,0:T(8,128)(2,1)} %get-tuple-element.198), channel_id=1, source_target_pairs={{0,24},{4,28},{8,16},{12,20},{16,8},{20,12},{24,0},{28,4},{1,25},{... | collective-permute-start | bytes 958472 | tf_op jit(solution)/shard_map/ppermute | solution.py:124
  213.9 17.7 %collective-permute-start.21 = (bf16[208,768]{1,0:T(8,128)(2,1)S(1)}, bf16[208,768]{1,0:T(8,128)(2,1)}, u32[]{:S(2)}, u32[]{:S(2)}) collective-permute-start(bf16[208,768]{1,0:T(8,128)(2,1)S(1)} %get-tuple-element.197), channel_id=1, source_target_pairs={{0,28},{4,24},{8,20},{12,16},{16,12},{20,8},{24,4},{28,0},{1,29},{... | collective-permute-start | bytes 958472 | tf_op jit(solution)/shard_map/ppermute | solution.py:124
  232.4 13.1 %all-to-all-start.10 = ((bf16[4,56,768]{2,1,0:T(8,128)(2,1)}), bf16[4,56,768]{2,1,0:T(8,128)(2,1)S(1)}, u32[]{:S(2)}, u32[]{:S(2)}) async-start(bf16[4,56,768]{2,1,0:T(8,128)(2,1)} %broadcast_in_dim.193), calls=%async_computation.10 | async-start | bytes 688128 | tf_op jit(solution)/shard_map/all_to_all | solution.py:161
  250.9 14.4 %all-to-all-start.11 = ((bf16[4,56,768]{2,1,0:T(8,128)(2,1)}), bf16[4,56,768]{2,1,0:T(8,128)(2,1)S(1)}, u32[]{:S(2)}, u32[]{:S(2)}) async-start(bf16[4,56,768]{2,1,0:T(8,128)(2,1)} %bitcast.97), calls=%async_computation.11 | async-start | bytes 688128 | tf_op jit(solution)/shard_map/all_to_all | solution.py:173
  268.2 11.9 %all-to-all-start.12 = ((bf16[4,56,768]{2,1,0:T(8,128)(2,1)}), bf16[4,56,768]{2,1,0:T(8,128)(2,1)S(1)}, u32[]{:S(2)}, u32[]{:S(2)}) async-start(bf16[4,56,768]{2,1,0:T(8,128)(2,1)} %broadcast_in_dim.194), calls=%async_computation.12 | async-start | bytes 688128 | tf_op jit(solution)/shard_map/all_to_all | solution.py:161
  284.9 17.3 %all-to-all-start.13 = ((bf16[4,56,768]{2,1,0:T(8,128)(2,1)}), bf16[4,56,768]{2,1,0:T(8,128)(2,1)S(1)}, u32[]{:S(2)}, u32[]{:S(2)}) async-start(bf16[4,56,768]{2,1,0:T(8,128)(2,1)} %bitcast.99), calls=%async_computation.13 | async-start | bytes 688128 | tf_op jit(solution)/shard_map/all_to_all | solution.py:173
  292.9 10.7 %collective-permute-start.22 = (bf16[208,768]{1,0:T(8,128)(2,1)}, bf16[208,768]{1,0:T(8,128)(2,1)}, u32[]{:S(2)}, u32[]{:S(2)}) collective-permute-start(bf16[208,768]{1,0:T(8,128)(2,1)} %get-tuple-element.238), channel_id=1, source_target_pairs={{0,4},{8,12},{16,20},{24,28},{1,5},{9,13},{17,21},{25,29},{2,6},{1... | collective-permute-start | bytes 958472 | tf_op jit(solution)/shard_map/ppermute | solution.py:124
  296.7 11.1 %collective-permute-start.24 = (bf16[208,768]{1,0:T(8,128)(2,1)}, bf16[208,768]{1,0:T(8,128)(2,1)}, u32[]{:S(2)}, u32[]{:S(2)}) collective-permute-start(bf16[208,768]{1,0:T(8,128)(2,1)} %get-tuple-element.236), channel_id=1, source_target_pairs={{0,12},{8,4},{16,28},{24,20},{1,13},{9,5},{17,29},{25,21},{2,14},{... | collective-permute-start | bytes 958472 | tf_op jit(solution)/shard_map/ppermute | solution.py:124
  315.0 13.7 %all-to-all-start.14 = ((bf16[4,56,768]{2,1,0:T(8,128)(2,1)}), bf16[4,56,768]{2,1,0:T(8,128)(2,1)S(1)}, u32[]{:S(2)}, u32[]{:S(2)}) async-start(bf16[4,56,768]{2,1,0:T(8,128)(2,1)} %broadcast_in_dim.195), calls=%async_computation.14 | async-start | bytes 688128 | tf_op jit(solution)/shard_map/all_to_all | solution.py:161
  333.9 12.1 %collective-permute-start.30 = (bf16[208,768]{1,0:T(8,128)(2,1)S(1)}, bf16[208,768]{1,0:T(8,128)(2,1)S(1)}, u32[]{:S(2)}, u32[]{:S(2)}) collective-permute-start(bf16[208,768]{1,0:T(8,128)(2,1)S(1)} %get-tuple-element.230), channel_id=1, source_target_pairs={{0,8},{8,0},{16,24},{24,16},{1,9},{9,1},{17,25},{25,17},{2,10},{10... | collective-permute-start | bytes 958472 | tf_op jit(solution)/shard_map/ppermute | solution.py:124
  341.1 11.6 %collective-permute-start.33 = (bf16[208,768]{1,0:T(8,128)(2,1)S(1)}, bf16[208,768]{1,0:T(8,128)(2,1)S(1)}, u32[]{:S(2)}, u32[]{:S(2)}) collective-permute-start(bf16[208,768]{1,0:T(8,128)(2,1)S(1)} %get-tuple-element.227), channel_id=1, source_target_pairs={{4,16},{12,24},{20,0},{28,8},{5,17},{13,25},{21,1},{29,9},{6,18},{... | collective-permute-start | bytes 958472 | tf_op jit(solution)/shard_map/ppermute | solution.py:124
  342.5 13.4 %collective-permute-start.34 = (bf16[208,768]{1,0:T(8,128)(2,1)S(1)}, bf16[208,768]{1,0:T(8,128)(2,1)S(1)}, u32[]{:S(2)}, u32[]{:S(2)}) collective-permute-start(bf16[208,768]{1,0:T(8,128)(2,1)S(1)} %get-tuple-element.226), channel_id=1, source_target_pairs={{0,24},{8,16},{16,8},{24,0},{1,25},{9,17},{17,9},{25,1},{2,26},{10... | collective-permute-start | bytes 958472 | tf_op jit(solution)/shard_map/ppermute | solution.py:124
  346.0 11.8 %collective-permute-start.35 = (bf16[208,768]{1,0:T(8,128)(2,1)S(1)}, bf16[208,768]{1,0:T(8,128)(2,1)S(1)}, u32[]{:S(2)}, u32[]{:S(2)}) collective-permute-start(bf16[208,768]{1,0:T(8,128)(2,1)S(1)} %get-tuple-element.225), channel_id=1, source_target_pairs={{4,24},{12,16},{20,8},{28,0},{5,25},{13,17},{21,9},{29,1},{6,26},{... | collective-permute-start | bytes 958472 | tf_op jit(solution)/shard_map/ppermute | solution.py:124
  368.1 39.6 %all-to-all-start.15 = ((f32[4,64,1536]{2,1,0:T(8,128)}), f32[4,64,1536]{2,1,0:T(8,128)}, u32[]{:S(2)}, u32[]{:S(2)}) async-start(f32[4,64,1536]{2,1,0:T(8,128)} %bitcast.463), calls=%async_computation.15 | async-start | bytes 3145728 | tf_op jit(solution)/shard_map/all_to_all | solution.py:192
  407.7 14.4 %all-to-all-start.18 = ((bf16[4,56,768]{2,1,0:T(8,128)(2,1)}), bf16[4,56,768]{2,1,0:T(8,128)(2,1)}, u32[]{:S(2)}, u32[]{:S(2)}) async-start(bf16[4,56,768]{2,1,0:T(8,128)(2,1)} %bitcast.139), calls=%async_computation.18 | async-start | bytes 688128 | tf_op jit(solution)/shard_map/all_to_all | solution.py:173
  423.5 39.7 %all-to-all-start.16 = ((f32[4,64,1536]{2,1,0:T(8,128)}), f32[4,64,1536]{2,1,0:T(8,128)}, u32[]{:S(2)}, u32[]{:S(2)}) async-start(f32[4,64,1536]{2,1,0:T(8,128)} %broadcast_in_dim.196), calls=%async_computation.16 | async-start | bytes 3145728 | tf_op jit(solution)/shard_map/all_to_all | solution.py:161
  530.4 47.6 %all-to-all-start.19 = ((f32[4,56,192]{2,1,0:T(8,128)}), f32[4,56,192]{2,1,0:T(8,128)S(1)}, u32[]{:S(2)}, u32[]{:S(2)}) async-start(f32[4,56,192]{2,1,0:T(8,128)} %bitcast.459), calls=%async_computation.19 | async-start | bytes 458752 | tf_op jit(solution)/shard_map/all_to_all | solution.py:455
  542.0 47.3 %collective-permute-start.38 = (bf16[192,768]{1,0:T(8,128)(2,1)}, bf16[192,768]{1,0:T(8,128)(2,1)}, u32[]{:S(2)}, u32[]{:S(2)}) collective-permute-start(bf16[192,768]{1,0:T(8,128)(2,1)} %get-tuple-element.254), channel_id=1, source_target_pairs={{0,4},{4,0},{8,12},{12,8},{16,20},{20,16},{24,28},{28,24},{1,5},{5... | collective-permute-start | bytes 884744 | tf_op jit(solution)/shard_map/ppermute | solution.py:124
  542.0 53.0 %collective-permute-start.40 = (bf16[192,768]{1,0:T(8,128)(2,1)}, bf16[192,768]{1,0:T(8,128)(2,1)}, u32[]{:S(2)}, u32[]{:S(2)}) collective-permute-start(bf16[192,768]{1,0:T(8,128)(2,1)} %get-tuple-element.252), channel_id=1, source_target_pairs={{0,12},{4,8},{8,4},{12,0},{16,28},{20,24},{24,20},{28,16},{1,13},{... | collective-permute-start | bytes 884744 | tf_op jit(solution)/shard_map/ppermute | solution.py:124
  543.7 53.8 %collective-permute-start.41 = (bf16[192,768]{1,0:T(8,128)(2,1)}, bf16[192,768]{1,0:T(8,128)(2,1)}, u32[]{:S(2)}, u32[]{:S(2)}) collective-permute-start(bf16[192,768]{1,0:T(8,128)(2,1)} %get-tuple-element.251), channel_id=1, source_target_pairs={{0,16},{4,20},{8,24},{12,28},{16,0},{20,4},{24,8},{28,12},{1,17},{... | collective-permute-start | bytes 884744 | tf_op jit(solution)/shard_map/ppermute | solution.py:124
  544.2 10.7 %collective-permute-start.45 = (f32[2,4,768]{2,1,0:T(4,128)S(1)}, f32[2,4,768]{2,1,0:T(4,128)S(1)}, u32[]{:S(2)}, u32[]{:S(2)}) collective-permute-start(f32[2,4,768]{2,1,0:T(4,128)S(1)} %pad_maximum_fusion.26), channel_id=1, source_target_pairs={{0,4},{4,0},{8,12},{12,8},{1,5},{5,1},{9,13},{13,9},{2,6},{6,2},{1... | collective-permute-start | bytes 73736 | tf_op jit(solution)/shard_map/ppermute | solution.py:124
  565.9 26.3 %collective-permute-start.39 = (bf16[192,768]{1,0:T(8,128)(2,1)}, bf16[192,768]{1,0:T(8,128)(2,1)}, u32[]{:S(2)}, u32[]{:S(2)}) collective-permute-start(bf16[192,768]{1,0:T(8,128)(2,1)} %get-tuple-element.253), channel_id=1, source_target_pairs={{0,8},{4,12},{8,0},{12,4},{16,24},{20,28},{24,16},{28,20},{1,9},{5... | collective-permute-start | bytes 884744 | tf_op jit(solution)/shard_map/ppermute | solution.py:124
  576.4 10.4 %collective-permute-start.49 = (f32[2,4,768]{2,1,0:T(4,128)S(1)}, f32[2,4,768]{2,1,0:T(4,128)S(1)}, u32[]{:S(2)}, u32[]{:S(2)}) collective-permute-start(f32[2,4,768]{2,1,0:T(4,128)S(1)} %add.546), channel_id=1, source_target_pairs={{0,16},{16,0},{1,17},{17,1},{2,18},{18,2},{3,19},{19,3},{4,20},{20... | collective-permute-start | bytes 73736 | tf_op jit(solution)/shard_map/ppermute | solution.py:124
  578.0 10.6 %all-to-all-start.20 = ((f32[4,56,192]{2,1,0:T(8,128)}), f32[4,56,192]{2,1,0:T(8,128)S(1)}, u32[]{:S(2)}, u32[]{:S(2)}) async-start(f32[4,56,192]{2,1,0:T(8,128)} %bitcast.458), calls=%async_computation.20 | async-start | bytes 458752 | tf_op jit(solution)/shard_map/all_to_all | solution.py:455
  586.7 13.1 %collective-permute-start.42 = (bf16[192,768]{1,0:T(8,128)(2,1)}, bf16[192,768]{1,0:T(8,128)(2,1)}, u32[]{:S(2)}, u32[]{:S(2)}) collective-permute-start(bf16[192,768]{1,0:T(8,128)(2,1)} %get-tuple-element.250), channel_id=1, source_target_pairs={{0,20},{4,16},{8,28},{12,24},{16,4},{20,0},{24,12},{28,8},{1,21},{... | collective-permute-start | bytes 884744 | tf_op jit(solution)/shard_map/ppermute | solution.py:124
  589.3 13.0 %collective-permute-start.43 = (bf16[192,768]{1,0:T(8,128)(2,1)}, bf16[192,768]{1,0:T(8,128)(2,1)S(1)}, u32[]{:S(2)}, u32[]{:S(2)}) collective-permute-start(bf16[192,768]{1,0:T(8,128)(2,1)} %get-tuple-element.249), channel_id=1, source_target_pairs={{0,24},{4,28},{8,16},{12,20},{16,8},{20,12},{24,0},{28,4},{1,25},{... | collective-permute-start | bytes 884744 | tf_op jit(solution)/shard_map/ppermute | solution.py:124
  592.3 16.5 %collective-permute-start.44 = (bf16[192,768]{1,0:T(8,128)(2,1)S(1)}, bf16[192,768]{1,0:T(8,128)(2,1)S(1)}, u32[]{:S(2)}, u32[]{:S(2)}) collective-permute-start(bf16[192,768]{1,0:T(8,128)(2,1)S(1)} %get-tuple-element.248), channel_id=1, source_target_pairs={{0,28},{4,24},{8,20},{12,16},{16,12},{20,8},{24,4},{28,0},{1,29},{... | collective-permute-start | bytes 884744 | tf_op jit(solution)/shard_map/ppermute | solution.py:124
  595.1 14.5 %collective-permute-start.50 = (bf16[192,768]{1,0:T(8,128)(2,1)}, bf16[192,768]{1,0:T(8,128)(2,1)S(1)}, u32[]{:S(2)}, u32[]{:S(2)}) collective-permute-start(bf16[192,768]{1,0:T(8,128)(2,1)} %get-tuple-element.246), channel_id=1, source_target_pairs={{0,4},{4,0},{8,12},{12,8},{16,20},{20,16},{24,28},{28,24},{1,5},{5... | collective-permute-start | bytes 884744 | tf_op jit(solution)/shard_map/ppermute | solution.py:124
  597.5 17.6 %collective-permute-start.51 = (bf16[192,768]{1,0:T(8,128)(2,1)}, bf16[192,768]{1,0:T(8,128)(2,1)S(1)}, u32[]{:S(2)}, u32[]{:S(2)}) collective-permute-start(bf16[192,768]{1,0:T(8,128)(2,1)} %get-tuple-element.245), channel_id=1, source_target_pairs={{0,8},{4,12},{8,0},{12,4},{16,24},{20,28},{24,16},{28,20},{1,9},{5... | collective-permute-start | bytes 884744 | tf_op jit(solution)/shard_map/ppermute | solution.py:124
  599.8 21.4 %collective-permute-start.52 = (bf16[192,768]{1,0:T(8,128)(2,1)}, bf16[192,768]{1,0:T(8,128)(2,1)S(1)}, u32[]{:S(2)}, u32[]{:S(2)}) collective-permute-start(bf16[192,768]{1,0:T(8,128)(2,1)} %get-tuple-element.244), channel_id=1, source_target_pairs={{0,12},{4,8},{8,4},{12,0},{16,28},{20,24},{24,20},{28,16},{1,13},{... | collective-permute-start | bytes 884744 | tf_op jit(solution)/shard_map/ppermute | solution.py:124
  602.3 21.4 %collective-permute-start.53 = (bf16[192,768]{1,0:T(8,128)(2,1)}, bf16[192,768]{1,0:T(8,128)(2,1)S(1)}, u32[]{:S(2)}, u32[]{:S(2)}) collective-permute-start(bf16[192,768]{1,0:T(8,128)(2,1)} %get-tuple-element.243), channel_id=1, source_target_pairs={{0,16},{4,20},{8,24},{12,28},{16,0},{20,4},{24,8},{28,12},{1,17},{... | collective-permute-start | bytes 884744 | tf_op jit(solution)/shard_map/ppermute | solution.py:124
  608.8 20.2 %collective-permute-start.54 = (bf16[192,768]{1,0:T(8,128)(2,1)}, bf16[192,768]{1,0:T(8,128)(2,1)S(1)}, u32[]{:S(2)}, u32[]{:S(2)}) collective-permute-start(bf16[192,768]{1,0:T(8,128)(2,1)} %get-tuple-element.242), channel_id=1, source_target_pairs={{0,20},{4,16},{8,28},{12,24},{16,4},{20,0},{24,12},{28,8},{1,21},{... | collective-permute-start | bytes 884744 | tf_op jit(solution)/shard_map/ppermute | solution.py:124
  609.6 20.3 %collective-permute-start.55 = (bf16[192,768]{1,0:T(8,128)(2,1)}, bf16[192,768]{1,0:T(8,128)(2,1)S(1)}, u32[]{:S(2)}, u32[]{:S(2)}) collective-permute-start(bf16[192,768]{1,0:T(8,128)(2,1)} %get-tuple-element.241), channel_id=1, source_target_pairs={{0,24},{4,28},{8,16},{12,20},{16,8},{20,12},{24,0},{28,4},{1,25},{... | collective-permute-start | bytes 884744 | tf_op jit(solution)/shard_map/ppermute | solution.py:124
  615.1 24.7 %collective-permute-start.56 = (bf16[192,768]{1,0:T(8,128)(2,1)S(1)}, bf16[192,768]{1,0:T(8,128)(2,1)S(1)}, u32[]{:S(2)}, u32[]{:S(2)}) collective-permute-start(bf16[192,768]{1,0:T(8,128)(2,1)S(1)} %copy-done.70), channel_id=1, source_target_pairs={{0,28},{4,24},{8,20},{12,16},{16,12},{20,8},{24,4},{28,0},{1,29},{... | collective-permute-start | bytes 884744 | tf_op jit(solution)/shard_map/ppermute | solution.py:124
  621.2 35.7 %collective-permute-start.36 = (f32[197,192]{1,0:T(8,128)}, f32[197,192]{1,0:T(8,128)}, u32[]{:S(2)}, u32[]{:S(2)}) collective-permute-start(f32[197,192]{1,0:T(8,128)} %slice.532), channel_id=1, source_target_pairs={{0,0},{1,4},{2,8},{3,12},{4,1},{5,5},{6,9},{7,13},{8,2},{9,6},{10,... | collective-permute-start | bytes 453896 | tf_op jit(solution)/shard_map/ppermute | solution.py:118
  623.8 34.9 %collective-permute-start.37 = (f32[197,192]{1,0:T(8,128)}, f32[197,192]{1,0:T(8,128)}, u32[]{:S(2)}, u32[]{:S(2)}) collective-permute-start(f32[197,192]{1,0:T(8,128)} %slice.533), channel_id=1, source_target_pairs={{0,0},{1,4},{2,8},{3,12},{4,1},{5,5},{6,9},{7,13},{8,2},{9,6},{10,... | collective-permute-start | bytes 453896 | tf_op jit(solution)/shard_map/ppermute | solution.py:118
  (99 other events, 1113.5 us)

commit v2 on v1

--- a/solution.py
+++ b/solution.py
@@ -1,8 +1,11 @@
+import functools
 import math
 
 import jax
 import jax.numpy as jnp
 from jax import lax
+from jax.experimental import pallas as pl
+from jax.experimental.pallas import tpu as pltpu
 from jax.sharding import PartitionSpec as P
 
 HD = 64
@@ -18,18 +21,6 @@
 kinds = 4
 
 
-def product(left_side, right_side):
-    return lax.dot_general(
-        left_side, right_side, (((1,), (0,)), ((), ())), preferred_element_type=jnp.float32
-    )
-
-
-def product_flipped(left_side, right_side):
-    return lax.dot_general(
-        left_side, right_side, (((1,), (1,)), ((), ())), preferred_element_type=jnp.float32
-    )
-
-
 def outer_grad(left_side, right_side):
     return lax.dot_general(
         left_side, right_side, (((0,), (0,)), ((), ())), preferred_element_type=jnp.float32
@@ -62,54 +53,192 @@
     return inverse * (scaled - first - plain * second)
 
 
-def split_heads(mixed_low):
-    token_count = mixed_low.shape[0]
-    heads_here = mixed_low.shape[1] // (3 * HD)
-    grouped = mixed_low.reshape(token_count, heads_here, 3, HD)
-    return (grouped[:, :, 0, :], grouped[:, :, 1, :], grouped[:, :, 2, :])
-
-
-def score_block(query_rows, key_rows):
-    return jnp.einsum(
-        "qhd,khd->hqk", query_rows, key_rows, preferred_element_type=jnp.float32
-    ) * HD ** (-0.5)
-
-
-def attend_forward(mixed_low):
-    query_rows, key_rows, value_rows = split_heads(mixed_low)
-    scores = score_block(query_rows, key_rows)
-    row_top = jnp.max(scores, axis=-1, keepdims=True)
-    log_total = jnp.log(jnp.sum(jnp.exp(scores - row_top), axis=-1, keepdims=True)) + row_top
-    weights = jnp.exp(scores - log_total).astype(jnp.bfloat16)
-    attended = jnp.einsum("hqk,khd->qhd", weights, value_rows, preferred_element_type=jnp.float32)
-    return (attended.reshape(mixed_low.shape[0], -1).astype(jnp.bfloat16), log_total)
-
-
-def attend_backward(mixed_low, log_total, grad_att):
-    query_rows, key_rows, value_rows = split_heads(mixed_low)
-    scores = score_block(query_rows, key_rows)
-    probs = jnp.exp(scores - log_total)
-    grad_out = grad_att.reshape(query_rows.shape)
-    grad_probs = jnp.einsum(
-        "qhd,khd->hqk", grad_out, value_rows, preferred_element_type=jnp.float32
-    )
-    grad_scores = (
-        probs * (grad_probs - jnp.sum(probs * grad_probs, axis=-1, keepdims=True))
-    ).astype(jnp.bfloat16)
+def wide_dot(left_side, right_side, left_dim, right_dim):
+    return lax.dot_general(
+        left_side,
+        right_side,
+        (((left_dim,), (right_dim,)), ((), ())),
+        preferred_element_type=jnp.float32,
+    )
+
+
+def in_vmem(count):
+    return [pl.BlockSpec(memory_space=pltpu.VMEM)] * count
+
+
+def kernel_call(body, inputs, outputs, scratch, flops, position=None):
+    specs = in_vmem(len(inputs))
+    operands = list(inputs)
+    if position is not None:
+        specs = [pl.BlockSpec(memory_space=pltpu.SMEM)] + specs
+        operands = [position] + operands
+    moved = sum(math.prod(o.shape) * o.dtype.itemsize for o in list(inputs) + list(outputs))
+    return pl.pallas_call(
+        body,
+        out_shape=list(outputs),
+        in_specs=specs,
+        out_specs=in_vmem(len(outputs)),
+        scratch_shapes=scratch,
+        compiler_params=pltpu.CompilerParams(vmem_limit_bytes=32 * 1024 * 1024),
+        cost_estimate=pl.CostEstimate(flops=flops, bytes_accessed=moved, transcendentals=0),
+    )(*operands)
+
+
+def put_chunks(position_ref, chunk_refs, whole_ref):
+    chunk = chunk_refs[0].shape[0]
+    for k, chunk_ref in enumerate(chunk_refs):
+        start = pl.multiple_of((position_ref[0] ^ k) * chunk, 8)
+        whole_ref[pl.ds(start, chunk), :] = chunk_ref[...].astype(jnp.float32)
+
+
+def take_chunks(position_ref, whole_ref, chunk_refs):
+    chunk = chunk_refs[0].shape[0]
+    for k, chunk_ref in enumerate(chunk_refs):
+        start = pl.multiple_of((position_ref[0] ^ k) * chunk, 8)
+        chunk_ref[...] = whole_ref[pl.ds(start, chunk), :].astype(chunk_ref.dtype)
+
+
+def keep_rows(values, tokens):
+    rows = lax.broadcasted_iota(jnp.int32, values.shape, 0)
+    return jnp.where(rows < tokens, values, jnp.zeros_like(values))
+
+
+def head_probs(mixed, head, tokens):
+    start = head * 3 * HD
+    query = mixed[:, start : start + HD]
+    key = mixed[:, start + HD : start + 2 * HD]
+    value = mixed[:, start + 2 * HD : start + 3 * HD]
+    scores = wide_dot(query, key, 1, 1) * HD ** (-0.5)
+    columns = lax.broadcasted_iota(jnp.int32, scores.shape, 1)
+    scores = jnp.where(columns < tokens, scores, -jnp.inf)
+    exps = jnp.exp(scores - jnp.max(scores, axis=1, keepdims=True))
+    probs = exps / jnp.sum(exps, axis=1, keepdims=True)
+    return (query, key, value, probs)
+
+
+def attend_kernel(tokens, heads, position, *refs):
+    size = (len(refs) - 7) // 2
+    chunks, (w_qkv, w_proj) = refs[:size], refs[size : size + 2]
+    outs = refs[size + 2 : 2 * size + 2]
+    mixed_out, normed_out, att_out, whole, att_all = refs[2 * size + 2 :]
+    put_chunks(position, chunks, whole)
+    normed = keep_rows(whole[...], tokens).astype(jnp.bfloat16)
+    normed_out[...] = normed[: normed_out.shape[0]]
+    mixed = wide_dot(normed, w_qkv[...], 1, 0).astype(jnp.bfloat16)
+    mixed_out[...] = mixed
+    for head in range(heads):
+        _, _, value, probs = head_probs(mixed, head, tokens)
+        att_all[:, head * HD : (head + 1) * HD] = wide_dot(probs.astype(jnp.bfloat16), value, 1, 0)
+    attended = keep_rows(att_all[...], tokens).astype(jnp.bfloat16)
+    att_out[...] = jnp.zeros_like(att_out)
+    att_out[:, : heads * HD] = attended[: att_out.shape[0]]
+    whole[...] = wide_dot(attended, w_proj[...], 1, 1)
+    take_chunks(position, whole, outs)
+
+
+def attend_back_kernel(tokens, heads, position, *refs):
+    size = (len(refs) - 7) // 2
+    chunks, (mixed_ref, w_qkv, w_proj) = refs[:size], refs[size : size + 3]
+    outs = refs[size + 3 : 2 * size + 3]
+    mixed_grad_out, back_out, whole, mixed_grad = refs[2 * size + 3 :]
+    put_chunks(position, chunks, whole)
+    back = whole[...].astype(jnp.bfloat16)
+    back_out[...] = back[: back_out.shape[0]]
+    att_grad = wide_dot(back, w_proj[...], 1, 0).astype(jnp.bfloat16)
+    mixed = mixed_ref[...]
     scaling = HD ** (-0.5)
-    grad_query = (
-        jnp.einsum("hqk,khd->qhd", grad_scores, key_rows, preferred_element_type=jnp.float32)
-        * scaling
-    )
-    grad_key = (
-        jnp.einsum("hqk,qhd->khd", grad_scores, query_rows, preferred_element_type=jnp.float32)
-        * scaling
-    )
-    grad_value = jnp.einsum(
-        "hqk,qhd->khd", probs.astype(jnp.bfloat16), grad_out, preferred_element_type=jnp.float32
-    )
-    stacked = jnp.stack((grad_query, grad_key, grad_value), axis=2)
-    return stacked.reshape(mixed_low.shape[0], -1).astype(jnp.bfloat16)
+    for head in range(heads):
+        query, key, value, probs = head_probs(mixed, head, tokens)
+        grad = att_grad[:, head * HD : (head + 1) * HD]
+        probs_grad = wide_dot(grad, value, 1, 1)
+        inner = jnp.sum(probs * probs_grad, axis=1, keepdims=True)
+        scores_grad = (probs * (probs_grad - inner)).astype(jnp.bfloat16)
+        start = head * 3 * HD
+        mixed_grad[:, start : start + HD] = wide_dot(scores_grad, key, 1, 0) * scaling
+        mixed_grad[:, start + HD : start + 2 * HD] = wide_dot(scores_grad, query, 0, 0) * scaling
+        mixed_grad[:, start + 2 * HD : start + 3 * HD] = wide_dot(
+            probs.astype(jnp.bfloat16), grad, 0, 0
+        )
+    grads = mixed_grad[...].astype(jnp.bfloat16)
+    mixed_grad_out[...] = jnp.zeros_like(mixed_grad_out)
+    mixed_grad_out[:, : grads.shape[1]] = grads[: mixed_grad_out.shape[0]]
+    whole[...] = wide_dot(grads, w_qkv[...], 1, 1)
+    take_chunks(position, whole, outs)
+
+
+def norm_kernel(level_index, first_row, size, *refs):
+    parts, (stream_ref, norms) = refs[:size], refs[size : size + 2]
+    stream_out, normed_out = refs[size + 2 :]
+    stream = stream_ref[...]
+    for part in parts:
+        stream = stream + part[...].astype(jnp.float32)
+    stream_out[...] = stream
+    plain, _ = norm_parts_of(stream)
+    gain = norms[level_index, first_row : first_row + 1, :]
+    bias = norms[level_index, first_row + 1 : first_row + 2, :]
+    normed_out[...] = (plain * gain + bias).astype(jnp.bfloat16)
+
+
+def norm_back_kernel(level_index, first_row, size, *refs):
+    parts, (stream_ref, upstream_ref, norms) = refs[:size], refs[size : size + 3]
+    upstream_out, low_out, sums_out = refs[size + 3 :]
+    grad = parts[0][...].astype(jnp.float32)
+    for part in parts[1:]:
+        grad = grad + part[...].astype(jnp.float32)
+    plain, inverse = norm_parts_of(stream_ref[...])
+    gain = norms[level_index, first_row : first_row + 1, :]
+    upstream = upstream_ref[...] + norm_backward(grad, plain, inverse, gain)
+    upstream_out[...] = upstream
+    low_out[...] = upstream.astype(jnp.bfloat16)
+    sums_out[0:1, :] = jnp.sum(grad * plain, axis=0, keepdims=True)
+    sums_out[1:2, :] = jnp.sum(grad, axis=0, keepdims=True)
+
+
+def first_kernel(tokens, position, blocks, norms, *refs):
+    outs, stream_out, whole = refs[:-2], refs[-2], refs[-1]
+    size, _, width = blocks.shape
+    whole[...] = jnp.zeros_like(whole)
+    for i in range(size):
+        whole[0:tokens, i * width : (i + 1) * width] = blocks[i].astype(jnp.float32)
+    chunk = stream_out.shape[0]
+    start = pl.multiple_of(position[0] * chunk, 8)
+    stream_out[...] = whole[pl.ds(start, chunk), :]
+    plain, _ = norm_parts_of(whole[...])
+    whole[...] = plain * norms[0, 0:1, :] + norms[0, 1:2, :]
+    take_chunks(position, whole, outs)
+
+
+def mlp_kernel(tokens, position, *refs):
+    size = (len(refs) - 6) // 2
+    chunks, (w_up, w_down) = refs[:size], refs[size : size + 2]
+    outs = refs[size + 2 : 2 * size + 2]
+    slope_out, normed_out, act_out, whole = refs[2 * size + 2 :]
+    put_chunks(position, chunks, whole)
+    normed = keep_rows(whole[...], tokens).astype(jnp.bfloat16)
+    normed_out[...] = normed[: normed_out.shape[0]]
+    hidden = wide_dot(normed, w_up[...], 1, 0)
+    below = 0.5 + 0.5 * lax.erf(hidden * math.sqrt(0.5))
+    slope_out[...] = below + hidden * jnp.exp(-0.5 * hidden * hidden) * (
+        1.0 / math.sqrt(2.0 * math.pi)
+    )
+    activated = keep_rows(hidden * below, tokens).astype(jnp.bfloat16)
+    act_out[...] = activated[: act_out.shape[0]]
+    whole[...] = wide_dot(activated, w_down[...], 1, 1)
+    take_chunks(position, whole, outs)
+
+
+def mlp_back_kernel(position, *refs):
+    size = (len(refs) - 6) // 2
+    chunks, (slope, w_up, w_down) = refs[:size], refs[size : size + 3]
+    outs = refs[size + 3 : 2 * size + 3]
+    hidden_grad_out, back_out, whole = refs[2 * size + 3 :]
+    put_chunks(position, chunks, whole)
+    back = whole[...].astype(jnp.bfloat16)
+    back_out[...] = back[: back_out.shape[0]]
+    hidden_grad = (wide_dot(back, w_down[...], 1, 0) * slope[...]).astype(jnp.bfloat16)
+    hidden_grad_out[...] = hidden_grad[: hidden_grad_out.shape[0]]
+    whole[...] = wide_dot(hidden_grad, w_up[...], 1, 1)
+    take_chunks(position, whole, outs)
 
 
 def swap_row_col(values):
@@ -161,17 +290,13 @@
     return lax.all_to_all(jnp.broadcast_to(block[None], (size,) + block.shape), axis, 0, 0)
 
 
-def gather_tokens(chunk):
-    blocks = to_all(chunk, "col")
-    return blocks.reshape(-1, chunk.shape[1])
-
-
-def sum_tokens(partial, padded):
+def to_partners(chunk):
     size = lax.axis_size("col")
-    blocks = pad_rows(partial.astype(jnp.bfloat16), padded)
-    blocks = blocks.reshape(size, padded // size, partial.shape[1])
-    blocks = lax.all_to_all(blocks, "col", 0, 0)
-    return jnp.sum(blocks.astype(jnp.float32), axis=0)
+    return [chunk] + [from_partner(chunk, k, ("col",)) for k in range(1, size)]
+
+
+def swap_parts(parts):
+    return [parts[0]] + [from_partner(parts[k], k, ("col",)) for k in range(1, len(parts))]
 
 
 def gram_of(raw):
@@ -278,12 +403,9 @@
     def features_first(blocks):
         return blocks.transpose(1, 0, 2).reshape(blocks.shape[1], model_width)
 
-    def own_chunk(values):
-        return lax.dynamic_slice_in_dim(pad_rows(values, padded), my_chunk, chunk, 0)
-
     all_norms = gather_by_pairs(norm_params, "row")
     all_norms = all_norms.transpose(1, 2, 0, 3).reshape(levels, kinds, model_width)
-    image = features_first(to_all(swap_row_col(residual_in), "col")).astype(jnp.float32)
+    image_blocks = to_all(swap_row_col(residual_in), "col")
     weight_sets = []
     for level_index in range(levels):
         attention = gathered_weights(level_index, (0, 1))
@@ -309,40 +431,91 @@
     own_moment = placed_blocks(moment_parts, [my_row ^ i for i in range(row_size)])
     own_moment = own_moment.reshape(model_width, widest)
 
-    stream = own_chunk(image)
+    position = lax.axis_index("col").astype(jnp.int32).reshape(1)
+    heads = widths[0] // (3 * HD)
+
+    def shaped(rows, columns, kind):
+        return jax.ShapeDtypeStruct((rows, columns), kind)
+
+    low_chunk = shaped(chunk, model_width, jnp.bfloat16)
+    full_chunk = shaped(chunk, model_width, jnp.float32)
+    low_chunks = [low_chunk] * col_size
+    sent = shaped(sent_rows, widest, jnp.bfloat16)
+    sent_model = shaped(sent_rows, model_width, jnp.bfloat16)
+    whole_scratch = pltpu.VMEM((padded, model_width), jnp.float32)
+    attention_flops = 2 * padded * (
+        model_width * (widths[0] + widths[1]) + 2 * padded * widths[1]
+    )
+    perceptron_flops = 2 * padded * model_width * (widths[2] + widths[3])
+    chunk_flops = 20 * chunk * model_width
+
+    def norm_step(parts, stream, level_index, first_row):
+        return kernel_call(
+            functools.partial(norm_kernel, level_index, first_row, len(parts)),
+            [*parts, stream, all_norms],
+            [full_chunk, low_chunk],
+            [],
+            chunk_flops,
+        )
+
+    def norm_back_step(parts, stream, upstream, level_index, first_row):
+        return kernel_call(
+            functools.partial(norm_back_kernel, level_index, first_row, len(parts)),
+            [*parts, stream, upstream, all_norms],
+            [full_chunk, low_chunk, shaped(2, model_width, jnp.float32)],
+            [],
+            chunk_flops,
+        )
+
+    *chunks, stream = kernel_call(
+        functools.partial(first_kernel, tokens),
+        [image_blocks, all_norms],
+        low_chunks + [full_chunk],
+        [whole_scratch],
+        20 * padded * model_width,
+        position,
+    )
     saved = []
     early = []
     for level_index in range(levels):
         weight_qkv, weight_proj, weight_up, weight_down = weight_sets[level_index]
-        gains = all_norms[level_index]
-        plain_one, inverse_one = norm_parts_of(stream)
-        if level_index == 0:
-            normed_one = (norm_parts_of(image)[0] * gains[0] + gains[1]).astype(jnp.bfloat16)
+        stream_one = stream
+        *parts, mixed, normed_one, attended = kernel_call(
+            functools.partial(attend_kernel, tokens, heads),
+            [*chunks, weight_qkv, weight_proj],
+            low_chunks + [shaped(padded, widths[0], jnp.bfloat16), sent_model, sent],
+            [whole_scratch, pltpu.VMEM((padded, widths[1]), jnp.float32)],
+            attention_flops,
+            position,
+        )
+        stream_two, normed = norm_step(swap_parts(parts), stream, level_index, 2)
+        chunks = to_partners(normed)
+        *parts, slope, normed_two, activated = kernel_call(
+            functools.partial(mlp_kernel, tokens),
+            [*chunks, weight_up, weight_down],
+            low_chunks + [shaped(padded, widths[2], jnp.float32), sent_model, sent],
+            [whole_scratch],
+            perceptron_flops,
+            position,
+        )
+        parts = swap_parts(parts)
+        if level_index < levels - 1:
+            stream, normed = norm_step(parts, stream_two, level_index + 1, 0)
+            chunks = to_partners(normed)
         else:
-            normed_one = gather_tokens(
-                (plain_one * gains[0] + gains[1]).astype(jnp.bfloat16)
-            )[:tokens]
-        mixed_low = product(normed_one, weight_qkv).astype(jnp.bfloat16)
-        attended, log_total = attend_forward(mixed_low)
-        stream = stream + sum_tokens(product_flipped(attended, weight_proj), padded)
-        plain_two, inverse_two = norm_parts_of(stream)
-        normed_two = gather_tokens((plain_two * gains[2] + gains[3]).astype(jnp.bfloat16))[:tokens]
-        hidden = product(normed_two, weight_up)
-        activated = jax.nn.gelu(hidden, approximate=False).astype(jnp.bfloat16)
-        stream = stream + sum_tokens(product_flipped(activated, weight_down), padded)
-        saved.append((plain_one, inverse_one, mixed_low, log_total, plain_two, inverse_two, hidden))
+            stream = stream_two
+            for part in parts:
+                stream = stream + part.astype(jnp.float32)
+        saved.append((stream_one, stream_two, mixed, slope))
         early.append((normed_one, attended, normed_two, activated))
 
-    def sent_form(values):
-        return pad_rows(pad_columns(values, widest), sent_rows)
-
-    early_stack = jnp.stack([sent_form(early[j % levels][j // levels]) for j in range(jobs)])
+    early_stack = jnp.stack([early[j % levels][j // levels] for j in range(jobs)])
     early_all = [pick(early_stack, me)]
     for step in range(1, jobs):
         early_all.append(from_partner(pick(early_stack, me ^ step), step))
 
     def send_late(parts, level_index):
-        stack = jnp.stack([sent_form(part) for part in parts])
+        stack = jnp.stack(parts)
         received = [pick(stack, me // levels)]
         for step in range(1, jobs):
             received.append(
@@ -357,41 +530,43 @@
     upstream, own_moment = lax.optimization_barrier((upstream, own_moment))
     late = [None] * levels
     norm_sums = [None] * levels
+    back_low = upstream.astype(jnp.bfloat16)
     for level_index in reversed(range(levels)):
         weight_qkv, weight_proj, weight_up, weight_down = weight_sets[level_index]
-        plain_one, inverse_one, mixed_low, log_total, plain_two, inverse_two, hidden = saved[
-            level_index
-        ]
-        gains = all_norms[level_index]
-        back_two = gather_tokens(upstream.astype(jnp.bfloat16))[:tokens]
-        act_grad = product(back_two, weight_down)
-        hidden_grad = jax.vjp(lambda inner: jax.nn.gelu(inner, approximate=False), hidden)[1](
-            act_grad
-        )[0].astype(jnp.bfloat16)
-        normed_grad_two = sum_tokens(product_flipped(hidden_grad, weight_up), padded)
-        upstream = upstream + norm_backward(normed_grad_two, plain_two, inverse_two, gains[2])
+        stream_one, stream_two, mixed, slope = saved[level_index]
+        *parts, hidden_grad, back_two = kernel_call(
+            mlp_back_kernel,
+            [*to_partners(back_low), slope, weight_up, weight_down],
+            low_chunks + [sent, sent_model],
+            [whole_scratch],
+            perceptron_flops,
+            position,
+        )
+        upstream, back_low, sums_two = norm_back_step(
+            swap_parts(parts), stream_two, upstream, level_index, 2
+        )
         if level_index == levels - 1:
-            upstream, early_all = lax.optimization_barrier((upstream, early_all))
+            back_low, early_all = lax.optimization_barrier((back_low, early_all))
         else:
-            upstream, late[level_index + 1] = lax.optimization_barrier(
-                (upstream, late[level_index + 1])
+            back_low, late[level_index + 1] = lax.optimization_barrier(
+                (back_low, late[level_index + 1])
             )
-        back_one = gather_tokens(upstream.astype(jnp.bfloat16))[:tokens]
-        att_grad = product(back_one, weight_proj).astype(jnp.bfloat16)
-        mixed_grad = attend_backward(mixed_low, log_total, att_grad)
-        normed_grad_one = sum_tokens(product_flipped(mixed_grad, weight_qkv), padded)
-        upstream = upstream + norm_backward(normed_grad_one, plain_one, inverse_one, gains[0])
-        norm_sums[level_index] = jnp.stack(
-            (
-                jnp.sum(normed_grad_one * plain_one, axis=0),
-                jnp.sum(normed_grad_one, axis=0),
-                jnp.sum(normed_grad_two * plain_two, axis=0),
-                jnp.sum(normed_grad_two, axis=0),
-            )
+        *parts, mixed_grad, back_one = kernel_call(
+            functools.partial(attend_back_kernel, tokens, heads),
+            [*to_partners(back_low), mixed, weight_qkv, weight_proj],
+            low_chunks + [sent, sent_model],
+            [whole_scratch, pltpu.VMEM((padded, widths[0]), jnp.float32)],
+            3 * attention_flops,
+            position,
         )
         late[level_index] = send_late(
             (mixed_grad, back_one, hidden_grad, back_two), level_index
         )
+        if level_index:
+            upstream, back_low, sums_one = norm_back_step(
+                swap_parts(parts), stream_one, upstream, level_index, 0
+            )
+            norm_sums[level_index] = jnp.concatenate([sums_one, sums_two])
 
     early_all = jnp.concatenate(early_all, axis=0)
     late_all = jnp.concatenate(late[0], axis=0)
@@ -418,9 +593,11 @@
         return [received[j].astype(jnp.float32) for j in range(jobs)]
 
     own_raw = moment_decay * own_moment + own_grad
-    gram, own_grad, stream, upstream, norm_sums = lax.optimization_barrier(
-        (gram_of(own_raw), own_grad, stream, upstream, norm_sums)
-    )
+    gram, own_grad, stream, parts = lax.optimization_barrier(
+        (gram_of(own_raw), own_grad, stream, parts)
+    )
+    upstream, _, sums_one = norm_back_step(swap_parts(parts), stream_one, upstream, 0, 0)
+    norm_sums[0] = jnp.concatenate([sums_one, sums_two])
     grads = returned(own_grad)
     norm_whole = jnp.stack(norm_sums)
     for axis in ("row", "col", "dp"):

time: 674 us -> 618 us (0.917)
  the two profiles are of different devices: /device:TPU:16 before, /device:TPU:25 now
where the time goes in v2:
time: 618 us; the launch traced here: 611 us
  starting transfers between devices  185 us (30%)
  waiting for transfers between devices  151 us (24%)
  local copies, waits for them, and re-layouts  111 us (18%)
  matrix products  72.6 us (12%)
  blocking collectives  39.4 us (6%)
  other arithmetic  36.7 us (6%)
  Pallas kernels  11.5 us (2%)
    ppermute x98, starting transfers between devices, from_partner(): return lax.ppermute(values, axes, pairs)  145 us
    ppermute x98, waiting for transfers between devices, from_partner(): return lax.ppermute(values, axes, pairs)  140 us
    dot_general x14, matrix products, dot_high(): return jnp.dot(left_side, right_side, precision=high)  65.8 us
    all_to_all x1, blocking collectives, gram_of(): lax.all_to_all(packed.reshape(size, third // size, -1), 'col', 0, 0)  39.4 us
    unnamed x195, local copies, waits for them, and re-layouts  37.7 us
    dynamic_update_slice x31, local copies, waits for them, and re-layouts, placed_blocks(): result = lax.dynamic_update_index_in_dim(result, block, place, 0)  28.3 us
    all_to_all x2, starting transfers between devices, placed(): blocks = lax.all_to_all(blocks, 'col', 0, 0)  12.9 us
    ppermute x4, starting transfers between devices, swap_row_col(): return lax.ppermute(values, ('row', 'col'), pairs)  12.7 us
  transfers between devices with their start and end apart: 107, of which 34 were waited for; matrix products, arithmetic and copies ran while one was open for 24% of the time, Pallas kernels for 1%

profile of v2, /device:TPU:25, one launch (start us, length us, event | category | flops | bytes accessed | tf_op | source)
XLA Modules:
  0.0 611.1 jit_solution(2702061758665596471)
XLA Ops:
  2.6 2.9 collective-permute-start
  14.0 3.9 collective-permute-start.7
  38.5 5.0 all-to-all-start
  51.6 4.8 all-to-all-start.1
  68.9 17.7 %collective-permute-done.18 = bf16[1,192,1536]{2,1,0:T(8,128)(2,1)} collective-permute-done((bf16[1,192,1536]{2,1,0:T(8,128)(2,1)}, bf16[1,192,1536]{2,1,0:T(8,128)(2,1)}, u32[]{:S(2)}, u32[]{:S(2)}) %collective-permute-start.18) | collective-permute-done | bytes 589856 | tf_op jit(solution)/shard_map/ppermute | solution.py:253
  102.8 3.2 collective-permute-start.14
  113.6 3.3 collective-permute-start.17
  127.2 2.9 collective-permute-done.21.refs_2_
  130.8 3.6 collective-permute-start.23
  142.8 3.5 collective-permute-start.28
  148.4 4.2 collective-permute-done.29.refs_2_
  152.8 4.1 collective-permute-start.31
  159.1 4.0 collective-permute-done.32
  166.2 4.0 collective-permute-start.39
  176.2 6.0 collective-permute-done.5.refs_2_
  192.3 3.1 collective-permute-done.37.refs_2_
  203.6 3.5 copy.118
  211.8 3.6 collective-permute-done.43
  217.0 9.1 %collective-permute-done.45 = bf16[208,768]{1,0:T(8,128)(2,1)} collective-permute-done((bf16[208,768]{1,0:T(8,128)(2,1)}, bf16[208,768]{1,0:T(8,128)(2,1)}, u32[]{:S(2)}, u32[]{:S(2)}) %collective-permute-start.45) | collective-permute-done | bytes 319520 | tf_op jit(solution)/shard_map/ppermute | solution.py:253
  226.8 2.9 collective-permute-start.48
  231.7 3.3 collective-permute-done.47.refs_2_
  246.7 2.8 collective-permute-start.59
  256.5 2.9 collective-permute-done.53.refs_2_
  260.8 4.0 collective-permute-start.55
  274.4 5.8 collective-permute-start.63
  284.8 3.0 collective-permute-done.63
  287.8 3.8 collective-permute-done.64
  291.6 3.5 collective-permute-start.67
  296.3 3.3 collective-permute-done.66.refs_2_
  304.4 4.8 collective-permute-start.70
  309.9 4.5 collective-permute-start.72
  315.3 4.1 collective-permute-start.74
  321.7 4.2 collective-permute-done.74
  325.9 3.8 multiply_add_fusion.12
  333.0 39.4 %all_to_all.30 = f32[4,64,1536]{2,1,0:T(8,128)} all-to-all(f32[4,64,1536]{2,1,0:T(8,128)S(1)} %bitcast.339), channel_id=1, replica_groups=mesh['dp'=2,'row'=4,'col'=4] {'col'}, dimensions={0} | all-to-all | bytes 3145728 | tf_op jit(solution)/shard_map/all_to_all | solution.py:317
  375.3 5.3 all-to-all-start.3
  385.2 21.4 %collective-permute-done.77 = bf16[56,768]{1,0:T(8,128)(2,1)S(1)} collective-permute-done((bf16[56,768]{1,0:T(8,128)(2,1)S(1)}, bf16[56,768]{1,0:T(8,128)(2,1)S(1)}, u32[]{:S(2)}, u32[]{:S(2)}) %collective-permute-start.77) | collective-permute-done | bytes 86048 | tf_op jit(solution)/shard_map/ppermute | solution.py:253
  406.6 14.1 %collective-permute-done.76 = bf16[56,768]{1,0:T(8,128)(2,1)S(1)} collective-permute-done((bf16[56,768]{1,0:T(8,128)(2,1)S(1)}, bf16[56,768]{1,0:T(8,128)(2,1)S(1)}, u32[]{:S(2)}, u32[]{:S(2)}) %collective-permute-start.76) | collective-permute-done | bytes 86048 | tf_op jit(solution)/shard_map/ppermute | solution.py:253
  427.6 3.2 broadcast_multiply_fusion
  432.6 3.3 fusion.108
  436.0 7.3 %multiply_add_fusion.3 = f32[768,1536]{0,1:T(8,128)S(1)} fusion(f32[768,768]{0,1:T(8,128)S(1)} %copy-done.54, f32[768,768]{0,1:T(8,128)S(1)} %broadcast_multiply_fusion.1, f32[768,768]{0,1:T(8,128)S(1)} %fusion.108), kind=kOutput, calls=%fused_computation.7 | convolution fusion | flops 5442306048 | bytes 11796480 | tf_op jit(solution)/shard_map/dot_general | solution.py:31
  445.4 4.0 multiply_add_fusion.10
  449.4 3.3 fusion.109
  452.7 7.4 %multiply_add_fusion.2 = f32[768,1536]{0,1:T(8,128)S(1)} fusion(f32[768,768]{0,1:T(8,128)S(1)} %slice-done, f32[768,768]{0,1:T(8,128)S(1)} %multiply_add_fusion.10, f32[768,768]{0,1:T(8,128)S(1)} %fusion.109), kind=kOutput, calls=%fused_computation.6 | convolution fusion | flops 5442306048 | bytes 11796480 | tf_op jit(solution)/shard_map/dot_general | solution.py:31
  462.3 4.9 multiply_add_fusion.8
  468.0 6.6 %all-to-all-start.4 = ((f32[4,56,192]{2,1,0:T(8,128)}), f32[4,56,192]{2,1,0:T(8,128)S(1)}, u32[]{:S(2)}, u32[]{:S(2)}) async-start(f32[4,56,192]{2,1,0:T(8,128)} %bitcast.324), calls=%async_computation.4 | async-start | bytes 458752 | tf_op jit(solution)/shard_map/all_to_all | solution.py:632
  475.0 3.2 collective-permute-start.81
  481.2 2.9 collective-permute-start.83
  484.1 3.3 fusion.110
  487.4 7.3 %multiply_add_fusion.1 = f32[768,1536]{0,1:T(8,128)S(1)} fusion(f32[768,768]{0,1:T(8,128)S(1)} %slice-done.1, f32[768,768]{0,1:T(8,128)S(1)} %copy-done.32, f32[768,768]{0,1:T(8,128)S(1)} %fusion.110), kind=kOutput, calls=%fused_computation.5 | convolution fusion | flops 5442306048 | bytes 11796480 | tf_op jit(solution)/shard_map/dot_general | solution.py:31
  494.6 4.0 multiply_add_fusion.6
  498.7 3.3 fusion.111
  506.6 7.3 %multiply_add_fusion = f32[768,1536]{0,1:T(8,128)S(1)} fusion(f32[768,768]{0,1:T(8,128)S(1)} %slice.377, f32[768,768]{0,1:T(8,128)S(1)} %multiply_add_fusion.6, f32[768,768]{0,1:T(8,128)S(1)} %fusion.111), kind=kOutput, calls=%fused_computation.4 | convolution fusion | flops 5442306048 | bytes 11796480 | tf_op jit(solution)/shard_map/dot_general | solution.py:31
  514.5 3.8 multiply_add_fusion.4
  518.4 3.3 fusion.112
  521.8 3.4 add_convert_fusion
  529.8 3.4 collective-permute-start.87
  533.9 6.3 %all-to-all-start.5 = ((f32[4,56,192]{2,1,0:T(8,128)}), f32[4,56,192]{2,1,0:T(8,128)S(1)}, u32[]{:S(2)}, u32[]{:S(2)}) async-start(f32[4,56,192]{2,1,0:T(8,128)} %bitcast.323), calls=%async_computation.5 | async-start | bytes 458752 | tf_op jit(solution)/shard_map/all_to_all | solution.py:632
  560.1 3.0 collective-permute-done.96
  564.3 5.7 collective-permute-done.97
  570.0 3.1 collective-permute-start.78
  576.8 9.5 %collective-permute-done.101 = bf16[192,768]{1,0:T(8,128)(2,1)S(1)} collective-permute-done((bf16[192,768]{1,0:T(8,128)(2,1)S(1)}, bf16[192,768]{1,0:T(8,128)(2,1)S(1)}, u32[]{:S(2)}, u32[]{:S(2)}) %collective-permute-start.101) | collective-permute-done | bytes 294944 | tf_op jit(solution)/shard_map/ppermute | solution.py:253
  595.5 2.8 collective-permute-start.82
  600.2 9.9 %collective-permute-done.82 = f32[197,192]{1,0:T(8,128)S(1)} collective-permute-done((f32[197,192]{1,0:T(8,128)S(1)}, f32[197,192]{1,0:T(8,128)S(1)}, u32[]{:S(2)}, u32[]{:S(2)}) %collective-permute-start.82) | collective-permute-done | bytes 151328 | tf_op jit(solution)/shard_map/ppermute | solution.py:247
  (526 shorter events, 252.9 us)
Async XLA Ops:
  2.6 31.9 %collective-permute-start = (f32[197,192]{1,0:T(8,128)}, f32[197,192]{1,0:T(8,128)}, u32[]{:S(2)}, u32[]{:S(2)}) collective-permute-start(f32[197,192]{1,0:T(8,128)} %copy.114), channel_id=1, source_target_pairs={{0,0},{1,4},{2,8},{3,12},{4,1},{5,5},{6,9},{7,13},{8,2},{9,6},{10,... | collective-permute-start | bytes 453896 | tf_op jit(solution)/shard_map/ppermute | solution.py:247
  13.7 75.5 %collective-permute-start.1 = (f32[192,768]{1,0:T(8,128)}, f32[192,768]{1,0:T(8,128)}, u32[]{:S(2)}, u32[]{:S(2)}) collective-permute-start(f32[192,768]{1,0:T(8,128)} %get-tuple-element.337), channel_id=1, source_target_pairs={{0,4},{4,0},{8,12},{12,8},{16,20},{20,16},{24,28},{28,24},{1,5},{5... | collective-permute-start | bytes 1769480 | tf_op jit(solution)/shard_map/ppermute | solution.py:253
  14.0 34.0 %collective-permute-start.7 = (bf16[197,192]{0,1:T(8,128)(2,1)}, bf16[197,192]{0,1:T(8,128)(2,1)}, u32[]{:S(2)}, u32[]{:S(2)}) collective-permute-start(bf16[197,192]{0,1:T(8,128)(2,1)} %param.12), channel_id=1, source_target_pairs={{0,0},{1,4},{2,8},{3,12},{4,1},{5,5},{6,9},{7,13},{8,2},{9,6},{10,... | collective-permute-start | bytes 226952 | tf_op jit(solution)/shard_map/ppermute | solution.py:247
  17.8 16.6 %collective-permute-start.8 = (f32[1,2,4,192]{3,2,1,0:T(4,128)S(1)}, f32[1,2,4,192]{3,2,1,0:T(4,128)S(1)}, u32[]{:S(2)}, u32[]{:S(2)}) collective-permute-start(f32[1,2,4,192]{3,2,1,0:T(4,128)S(1)} %bitcast.344), channel_id=1, source_target_pairs={{0,8},{4,12},{8,0},{12,4},{1,9},{5,13},{9,1},{13,5},{2,10},{6,14},... | collective-permute-start | bytes 18440 | tf_op jit(solution)/shard_map/ppermute | solution.py:253
  22.5 25.8 %collective-permute-start.26 = (bf16[1,192,768]{2,1,0:T(8,128)(2,1)}, bf16[1,192,768]{2,1,0:T(8,128)(2,1)}, u32[]{:S(2)}, u32[]{:S(2)}) collective-permute-start(bf16[1,192,768]{2,1,0:T(8,128)(2,1)} %get-tuple-element.308), channel_id=1, source_target_pairs={{0,8},{4,12},{8,0},{12,4},{1,9},{5,13},{9,1},{13,5},{2,10},{6,14},... | collective-permute-start | bytes 884744 | tf_op jit(solution)/shard_map/ppermute | solution.py:253
  34.4 25.6 %collective-permute-start.10 = (bf16[1,192,768]{2,1,0:T(8,128)(2,1)S(1)}, bf16[1,192,768]{2,1,0:T(8,128)(2,1)}, u32[]{:S(2)}, u32[]{:S(2)}) collective-permute-start(bf16[1,192,768]{2,1,0:T(8,128)(2,1)S(1)} %get-tuple-element.310), channel_id=1, source_target_pairs={{0,8},{4,12},{8,0},{12,4},{1,9},{5,13},{9,1},{13,5},{2,10},{6,14},... | collective-permute-start | bytes 884744 | tf_op jit(solution)/shard_map/ppermute | solution.py:253
  34.5 11.9 %collective-permute-start.9 = (f32[2,2,4,192]{3,2,1,0:T(4,128)S(1)}, f32[2,2,4,192]{3,2,1,0:T(4,128)S(1)}, u32[]{:S(2)}, u32[]{:S(2)}) collective-permute-start(f32[2,2,4,192]{3,2,1,0:T(4,128)S(1)} %pad_maximum_fusion.25), channel_id=1, source_target_pairs={{0,4},{4,0},{8,12},{12,8},{1,5},{5,1},{9,13},{13,9},{2,6},{6,2},{1... | collective-permute-start | bytes 36872 | tf_op jit(solution)/shard_map/ppermute | solution.py:253
  38.5 11.4 %all-to-all-start = ((f32[4,56,192]{2,1,0:T(8,128)}), f32[4,56,192]{2,1,0:T(8,128)}, u32[]{:S(2)}, u32[]{:S(2)}) async-start(f32[4,56,192]{2,1,0:T(8,128)} %bitcast.340), calls=%async_computation | async-start | bytes 458752 | tf_op jit(solution)/shard_map/all_to_all | solution.py:416
  46.4 20.9 %collective-permute-start.34 = (bf16[1,192,1536]{2,1,0:T(8,128)(2,1)}, bf16[1,192,1536]{2,1,0:T(8,128)(2,1)}, u32[]{:S(2)}, u32[]{:S(2)}) collective-permute-start(bf16[1,192,1536]{2,1,0:T(8,128)(2,1)} %maximum_bitcast_fusion.1), channel_id=1, source_target_pairs={{0,8},{4,12},{8,0},{12,4},{1,9},{5,13},{9,1},{13,5},{2,10},{6,14},... | collective-permute-start | bytes 1769480 | tf_op jit(solution)/shard_map/ppermute | solution.py:253
  48.0 44.3 %collective-permute-start.2 = (f32[192,768]{1,0:T(8,128)}, f32[192,768]{1,0:T(8,128)}, u32[]{:S(2)}, u32[]{:S(2)}) collective-permute-start(f32[192,768]{1,0:T(8,128)} %get-tuple-element.336), channel_id=1, source_target_pairs={{0,8},{4,12},{8,0},{12,4},{16,24},{20,28},{24,16},{28,20},{1,9},{5... | collective-permute-start | bytes 1769480 | tf_op jit(solution)/shard_map/ppermute | solution.py:253
  48.3 38.4 %collective-permute-start.18 = (bf16[1,192,1536]{2,1,0:T(8,128)(2,1)}, bf16[1,192,1536]{2,1,0:T(8,128)(2,1)}, u32[]{:S(2)}, u32[]{:S(2)}) collective-permute-start(bf16[1,192,1536]{2,1,0:T(8,128)(2,1)} %maximum_bitcast_fusion), channel_id=1, source_target_pairs={{0,8},{4,12},{8,0},{12,4},{1,9},{5,13},{9,1},{13,5},{2,10},{6,14},... | collective-permute-start | bytes 1769480 | tf_op jit(solution)/shard_map/ppermute | solution.py:253
  51.6 15.1 %all-to-all-start.1 = ((bf16[4,197,192]{1,2,0:T(8,128)(2,1)}), bf16[4,197,192]{1,2,0:T(8,128)(2,1)S(1)}, u32[]{:S(2)}, u32[]{:S(2)}) async-start(bf16[4,197,192]{1,2,0:T(8,128)(2,1)} %broadcast_in_dim.116), calls=%async_computation.1 | async-start | bytes 786432 | tf_op jit(solution)/shard_map/all_to_all | solution.py:290
  60.0 35.9 %collective-permute-start.27 = (bf16[2,192,768]{2,1,0:T(8,128)(2,1)}, bf16[2,192,768]{2,1,0:T(8,128)(2,1)}, u32[]{:S(2)}, u32[]{:S(2)}) collective-permute-start(bf16[2,192,768]{2,1,0:T(8,128)(2,1)} %pad_maximum_fusion.23), channel_id=1, source_target_pairs={{0,4},{4,0},{8,12},{12,8},{1,5},{5,1},{9,13},{13,9},{2,6},{6,2},{1... | collective-permute-start | bytes 1769480 | tf_op jit(solution)/shard_map/ppermute | solution.py:253
  67.3 28.6 %collective-permute-start.11 = (bf16[2,192,768]{2,1,0:T(8,128)(2,1)}, bf16[2,192,768]{2,1,0:T(8,128)(2,1)S(1)}, u32[]{:S(2)}, u32[]{:S(2)}) collective-permute-start(bf16[2,192,768]{2,1,0:T(8,128)(2,1)} %pad_maximum_fusion.22), channel_id=1, source_target_pairs={{0,4},{4,0},{8,12},{12,8},{1,5},{5,1},{9,13},{13,9},{2,6},{6,2},{1... | collective-permute-start | bytes 1769480 | tf_op jit(solution)/shard_map/ppermute | solution.py:253
  86.7 26.9 %collective-permute-start.35 = (bf16[2,192,1536]{2,1,0:T(8,128)(2,1)S(1)}, bf16[2,192,1536]{2,1,0:T(8,128)(2,1)S(1)}, u32[]{:S(2)}, u32[]{:S(2)}) collective-permute-start(bf16[2,192,1536]{2,1,0:T(8,128)(2,1)S(1)} %pad_maximum_fusion.21), channel_id=1, source_target_pairs={{0,4},{4,0},{8,12},{12,8},{1,5},{5,1},{9,13},{13,9},{2,6},{6,2},{1... | collective-permute-start | bytes 3538952 | tf_op jit(solution)/shard_map/ppermute | solution.py:253
  89.2 27.7 %collective-permute-start.19 = (bf16[2,192,1536]{2,1,0:T(8,128)(2,1)S(1)}, bf16[2,192,1536]{2,1,0:T(8,128)(2,1)S(1)}, u32[]{:S(2)}, u32[]{:S(2)}) collective-permute-start(bf16[2,192,1536]{2,1,0:T(8,128)(2,1)S(1)} %pad_maximum_fusion.20), channel_id=1, source_target_pairs={{0,4},{4,0},{8,12},{12,8},{1,5},{5,1},{9,13},{13,9},{2,6},{6,2},{1... | collective-permute-start | bytes 3538952 | tf_op jit(solution)/shard_map/ppermute | solution.py:253
  102.7 10.3 %collective-permute-start.13 = (bf16[56,768]{1,0:T(8,128)(2,1)S(1)}, bf16[56,768]{1,0:T(8,128)(2,1)S(1)}, u32[]{:S(2)}, u32[]{:S(2)}) collective-permute-start(bf16[56,768]{1,0:T(8,128)(2,1)S(1)} %get-tuple-element.126), channel_id=1, source_target_pairs={{0,2},{1,3},{2,0},{3,1},{4,6},{5,7},{6,4},{7,5},{8,10},{9,11},{10,... | collective-permute-start | bytes 258056 | tf_op jit(solution)/shard_map/ppermute | solution.py:253
  102.8 10.3 %collective-permute-start.14 = (bf16[56,768]{1,0:T(8,128)(2,1)S(1)}, bf16[56,768]{1,0:T(8,128)(2,1)S(1)}, u32[]{:S(2)}, u32[]{:S(2)}) collective-permute-start(bf16[56,768]{1,0:T(8,128)(2,1)S(1)} %get-tuple-element.127), channel_id=1, source_target_pairs={{0,3},{1,2},{2,1},{3,0},{4,7},{5,6},{6,5},{7,4},{8,11},{9,10},{10,... | collective-permute-start | bytes 258056 | tf_op jit(solution)/shard_map/ppermute | solution.py:253
  110.5 60.9 %collective-permute-start.3 = (f32[192,768]{1,0:T(8,128)S(1)}, f32[192,768]{1,0:T(8,128)S(1)}, u32[]{:S(2)}, u32[]{:S(2)}) collective-permute-start(f32[192,768]{1,0:T(8,128)S(1)} %copy-done.61), channel_id=1, source_target_pairs={{0,12},{4,8},{8,4},{12,0},{16,28},{20,24},{24,20},{28,16},{1,13},{... | collective-permute-start | bytes 1769480 | tf_op jit(solution)/shard_map/ppermute | solution.py:253
  166.2 34.2 %collective-permute-start.39 = (bf16[208,768]{1,0:T(8,128)(2,1)S(1)}, bf16[208,768]{1,0:T(8,128)(2,1)S(1)}, u32[]{:S(2)}, u32[]{:S(2)}) collective-permute-start(bf16[208,768]{1,0:T(8,128)(2,1)S(1)} %get-tuple-element.317), channel_id=1, source_target_pairs={{0,4},{4,0},{8,12},{12,8},{16,20},{20,16},{24,28},{28,24},{1,5},{5... | collective-permute-start | bytes 958472 | tf_op jit(solution)/shard_map/ppermute | solution.py:253
  170.1 31.4 %collective-permute-start.40 = (bf16[208,768]{1,0:T(8,128)(2,1)S(1)}, bf16[208,768]{1,0:T(8,128)(2,1)S(1)}, u32[]{:S(2)}, u32[]{:S(2)}) collective-permute-start(bf16[208,768]{1,0:T(8,128)(2,1)S(1)} %get-tuple-element.316), channel_id=1, source_target_pairs={{0,8},{4,12},{8,0},{12,4},{16,24},{20,28},{24,16},{28,20},{1,9},{5... | collective-permute-start | bytes 958472 | tf_op jit(solution)/shard_map/ppermute | solution.py:253
  190.1 21.6 %collective-permute-start.41 = (bf16[208,768]{1,0:T(8,128)(2,1)}, bf16[208,768]{1,0:T(8,128)(2,1)}, u32[]{:S(2)}, u32[]{:S(2)}) collective-permute-start(bf16[208,768]{1,0:T(8,128)(2,1)} %get-tuple-element.315), channel_id=1, source_target_pairs={{0,12},{4,8},{8,4},{12,0},{16,28},{20,24},{24,20},{28,16},{1,13},{... | collective-permute-start | bytes 958472 | tf_op jit(solution)/shard_map/ppermute | solution.py:253
  196.1 15.7 %collective-permute-start.42 = (bf16[208,768]{1,0:T(8,128)(2,1)}, bf16[208,768]{1,0:T(8,128)(2,1)}, u32[]{:S(2)}, u32[]{:S(2)}) collective-permute-start(bf16[208,768]{1,0:T(8,128)(2,1)} %get-tuple-element.314), channel_id=1, source_target_pairs={{0,16},{4,20},{8,24},{12,28},{16,0},{20,4},{24,8},{28,12},{1,17},{... | collective-permute-start | bytes 958472 | tf_op jit(solution)/shard_map/ppermute | solution.py:253
  197.9 17.4 %collective-permute-start.43 = (bf16[208,768]{1,0:T(8,128)(2,1)}, bf16[208,768]{1,0:T(8,128)(2,1)}, u32[]{:S(2)}, u32[]{:S(2)}) collective-permute-start(bf16[208,768]{1,0:T(8,128)(2,1)} %get-tuple-element.313), channel_id=1, source_target_pairs={{0,20},{4,16},{8,28},{12,24},{16,4},{20,0},{24,12},{28,8},{1,21},{... | collective-permute-start | bytes 958472 | tf_op jit(solution)/shard_map/ppermute | solution.py:253
  200.4 16.7 %collective-permute-start.44 = (bf16[208,768]{1,0:T(8,128)(2,1)}, bf16[208,768]{1,0:T(8,128)(2,1)}, u32[]{:S(2)}, u32[]{:S(2)}) collective-permute-start(bf16[208,768]{1,0:T(8,128)(2,1)} %get-tuple-element.312), channel_id=1, source_target_pairs={{0,24},{4,28},{8,16},{12,20},{16,8},{20,12},{24,0},{28,4},{1,25},{... | collective-permute-start | bytes 958472 | tf_op jit(solution)/shard_map/ppermute | solution.py:253
  202.3 23.9 %collective-permute-start.45 = (bf16[208,768]{1,0:T(8,128)(2,1)}, bf16[208,768]{1,0:T(8,128)(2,1)}, u32[]{:S(2)}, u32[]{:S(2)}) collective-permute-start(bf16[208,768]{1,0:T(8,128)(2,1)} %get-tuple-element.311), channel_id=1, source_target_pairs={{0,28},{4,24},{8,20},{12,16},{16,12},{20,8},{24,4},{28,0},{1,29},{... | collective-permute-start | bytes 958472 | tf_op jit(solution)/shard_map/ppermute | solution.py:253
  245.3 29.1 %collective-permute-start.58 = (bf16[208,768]{1,0:T(8,128)(2,1)S(1)}, bf16[208,768]{1,0:T(8,128)(2,1)S(1)}, u32[]{:S(2)}, u32[]{:S(2)}) collective-permute-start(bf16[208,768]{1,0:T(8,128)(2,1)S(1)} %get-tuple-element.356), channel_id=1, source_target_pairs={{0,4},{8,12},{16,20},{24,28},{1,5},{9,13},{17,21},{25,29},{2,6},{1... | collective-permute-start | bytes 958472 | tf_op jit(solution)/shard_map/ppermute | solution.py:253
  246.7 33.5 %collective-permute-start.59 = (bf16[208,768]{1,0:T(8,128)(2,1)S(1)}, bf16[208,768]{1,0:T(8,128)(2,1)S(1)}, u32[]{:S(2)}, u32[]{:S(2)}) collective-permute-start(bf16[208,768]{1,0:T(8,128)(2,1)S(1)} %get-tuple-element.355), channel_id=1, source_target_pairs={{4,12},{12,4},{20,28},{28,20},{5,13},{13,5},{21,29},{29,21},{6,14}... | collective-permute-start | bytes 958472 | tf_op jit(solution)/shard_map/ppermute | solution.py:253
  267.9 16.8 %collective-permute-start.60 = (bf16[208,768]{1,0:T(8,128)(2,1)S(1)}, bf16[208,768]{1,0:T(8,128)(2,1)S(1)}, u32[]{:S(2)}, u32[]{:S(2)}) collective-permute-start(bf16[208,768]{1,0:T(8,128)(2,1)S(1)} %get-tuple-element.354), channel_id=1, source_target_pairs={{0,12},{8,4},{16,28},{24,20},{1,13},{9,5},{17,29},{25,21},{2,14},{... | collective-permute-start | bytes 958472 | tf_op jit(solution)/shard_map/ppermute | solution.py:253
  270.9 13.9 %collective-permute-start.61 = (bf16[208,768]{1,0:T(8,128)(2,1)S(1)}, bf16[208,768]{1,0:T(8,128)(2,1)S(1)}, u32[]{:S(2)}, u32[]{:S(2)}) collective-permute-start(bf16[208,768]{1,0:T(8,128)(2,1)S(1)} %get-tuple-element.353), channel_id=1, source_target_pairs={{4,20},{12,28},{20,4},{28,12},{5,21},{13,29},{21,5},{29,13},{6,22}... | collective-permute-start | bytes 958472 | tf_op jit(solution)/shard_map/ppermute | solution.py:253
  273.1 11.6 %collective-permute-start.62 = (bf16[208,768]{1,0:T(8,128)(2,1)S(1)}, bf16[208,768]{1,0:T(8,128)(2,1)S(1)}, u32[]{:S(2)}, u32[]{:S(2)}) collective-permute-start(bf16[208,768]{1,0:T(8,128)(2,1)S(1)} %get-tuple-element.352), channel_id=1, source_target_pairs={{0,20},{8,28},{16,4},{24,12},{1,21},{9,29},{17,5},{25,13},{2,22},{... | collective-permute-start | bytes 958472 | tf_op jit(solution)/shard_map/ppermute | solution.py:253
  274.4 13.4 %collective-permute-start.63 = (bf16[208,768]{1,0:T(8,128)(2,1)S(1)}, bf16[208,768]{1,0:T(8,128)(2,1)S(1)}, u32[]{:S(2)}, u32[]{:S(2)}) collective-permute-start(bf16[208,768]{1,0:T(8,128)(2,1)S(1)} %get-tuple-element.351), channel_id=1, source_target_pairs={{4,28},{12,20},{20,12},{28,4},{5,29},{13,21},{21,13},{29,5},{6,30}... | collective-permute-start | bytes 958472 | tf_op jit(solution)/shard_map/ppermute | solution.py:253
  280.2 11.4 %collective-permute-start.64 = (bf16[208,768]{1,0:T(8,128)(2,1)S(1)}, bf16[208,768]{1,0:T(8,128)(2,1)S(1)}, u32[]{:S(2)}, u32[]{:S(2)}) collective-permute-start(bf16[208,768]{1,0:T(8,128)(2,1)S(1)} %get-tuple-element.350), channel_id=1, source_target_pairs={{0,28},{8,20},{16,12},{24,4},{1,29},{9,21},{17,13},{25,5},{2,30},{... | collective-permute-start | bytes 958472 | tf_op jit(solution)/shard_map/ppermute | solution.py:253
  302.3 12.1 %collective-permute-start.68 = (bf16[208,768]{1,0:T(8,128)(2,1)S(1)}, bf16[208,768]{1,0:T(8,128)(2,1)S(1)}, u32[]{:S(2)}, u32[]{:S(2)}) collective-permute-start(bf16[208,768]{1,0:T(8,128)(2,1)S(1)} %get-tuple-element.349), channel_id=1, source_target_pairs={{4,0},{12,8},{20,16},{28,24},{5,1},{13,9},{21,17},{29,25},{6,2},{1... | collective-permute-start | bytes 958472 | tf_op jit(solution)/shard_map/ppermute | solution.py:253
  303.7 11.7 %collective-permute-start.69 = (bf16[208,768]{1,0:T(8,128)(2,1)S(1)}, bf16[208,768]{1,0:T(8,128)(2,1)S(1)}, u32[]{:S(2)}, u32[]{:S(2)}) collective-permute-start(bf16[208,768]{1,0:T(8,128)(2,1)S(1)} %get-tuple-element.348), channel_id=1, source_target_pairs={{0,8},{8,0},{16,24},{24,16},{1,9},{9,1},{17,25},{25,17},{2,10},{10... | collective-permute-start | bytes 958472 | tf_op jit(solution)/shard_map/ppermute | solution.py:253
  304.4 15.1 %collective-permute-start.70 = (bf16[208,768]{1,0:T(8,128)(2,1)S(1)}, bf16[208,768]{1,0:T(8,128)(2,1)S(1)}, u32[]{:S(2)}, u32[]{:S(2)}) collective-permute-start(bf16[208,768]{1,0:T(8,128)(2,1)S(1)} %get-tuple-element.347), channel_id=1, source_target_pairs={{4,8},{12,0},{20,24},{28,16},{5,9},{13,1},{21,25},{29,17},{6,10},{... | collective-permute-start | bytes 958472 | tf_op jit(solution)/shard_map/ppermute | solution.py:253
  309.2 10.4 %collective-permute-start.71 = (bf16[208,768]{1,0:T(8,128)(2,1)S(1)}, bf16[208,768]{1,0:T(8,128)(2,1)S(1)}, u32[]{:S(2)}, u32[]{:S(2)}) collective-permute-start(bf16[208,768]{1,0:T(8,128)(2,1)S(1)} %get-tuple-element.346), channel_id=1, source_target_pairs={{0,16},{8,24},{16,0},{24,8},{1,17},{9,25},{17,1},{25,9},{2,18},{10... | collective-permute-start | bytes 958472 | tf_op jit(solution)/shard_map/ppermute | solution.py:253
  309.9 11.8 %collective-permute-start.72 = (bf16[208,768]{1,0:T(8,128)(2,1)S(1)}, bf16[208,768]{1,0:T(8,128)(2,1)S(1)}, u32[]{:S(2)}, u32[]{:S(2)}) collective-permute-start(bf16[208,768]{1,0:T(8,128)(2,1)S(1)} %get-tuple-element.345), channel_id=1, source_target_pairs={{4,16},{12,24},{20,0},{28,8},{5,17},{13,25},{21,1},{29,9},{6,18},{... | collective-permute-start | bytes 958472 | tf_op jit(solution)/shard_map/ppermute | solution.py:253
  315.3 10.6 %collective-permute-start.74 = (bf16[208,768]{1,0:T(8,128)(2,1)S(1)}, bf16[208,768]{1,0:T(8,128)(2,1)S(1)}, u32[]{:S(2)}, u32[]{:S(2)}) collective-permute-start(bf16[208,768]{1,0:T(8,128)(2,1)S(1)} %get-tuple-element.343), channel_id=1, source_target_pairs={{4,24},{12,16},{20,8},{28,0},{5,25},{13,17},{21,9},{29,1},{6,26},{... | collective-permute-start | bytes 958472 | tf_op jit(solution)/shard_map/ppermute | solution.py:253
  375.3 45.5 %all-to-all-start.3 = ((f32[4,64,1536]{2,1,0:T(8,128)}), f32[4,64,1536]{2,1,0:T(8,128)S(1)}, u32[]{:S(2)}, u32[]{:S(2)}) async-start(f32[4,64,1536]{2,1,0:T(8,128)} %broadcast_in_dim.123), calls=%async_computation.3 | async-start | bytes 3145728 | tf_op jit(solution)/shard_map/all_to_all | solution.py:290
  380.6 26.0 %collective-permute-start.77 = (bf16[56,768]{1,0:T(8,128)(2,1)S(1)}, bf16[56,768]{1,0:T(8,128)(2,1)S(1)}, u32[]{:S(2)}, u32[]{:S(2)}) collective-permute-start(bf16[56,768]{1,0:T(8,128)(2,1)S(1)} %copy-done.75), channel_id=1, source_target_pairs={{0,3},{1,2},{2,1},{3,0},{4,7},{5,6},{6,5},{7,4},{8,11},{9,10},{10,... | collective-permute-start | bytes 258056 | tf_op jit(solution)/shard_map/ppermute | solution.py:253
  380.7 40.0 %collective-permute-start.76 = (bf16[56,768]{1,0:T(8,128)(2,1)S(1)}, bf16[56,768]{1,0:T(8,128)(2,1)S(1)}, u32[]{:S(2)}, u32[]{:S(2)}) collective-permute-start(bf16[56,768]{1,0:T(8,128)(2,1)S(1)} %copy-done.74), channel_id=1, source_target_pairs={{0,2},{1,3},{2,0},{3,1},{4,6},{5,7},{6,4},{7,5},{8,10},{9,11},{10,... | collective-permute-start | bytes 258056 | tf_op jit(solution)/shard_map/ppermute | solution.py:253
  382.1 38.6 %collective-permute-start.75 = (bf16[56,768]{1,0:T(8,128)(2,1)S(1)}, bf16[56,768]{1,0:T(8,128)(2,1)S(1)}, u32[]{:S(2)}, u32[]{:S(2)}) collective-permute-start(bf16[56,768]{1,0:T(8,128)(2,1)S(1)} %copy-done.73), channel_id=1, source_target_pairs={{0,1},{1,0},{2,3},{3,2},{4,5},{5,4},{6,7},{7,6},{8,9},{9,8},{10,11... | collective-permute-start | bytes 258056 | tf_op jit(solution)/shard_map/ppermute | solution.py:253
  468.0 65.8 %all-to-all-start.4 = ((f32[4,56,192]{2,1,0:T(8,128)}), f32[4,56,192]{2,1,0:T(8,128)S(1)}, u32[]{:S(2)}, u32[]{:S(2)}) async-start(f32[4,56,192]{2,1,0:T(8,128)} %bitcast.324), calls=%async_computation.4 | async-start | bytes 458752 | tf_op jit(solution)/shard_map/all_to_all | solution.py:632
  474.6 27.5 %collective-permute-start.79 = (bf16[56,768]{1,0:T(8,128)(2,1)S(1)}, bf16[56,768]{1,0:T(8,128)(2,1)S(1)}, u32[]{:S(2)}, u32[]{:S(2)}) collective-permute-start(bf16[56,768]{1,0:T(8,128)(2,1)S(1)} %get-tuple-element.208), channel_id=1, source_target_pairs={{0,1},{1,0},{2,3},{3,2},{4,5},{5,4},{6,7},{7,6},{8,9},{9,8},{10,11... | collective-permute-start | bytes 258056 | tf_op jit(solution)/shard_map/ppermute | solution.py:253
  474.9 29.0 %collective-permute-start.80 = (bf16[56,768]{1,0:T(8,128)(2,1)S(1)}, bf16[56,768]{1,0:T(8,128)(2,1)S(1)}, u32[]{:S(2)}, u32[]{:S(2)}) collective-permute-start(bf16[56,768]{1,0:T(8,128)(2,1)S(1)} %get-tuple-element.209), channel_id=1, source_target_pairs={{0,2},{1,3},{2,0},{3,1},{4,6},{5,7},{6,4},{7,5},{8,10},{9,11},{10,... | collective-permute-start | bytes 258056 | tf_op jit(solution)/shard_map/ppermute | solution.py:253
  475.0 30.2 %collective-permute-start.81 = (bf16[56,768]{1,0:T(8,128)(2,1)S(1)}, bf16[56,768]{1,0:T(8,128)(2,1)S(1)}, u32[]{:S(2)}, u32[]{:S(2)}) collective-permute-start(bf16[56,768]{1,0:T(8,128)(2,1)S(1)} %get-tuple-element.210), channel_id=1, source_target_pairs={{0,3},{1,2},{2,1},{3,0},{4,7},{5,6},{6,5},{7,4},{8,11},{9,10},{10,... | collective-permute-start | bytes 258056 | tf_op jit(solution)/shard_map/ppermute | solution.py:253
  481.2 59.8 %collective-permute-start.83 = (bf16[192,768]{1,0:T(8,128)(2,1)}, bf16[192,768]{1,0:T(8,128)(2,1)}, u32[]{:S(2)}, u32[]{:S(2)}) collective-permute-start(bf16[192,768]{1,0:T(8,128)(2,1)} %get-tuple-element.372), channel_id=1, source_target_pairs={{0,4},{4,0},{8,12},{12,8},{16,20},{20,16},{24,28},{28,24},{1,5},{5... | collective-permute-start | bytes 884744 | tf_op jit(solution)/shard_map/ppermute | solution.py:253
  484.1 59.0 %collective-permute-start.84 = (bf16[192,768]{1,0:T(8,128)(2,1)}, bf16[192,768]{1,0:T(8,128)(2,1)}, u32[]{:S(2)}, u32[]{:S(2)}) collective-permute-start(bf16[192,768]{1,0:T(8,128)(2,1)} %get-tuple-element.371), channel_id=1, source_target_pairs={{0,8},{4,12},{8,0},{12,4},{16,24},{20,28},{24,16},{28,20},{1,9},{5... | collective-permute-start | bytes 884744 | tf_op jit(solution)/shard_map/ppermute | solution.py:253
  502.1 43.9 %collective-permute-start.85 = (bf16[192,768]{1,0:T(8,128)(2,1)}, bf16[192,768]{1,0:T(8,128)(2,1)}, u32[]{:S(2)}, u32[]{:S(2)}) collective-permute-start(bf16[192,768]{1,0:T(8,128)(2,1)} %get-tuple-element.370), channel_id=1, source_target_pairs={{0,12},{4,8},{8,4},{12,0},{16,28},{20,24},{24,20},{28,16},{1,13},{... | collective-permute-start | bytes 884744 | tf_op jit(solution)/shard_map/ppermute | solution.py:253
  503.9 44.9 %collective-permute-start.86 = (bf16[192,768]{1,0:T(8,128)(2,1)}, bf16[192,768]{1,0:T(8,128)(2,1)}, u32[]{:S(2)}, u32[]{:S(2)}) collective-permute-start(bf16[192,768]{1,0:T(8,128)(2,1)} %get-tuple-element.369), channel_id=1, source_target_pairs={{0,16},{4,20},{8,24},{12,28},{16,0},{20,4},{24,8},{28,12},{1,17},{... | collective-permute-start | bytes 884744 | tf_op jit(solution)/shard_map/ppermute | solution.py:253
  529.8 21.3 %collective-permute-start.87 = (bf16[192,768]{1,0:T(8,128)(2,1)S(1)}, bf16[192,768]{1,0:T(8,128)(2,1)}, u32[]{:S(2)}, u32[]{:S(2)}) collective-permute-start(bf16[192,768]{1,0:T(8,128)(2,1)S(1)} %copy-done.68), channel_id=1, source_target_pairs={{0,20},{4,16},{8,28},{12,24},{16,4},{20,0},{24,12},{28,8},{1,21},{... | collective-permute-start | bytes 884744 | tf_op jit(solution)/shard_map/ppermute | solution.py:253
  533.9 61.6 %all-to-all-start.5 = ((f32[4,56,192]{2,1,0:T(8,128)}), f32[4,56,192]{2,1,0:T(8,128)S(1)}, u32[]{:S(2)}, u32[]{:S(2)}) async-start(f32[4,56,192]{2,1,0:T(8,128)} %bitcast.323), calls=%async_computation.5 | async-start | bytes 458752 | tf_op jit(solution)/shard_map/all_to_all | solution.py:632
  540.9 12.9 %collective-permute-start.88 = (bf16[192,768]{1,0:T(8,128)(2,1)S(1)}, bf16[192,768]{1,0:T(8,128)(2,1)S(1)}, u32[]{:S(2)}, u32[]{:S(2)}) collective-permute-start(bf16[192,768]{1,0:T(8,128)(2,1)S(1)} %copy-done.67), channel_id=1, source_target_pairs={{0,24},{4,28},{8,16},{12,20},{16,8},{20,12},{24,0},{28,4},{1,25},{... | collective-permute-start | bytes 884744 | tf_op jit(solution)/shard_map/ppermute | solution.py:253
  543.1 13.5 %collective-permute-start.89 = (bf16[192,768]{1,0:T(8,128)(2,1)S(1)}, bf16[192,768]{1,0:T(8,128)(2,1)S(1)}, u32[]{:S(2)}, u32[]{:S(2)}) collective-permute-start(bf16[192,768]{1,0:T(8,128)(2,1)S(1)} %get-tuple-element.366), channel_id=1, source_target_pairs={{0,28},{4,24},{8,20},{12,16},{16,12},{20,8},{24,4},{28,0},{1,29},{... | collective-permute-start | bytes 884744 | tf_op jit(solution)/shard_map/ppermute | solution.py:253
  546.0 11.6 %collective-permute-start.95 = (bf16[192,768]{1,0:T(8,128)(2,1)}, bf16[192,768]{1,0:T(8,128)(2,1)S(1)}, u32[]{:S(2)}, u32[]{:S(2)}) collective-permute-start(bf16[192,768]{1,0:T(8,128)(2,1)} %get-tuple-element.364), channel_id=1, source_target_pairs={{0,4},{4,0},{8,12},{12,8},{16,20},{20,16},{24,28},{28,24},{1,5},{5... | collective-permute-start | bytes 884744 | tf_op jit(solution)/shard_map/ppermute | solution.py:253
  548.8 14.3 %collective-permute-start.96 = (bf16[192,768]{1,0:T(8,128)(2,1)S(1)}, bf16[192,768]{1,0:T(8,128)(2,1)S(1)}, u32[]{:S(2)}, u32[]{:S(2)}) collective-permute-start(bf16[192,768]{1,0:T(8,128)(2,1)S(1)} %copy-done.72), channel_id=1, source_target_pairs={{0,8},{4,12},{8,0},{12,4},{16,24},{20,28},{24,16},{28,20},{1,9},{5... | collective-permute-start | bytes 884744 | tf_op jit(solution)/shard_map/ppermute | solution.py:253
  551.1 18.8 %collective-permute-start.97 = (bf16[192,768]{1,0:T(8,128)(2,1)S(1)}, bf16[192,768]{1,0:T(8,128)(2,1)S(1)}, u32[]{:S(2)}, u32[]{:S(2)}) collective-permute-start(bf16[192,768]{1,0:T(8,128)(2,1)S(1)} %copy-done.71), channel_id=1, source_target_pairs={{0,12},{4,8},{8,4},{12,0},{16,28},{20,24},{24,20},{28,16},{1,13},{... | collective-permute-start | bytes 884744 | tf_op jit(solution)/shard_map/ppermute | solution.py:253
  553.8 19.3 %collective-permute-start.98 = (bf16[192,768]{1,0:T(8,128)(2,1)S(1)}, bf16[192,768]{1,0:T(8,128)(2,1)S(1)}, u32[]{:S(2)}, u32[]{:S(2)}) collective-permute-start(bf16[192,768]{1,0:T(8,128)(2,1)S(1)} %copy-done.70), channel_id=1, source_target_pairs={{0,16},{4,20},{8,24},{12,28},{16,0},{20,4},{24,8},{28,12},{1,17},{... | collective-permute-start | bytes 884744 | tf_op jit(solution)/shard_map/ppermute | solution.py:253
  556.6 16.6 %collective-permute-start.99 = (bf16[192,768]{1,0:T(8,128)(2,1)S(1)}, bf16[192,768]{1,0:T(8,128)(2,1)S(1)}, u32[]{:S(2)}, u32[]{:S(2)}) collective-permute-start(bf16[192,768]{1,0:T(8,128)(2,1)S(1)} %copy-done.69), channel_id=1, source_target_pairs={{0,20},{4,16},{8,28},{12,24},{16,4},{20,0},{24,12},{28,8},{1,21},{... | collective-permute-start | bytes 884744 | tf_op jit(solution)/shard_map/ppermute | solution.py:253
  557.7 17.5 %collective-permute-start.100 = (bf16[192,768]{1,0:T(8,128)(2,1)S(1)}, bf16[192,768]{1,0:T(8,128)(2,1)S(1)}, u32[]{:S(2)}, u32[]{:S(2)}) collective-permute-start(bf16[192,768]{1,0:T(8,128)(2,1)S(1)} %get-tuple-element.359), channel_id=1, source_target_pairs={{0,24},{4,28},{8,16},{12,20},{16,8},{20,12},{24,0},{28,4},{1,25},{... | collective-permute-start | bytes 884744 | tf_op jit(solution)/shard_map/ppermute | solution.py:253
  563.1 23.2 %collective-permute-start.101 = (bf16[192,768]{1,0:T(8,128)(2,1)S(1)}, bf16[192,768]{1,0:T(8,128)(2,1)S(1)}, u32[]{:S(2)}, u32[]{:S(2)}) collective-permute-start(bf16[192,768]{1,0:T(8,128)(2,1)S(1)} %get-tuple-element.358), channel_id=1, source_target_pairs={{0,28},{4,24},{8,20},{12,16},{16,12},{20,8},{24,4},{28,0},{1,29},{... | collective-permute-start | bytes 884744 | tf_op jit(solution)/shard_map/ppermute | solution.py:253
  570.0 29.5 %collective-permute-start.78 = (f32[197,192]{1,0:T(8,128)}, f32[197,192]{1,0:T(8,128)S(1)}, u32[]{:S(2)}, u32[]{:S(2)}) collective-permute-start(f32[197,192]{1,0:T(8,128)} %slice.360), channel_id=1, source_target_pairs={{0,0},{1,4},{2,8},{3,12},{4,1},{5,5},{6,9},{7,13},{8,2},{9,6},{10,... | collective-permute-start | bytes 453896 | tf_op jit(solution)/shard_map/ppermute | solution.py:247
  595.5 14.6 %collective-permute-start.82 = (f32[197,192]{1,0:T(8,128)S(1)}, f32[197,192]{1,0:T(8,128)S(1)}, u32[]{:S(2)}, u32[]{:S(2)}) collective-permute-start(f32[197,192]{1,0:T(8,128)S(1)} %slice.361), channel_id=1, source_target_pairs={{0,0},{1,4},{2,8},{3,12},{4,1},{5,5},{6,9},{7,13},{8,2},{9,6},{10,... | collective-permute-start | bytes 453896 | tf_op jit(solution)/shard_map/ppermute | solution.py:247
  (124 other events, 1072.7 us)

commit v3 on v2

--- a/solution.py
+++ b/solution.py
@@ -17,7 +17,6 @@
 schulz_first = 3.4445
 schulz_second = -4.775
 schulz_third = 2.0315
-high = lax.Precision.HIGH
 kinds = 4
 
 
@@ -25,10 +24,6 @@
     return lax.dot_general(
         left_side, right_side, (((0,), (0,)), ((), ())), preferred_element_type=jnp.float32
     )
-
-
-def dot_high(left_side, right_side):
-    return jnp.dot(left_side, right_side, precision=high)
 
 
 def pad_rows(values, rows):
@@ -79,7 +74,7 @@
         in_specs=specs,
         out_specs=in_vmem(len(outputs)),
         scratch_shapes=scratch,
-        compiler_params=pltpu.CompilerParams(vmem_limit_bytes=32 * 1024 * 1024),
+        compiler_params=pltpu.CompilerParams(vmem_limit_bytes=40 * 1024 * 1024),
         cost_estimate=pl.CostEstimate(flops=flops, bytes_accessed=moved, transcendentals=0),
     )(*operands)
 
@@ -299,53 +294,118 @@
     return [parts[0]] + [from_partner(parts[k], k, ("col",)) for k in range(1, len(parts))]
 
 
-def gram_of(raw):
+def gram_strips(raw):
     size = lax.axis_size("col")
-    height = raw.shape[0]
-    third = height // 3
+    third = raw.shape[0] // 3
     strips = [
         lax.dot_general(
             raw[i * third : (i + 1) * third],
             raw[i * third :],
             (((1,), (1,)), ((), ())),
-            precision=high,
+            precision=lax.Precision.HIGH,
             preferred_element_type=jnp.float32,
         )
         for i in range(3)
     ]
     packed = jnp.concatenate(strips, axis=1)
     blocks = lax.all_to_all(packed.reshape(size, third // size, -1), "col", 0, 0)
-    packed = to_all(jnp.sum(blocks, axis=0), "col").reshape(third, -1)
-    first = packed[:, :height]
-    second = packed[:, height : 2 * height - third]
-    last = packed[:, 2 * height - third :]
-    return jnp.concatenate(
-        [
-            first,
-            jnp.concatenate([first[:, third : 2 * third].T, second], axis=1),
-            jnp.concatenate([first[:, 2 * third :].T, second[:, third:].T, last], axis=1),
-        ],
-        axis=0,
-    )
-
-
-def schulz(raw, gram):
+    return to_all(jnp.sum(blocks, axis=0), "col").reshape(third, -1)
+
+
+def halves(values):
+    high = values.astype(jnp.bfloat16)
+    return (high, (values - high.astype(jnp.float32)).astype(jnp.bfloat16))
+
+
+def put_halves(refs, rows, columns, values):
+    for ref, half in zip(refs, halves(values)):
+        ref[rows, columns] = half
+
+
+def dot_halves(left, rows, right, columns):
+    left_high, left_low = left[0][rows, :], left[1][rows, :]
+    right_high, right_low = right[0][:, columns], right[1][:, columns]
+    return (
+        wide_dot(left_high, right_high, 1, 0)
+        + wide_dot(left_high, right_low, 1, 0)
+        + wide_dot(left_low, right_high, 1, 0)
+    )
+
+
+def schulz_kernel(sweeps, packed, raw, out, gram, half, current, *pairs):
+    gram_pair, square_pair, half_pair, current_pair = [pairs[i : i + 2] for i in range(0, 8, 2)]
     height = raw.shape[0]
-    eye = jnp.eye(height, dtype=jnp.float32)
-    scale = 1.0 / (jnp.sqrt(jnp.sum(gram * eye)) + 1e-07)
-    current = raw * scale
-    gram = gram * (scale * scale)
-    for sweep_index in range(5):
-        square = schulz_second * gram + schulz_third * dot_high(gram, gram)
-        if sweep_index < 4:
-            both = jnp.concatenate([gram, current], axis=1)
-            both = schulz_first * both + dot_high(square, both)
-            half = both[:, :height]
-            current = both[:, height:]
-            gram = schulz_first * half + dot_high(half, square)
-        else:
-            current = schulz_first * current + dot_high(square, current)
-    return current
+    third = height // 3
+    bands = [slice(i * third, (i + 1) * third) for i in range(3)]
+    tails = [slice(i * third, height) for i in range(3)]
+    everything = slice(0, height)
+
+    def put_symmetric(pair, i, values):
+        put_halves(pair, bands[i], tails[i], values)
+        for j in range(i + 1, 3):
+            block = values[:, (j - i) * third : (j - i + 1) * third]
+            put_halves(pair, bands[j], bands[i], block.T)
+
+    total = jnp.zeros((1, 1), jnp.float32)
+    start = 0
+    for i in range(3):
+        strip = packed[:, start : start + height - i * third]
+        start += height - i * third
+        gram[bands[i], tails[i]] = strip
+        rows = lax.broadcasted_iota(jnp.int32, (third, third), 0)
+        columns = lax.broadcasted_iota(jnp.int32, (third, third), 1)
+        diagonal = jnp.where(rows == columns, strip[:, :third], 0.0)
+        total = total + jnp.sum(jnp.sum(diagonal, axis=1, keepdims=True), axis=0, keepdims=True)
+    scale = 1.0 / (jnp.sqrt(total) + 1e-07)
+    for i in range(3):
+        values = gram[bands[i], tails[i]] * (scale * scale)
+        gram[bands[i], tails[i]] = values
+        put_symmetric(gram_pair, i, values)
+        values = raw[bands[i], :] * scale
+        current[bands[i], :] = values
+        put_halves(current_pair, bands[i], everything, values)
+
+    def sweep(index, carry):
+        for i in range(3):
+            product = dot_halves(gram_pair, bands[i], gram_pair, tails[i])
+            square = schulz_second * gram[bands[i], tails[i]] + schulz_third * product
+            put_symmetric(square_pair, i, square)
+        for i in range(3):
+            product = dot_halves(square_pair, bands[i], current_pair, everything)
+            current[bands[i], :] = schulz_first * current[bands[i], :] + product
+
+        @pl.when(index < sweeps - 1)
+        def _():
+            for i in range(3):
+                put_halves(current_pair, bands[i], everything, current[bands[i], :])
+                product = dot_halves(square_pair, bands[i], gram_pair, tails[i])
+                values = schulz_first * gram[bands[i], tails[i]] + product
+                half[bands[i], tails[i]] = values
+                put_symmetric(half_pair, i, values)
+            for i in range(3):
+                product = dot_halves(square_pair, bands[i], half_pair, tails[i])
+                values = schulz_first * half[bands[i], tails[i]] + product
+                gram[bands[i], tails[i]] = values
+                put_symmetric(gram_pair, i, values)
+
+        return carry
+
+    lax.fori_loop(0, sweeps, sweep, 0)
+    out[...] = current[...].astype(out.dtype)
+
+
+def schulz(raw, packed):
+    height, width = raw.shape
+    square_shape = (height, height)
+    whole = [pltpu.VMEM(square_shape, jnp.float32)] * 2 + [pltpu.VMEM(raw.shape, jnp.float32)]
+    pairs = [pltpu.VMEM(square_shape, jnp.bfloat16)] * 6 + [pltpu.VMEM(raw.shape, jnp.bfloat16)] * 2
+    return kernel_call(
+        functools.partial(schulz_kernel, 5),
+        [packed, raw],
+        [jax.ShapeDtypeStruct(raw.shape, jnp.bfloat16)],
+        whole + pairs,
+        2 * 3 * 14 * height * height * width,
+    )[0]
 
 
 def on_device(
@@ -389,9 +449,12 @@
     ]
     widest = max(widths)
 
-    def gathered_weights(level_index, which):
+    def own_weights(level_index, which):
         parts = [upright(weights[k], k, level_index).astype(jnp.bfloat16) for k in which]
-        whole = gather_by_pairs(jnp.concatenate(parts, axis=1), "row")
+        return jnp.concatenate(parts, axis=1)
+
+    def gathered_weights(own, which):
+        whole = gather_by_pairs(own, "row")
         whole = whole.reshape(model_width, -1)
         result = []
         start = 0
@@ -406,16 +469,110 @@
     all_norms = gather_by_pairs(norm_params, "row")
     all_norms = all_norms.transpose(1, 2, 0, 3).reshape(levels, kinds, model_width)
     image_blocks = to_all(swap_row_col(residual_in), "col")
-    weight_sets = []
+    position = lax.axis_index("col").astype(jnp.int32).reshape(1)
+    heads = widths[0] // (3 * HD)
+
+    def shaped(rows, columns, kind):
+        return jax.ShapeDtypeStruct((rows, columns), kind)
+
+    low_chunk = shaped(chunk, model_width, jnp.bfloat16)
+    full_chunk = shaped(chunk, model_width, jnp.float32)
+    low_chunks = [low_chunk] * col_size
+    sent = shaped(sent_rows, widest, jnp.bfloat16)
+    sent_model = shaped(sent_rows, model_width, jnp.bfloat16)
+    whole_scratch = pltpu.VMEM((padded, model_width), jnp.float32)
+    attention_flops = 2 * padded * (
+        model_width * (widths[0] + widths[1]) + 2 * padded * widths[1]
+    )
+    perceptron_flops = 2 * padded * model_width * (widths[2] + widths[3])
+    chunk_flops = 20 * chunk * model_width
+
+    def norm_step(parts, stream, level_index, first_row):
+        return kernel_call(
+            functools.partial(norm_kernel, level_index, first_row, len(parts)),
+            [*parts, stream, all_norms],
+            [full_chunk, low_chunk],
+            [],
+            chunk_flops,
+        )
+
+    def norm_back_step(parts, stream, upstream, level_index, first_row):
+        return kernel_call(
+            functools.partial(norm_back_kernel, level_index, first_row, len(parts)),
+            [*parts, stream, upstream, all_norms],
+            [full_chunk, low_chunk, shaped(2, model_width, jnp.float32)],
+            [],
+            chunk_flops,
+        )
+
+    *chunks, stream = kernel_call(
+        functools.partial(first_kernel, tokens),
+        [image_blocks, all_norms],
+        low_chunks + [full_chunk],
+        [whole_scratch],
+        20 * padded * model_width,
+        position,
+    )
+    groups = ((0, 1), (2, 3))
+
+    def weights_of(own_groups):
+        return sum([gathered_weights(own, which) for own, which in zip(own_groups, groups)], [])
+
+    own_groups = [[own_weights(i, which) for which in groups] for i in range(levels)]
+    weight_sets = [weights_of(own_groups[0])] + [None] * (levels - 1)
+    chunks, own_groups[1:] = lax.optimization_barrier((chunks, own_groups[1:]))
+    for level_index in range(1, levels):
+        weight_sets[level_index] = weights_of(own_groups[level_index])
+    saved = []
+    early = [None] * levels
     for level_index in range(levels):
-        attention = gathered_weights(level_index, (0, 1))
-        perceptron = gathered_weights(level_index, (2, 3))
-        weight_sets.append(attention + perceptron)
-    cotangent_blocks = pad_rows(swap_row_col(cotangent), padded)
-    cotangent_blocks = cotangent_blocks.reshape(col_size, chunk, width_row)
-    upstream = features_first(lax.all_to_all(cotangent_blocks, "col", 0, 0))
-
-    upper = (me // row_size) % 2 == 1
+        weight_qkv, weight_proj, weight_up, weight_down = weight_sets[level_index]
+        stream_one = stream
+        *parts, mixed, normed_one, attended = kernel_call(
+            functools.partial(attend_kernel, tokens, heads),
+            [*chunks, weight_qkv, weight_proj],
+            low_chunks + [shaped(padded, widths[0], jnp.bfloat16), sent_model, sent],
+            [whole_scratch, pltpu.VMEM((padded, widths[1]), jnp.float32)],
+            attention_flops,
+            position,
+        )
+        stream_two, normed = norm_step(swap_parts(parts), stream, level_index, 2)
+        chunks = to_partners(normed)
+        *parts, slope, normed_two, activated = kernel_call(
+            functools.partial(mlp_kernel, tokens),
+            [*chunks, weight_up, weight_down],
+            low_chunks + [shaped(padded, widths[2], jnp.float32), sent_model, sent],
+            [whole_scratch],
+            perceptron_flops,
+            position,
+        )
+        parts = swap_parts(parts)
+        early[level_index] = (normed_one, attended, normed_two, activated)
+        if level_index < levels - 1:
+            stream, normed = norm_step(parts, stream_two, level_index + 1, 0)
+            if level_index == 0:
+                normed, late_me, cotangent = lax.optimization_barrier((normed, me, cotangent))
+            chunks = to_partners(normed)
+        else:
+            stream = stream_two
+            for part in parts:
+                stream = stream + part.astype(jnp.float32)
+        saved.append((stream_one, stream_two, mixed, slope))
+
+    def send_level(parts, level_index):
+        stack = jnp.stack(parts)
+        received = [pick(stack, me // levels)]
+        for step in range(1, jobs):
+            received.append(
+                from_partner(
+                    pick(stack, (me ^ step) // levels),
+                    step,
+                    wanted=lambda i: i % levels == level_index,
+                )
+            )
+        return received
+
+    upper = (late_me // row_size) % 2 == 1
     half = jobs // 2
     near_moments = []
     for j in range(half):
@@ -431,103 +588,12 @@
     own_moment = placed_blocks(moment_parts, [my_row ^ i for i in range(row_size)])
     own_moment = own_moment.reshape(model_width, widest)
 
-    position = lax.axis_index("col").astype(jnp.int32).reshape(1)
-    heads = widths[0] // (3 * HD)
-
-    def shaped(rows, columns, kind):
-        return jax.ShapeDtypeStruct((rows, columns), kind)
-
-    low_chunk = shaped(chunk, model_width, jnp.bfloat16)
-    full_chunk = shaped(chunk, model_width, jnp.float32)
-    low_chunks = [low_chunk] * col_size
-    sent = shaped(sent_rows, widest, jnp.bfloat16)
-    sent_model = shaped(sent_rows, model_width, jnp.bfloat16)
-    whole_scratch = pltpu.VMEM((padded, model_width), jnp.float32)
-    attention_flops = 2 * padded * (
-        model_width * (widths[0] + widths[1]) + 2 * padded * widths[1]
-    )
-    perceptron_flops = 2 * padded * model_width * (widths[2] + widths[3])
-    chunk_flops = 20 * chunk * model_width
-
-    def norm_step(parts, stream, level_index, first_row):
-        return kernel_call(
-            functools.partial(norm_kernel, level_index, first_row, len(parts)),
-            [*parts, stream, all_norms],
-            [full_chunk, low_chunk],
-            [],
-            chunk_flops,
-        )
-
-    def norm_back_step(parts, stream, upstream, level_index, first_row):
-        return kernel_call(
-            functools.partial(norm_back_kernel, level_index, first_row, len(parts)),
-            [*parts, stream, upstream, all_norms],
-            [full_chunk, low_chunk, shaped(2, model_width, jnp.float32)],
-            [],
-            chunk_flops,
-        )
-
-    *chunks, stream = kernel_call(
-        functools.partial(first_kernel, tokens),
-        [image_blocks, all_norms],
-        low_chunks + [full_chunk],
-        [whole_scratch],
-        20 * padded * model_width,
-        position,
-    )
-    saved = []
-    early = []
-    for level_index in range(levels):
-        weight_qkv, weight_proj, weight_up, weight_down = weight_sets[level_index]
-        stream_one = stream
-        *parts, mixed, normed_one, attended = kernel_call(
-            functools.partial(attend_kernel, tokens, heads),
-            [*chunks, weight_qkv, weight_proj],
-            low_chunks + [shaped(padded, widths[0], jnp.bfloat16), sent_model, sent],
-            [whole_scratch, pltpu.VMEM((padded, widths[1]), jnp.float32)],
-            attention_flops,
-            position,
-        )
-        stream_two, normed = norm_step(swap_parts(parts), stream, level_index, 2)
-        chunks = to_partners(normed)
-        *parts, slope, normed_two, activated = kernel_call(
-            functools.partial(mlp_kernel, tokens),
-            [*chunks, weight_up, weight_down],
-            low_chunks + [shaped(padded, widths[2], jnp.float32), sent_model, sent],
-            [whole_scratch],
-            perceptron_flops,
-            position,
-        )
-        parts = swap_parts(parts)
-        if level_index < levels - 1:
-            stream, normed = norm_step(parts, stream_two, level_index + 1, 0)
-            chunks = to_partners(normed)
-        else:
-            stream = stream_two
-            for part in parts:
-                stream = stream + part.astype(jnp.float32)
-        saved.append((stream_one, stream_two, mixed, slope))
-        early.append((normed_one, attended, normed_two, activated))
-
-    early_stack = jnp.stack([early[j % levels][j // levels] for j in range(jobs)])
-    early_all = [pick(early_stack, me)]
-    for step in range(1, jobs):
-        early_all.append(from_partner(pick(early_stack, me ^ step), step))
-
-    def send_late(parts, level_index):
-        stack = jnp.stack(parts)
-        received = [pick(stack, me // levels)]
-        for step in range(1, jobs):
-            received.append(
-                from_partner(
-                    pick(stack, (me ^ step) // levels),
-                    step,
-                    wanted=lambda i: i % levels == level_index,
-                )
-            )
-        return received
-
-    upstream, own_moment = lax.optimization_barrier((upstream, own_moment))
+    cotangent_blocks = pad_rows(swap_row_col(cotangent), padded)
+    cotangent_blocks = cotangent_blocks.reshape(col_size, chunk, width_row)
+    upstream = features_first(lax.all_to_all(cotangent_blocks, "col", 0, 0))
+
+    early = [send_level(early[i], i) for i in range(levels)]
+    upstream, own_moment, early[0] = lax.optimization_barrier((upstream, own_moment, early[0]))
     late = [None] * levels
     norm_sums = [None] * levels
     back_low = upstream.astype(jnp.bfloat16)
@@ -545,9 +611,7 @@
         upstream, back_low, sums_two = norm_back_step(
             swap_parts(parts), stream_two, upstream, level_index, 2
         )
-        if level_index == levels - 1:
-            back_low, early_all = lax.optimization_barrier((back_low, early_all))
-        else:
+        if level_index < levels - 1:
             back_low, late[level_index + 1] = lax.optimization_barrier(
                 (back_low, late[level_index + 1])
             )
@@ -559,7 +623,7 @@
             3 * attention_flops,
             position,
         )
-        late[level_index] = send_late(
+        late[level_index] = send_level(
             (mixed_grad, back_one, hidden_grad, back_two), level_index
         )
         if level_index:
@@ -567,13 +631,17 @@
                 swap_parts(parts), stream_one, upstream, level_index, 0
             )
             norm_sums[level_index] = jnp.concatenate([sums_one, sums_two])
-
-    early_all = jnp.concatenate(early_all, axis=0)
-    late_all = jnp.concatenate(late[0], axis=0)
-    for level_index in range(1, levels):
-        late_all = jnp.where(
-            me % levels == level_index, jnp.concatenate(late[level_index], axis=0), late_all
-        )
+            back_low, early[level_index] = lax.optimization_barrier((back_low, early[level_index]))
+
+    def own_level(sets):
+        result = jnp.concatenate(sets[0], axis=0)
+        for level_index in range(1, levels):
+            other = jnp.concatenate(sets[level_index], axis=0)
+            result = jnp.where(me % levels == level_index, other, result)
+        return result
+
+    early_all = own_level(early)
+    late_all = own_level(late)
     turned = (me // levels) % 2 == 1
     model_side = jnp.where(turned, late_all, early_all)
     hidden_side = jnp.where(turned, early_all, late_all)
@@ -594,7 +662,7 @@
 
     own_raw = moment_decay * own_moment + own_grad
     gram, own_grad, stream, parts = lax.optimization_barrier(
-        (gram_of(own_raw), own_grad, stream, parts)
+        (gram_strips(own_raw), own_grad, stream, parts)
     )
     upstream, _, sums_one = norm_back_step(swap_parts(parts), stream_one, upstream, 0, 0)
     norm_sums[0] = jnp.concatenate([sums_one, sums_two])

time: 618 us -> 618 us (level)
  the two profiles are of different devices: /device:TPU:25 before, /device:TPU:17 now
where the time goes in v3:
time: 618 us; the launch traced here: 607 us
  starting transfers between devices  194 us (31%)
  waiting for transfers between devices  192 us (31%)
  local copies, waits for them, and re-layouts  83.2 us (13%)
  Pallas kernels  62.5 us (10%)
  blocking collectives  36.8 us (6%)
  other arithmetic  27.7 us (4%)
    ppermute x105, waiting for transfers between devices, from_partner(): return lax.ppermute(values, axes, pairs)  179 us
    ppermute x105, starting transfers between devices, from_partner(): return lax.ppermute(values, axes, pairs)  151 us
    pallas_call x17, Pallas kernels, kernel_call(): pl.pallas_call(body, out_shape=list(outputs), in_specs=specs, out_specs=i...  62.5 us
    all_to_all x1, blocking collectives, gram_strips(): lax.all_to_all(packed.reshape(size, third // size, -1), 'col', 0, 0)  36.8 us
    unnamed x233, local copies, waits for them, and re-layouts  23.5 us
    dynamic_update_slice x33, local copies, waits for them, and re-layouts, placed_blocks(): result = lax.dynamic_update_index_in_dim(result, block, place, 0)  21.6 us
    ppermute x4, starting transfers between devices, swap_row_col(): return lax.ppermute(values, ('row', 'col'), pairs)  14.8 us
    all_to_all x2, starting transfers between devices, to_all(): lax.all_to_all(jnp.broadcast_to(block[None], (size,) + block.shape), axis...  12.6 us
  transfers between devices with their start and end apart: 114, of which 48 were waited for; matrix products, arithmetic and copies ran while one was open for 15% of the time, Pallas kernels for 10%

profile of v3, /device:TPU:17, one launch (start us, length us, event | category | flops | bytes accessed | tf_op | source)
XLA Modules:
  0.0 606.5 jit_solution(10694293857763758466)
XLA Ops:
  0.7 3.6 collective-permute-start
  22.4 6.1 %all-to-all-start = ((bf16[4,197,192]{1,2,0:T(8,128)(2,1)}), bf16[4,197,192]{1,2,0:T(8,128)(2,1)}, u32[]{:S(2)}, u32[]{:S(2)}) async-start(bf16[4,197,192]{1,2,0:T(8,128)(2,1)} %broadcast_in_dim.112), calls=%async_computation | async-start | bytes 786432 | tf_op jit(solution)/shard_map/all_to_all | solution.py:285
  32.9 4.1 all-to-all-done
  43.6 2.5 collective-permute-done.33
  46.2 3.9 collective-permute-start.34
  50.1 8.7 %collective-permute-done.41 = bf16[1,192,1536]{2,1,0:T(8,128)(2,1)S(1)} collective-permute-done((bf16[1,192,1536]{2,1,0:T(8,128)(2,1)S(1)}, bf16[1,192,1536]{2,1,0:T(8,128)(2,1)S(1)}, u32[]{:S(2)}, u32[]{:S(2)}) %collective-permute-start.41) | collective-permute-done | bytes 589856 | tf_op jit(solution)/shard_map/ppermute | solution.py:248
  66.7 2.3 collective-permute-start.5
  74.5 4.0 collective-permute-done.7.refs_3_
  78.7 2.4 collective-permute-start.9
  84.8 3.9 collective-permute-done.10.refs_3_
  89.8 2.6 collective-permute-start.14
  95.4 4.1 collective-permute-done.15.refs_3_
  100.9 3.3 collective-permute-start.31
  111.7 3.0 shard_map.256
  117.5 3.0 collective-permute-start.36
  123.5 5.8 collective-permute-start.16
  136.3 3.3 dynamic-slice_bitcast_fusion.26
  139.6 4.7 collective-permute-start.20
  145.0 5.3 all-to-all-start.1
  164.3 2.4 collective-permute-start.22
  169.3 3.1 collective-permute-start.24
  173.1 16.8 %collective-permute-done.19 = f32[192,768]{1,0:T(8,128)} collective-permute-done((f32[192,768]{1,0:T(8,128)}, f32[192,768]{1,0:T(8,128)}, u32[]{:S(2)}, u32[]{:S(2)}) %collective-permute-start.19) | collective-permute-done | bytes 589856 | tf_op jit(solution)/shard_map/ppermute | solution.py:248
  189.9 2.5 collective-permute-start.26
  197.8 3.1 collective-permute-start.53
  205.7 2.7 collective-permute-done.28.refs_2_
  208.4 3.0 collective-permute-done.29.refs_3_
  218.2 5.0 collective-permute-done.45.refs_3_
  228.5 5.3 collective-permute-done.48.refs_3_
  233.8 2.4 shard_map.261
  243.8 3.2 collective-permute-start.57
  250.9 3.0 collective-permute-start.66
  256.0 2.4 collective-permute-done.58
  262.9 2.6 collective-permute-done.60.refs_2_
  265.6 3.5 collective-permute-done.61.refs_3_
  275.6 3.0 collective-permute-start.68
  282.0 3.1 collective-permute-start.70
  287.0 4.3 collective-permute-done.69
  291.2 2.8 collective-permute-done.70
  303.7 3.9 collective-permute-done.74.refs_3_
  307.6 2.4 shard_map.265
  313.4 4.2 collective-permute-start.77
  318.3 2.7 collective-permute-start.79
  321.8 3.9 collective-permute-start.81
  326.2 6.1 %collective-permute-done.81 = bf16[208,768]{1,0:T(8,128)(2,1)S(1)} collective-permute-done((bf16[208,768]{1,0:T(8,128)(2,1)S(1)}, bf16[208,768]{1,0:T(8,128)(2,1)S(1)}, u32[]{:S(2)}, u32[]{:S(2)}) %collective-permute-start.81) | collective-permute-done | bytes 319520 | tf_op jit(solution)/shard_map/ppermute | solution.py:248
  332.3 3.1 fusion
  338.5 36.8 %all_to_all.30 = f32[4,64,1536]{2,1,0:T(8,128)} all-to-all(f32[4,64,1536]{2,1,0:T(8,128)S(1)} %bitcast.335), channel_id=1, replica_groups=mesh['dp'=2,'row'=4,'col'=4] {'col'}, dimensions={0} | all-to-all | bytes 3145728 | tf_op jit(solution)/shard_map/all_to_all | solution.py:311
  377.6 2.4 broadcast_in_dim.123
  380.0 6.5 %all-to-all-start.3 = ((f32[4,64,1536]{2,1,0:T(8,128)}), f32[4,64,1536]{2,1,0:T(8,128)}, u32[]{:S(2)}, u32[]{:S(2)}) async-start(f32[4,64,1536]{2,1,0:T(8,128)} %broadcast_in_dim.123), calls=%async_computation.3 | async-start | bytes 3145728 | tf_op jit(solution)/shard_map/all_to_all | solution.py:285
  386.9 3.0 collective-permute-start.83
  389.8 35.6 %collective-permute-done.84 = bf16[56,768]{1,0:T(8,128)(2,1)S(1)} collective-permute-done((bf16[56,768]{1,0:T(8,128)(2,1)S(1)}, bf16[56,768]{1,0:T(8,128)(2,1)S(1)}, u32[]{:S(2)}, u32[]{:S(2)}) %collective-permute-start.84) | collective-permute-done | bytes 86048 | tf_op jit(solution)/shard_map/ppermute | solution.py:248
  427.7 2.6 collective-permute-start.87
  431.0 2.4 collective-permute-done.87.refs_2_
  435.6 4.9 collective-permute-start.97
  445.6 4.8 all-to-all-start.4
  459.7 44.3 %shard_map.267 = bf16[768,768]{1,0:T(8,128)(2,1)S(1)} custom-call(f32[256,1536]{1,0:T(8,128)} %bitcast.97.packed, f32[768,768]{1,0:T(8,128)S(1)} %multiply_add_fusion.raw), custom_call_target="tpu_custom_call" | custom-call | flops 38050725888 | bytes 5111808 | tf_op jit(solution)/shard_map/pallas_call | solution.py:71
  510.2 5.4 all-to-all-start.5
  524.6 9.9 %collective-permute-done.103 = bf16[192,768]{1,0:T(8,128)(2,1)S(1)} collective-permute-done((bf16[192,768]{1,0:T(8,128)(2,1)}, bf16[192,768]{1,0:T(8,128)(2,1)S(1)}, u32[]{:S(2)}, u32[]{:S(2)}) %collective-permute-start.103) | collective-permute-done | bytes 294944 | tf_op jit(solution)/shard_map/ppermute | solution.py:248
  538.9 11.4 %collective-permute-done.104 = bf16[192,768]{1,0:T(8,128)(2,1)S(1)} collective-permute-done((bf16[192,768]{1,0:T(8,128)(2,1)}, bf16[192,768]{1,0:T(8,128)(2,1)S(1)}, u32[]{:S(2)}, u32[]{:S(2)}) %collective-permute-start.104) | collective-permute-done | bytes 294944 | tf_op jit(solution)/shard_map/ppermute | solution.py:248
  554.5 3.8 collective-permute-done.105
  559.8 7.1 %collective-permute-start.108 = (bf16[192,768]{1,0:T(8,128)(2,1)S(1)}, bf16[192,768]{1,0:T(8,128)(2,1)S(1)}, u32[]{:S(2)}, u32[]{:S(2)}) collective-permute-start(bf16[192,768]{1,0:T(8,128)(2,1)S(1)} %copy-done.94), channel_id=1, source_target_pairs={{0,28},{4,24},{8,20},{12,16},{16,12},{20,8},{24,4},{28,0},{1,29},{... | collective-permute-start | bytes 884744 | tf_op jit(solution)/shard_map/ppermute | solution.py:248
  567.6 3.6 collective-permute-start.85
  574.3 2.6 multiply_add_fusion.2
  577.0 5.2 collective-permute-done.108
  596.1 9.2 %collective-permute-done.89 = f32[197,192]{1,0:T(8,128)S(1)} collective-permute-done((f32[197,192]{1,0:T(8,128)S(1)}, f32[197,192]{1,0:T(8,128)S(1)}, u32[]{:S(2)}, u32[]{:S(2)}) %collective-permute-start.89) | collective-permute-done | bytes 151328 | tf_op jit(solution)/shard_map/ppermute | solution.py:242
  (558 shorter events, 224.1 us)
Async XLA Ops:
  0.7 20.0 %collective-permute-start = (bf16[197,192]{0,1:T(8,128)(2,1)}, bf16[197,192]{0,1:T(8,128)(2,1)}, u32[]{:S(2)}, u32[]{:S(2)}) collective-permute-start(bf16[197,192]{0,1:T(8,128)(2,1)} %param.12), channel_id=1, source_target_pairs={{0,0},{1,4},{2,8},{3,12},{4,1},{5,5},{6,9},{7,13},{8,2},{9,6},{10,... | collective-permute-start | bytes 226952 | tf_op jit(solution)/shard_map/ppermute | solution.py:242
  4.3 15.8 %collective-permute-start.1 = (f32[1,2,4,192]{3,2,1,0:T(4,128)}, f32[1,2,4,192]{3,2,1,0:T(4,128)S(1)}, u32[]{:S(2)}, u32[]{:S(2)}) collective-permute-start(f32[1,2,4,192]{3,2,1,0:T(4,128)} %bitcast.348), channel_id=1, source_target_pairs={{0,8},{4,12},{8,0},{12,4},{1,9},{5,13},{9,1},{13,5},{2,10},{6,14},... | collective-permute-start | bytes 18440 | tf_op jit(solution)/shard_map/ppermute | solution.py:248
  9.9 18.8 %collective-permute-start.3 = (bf16[1,192,768]{2,1,0:T(8,128)(2,1)}, bf16[1,192,768]{2,1,0:T(8,128)(2,1)}, u32[]{:S(2)}, u32[]{:S(2)}) collective-permute-start(bf16[1,192,768]{2,1,0:T(8,128)(2,1)} %get-tuple-element.314), channel_id=1, source_target_pairs={{0,8},{4,12},{8,0},{12,4},{1,9},{5,13},{9,1},{13,5},{2,10},{6,14},... | collective-permute-start | bytes 884744 | tf_op jit(solution)/shard_map/ppermute | solution.py:248
  12.6 27.8 %collective-permute-start.11 = (bf16[1,192,1536]{2,1,0:T(8,128)(2,1)}, bf16[1,192,1536]{2,1,0:T(8,128)(2,1)}, u32[]{:S(2)}, u32[]{:S(2)}) collective-permute-start(bf16[1,192,1536]{2,1,0:T(8,128)(2,1)} %maximum_bitcast_fusion), channel_id=1, source_target_pairs={{0,8},{4,12},{8,0},{12,4},{1,9},{5,13},{9,1},{13,5},{2,10},{6,14},... | collective-permute-start | bytes 1769480 | tf_op jit(solution)/shard_map/ppermute | solution.py:248
  22.4 14.6 %all-to-all-start = ((bf16[4,197,192]{1,2,0:T(8,128)(2,1)}), bf16[4,197,192]{1,2,0:T(8,128)(2,1)}, u32[]{:S(2)}, u32[]{:S(2)}) async-start(bf16[4,197,192]{1,2,0:T(8,128)(2,1)} %broadcast_in_dim.112), calls=%async_computation | async-start | bytes 786432 | tf_op jit(solution)/shard_map/all_to_all | solution.py:285
  30.7 31.6 %collective-permute-start.4 = (bf16[2,192,768]{2,1,0:T(8,128)(2,1)}, bf16[2,192,768]{2,1,0:T(8,128)(2,1)}, u32[]{:S(2)}, u32[]{:S(2)}) collective-permute-start(bf16[2,192,768]{2,1,0:T(8,128)(2,1)} %pad_maximum_fusion.9), channel_id=1, source_target_pairs={{0,4},{4,0},{8,12},{12,8},{1,5},{5,1},{9,13},{13,9},{2,6},{6,2},{1... | collective-permute-start | bytes 1769480 | tf_op jit(solution)/shard_map/ppermute | solution.py:248
  38.9 19.9 %collective-permute-start.41 = (bf16[1,192,1536]{2,1,0:T(8,128)(2,1)S(1)}, bf16[1,192,1536]{2,1,0:T(8,128)(2,1)S(1)}, u32[]{:S(2)}, u32[]{:S(2)}) collective-permute-start(bf16[1,192,1536]{2,1,0:T(8,128)(2,1)S(1)} %bitcast.340), channel_id=1, source_target_pairs={{0,8},{4,12},{8,0},{12,4},{1,9},{5,13},{9,1},{13,5},{2,10},{6,14},... | collective-permute-start | bytes 1769480 | tf_op jit(solution)/shard_map/ppermute | solution.py:248
  41.8 39.6 %collective-permute-start.12 = (bf16[2,192,1536]{2,1,0:T(8,128)(2,1)S(1)}, bf16[2,192,1536]{2,1,0:T(8,128)(2,1)S(1)}, u32[]{:S(2)}, u32[]{:S(2)}) collective-permute-start(bf16[2,192,1536]{2,1,0:T(8,128)(2,1)S(1)} %pad_maximum_fusion.6), channel_id=1, source_target_pairs={{0,4},{4,0},{8,12},{12,8},{1,5},{5,1},{9,13},{13,9},{2,6},{6,2},{1... | collective-permute-start | bytes 3538952 | tf_op jit(solution)/shard_map/ppermute | solution.py:248
  46.2 16.1 %collective-permute-start.34 = (bf16[2,192,768]{2,1,0:T(8,128)(2,1)S(1)}, bf16[2,192,768]{2,1,0:T(8,128)(2,1)S(1)}, u32[]{:S(2)}, u32[]{:S(2)}) collective-permute-start(bf16[2,192,768]{2,1,0:T(8,128)(2,1)S(1)} %pad_maximum_fusion.10), channel_id=1, source_target_pairs={{0,4},{4,0},{8,12},{12,8},{1,5},{5,1},{9,13},{13,9},{2,6},{6,2},{1... | collective-permute-start | bytes 1769480 | tf_op jit(solution)/shard_map/ppermute | solution.py:248
  58.9 22.5 %collective-permute-start.42 = (bf16[2,192,1536]{2,1,0:T(8,128)(2,1)S(1)}, bf16[2,192,1536]{2,1,0:T(8,128)(2,1)S(1)}, u32[]{:S(2)}, u32[]{:S(2)}) collective-permute-start(bf16[2,192,1536]{2,1,0:T(8,128)(2,1)S(1)} %pad_maximum_fusion.7), channel_id=1, source_target_pairs={{0,4},{4,0},{8,12},{12,8},{1,5},{5,1},{9,13},{13,9},{2,6},{6,2},{1... | collective-permute-start | bytes 3538952 | tf_op jit(solution)/shard_map/ppermute | solution.py:248
  108.1 56.2 %collective-permute-start.17 = (f32[192,768]{1,0:T(8,128)}, f32[192,768]{1,0:T(8,128)}, u32[]{:S(2)}, u32[]{:S(2)}) collective-permute-start(f32[192,768]{1,0:T(8,128)} %get-tuple-element.331), channel_id=1, source_target_pairs={{0,4},{4,0},{8,12},{12,8},{16,20},{20,16},{24,28},{28,24},{1,5},{5... | collective-permute-start | bytes 1769480 | tf_op jit(solution)/shard_map/ppermute | solution.py:248
  117.5 11.8 %collective-permute-start.35 = (bf16[56,768]{1,0:T(8,128)(2,1)}, bf16[56,768]{1,0:T(8,128)(2,1)}, u32[]{:S(2)}, u32[]{:S(2)}) collective-permute-start(bf16[56,768]{1,0:T(8,128)(2,1)} %get-tuple-element.166), channel_id=1, source_target_pairs={{0,1},{1,0},{2,3},{3,2},{4,5},{5,4},{6,7},{7,6},{8,9},{9,8},{10,11... | collective-permute-start | bytes 258056 | tf_op jit(solution)/shard_map/ppermute | solution.py:248
  117.5 11.8 %collective-permute-start.36 = (bf16[56,768]{1,0:T(8,128)(2,1)}, bf16[56,768]{1,0:T(8,128)(2,1)}, u32[]{:S(2)}, u32[]{:S(2)}) collective-permute-start(bf16[56,768]{1,0:T(8,128)(2,1)} %get-tuple-element.167), channel_id=1, source_target_pairs={{0,2},{1,3},{2,0},{3,1},{4,6},{5,7},{6,4},{7,5},{8,10},{9,11},{10,... | collective-permute-start | bytes 258056 | tf_op jit(solution)/shard_map/ppermute | solution.py:248
  123.5 16.1 %collective-permute-start.16 = (f32[197,192]{1,0:T(8,128)}, f32[197,192]{1,0:T(8,128)S(1)}, u32[]{:S(2)}, u32[]{:S(2)}) collective-permute-start(f32[197,192]{1,0:T(8,128)} %copy.75), channel_id=1, source_target_pairs={{0,0},{1,4},{2,8},{3,12},{4,1},{5,5},{6,9},{7,13},{8,2},{9,6},{10,... | collective-permute-start | bytes 453896 | tf_op jit(solution)/shard_map/ppermute | solution.py:242
  133.7 16.7 %collective-permute-start.38 = (bf16[56,768]{1,0:T(8,128)(2,1)}, bf16[56,768]{1,0:T(8,128)(2,1)}, u32[]{:S(2)}, u32[]{:S(2)}) collective-permute-start(bf16[56,768]{1,0:T(8,128)(2,1)} %get-tuple-element.170.refs_0_), channel_id=1, source_target_pairs={{0,1},{1,0},{2,3},{3,2},{4,5},{5,4},{6,7},{7,6},{8,9},{9,8},{10,11... | collective-permute-start | bytes 258056 | tf_op jit(solution)/shard_map/ppermute | solution.py:248
  133.7 18.0 %collective-permute-start.39 = (bf16[56,768]{1,0:T(8,128)(2,1)}, bf16[56,768]{1,0:T(8,128)(2,1)}, u32[]{:S(2)}, u32[]{:S(2)}) collective-permute-start(bf16[56,768]{1,0:T(8,128)(2,1)} %get-tuple-element.170.refs_0_), channel_id=1, source_target_pairs={{0,2},{1,3},{2,0},{3,1},{4,6},{5,7},{6,4},{7,5},{8,10},{9,11},{10,... | collective-permute-start | bytes 258056 | tf_op jit(solution)/shard_map/ppermute | solution.py:248
  135.2 17.6 %collective-permute-start.40 = (bf16[56,768]{1,0:T(8,128)(2,1)}, bf16[56,768]{1,0:T(8,128)(2,1)}, u32[]{:S(2)}, u32[]{:S(2)}) collective-permute-start(bf16[56,768]{1,0:T(8,128)(2,1)} %get-tuple-element.170.refs_0_), channel_id=1, source_target_pairs={{0,3},{1,2},{2,1},{3,0},{4,7},{5,6},{6,5},{7,4},{8,11},{9,10},{10,... | collective-permute-start | bytes 258056 | tf_op jit(solution)/shard_map/ppermute | solution.py:248
  139.6 28.9 %collective-permute-start.20 = (bf16[208,768]{1,0:T(8,128)(2,1)}, bf16[208,768]{1,0:T(8,128)(2,1)}, u32[]{:S(2)}, u32[]{:S(2)}) collective-permute-start(bf16[208,768]{1,0:T(8,128)(2,1)} %get-tuple-element.364), channel_id=1, source_target_pairs={{4,0},{12,8},{20,16},{28,24},{5,1},{13,9},{21,17},{29,25},{6,2},{1... | collective-permute-start | bytes 958472 | tf_op jit(solution)/shard_map/ppermute | solution.py:248
  145.0 15.7 %all-to-all-start.1 = ((f32[4,56,192]{2,1,0:T(8,128)}), f32[4,56,192]{2,1,0:T(8,128)}, u32[]{:S(2)}, u32[]{:S(2)}) async-start(f32[4,56,192]{2,1,0:T(8,128)} %bitcast.344), calls=%async_computation.1 | async-start | bytes 458752 | tf_op jit(solution)/shard_map/all_to_all | solution.py:593
  150.3 18.9 %collective-permute-start.21 = (bf16[208,768]{1,0:T(8,128)(2,1)}, bf16[208,768]{1,0:T(8,128)(2,1)}, u32[]{:S(2)}, u32[]{:S(2)}) collective-permute-start(bf16[208,768]{1,0:T(8,128)(2,1)} %get-tuple-element.363), channel_id=1, source_target_pairs={{0,8},{8,0},{16,24},{24,16},{1,9},{9,1},{17,25},{25,17},{2,10},{10... | collective-permute-start | bytes 958472 | tf_op jit(solution)/shard_map/ppermute | solution.py:248
  151.7 20.7 %collective-permute-start.18 = (f32[192,768]{1,0:T(8,128)}, f32[192,768]{1,0:T(8,128)}, u32[]{:S(2)}, u32[]{:S(2)}) collective-permute-start(f32[192,768]{1,0:T(8,128)} %get-tuple-element.330), channel_id=1, source_target_pairs={{0,8},{4,12},{8,0},{12,4},{16,24},{20,28},{24,16},{28,20},{1,9},{5... | collective-permute-start | bytes 1769480 | tf_op jit(solution)/shard_map/ppermute | solution.py:248
  152.9 37.1 %collective-permute-start.19 = (f32[192,768]{1,0:T(8,128)}, f32[192,768]{1,0:T(8,128)}, u32[]{:S(2)}, u32[]{:S(2)}) collective-permute-start(f32[192,768]{1,0:T(8,128)} %get-tuple-element.329), channel_id=1, source_target_pairs={{0,12},{4,8},{8,4},{12,0},{16,28},{20,24},{24,20},{28,16},{1,13},{... | collective-permute-start | bytes 1769480 | tf_op jit(solution)/shard_map/ppermute | solution.py:248
  164.3 32.2 %collective-permute-start.22 = (bf16[208,768]{1,0:T(8,128)(2,1)}, bf16[208,768]{1,0:T(8,128)(2,1)S(1)}, u32[]{:S(2)}, u32[]{:S(2)}) collective-permute-start(bf16[208,768]{1,0:T(8,128)(2,1)} %get-tuple-element.362), channel_id=1, source_target_pairs={{4,8},{12,0},{20,24},{28,16},{5,9},{13,1},{21,25},{29,17},{6,10},{... | collective-permute-start | bytes 958472 | tf_op jit(solution)/shard_map/ppermute | solution.py:248
  168.6 29.2 %collective-permute-start.23 = (bf16[208,768]{1,0:T(8,128)(2,1)}, bf16[208,768]{1,0:T(8,128)(2,1)S(1)}, u32[]{:S(2)}, u32[]{:S(2)}) collective-permute-start(bf16[208,768]{1,0:T(8,128)(2,1)} %get-tuple-element.361), channel_id=1, source_target_pairs={{0,16},{8,24},{16,0},{24,8},{1,17},{9,25},{17,1},{25,9},{2,18},{10... | collective-permute-start | bytes 958472 | tf_op jit(solution)/shard_map/ppermute | solution.py:248
  169.3 31.6 %collective-permute-start.24 = (bf16[208,768]{1,0:T(8,128)(2,1)}, bf16[208,768]{1,0:T(8,128)(2,1)S(1)}, u32[]{:S(2)}, u32[]{:S(2)}) collective-permute-start(bf16[208,768]{1,0:T(8,128)(2,1)} %get-tuple-element.360), channel_id=1, source_target_pairs={{4,16},{12,24},{20,0},{28,8},{5,17},{13,25},{21,1},{29,9},{6,18},{... | collective-permute-start | bytes 958472 | tf_op jit(solution)/shard_map/ppermute | solution.py:248
  172.4 28.4 %collective-permute-start.25 = (bf16[208,768]{1,0:T(8,128)(2,1)}, bf16[208,768]{1,0:T(8,128)(2,1)S(1)}, u32[]{:S(2)}, u32[]{:S(2)}) collective-permute-start(bf16[208,768]{1,0:T(8,128)(2,1)} %get-tuple-element.359), channel_id=1, source_target_pairs={{0,24},{8,16},{16,8},{24,0},{1,25},{9,17},{17,9},{25,1},{2,26},{10... | collective-permute-start | bytes 958472 | tf_op jit(solution)/shard_map/ppermute | solution.py:248
  189.9 10.9 %collective-permute-start.26 = (bf16[208,768]{1,0:T(8,128)(2,1)}, bf16[208,768]{1,0:T(8,128)(2,1)S(1)}, u32[]{:S(2)}, u32[]{:S(2)}) collective-permute-start(bf16[208,768]{1,0:T(8,128)(2,1)} %get-tuple-element.358), channel_id=1, source_target_pairs={{4,24},{12,16},{20,8},{28,0},{5,25},{13,17},{21,9},{29,1},{6,26},{... | collective-permute-start | bytes 958472 | tf_op jit(solution)/shard_map/ppermute | solution.py:248
  196.4 42.5 %collective-permute-start.52 = (bf16[208,768]{1,0:T(8,128)(2,1)S(1)}, bf16[208,768]{1,0:T(8,128)(2,1)S(1)}, u32[]{:S(2)}, u32[]{:S(2)}) collective-permute-start(bf16[208,768]{1,0:T(8,128)(2,1)S(1)} %copy-done.92), channel_id=1, source_target_pairs={{0,4},{8,12},{16,20},{24,28},{1,5},{9,13},{17,21},{25,29},{2,6},{1... | collective-permute-start | bytes 958472 | tf_op jit(solution)/shard_map/ppermute | solution.py:248
  197.8 42.5 %collective-permute-start.53 = (bf16[208,768]{1,0:T(8,128)(2,1)S(1)}, bf16[208,768]{1,0:T(8,128)(2,1)S(1)}, u32[]{:S(2)}, u32[]{:S(2)}) collective-permute-start(bf16[208,768]{1,0:T(8,128)(2,1)S(1)} %copy-done.91), channel_id=1, source_target_pairs={{4,12},{12,4},{20,28},{28,20},{5,13},{13,5},{21,29},{29,21},{6,14}... | collective-permute-start | bytes 958472 | tf_op jit(solution)/shard_map/ppermute | solution.py:248
  239.0 10.6 %collective-permute-start.54 = (bf16[208,768]{1,0:T(8,128)(2,1)S(1)}, bf16[208,768]{1,0:T(8,128)(2,1)S(1)}, u32[]{:S(2)}, u32[]{:S(2)}) collective-permute-start(bf16[208,768]{1,0:T(8,128)(2,1)S(1)} %copy-done.90), channel_id=1, source_target_pairs={{0,12},{8,4},{16,28},{24,20},{1,13},{9,5},{17,29},{25,21},{2,14},{... | collective-permute-start | bytes 958472 | tf_op jit(solution)/shard_map/ppermute | solution.py:248
  242.5 11.8 %collective-permute-start.56 = (bf16[208,768]{1,0:T(8,128)(2,1)S(1)}, bf16[208,768]{1,0:T(8,128)(2,1)S(1)}, u32[]{:S(2)}, u32[]{:S(2)}) collective-permute-start(bf16[208,768]{1,0:T(8,128)(2,1)S(1)} %copy-done.88), channel_id=1, source_target_pairs={{0,20},{8,28},{16,4},{24,12},{1,21},{9,29},{17,5},{25,13},{2,22},{... | collective-permute-start | bytes 958472 | tf_op jit(solution)/shard_map/ppermute | solution.py:248
  243.8 12.2 %collective-permute-start.57 = (bf16[208,768]{1,0:T(8,128)(2,1)S(1)}, bf16[208,768]{1,0:T(8,128)(2,1)S(1)}, u32[]{:S(2)}, u32[]{:S(2)}) collective-permute-start(bf16[208,768]{1,0:T(8,128)(2,1)S(1)} %copy-done.87), channel_id=1, source_target_pairs={{4,28},{12,20},{20,12},{28,4},{5,29},{13,21},{21,13},{29,5},{6,30}... | collective-permute-start | bytes 958472 | tf_op jit(solution)/shard_map/ppermute | solution.py:248
  247.0 11.4 %collective-permute-start.58 = (bf16[208,768]{1,0:T(8,128)(2,1)S(1)}, bf16[208,768]{1,0:T(8,128)(2,1)S(1)}, u32[]{:S(2)}, u32[]{:S(2)}) collective-permute-start(bf16[208,768]{1,0:T(8,128)(2,1)S(1)} %copy-done.86), channel_id=1, source_target_pairs={{0,28},{8,20},{16,12},{24,4},{1,29},{9,21},{17,13},{25,5},{2,30},{... | collective-permute-start | bytes 958472 | tf_op jit(solution)/shard_map/ppermute | solution.py:248
  249.6 32.3 %collective-permute-start.65 = (bf16[208,768]{1,0:T(8,128)(2,1)S(1)}, bf16[208,768]{1,0:T(8,128)(2,1)S(1)}, u32[]{:S(2)}, u32[]{:S(2)}) collective-permute-start(bf16[208,768]{1,0:T(8,128)(2,1)S(1)} %get-tuple-element.348), channel_id=1, source_target_pairs={{0,4},{8,12},{16,20},{24,28},{1,5},{9,13},{17,21},{25,29},{2,6},{1... | collective-permute-start | bytes 958472 | tf_op jit(solution)/shard_map/ppermute | solution.py:248
  250.9 34.2 %collective-permute-start.66 = (bf16[208,768]{1,0:T(8,128)(2,1)S(1)}, bf16[208,768]{1,0:T(8,128)(2,1)S(1)}, u32[]{:S(2)}, u32[]{:S(2)}) collective-permute-start(bf16[208,768]{1,0:T(8,128)(2,1)S(1)} %get-tuple-element.347), channel_id=1, source_target_pairs={{4,12},{12,4},{20,28},{28,20},{5,13},{13,5},{21,29},{29,21},{6,14}... | collective-permute-start | bytes 958472 | tf_op jit(solution)/shard_map/ppermute | solution.py:248
  273.8 13.1 %collective-permute-start.67 = (bf16[208,768]{1,0:T(8,128)(2,1)S(1)}, bf16[208,768]{1,0:T(8,128)(2,1)S(1)}, u32[]{:S(2)}, u32[]{:S(2)}) collective-permute-start(bf16[208,768]{1,0:T(8,128)(2,1)S(1)} %get-tuple-element.346), channel_id=1, source_target_pairs={{0,12},{8,4},{16,28},{24,20},{1,13},{9,5},{17,29},{25,21},{2,14},{... | collective-permute-start | bytes 958472 | tf_op jit(solution)/shard_map/ppermute | solution.py:248
  275.6 11.4 %collective-permute-start.68 = (bf16[208,768]{1,0:T(8,128)(2,1)S(1)}, bf16[208,768]{1,0:T(8,128)(2,1)S(1)}, u32[]{:S(2)}, u32[]{:S(2)}) collective-permute-start(bf16[208,768]{1,0:T(8,128)(2,1)S(1)} %get-tuple-element.345), channel_id=1, source_target_pairs={{4,20},{12,28},{20,4},{28,12},{5,21},{13,29},{21,5},{29,13},{6,22}... | collective-permute-start | bytes 958472 | tf_op jit(solution)/shard_map/ppermute | solution.py:248
  282.0 12.1 %collective-permute-start.70 = (bf16[208,768]{1,0:T(8,128)(2,1)S(1)}, bf16[208,768]{1,0:T(8,128)(2,1)S(1)}, u32[]{:S(2)}, u32[]{:S(2)}) collective-permute-start(bf16[208,768]{1,0:T(8,128)(2,1)S(1)} %get-tuple-element.343), channel_id=1, source_target_pairs={{4,28},{12,20},{20,12},{28,4},{5,29},{13,21},{21,13},{29,5},{6,30}... | collective-permute-start | bytes 958472 | tf_op jit(solution)/shard_map/ppermute | solution.py:248
  285.1 11.1 %collective-permute-start.71 = (bf16[208,768]{1,0:T(8,128)(2,1)S(1)}, bf16[208,768]{1,0:T(8,128)(2,1)S(1)}, u32[]{:S(2)}, u32[]{:S(2)}) collective-permute-start(bf16[208,768]{1,0:T(8,128)(2,1)S(1)} %get-tuple-element.342), channel_id=1, source_target_pairs={{0,28},{8,20},{16,12},{24,4},{1,29},{9,21},{17,13},{25,5},{2,30},{... | collective-permute-start | bytes 958472 | tf_op jit(solution)/shard_map/ppermute | solution.py:248
  310.4 10.7 %collective-permute-start.75 = (bf16[208,768]{1,0:T(8,128)(2,1)S(1)}, bf16[208,768]{1,0:T(8,128)(2,1)S(1)}, u32[]{:S(2)}, u32[]{:S(2)}) collective-permute-start(bf16[208,768]{1,0:T(8,128)(2,1)S(1)} %get-tuple-element.341), channel_id=1, source_target_pairs={{4,0},{12,8},{20,16},{28,24},{5,1},{13,9},{21,17},{29,25},{6,2},{1... | collective-permute-start | bytes 958472 | tf_op jit(solution)/shard_map/ppermute | solution.py:248
  313.4 12.3 %collective-permute-start.77 = (bf16[208,768]{1,0:T(8,128)(2,1)S(1)}, bf16[208,768]{1,0:T(8,128)(2,1)S(1)}, u32[]{:S(2)}, u32[]{:S(2)}) collective-permute-start(bf16[208,768]{1,0:T(8,128)(2,1)S(1)} %get-tuple-element.339), channel_id=1, source_target_pairs={{4,8},{12,0},{20,24},{28,16},{5,9},{13,1},{21,25},{29,17},{6,10},{... | collective-permute-start | bytes 958472 | tf_op jit(solution)/shard_map/ppermute | solution.py:248
  380.0 47.3 %all-to-all-start.3 = ((f32[4,64,1536]{2,1,0:T(8,128)}), f32[4,64,1536]{2,1,0:T(8,128)}, u32[]{:S(2)}, u32[]{:S(2)}) async-start(f32[4,64,1536]{2,1,0:T(8,128)} %broadcast_in_dim.123), calls=%async_computation.3 | async-start | bytes 3145728 | tf_op jit(solution)/shard_map/all_to_all | solution.py:285
  386.6 38.9 %collective-permute-start.84 = (bf16[56,768]{1,0:T(8,128)(2,1)S(1)}, bf16[56,768]{1,0:T(8,128)(2,1)S(1)}, u32[]{:S(2)}, u32[]{:S(2)}) collective-permute-start(bf16[56,768]{1,0:T(8,128)(2,1)S(1)} %copy-done.57), channel_id=1, source_target_pairs={{0,3},{1,2},{2,1},{3,0},{4,7},{5,6},{6,5},{7,4},{8,11},{9,10},{10,... | collective-permute-start | bytes 258056 | tf_op jit(solution)/shard_map/ppermute | solution.py:248
  386.9 40.4 %collective-permute-start.83 = (bf16[56,768]{1,0:T(8,128)(2,1)S(1)}, bf16[56,768]{1,0:T(8,128)(2,1)S(1)}, u32[]{:S(2)}, u32[]{:S(2)}) collective-permute-start(bf16[56,768]{1,0:T(8,128)(2,1)S(1)} %copy-done.55), channel_id=1, source_target_pairs={{0,2},{1,3},{2,0},{3,1},{4,6},{5,7},{6,4},{7,5},{8,10},{9,11},{10,... | collective-permute-start | bytes 258056 | tf_op jit(solution)/shard_map/ppermute | solution.py:248
  389.8 37.5 %collective-permute-start.82 = (bf16[56,768]{1,0:T(8,128)(2,1)S(1)}, bf16[56,768]{1,0:T(8,128)(2,1)S(1)}, u32[]{:S(2)}, u32[]{:S(2)}) collective-permute-start(bf16[56,768]{1,0:T(8,128)(2,1)S(1)} %copy-done.53), channel_id=1, source_target_pairs={{0,1},{1,0},{2,3},{3,2},{4,5},{5,4},{6,7},{7,6},{8,9},{9,8},{10,11... | collective-permute-start | bytes 258056 | tf_op jit(solution)/shard_map/ppermute | solution.py:248
  441.4 10.9 %collective-permute-start.98 = (f32[2,4,768]{2,1,0:T(4,128)S(1)}, f32[2,4,768]{2,1,0:T(4,128)S(1)}, u32[]{:S(2)}, u32[]{:S(2)}) collective-permute-start(f32[2,4,768]{2,1,0:T(4,128)S(1)} %fusion.19), channel_id=1, source_target_pairs={{0,8},{4,12},{8,0},{12,4},{1,9},{5,13},{9,1},{13,5},{2,10},{6,14},... | collective-permute-start | bytes 73736 | tf_op jit(solution)/shard_map/ppermute | solution.py:248
  445.6 63.8 %all-to-all-start.4 = ((f32[4,56,192]{2,1,0:T(8,128)}), f32[4,56,192]{2,1,0:T(8,128)S(1)}, u32[]{:S(2)}, u32[]{:S(2)}) async-start(f32[4,56,192]{2,1,0:T(8,128)} %bitcast.313), calls=%async_computation.4 | async-start | bytes 458752 | tf_op jit(solution)/shard_map/all_to_all | solution.py:700
  455.0 62.3 %collective-permute-start.90 = (bf16[192,768]{1,0:T(8,128)(2,1)}, bf16[192,768]{1,0:T(8,128)(2,1)}, u32[]{:S(2)}, u32[]{:S(2)}) collective-permute-start(bf16[192,768]{1,0:T(8,128)(2,1)} %get-tuple-element.380), channel_id=1, source_target_pairs={{0,4},{4,0},{8,12},{12,8},{16,20},{20,16},{24,28},{28,24},{1,5},{5... | collective-permute-start | bytes 884744 | tf_op jit(solution)/shard_map/ppermute | solution.py:248
  456.2 64.4 %collective-permute-start.91 = (bf16[192,768]{1,0:T(8,128)(2,1)}, bf16[192,768]{1,0:T(8,128)(2,1)}, u32[]{:S(2)}, u32[]{:S(2)}) collective-permute-start(bf16[192,768]{1,0:T(8,128)(2,1)} %get-tuple-element.379), channel_id=1, source_target_pairs={{0,8},{4,12},{8,0},{12,4},{16,24},{20,28},{24,16},{28,20},{1,9},{5... | collective-permute-start | bytes 884744 | tf_op jit(solution)/shard_map/ppermute | solution.py:248
  456.2 79.3 %collective-permute-start.92 = (bf16[192,768]{1,0:T(8,128)(2,1)}, bf16[192,768]{1,0:T(8,128)(2,1)}, u32[]{:S(2)}, u32[]{:S(2)}) collective-permute-start(bf16[192,768]{1,0:T(8,128)(2,1)} %get-tuple-element.378), channel_id=1, source_target_pairs={{0,12},{4,8},{8,4},{12,0},{16,28},{20,24},{24,20},{28,16},{1,13},{... | collective-permute-start | bytes 884744 | tf_op jit(solution)/shard_map/ppermute | solution.py:248
  457.9 93.6 %collective-permute-start.93 = (bf16[192,768]{1,0:T(8,128)(2,1)}, bf16[192,768]{1,0:T(8,128)(2,1)}, u32[]{:S(2)}, u32[]{:S(2)}) collective-permute-start(bf16[192,768]{1,0:T(8,128)(2,1)} %get-tuple-element.377), channel_id=1, source_target_pairs={{0,16},{4,20},{8,24},{12,28},{16,0},{20,4},{24,8},{28,12},{1,17},{... | collective-permute-start | bytes 884744 | tf_op jit(solution)/shard_map/ppermute | solution.py:248
  459.4 44.7 %collective-permute-start.100 = (f32[2,4,768]{2,1,0:T(4,128)S(1)}, f32[2,4,768]{2,1,0:T(4,128)S(1)}, u32[]{:S(2)}, u32[]{:S(2)}) collective-permute-start(f32[2,4,768]{2,1,0:T(4,128)S(1)} %add.325), channel_id=1, source_target_pairs={{0,2},{1,3},{2,0},{3,1},{4,6},{5,7},{6,4},{7,5},{8,10},{9,11},{10,... | collective-permute-start | bytes 73736 | tf_op jit(solution)/shard_map/ppermute | solution.py:248
  506.8 12.8 %collective-permute-start.102 = (bf16[192,768]{1,0:T(8,128)(2,1)}, bf16[192,768]{1,0:T(8,128)(2,1)}, u32[]{:S(2)}, u32[]{:S(2)}) collective-permute-start(bf16[192,768]{1,0:T(8,128)(2,1)} %get-tuple-element.372), channel_id=1, source_target_pairs={{0,4},{4,0},{8,12},{12,8},{16,20},{20,16},{24,28},{28,24},{1,5},{5... | collective-permute-start | bytes 884744 | tf_op jit(solution)/shard_map/ppermute | solution.py:248
  510.2 81.2 %all-to-all-start.5 = ((f32[4,56,192]{2,1,0:T(8,128)}), f32[4,56,192]{2,1,0:T(8,128)S(1)}, u32[]{:S(2)}, u32[]{:S(2)}) async-start(f32[4,56,192]{2,1,0:T(8,128)} %bitcast.312), calls=%async_computation.5 | async-start | bytes 458752 | tf_op jit(solution)/shard_map/all_to_all | solution.py:700
  517.3 42.5 %collective-permute-start.94 = (bf16[192,768]{1,0:T(8,128)(2,1)}, bf16[192,768]{1,0:T(8,128)(2,1)S(1)}, u32[]{:S(2)}, u32[]{:S(2)}) collective-permute-start(bf16[192,768]{1,0:T(8,128)(2,1)} %get-tuple-element.376), channel_id=1, source_target_pairs={{0,20},{4,16},{8,28},{12,24},{16,4},{20,0},{24,12},{28,8},{1,21},{... | collective-permute-start | bytes 884744 | tf_op jit(solution)/shard_map/ppermute | solution.py:248
  519.6 14.9 %collective-permute-start.103 = (bf16[192,768]{1,0:T(8,128)(2,1)}, bf16[192,768]{1,0:T(8,128)(2,1)S(1)}, u32[]{:S(2)}, u32[]{:S(2)}) collective-permute-start(bf16[192,768]{1,0:T(8,128)(2,1)} %get-tuple-element.371), channel_id=1, source_target_pairs={{0,8},{4,12},{8,0},{12,4},{16,24},{20,28},{24,16},{28,20},{1,9},{5... | collective-permute-start | bytes 884744 | tf_op jit(solution)/shard_map/ppermute | solution.py:248
  520.6 50.6 %collective-permute-start.95 = (bf16[192,768]{1,0:T(8,128)(2,1)}, bf16[192,768]{1,0:T(8,128)(2,1)S(1)}, u32[]{:S(2)}, u32[]{:S(2)}) collective-permute-start(bf16[192,768]{1,0:T(8,128)(2,1)} %get-tuple-element.375), channel_id=1, source_target_pairs={{0,24},{4,28},{8,16},{12,20},{16,8},{20,12},{24,0},{28,4},{1,25},{... | collective-permute-start | bytes 884744 | tf_op jit(solution)/shard_map/ppermute | solution.py:248
  534.5 15.9 %collective-permute-start.104 = (bf16[192,768]{1,0:T(8,128)(2,1)}, bf16[192,768]{1,0:T(8,128)(2,1)S(1)}, u32[]{:S(2)}, u32[]{:S(2)}) collective-permute-start(bf16[192,768]{1,0:T(8,128)(2,1)} %get-tuple-element.370), channel_id=1, source_target_pairs={{0,12},{4,8},{8,4},{12,0},{16,28},{20,24},{24,20},{28,16},{1,13},{... | collective-permute-start | bytes 884744 | tf_op jit(solution)/shard_map/ppermute | solution.py:248
  535.5 36.5 %collective-permute-start.96 = (bf16[192,768]{1,0:T(8,128)(2,1)S(1)}, bf16[192,768]{1,0:T(8,128)(2,1)S(1)}, u32[]{:S(2)}, u32[]{:S(2)}) collective-permute-start(bf16[192,768]{1,0:T(8,128)(2,1)S(1)} %copy-done.93), channel_id=1, source_target_pairs={{0,28},{4,24},{8,20},{12,16},{16,12},{20,8},{24,4},{28,0},{1,29},{... | collective-permute-start | bytes 884744 | tf_op jit(solution)/shard_map/ppermute | solution.py:248
  551.5 16.2 %collective-permute-start.106 = (bf16[192,768]{1,0:T(8,128)(2,1)}, bf16[192,768]{1,0:T(8,128)(2,1)S(1)}, u32[]{:S(2)}, u32[]{:S(2)}) collective-permute-start(bf16[192,768]{1,0:T(8,128)(2,1)} %get-tuple-element.368), channel_id=1, source_target_pairs={{0,20},{4,16},{8,28},{12,24},{16,4},{20,0},{24,12},{28,8},{1,21},{... | collective-permute-start | bytes 884744 | tf_op jit(solution)/shard_map/ppermute | solution.py:248
  558.3 16.0 %collective-permute-start.107 = (bf16[192,768]{1,0:T(8,128)(2,1)S(1)}, bf16[192,768]{1,0:T(8,128)(2,1)S(1)}, u32[]{:S(2)}, u32[]{:S(2)}) collective-permute-start(bf16[192,768]{1,0:T(8,128)(2,1)S(1)} %copy-done.95), channel_id=1, source_target_pairs={{0,24},{4,28},{8,16},{12,20},{16,8},{20,12},{24,0},{28,4},{1,25},{... | collective-permute-start | bytes 884744 | tf_op jit(solution)/shard_map/ppermute | solution.py:248
  559.8 22.3 %collective-permute-start.108 = (bf16[192,768]{1,0:T(8,128)(2,1)S(1)}, bf16[192,768]{1,0:T(8,128)(2,1)S(1)}, u32[]{:S(2)}, u32[]{:S(2)}) collective-permute-start(bf16[192,768]{1,0:T(8,128)(2,1)S(1)} %copy-done.94), channel_id=1, source_target_pairs={{0,28},{4,24},{8,20},{12,16},{16,12},{20,8},{24,4},{28,0},{1,29},{... | collective-permute-start | bytes 884744 | tf_op jit(solution)/shard_map/ppermute | solution.py:248
  567.6 26.8 %collective-permute-start.85 = (f32[197,192]{1,0:T(8,128)}, f32[197,192]{1,0:T(8,128)}, u32[]{:S(2)}, u32[]{:S(2)}) collective-permute-start(f32[197,192]{1,0:T(8,128)} %slice.295), channel_id=1, source_target_pairs={{0,0},{1,4},{2,8},{3,12},{4,1},{5,5},{6,9},{7,13},{8,2},{9,6},{10,... | collective-permute-start | bytes 453896 | tf_op jit(solution)/shard_map/ppermute | solution.py:242
  591.4 13.9 %collective-permute-start.89 = (f32[197,192]{1,0:T(8,128)S(1)}, f32[197,192]{1,0:T(8,128)S(1)}, u32[]{:S(2)}, u32[]{:S(2)}) collective-permute-start(f32[197,192]{1,0:T(8,128)S(1)} %slice.296), channel_id=1, source_target_pairs={{0,0},{1,4},{2,8},{3,12},{4,1},{5,5},{6,9},{7,13},{8,2},{9,6},{10,... | collective-permute-start | bytes 453896 | tf_op jit(solution)/shard_map/ppermute | solution.py:242
  (149 other events, 1592.8 us)

commit v4 on v3

--- a/solution.py
+++ b/solution.py
@@ -559,18 +559,21 @@
                 stream = stream + part.astype(jnp.float32)
         saved.append((stream_one, stream_two, mixed, slope))
 
-    def send_level(parts, level_index):
-        stack = jnp.stack(parts)
-        received = [pick(stack, me // levels)]
-        for step in range(1, jobs):
-            received.append(
-                from_partner(
-                    pick(stack, (me ^ step) // levels),
-                    step,
-                    wanted=lambda i: i % levels == level_index,
-                )
-            )
-        return received
+    def placed(chunk_values):
+        blocks = chunk_values.reshape(chunk, col_size, width_row).transpose(1, 0, 2)
+        col = lax.axis_index("col")
+        received = [pick(blocks, col)]
+        for k in range(1, col_size):
+            received.append(from_partner(pick(blocks, col ^ k), k, ("col",)))
+        whole = placed_blocks(received, [col ^ k for k in range(col_size)])
+        return swap_row_col(whole.reshape(padded, width_row)[:tokens])
+
+    groups_of_jobs = dp_size * row_size // jobs
+
+    def spread(parts_of_levels):
+        stack = jnp.stack([parts_of_levels[j % levels][j // levels] for j in range(jobs)])
+        stack = jnp.concatenate([stack] * groups_of_jobs) if groups_of_jobs > 1 else stack
+        return lax.all_to_all(stack, ("dp", "row"), 0, 0).reshape(-1, widest)
 
     upper = (late_me // row_size) % 2 == 1
     half = jobs // 2
@@ -582,18 +585,17 @@
         ]
         near_moments.append(jnp.where(upper, high_job, low_job))
     stacked_moment = jnp.stack(near_moments)
-    moment_parts = [pick(stacked_moment, me % half)]
-    for step in range(1, row_size):
-        moment_parts.append(from_partner(pick(stacked_moment, (me ^ step) % half), step))
-    own_moment = placed_blocks(moment_parts, [my_row ^ i for i in range(row_size)])
-    own_moment = own_moment.reshape(model_width, widest)
+    own_moment = lax.all_to_all(stacked_moment, "row", 0, 0).reshape(model_width, widest)
 
     cotangent_blocks = pad_rows(swap_row_col(cotangent), padded)
     cotangent_blocks = cotangent_blocks.reshape(col_size, chunk, width_row)
     upstream = features_first(lax.all_to_all(cotangent_blocks, "col", 0, 0))
 
-    early = [send_level(early[i], i) for i in range(levels)]
-    upstream, own_moment, early[0] = lax.optimization_barrier((upstream, own_moment, early[0]))
+    block_output = placed(stream)
+    upstream, own_moment, block_output = lax.optimization_barrier(
+        (upstream, own_moment, block_output)
+    )
+    early_all = spread(early)
     late = [None] * levels
     norm_sums = [None] * levels
     back_low = upstream.astype(jnp.bfloat16)
@@ -611,10 +613,6 @@
         upstream, back_low, sums_two = norm_back_step(
             swap_parts(parts), stream_two, upstream, level_index, 2
         )
-        if level_index < levels - 1:
-            back_low, late[level_index + 1] = lax.optimization_barrier(
-                (back_low, late[level_index + 1])
-            )
         *parts, mixed_grad, back_one = kernel_call(
             functools.partial(attend_back_kernel, tokens, heads),
             [*to_partners(back_low), mixed, weight_qkv, weight_proj],
@@ -623,56 +621,37 @@
             3 * attention_flops,
             position,
         )
-        late[level_index] = send_level(
-            (mixed_grad, back_one, hidden_grad, back_two), level_index
-        )
-        if level_index:
-            upstream, back_low, sums_one = norm_back_step(
-                swap_parts(parts), stream_one, upstream, level_index, 0
-            )
-            norm_sums[level_index] = jnp.concatenate([sums_one, sums_two])
-            back_low, early[level_index] = lax.optimization_barrier((back_low, early[level_index]))
-
-    def own_level(sets):
-        result = jnp.concatenate(sets[0], axis=0)
-        for level_index in range(1, levels):
-            other = jnp.concatenate(sets[level_index], axis=0)
-            result = jnp.where(me % levels == level_index, other, result)
-        return result
-
-    early_all = own_level(early)
-    late_all = own_level(late)
-    turned = (me // levels) % 2 == 1
-    model_side = jnp.where(turned, late_all, early_all)
-    hidden_side = jnp.where(turned, early_all, late_all)
-    own_grad = outer_grad(model_side, hidden_side)
-    step = jobs // row_size
-    while step < dp_size:
-        pairs = [(i, i ^ step) for i in range(dp_size)]
-        own_grad = own_grad + lax.ppermute(own_grad, "dp", pairs)
-        step *= 2
-
-    def returned(whole):
-        blocks = whole.astype(jnp.bfloat16).reshape(row_size, width_row, widest)
-        received = [pick(blocks, my_row)]
-        for step in range(1, jobs):
-            received.append(from_partner(pick(blocks, (me ^ step) % row_size), step))
-        received = placed_blocks(received, [me ^ j for j in range(jobs)])
-        return [received[j].astype(jnp.float32) for j in range(jobs)]
-
-    own_raw = moment_decay * own_moment + own_grad
-    gram, own_grad, stream, parts = lax.optimization_barrier(
-        (gram_strips(own_raw), own_grad, stream, parts)
-    )
-    upstream, _, sums_one = norm_back_step(swap_parts(parts), stream_one, upstream, 0, 0)
-    norm_sums[0] = jnp.concatenate([sums_one, sums_two])
-    grads = returned(own_grad)
+        late[level_index] = (mixed_grad, back_one, hidden_grad, back_two)
+        if level_index == 0:
+            late_all = spread(late)
+        upstream, back_low, sums_one = norm_back_step(
+            swap_parts(parts), stream_one, upstream, level_index, 0
+        )
+        norm_sums[level_index] = jnp.concatenate([sums_one, sums_two])
+
     norm_whole = jnp.stack(norm_sums)
     for axis in ("row", "col", "dp"):
         norm_whole = sum_by_pairs(norm_whole, axis)
     norm_grad = lax.dynamic_slice_in_dim(norm_whole, my_row * width_row, width_row, 2)
     norm_moment_new = moment_decay * norm_moment + norm_grad
-
+    late_all, norm_grad, norm_moment_new = lax.optimization_barrier(
+        (late_all, norm_grad, norm_moment_new)
+    )
+
+    turned = (me // levels) % 2 == 1
+    model_side = jnp.where(turned, late_all, early_all)
+    hidden_side = jnp.where(turned, early_all, late_all)
+    own_grad = outer_grad(model_side, hidden_side)
+
+    def returned(whole):
+        blocks = whole.astype(jnp.bfloat16).reshape(row_size, width_row, widest)
+        blocks = jnp.concatenate([blocks] * dp_size)
+        received = lax.all_to_all(blocks, ("dp", "row"), 0, 0)
+        return [received[j].astype(jnp.float32) for j in range(jobs)]
+
+    own_raw = moment_decay * own_moment + own_grad
+    gram, own_grad = lax.optimization_barrier((gram_strips(own_raw), own_grad))
+    grads = returned(own_grad)
     orths = returned(schulz(own_raw, gram))
 
     grad_outs = []
@@ -695,15 +674,10 @@
         moment_outs.append(moment_decay * moments[kind_index] + grad_out)
         new_outs.append(weights[kind_index] - step_rates[kind_index] * jnp.stack(orth_levels))
 
-    def placed(chunk_values):
-        blocks = chunk_values.reshape(chunk, col_size, width_row).transpose(1, 0, 2)
-        blocks = lax.all_to_all(blocks, "col", 0, 0)
-        return swap_row_col(blocks.reshape(padded, width_row)[:tokens])
-
     tokens_all = tokens * col_size * dp_size
     norm_new = norm_params - norm_rate / math.sqrt(tokens_all) * norm_moment_new
     return (
-        placed(stream),
+        block_output,
         placed(upstream),
         *grad_outs,
         norm_grad,

time: 618 us -> 603 us (0.976)
  the two profiles are of different devices: /device:TPU:17 before, /device:TPU:0 now
where the time goes in v4:
time: 603 us; the launch traced here: 593 us
  waiting for transfers between devices  200 us (33%)
  starting transfers between devices  142 us (24%)
  blocking collectives  75 us (12%)
  local copies, waits for them, and re-layouts  63.8 us (11%)
  Pallas kernels  56.1 us (9%)
  other arithmetic  47.5 us (8%)
    ppermute x66, waiting for transfers between devices, from_partner(): return lax.ppermute(values, axes, pairs)  123 us
    ppermute x66, starting transfers between devices, from_partner(): return lax.ppermute(values, axes, pairs)  98 us
    pallas_call x15, Pallas kernels, kernel_call(): pl.pallas_call(body, out_shape=list(outputs), in_specs=specs, out_specs=i...  56.1 us
    all_to_all x2, waiting for transfers between devices, returned(): received = lax.all_to_all(blocks, ('dp', 'row'), 0, 0)  43.6 us
    all_to_all x1, blocking collectives, to_all(): lax.all_to_all(jnp.broadcast_to(block[None], (size,) + block.shape), axis...  37.9 us
    all_to_all x1, blocking collectives, gram_strips(): lax.all_to_all(packed.reshape(size, third // size, -1), 'col', 0, 0)  37.1 us
    all_to_all x2, waiting for transfers between devices, spread(): return lax.all_to_all(stack, ('dp', 'row'), 0, 0).reshape(-1, widest)  29.1 us
    unnamed x173, local copies, waits for them, and re-layouts  26.7 us
  transfers between devices with their start and end apart: 77, of which 39 were waited for; matrix products, arithmetic and copies ran while one was open for 12% of the time, Pallas kernels for 1%

profile of v4, /device:TPU:0, one launch (start us, length us, event | category | flops | bytes accessed | tf_op | source)
XLA Modules:
  0.0 592.6 jit_solution(9685062958682514319)
XLA Ops:
  0.7 3.0 collective-permute-start.1
  3.7 2.1 collective-permute-start
  9.7 3.8 collective-permute-start.11
  26.4 4.1 all-to-all-start
  30.8 3.2 collective-permute-done.3
  37.7 5.0 all-to-all-done
  50.3 14.8 %collective-permute-done.20 = bf16[1,192,768]{2,1,0:T(8,128)(2,1)S(1)} collective-permute-done((bf16[1,192,768]{2,1,0:T(8,128)(2,1)}, bf16[1,192,768]{2,1,0:T(8,128)(2,1)S(1)}, u32[]{:S(2)}, u32[]{:S(2)}) %collective-permute-start.20) | collective-permute-done | bytes 294944 | tf_op jit(solution)/shard_map/ppermute | solution.py:248
  71.7 2.0 collective-permute-start.6
  73.7 2.4 collective-permute-start.7
  78.8 2.9 collective-permute-done.6.refs_2_
  84.1 2.2 collective-permute-start.9
  86.7 2.2 collective-permute-done.10.refs_3_
  89.0 3.0 collective-permute-done.9.refs_2_
  93.1 2.1 collective-permute-start.14
  95.2 2.3 collective-permute-start.15
  97.8 4.4 collective-permute-done.14.refs_2_
  111.5 2.7 fusion.10
  116.1 10.1 %all-to-all-start.1 = ((f32[4,56,192]{2,1,0:T(8,128)}), f32[4,56,192]{2,1,0:T(8,128)}, u32[]{:S(2)}, u32[]{:S(2)}) async-start(f32[4,56,192]{2,1,0:T(8,128)} %bitcast.248), calls=%async_computation.1 | async-start | bytes 458752 | tf_op jit(solution)/shard_map/all_to_all | solution.py:592
  126.2 3.3 pad_maximum_fusion
  129.5 3.3 shard_map.267
  132.7 2.0 collective-permute-start.22
  134.8 2.4 collective-permute-start.23
  138.0 4.7 all-to-all-start.2
  148.5 2.2 collective-permute-start.25
  155.3 5.2 collective-permute-done.26
  168.1 5.7 collective-permute-done.31
  183.8 3.0 collective-permute-done.34
  188.7 3.4 collective-permute-start.36
  196.6 2.4 collective-permute-start.37
  199.0 5.0 collective-permute-start.38
  204.3 2.7 collective-permute-done.38.refs_2_
  206.9 3.8 collective-permute-done.39.refs_3_
  217.6 6.8 %collective-permute-done.41.refs_2_ = bf16[56,768]{1,0:T(8,128)(2,1)S(1)} collective-permute-done((bf16[56,768]{1,0:T(8,128)(2,1)S(1)}, bf16[56,768]{1,0:T(8,128)(2,1)S(1)}, u32[]{:S(2)}, u32[]{:S(2)}) %collective-permute-start.41) | collective-permute-done | bytes 86048 | tf_op jit(solution)/shard_map/ppermute | solution.py:248
  230.1 5.4 collective-permute-done.44.refs_2_
  235.5 2.4 shard_map.259
  243.2 4.9 collective-permute-done.47.refs_2_
  253.6 5.1 collective-permute-done.50.refs_2_
  264.8 5.1 collective-permute-done.53.refs_2_
  275.3 5.1 collective-permute-done.56.refs_2_
  280.4 2.4 shard_map.263
  288.9 4.5 all-to-all-start.3
  294.9 29.1 %all-to-all-done.3 = bf16[8,208,768]{2,1,0:T(8,128)(2,1)} async-done(((bf16[8,208,768]{2,1,0:T(8,128)(2,1)}), bf16[8,208,768]{2,1,0:T(8,128)(2,1)}, u32[]{:S(2)}, u32[]{:S(2)}) %all-to-all-start.3) | async-done | bytes 2555936 | tf_op jit(solution)/shard_map/all_to_all | solution.py:576
  324.0 4.6 all-to-all-start.4
  333.6 6.4 %collective-permute-done.59.refs_2_ = bf16[56,768]{1,0:T(8,128)(2,1)S(1)} collective-permute-done((bf16[56,768]{1,0:T(8,128)(2,1)S(1)}, bf16[56,768]{1,0:T(8,128)(2,1)S(1)}, u32[]{:S(2)}, u32[]{:S(2)}) %collective-permute-start.59) | collective-permute-done | bytes 86048 | tf_op jit(solution)/shard_map/ppermute | solution.py:248
  342.2 2.0 collective-permute-start.66
  344.2 15.5 %collective-permute-done.66 = f32[2,4,768]{2,1,0:T(4,128)S(1)} collective-permute-done((f32[2,4,768]{2,1,0:T(4,128)S(1)}, f32[2,4,768]{2,1,0:T(4,128)S(1)}, u32[]{:S(2)}, u32[]{:S(2)}) %collective-permute-start.66) | collective-permute-done | bytes 24608 | tf_op jit(solution)/shard_map/ppermute | solution.py:248
  361.2 2.4 collective-permute-done.67
  363.6 2.5 collective-permute-start.68
  366.1 2.3 collective-permute-done.68
  369.9 2.3 collective-permute-done.69
  373.0 2.8 bitcast_select_fusion
  375.8 2.4 fusion.36
  378.3 2.8 multiply_add_fusion.raw
  384.0 37.1 %all_to_all.46 = f32[4,64,1536]{2,1,0:T(8,128)} all-to-all(f32[4,64,1536]{2,1,0:T(8,128)S(1)} %bitcast.238), channel_id=1, replica_groups=mesh['dp'=2,'row'=4,'col'=4] {'col'}, dimensions={0} | all-to-all | bytes 3145728 | tf_op jit(solution)/shard_map/all_to_all | solution.py:311
  422.8 37.9 %all_to_all.45 = f32[4,64,1536]{2,1,0:T(8,128)S(1)} all-to-all(f32[4,64,1536]{2,1,0:T(8,128)S(1)} %broadcast_in_dim.87), channel_id=1, replica_groups=mesh['dp'=2,'row'=4,'col'=4] {'col'}, dimensions={0} | all-to-all | bytes 3145728 | tf_op jit(solution)/shard_map/all_to_all | solution.py:285
  460.8 43.0 %shard_map.265 = bf16[768,768]{1,0:T(8,128)(2,1)S(1)} custom-call(f32[256,1536]{1,0:T(8,128)S(1)} %bitcast.234, f32[768,768]{1,0:T(8,128)S(1)} %multiply_add_fusion.raw), custom_call_target="tpu_custom_call" | custom-call | flops 38050725888 | bytes 5111808 | tf_op jit(solution)/shard_map/pallas_call | solution.py:71
  505.5 4.5 all-to-all-start.8
  512.5 2.4 collective-permute-start.63
  517.2 21.3 %all-to-all-done.8 = bf16[8,192,768]{2,1,0:T(8,128)(2,1)} async-done(((bf16[8,192,768]{2,1,0:T(8,128)(2,1)}), bf16[8,192,768]{2,1,0:T(8,128)(2,1)}, u32[]{:S(2)}, u32[]{:S(2)}) %all-to-all-start.8) | async-done | bytes 2359328 | tf_op jit(solution)/shard_map/all_to_all | solution.py:649
  538.5 3.6 all-to-all-start.7
  546.9 2.3 slice_bitcast_fusion.3
  552.7 22.2 %all-to-all-done.7 = bf16[8,192,768]{2,1,0:T(8,128)(2,1)S(1)} async-done(((bf16[8,192,768]{2,1,0:T(8,128)(2,1)}), bf16[8,192,768]{2,1,0:T(8,128)(2,1)S(1)}, u32[]{:S(2)}, u32[]{:S(2)}) %all-to-all-start.7) | async-done | bytes 2359328 | tf_op jit(solution)/shard_map/all_to_all | solution.py:649
  578.7 2.1 multiply_add_fusion.4
  588.3 2.2 multiply_subtract_fusion
  (406 shorter events, 173.2 us)
Async XLA Ops:
  0.7 18.6 %collective-permute-start.1 = (f32[1,2,4,192]{3,2,1,0:T(4,128)}, f32[1,2,4,192]{3,2,1,0:T(4,128)S(1)}, u32[]{:S(2)}, u32[]{:S(2)}) collective-permute-start(f32[1,2,4,192]{3,2,1,0:T(4,128)} %bitcast.254), channel_id=1, source_target_pairs={{0,8},{4,12},{8,0},{12,4},{1,9},{5,13},{9,1},{13,5},{2,10},{6,14},... | collective-permute-start | bytes 18440 | tf_op jit(solution)/shard_map/ppermute | solution.py:248
  3.7 21.0 %collective-permute-start = (bf16[197,192]{0,1:T(8,128)(2,1)}, bf16[197,192]{0,1:T(8,128)(2,1)}, u32[]{:S(2)}, u32[]{:S(2)}) collective-permute-start(bf16[197,192]{0,1:T(8,128)(2,1)} %param.12), channel_id=1, source_target_pairs={{0,0},{1,4},{2,8},{3,12},{4,1},{5,5},{6,9},{7,13},{8,2},{9,6},{10,... | collective-permute-start | bytes 226952 | tf_op jit(solution)/shard_map/ppermute | solution.py:242
  9.7 38.0 %collective-permute-start.11 = (bf16[1,192,1536]{2,1,0:T(8,128)(2,1)}, bf16[1,192,1536]{2,1,0:T(8,128)(2,1)}, u32[]{:S(2)}, u32[]{:S(2)}) collective-permute-start(bf16[1,192,1536]{2,1,0:T(8,128)(2,1)} %maximum_bitcast_fusion), channel_id=1, source_target_pairs={{0,8},{4,12},{8,0},{12,4},{1,9},{5,13},{9,1},{13,5},{2,10},{6,14},... | collective-permute-start | bytes 1769480 | tf_op jit(solution)/shard_map/ppermute | solution.py:248
  17.0 16.9 %collective-permute-start.3 = (bf16[1,192,768]{2,1,0:T(8,128)(2,1)}, bf16[1,192,768]{2,1,0:T(8,128)(2,1)}, u32[]{:S(2)}, u32[]{:S(2)}) collective-permute-start(bf16[1,192,768]{2,1,0:T(8,128)(2,1)} %get-tuple-element.287), channel_id=1, source_target_pairs={{0,8},{4,12},{8,0},{12,4},{1,9},{5,13},{9,1},{13,5},{2,10},{6,14},... | collective-permute-start | bytes 884744 | tf_op jit(solution)/shard_map/ppermute | solution.py:248
  19.3 11.2 %collective-permute-start.2 = (f32[2,2,4,192]{3,2,1,0:T(4,128)S(1)}, f32[2,2,4,192]{3,2,1,0:T(4,128)S(1)}, u32[]{:S(2)}, u32[]{:S(2)}) collective-permute-start(f32[2,2,4,192]{3,2,1,0:T(4,128)S(1)} %pad_maximum_fusion.11), channel_id=1, source_target_pairs={{0,4},{4,0},{8,12},{12,8},{1,5},{5,1},{9,13},{13,9},{2,6},{6,2},{1... | collective-permute-start | bytes 36872 | tf_op jit(solution)/shard_map/ppermute | solution.py:248
  26.4 16.3 %all-to-all-start = ((bf16[4,197,192]{1,2,0:T(8,128)(2,1)}), bf16[4,197,192]{1,2,0:T(8,128)(2,1)}, u32[]{:S(2)}, u32[]{:S(2)}) async-start(bf16[4,197,192]{1,2,0:T(8,128)(2,1)} %broadcast_in_dim.74), calls=%async_computation | async-start | bytes 786432 | tf_op jit(solution)/shard_map/all_to_all | solution.py:285
  35.9 30.1 %collective-permute-start.4 = (bf16[2,192,768]{2,1,0:T(8,128)(2,1)}, bf16[2,192,768]{2,1,0:T(8,128)(2,1)}, u32[]{:S(2)}, u32[]{:S(2)}) collective-permute-start(bf16[2,192,768]{2,1,0:T(8,128)(2,1)} %pad_maximum_fusion.7), channel_id=1, source_target_pairs={{0,4},{4,0},{8,12},{12,8},{1,5},{5,1},{9,13},{13,9},{2,6},{6,2},{1... | collective-permute-start | bytes 1769480 | tf_op jit(solution)/shard_map/ppermute | solution.py:248
  44.3 21.0 %collective-permute-start.28 = (bf16[1,192,1536]{2,1,0:T(8,128)(2,1)S(1)}, bf16[1,192,1536]{2,1,0:T(8,128)(2,1)S(1)}, u32[]{:S(2)}, u32[]{:S(2)}) collective-permute-start(bf16[1,192,1536]{2,1,0:T(8,128)(2,1)S(1)} %bitcast.243), channel_id=1, source_target_pairs={{0,8},{4,12},{8,0},{12,4},{1,9},{5,13},{9,1},{13,5},{2,10},{6,14},... | collective-permute-start | bytes 1769480 | tf_op jit(solution)/shard_map/ppermute | solution.py:248
  46.1 19.0 %collective-permute-start.20 = (bf16[1,192,768]{2,1,0:T(8,128)(2,1)}, bf16[1,192,768]{2,1,0:T(8,128)(2,1)S(1)}, u32[]{:S(2)}, u32[]{:S(2)}) collective-permute-start(bf16[1,192,768]{2,1,0:T(8,128)(2,1)} %bitcast.246), channel_id=1, source_target_pairs={{0,8},{4,12},{8,0},{12,4},{1,9},{5,13},{9,1},{13,5},{2,10},{6,14},... | collective-permute-start | bytes 884744 | tf_op jit(solution)/shard_map/ppermute | solution.py:248
  49.1 37.3 %collective-permute-start.12 = (bf16[2,192,1536]{2,1,0:T(8,128)(2,1)S(1)}, bf16[2,192,1536]{2,1,0:T(8,128)(2,1)S(1)}, u32[]{:S(2)}, u32[]{:S(2)}) collective-permute-start(bf16[2,192,1536]{2,1,0:T(8,128)(2,1)S(1)} %pad_maximum_fusion.4), channel_id=1, source_target_pairs={{0,4},{4,0},{8,12},{12,8},{1,5},{5,1},{9,13},{13,9},{2,6},{6,2},{1... | collective-permute-start | bytes 3538952 | tf_op jit(solution)/shard_map/ppermute | solution.py:248
  65.4 21.0 %collective-permute-start.29 = (bf16[2,192,1536]{2,1,0:T(8,128)(2,1)S(1)}, bf16[2,192,1536]{2,1,0:T(8,128)(2,1)S(1)}, u32[]{:S(2)}, u32[]{:S(2)}) collective-permute-start(bf16[2,192,1536]{2,1,0:T(8,128)(2,1)S(1)} %pad_maximum_fusion.5), channel_id=1, source_target_pairs={{0,4},{4,0},{8,12},{12,8},{1,5},{5,1},{9,13},{13,9},{2,6},{6,2},{1... | collective-permute-start | bytes 3538952 | tf_op jit(solution)/shard_map/ppermute | solution.py:248
  71.7 7.1 %collective-permute-start.5 = (bf16[56,768]{1,0:T(8,128)(2,1)S(1)}, bf16[56,768]{1,0:T(8,128)(2,1)S(1)}, u32[]{:S(2)}, u32[]{:S(2)}) collective-permute-start(bf16[56,768]{1,0:T(8,128)(2,1)S(1)} %get-tuple-element.117), channel_id=1, source_target_pairs={{0,1},{1,0},{2,3},{3,2},{4,5},{5,4},{6,7},{7,6},{8,9},{9,8},{10,11... | collective-permute-start | bytes 258056 | tf_op jit(solution)/shard_map/ppermute | solution.py:248
  71.7 10.0 %collective-permute-start.6 = (bf16[56,768]{1,0:T(8,128)(2,1)S(1)}, bf16[56,768]{1,0:T(8,128)(2,1)S(1)}, u32[]{:S(2)}, u32[]{:S(2)}) collective-permute-start(bf16[56,768]{1,0:T(8,128)(2,1)S(1)} %get-tuple-element.118), channel_id=1, source_target_pairs={{0,2},{1,3},{2,0},{3,1},{4,6},{5,7},{6,4},{7,5},{8,10},{9,11},{10,... | collective-permute-start | bytes 258056 | tf_op jit(solution)/shard_map/ppermute | solution.py:248
  73.7 8.0 %collective-permute-start.7 = (bf16[56,768]{1,0:T(8,128)(2,1)S(1)}, bf16[56,768]{1,0:T(8,128)(2,1)S(1)}, u32[]{:S(2)}, u32[]{:S(2)}) collective-permute-start(bf16[56,768]{1,0:T(8,128)(2,1)S(1)} %get-tuple-element.119), channel_id=1, source_target_pairs={{0,3},{1,2},{2,1},{3,0},{4,7},{5,6},{6,5},{7,4},{8,11},{9,10},{10,... | collective-permute-start | bytes 258056 | tf_op jit(solution)/shard_map/ppermute | solution.py:248
  81.9 7.0 %collective-permute-start.10 = (bf16[56,768]{1,0:T(8,128)(2,1)S(1)}, bf16[56,768]{1,0:T(8,128)(2,1)S(1)}, u32[]{:S(2)}, u32[]{:S(2)}) collective-permute-start(bf16[56,768]{1,0:T(8,128)(2,1)S(1)} %get-tuple-element.121.refs_0_), channel_id=1, source_target_pairs={{0,3},{1,2},{2,1},{3,0},{4,7},{5,6},{6,5},{7,4},{8,11},{9,10},{10,... | collective-permute-start | bytes 258056 | tf_op jit(solution)/shard_map/ppermute | solution.py:248
  83.4 5.6 collective-permute-start.8
  84.1 7.9 %collective-permute-start.9 = (bf16[56,768]{1,0:T(8,128)(2,1)S(1)}, bf16[56,768]{1,0:T(8,128)(2,1)S(1)}, u32[]{:S(2)}, u32[]{:S(2)}) collective-permute-start(bf16[56,768]{1,0:T(8,128)(2,1)S(1)} %get-tuple-element.121.refs_0_), channel_id=1, source_target_pairs={{0,2},{1,3},{2,0},{3,1},{4,6},{5,7},{6,4},{7,5},{8,10},{9,11},{10,... | collective-permute-start | bytes 258056 | tf_op jit(solution)/shard_map/ppermute | solution.py:248
  93.1 9.1 %collective-permute-start.14 = (bf16[56,768]{1,0:T(8,128)(2,1)S(1)}, bf16[56,768]{1,0:T(8,128)(2,1)S(1)}, u32[]{:S(2)}, u32[]{:S(2)}) collective-permute-start(bf16[56,768]{1,0:T(8,128)(2,1)S(1)} %get-tuple-element.124), channel_id=1, source_target_pairs={{0,2},{1,3},{2,0},{3,1},{4,6},{5,7},{6,4},{7,5},{8,10},{9,11},{10,... | collective-permute-start | bytes 258056 | tf_op jit(solution)/shard_map/ppermute | solution.py:248
  95.2 7.0 %collective-permute-start.15 = (bf16[56,768]{1,0:T(8,128)(2,1)S(1)}, bf16[56,768]{1,0:T(8,128)(2,1)S(1)}, u32[]{:S(2)}, u32[]{:S(2)}) collective-permute-start(bf16[56,768]{1,0:T(8,128)(2,1)S(1)} %get-tuple-element.125), channel_id=1, source_target_pairs={{0,3},{1,2},{2,1},{3,0},{4,7},{5,6},{6,5},{7,4},{8,11},{9,10},{10,... | collective-permute-start | bytes 258056 | tf_op jit(solution)/shard_map/ppermute | solution.py:248
  103.7 25.7 %collective-permute-start.17 = (bf16[56,768]{1,0:T(8,128)(2,1)}, bf16[56,768]{1,0:T(8,128)(2,1)}, u32[]{:S(2)}, u32[]{:S(2)}) collective-permute-start(bf16[56,768]{1,0:T(8,128)(2,1)} %get-tuple-element.130), channel_id=1, source_target_pairs={{0,1},{1,0},{2,3},{3,2},{4,5},{5,4},{6,7},{7,6},{8,9},{9,8},{10,11... | collective-permute-start | bytes 258056 | tf_op jit(solution)/shard_map/ppermute | solution.py:248
  105.2 24.2 %collective-permute-start.18 = (bf16[56,768]{1,0:T(8,128)(2,1)}, bf16[56,768]{1,0:T(8,128)(2,1)}, u32[]{:S(2)}, u32[]{:S(2)}) collective-permute-start(bf16[56,768]{1,0:T(8,128)(2,1)} %get-tuple-element.130), channel_id=1, source_target_pairs={{0,2},{1,3},{2,0},{3,1},{4,6},{5,7},{6,4},{7,5},{8,10},{9,11},{10,... | collective-permute-start | bytes 258056 | tf_op jit(solution)/shard_map/ppermute | solution.py:248
  106.5 22.9 %collective-permute-start.19 = (bf16[56,768]{1,0:T(8,128)(2,1)}, bf16[56,768]{1,0:T(8,128)(2,1)}, u32[]{:S(2)}, u32[]{:S(2)}) collective-permute-start(bf16[56,768]{1,0:T(8,128)(2,1)} %get-tuple-element.130), channel_id=1, source_target_pairs={{0,3},{1,2},{2,1},{3,0},{4,7},{5,6},{6,5},{7,4},{8,11},{9,10},{10,... | collective-permute-start | bytes 258056 | tf_op jit(solution)/shard_map/ppermute | solution.py:248
  109.8 5.6 collective-permute-start.16
  116.1 21.9 %all-to-all-start.1 = ((f32[4,56,192]{2,1,0:T(8,128)}), f32[4,56,192]{2,1,0:T(8,128)}, u32[]{:S(2)}, u32[]{:S(2)}) async-start(f32[4,56,192]{2,1,0:T(8,128)} %bitcast.248), calls=%async_computation.1 | async-start | bytes 458752 | tf_op jit(solution)/shard_map/all_to_all | solution.py:592
  132.7 11.6 %collective-permute-start.22 = (bf16[56,768]{1,0:T(8,128)(2,1)}, bf16[56,768]{1,0:T(8,128)(2,1)}, u32[]{:S(2)}, u32[]{:S(2)}) collective-permute-start(bf16[56,768]{1,0:T(8,128)(2,1)} %get-tuple-element.268), channel_id=1, source_target_pairs={{0,1},{1,0},{2,3},{3,2},{4,5},{5,4},{6,7},{7,6},{8,9},{9,8},{10,11... | collective-permute-start | bytes 258056 | tf_op jit(solution)/shard_map/ppermute | solution.py:248
  134.8 10.1 %collective-permute-start.23 = (bf16[56,768]{1,0:T(8,128)(2,1)}, bf16[56,768]{1,0:T(8,128)(2,1)}, u32[]{:S(2)}, u32[]{:S(2)}) collective-permute-start(bf16[56,768]{1,0:T(8,128)(2,1)} %get-tuple-element.270), channel_id=1, source_target_pairs={{0,2},{1,3},{2,0},{3,1},{4,6},{5,7},{6,4},{7,5},{8,10},{9,11},{10,... | collective-permute-start | bytes 258056 | tf_op jit(solution)/shard_map/ppermute | solution.py:248
  137.1 7.7 %collective-permute-start.24 = (bf16[56,768]{1,0:T(8,128)(2,1)}, bf16[56,768]{1,0:T(8,128)(2,1)}, u32[]{:S(2)}, u32[]{:S(2)}) collective-permute-start(bf16[56,768]{1,0:T(8,128)(2,1)} %get-tuple-element.272), channel_id=1, source_target_pairs={{0,3},{1,2},{2,1},{3,0},{4,7},{5,6},{6,5},{7,4},{8,11},{9,10},{10,... | collective-permute-start | bytes 258056 | tf_op jit(solution)/shard_map/ppermute | solution.py:248
  138.0 57.6 %all-to-all-start.2 = ((f32[4,192,768]{2,1,0:T(8,128)}), f32[4,192,768]{2,1,0:T(8,128)}, u32[]{:S(2)}, u32[]{:S(2)}) async-start(f32[4,192,768]{2,1,0:T(8,128)} %pad_maximum_fusion), calls=%async_computation.2 | async-start | bytes 4718592 | tf_op jit(solution)/shard_map/all_to_all | solution.py:588
  148.5 6.7 %collective-permute-start.25 = (bf16[56,768]{1,0:T(8,128)(2,1)S(1)}, bf16[56,768]{1,0:T(8,128)(2,1)S(1)}, u32[]{:S(2)}, u32[]{:S(2)}) collective-permute-start(bf16[56,768]{1,0:T(8,128)(2,1)S(1)} %get-tuple-element.138), channel_id=1, source_target_pairs={{0,1},{1,0},{2,3},{3,2},{4,5},{5,4},{6,7},{7,6},{8,9},{9,8},{10,11... | collective-permute-start | bytes 258056 | tf_op jit(solution)/shard_map/ppermute | solution.py:248
  150.7 9.7 %collective-permute-start.26 = (bf16[56,768]{1,0:T(8,128)(2,1)S(1)}, bf16[56,768]{1,0:T(8,128)(2,1)S(1)}, u32[]{:S(2)}, u32[]{:S(2)}) collective-permute-start(bf16[56,768]{1,0:T(8,128)(2,1)S(1)} %get-tuple-element.138), channel_id=1, source_target_pairs={{0,2},{1,3},{2,0},{3,1},{4,6},{5,7},{6,4},{7,5},{8,10},{9,11},{10,... | collective-permute-start | bytes 258056 | tf_op jit(solution)/shard_map/ppermute | solution.py:248
  152.5 8.0 %collective-permute-start.27 = (bf16[56,768]{1,0:T(8,128)(2,1)S(1)}, bf16[56,768]{1,0:T(8,128)(2,1)S(1)}, u32[]{:S(2)}, u32[]{:S(2)}) collective-permute-start(bf16[56,768]{1,0:T(8,128)(2,1)S(1)} %get-tuple-element.138), channel_id=1, source_target_pairs={{0,3},{1,2},{2,1},{3,0},{4,7},{5,6},{6,5},{7,4},{8,11},{9,10},{10,... | collective-permute-start | bytes 258056 | tf_op jit(solution)/shard_map/ppermute | solution.py:248
  162.4 5.7 collective-permute-start.30
  164.1 9.8 %collective-permute-start.31 = (bf16[56,768]{1,0:T(8,128)(2,1)}, bf16[56,768]{1,0:T(8,128)(2,1)}, u32[]{:S(2)}, u32[]{:S(2)}) collective-permute-start(bf16[56,768]{1,0:T(8,128)(2,1)} %get-tuple-element.256), channel_id=1, source_target_pairs={{0,2},{1,3},{2,0},{3,1},{4,6},{5,7},{6,4},{7,5},{8,10},{9,11},{10,... | collective-permute-start | bytes 258056 | tf_op jit(solution)/shard_map/ppermute | solution.py:248
  165.3 8.6 %collective-permute-start.32 = (bf16[56,768]{1,0:T(8,128)(2,1)}, bf16[56,768]{1,0:T(8,128)(2,1)}, u32[]{:S(2)}, u32[]{:S(2)}) collective-permute-start(bf16[56,768]{1,0:T(8,128)(2,1)} %get-tuple-element.258), channel_id=1, source_target_pairs={{0,3},{1,2},{2,1},{3,0},{4,7},{5,6},{6,5},{7,4},{8,11},{9,10},{10,... | collective-permute-start | bytes 258056 | tf_op jit(solution)/shard_map/ppermute | solution.py:248
  180.5 6.3 %collective-permute-start.34 = (f32[56,192]{1,0:T(8,128)S(1)}, f32[56,192]{1,0:T(8,128)S(1)}, u32[]{:S(2)}, u32[]{:S(2)}) collective-permute-start(f32[56,192]{1,0:T(8,128)S(1)} %bitcast.261), channel_id=1, source_target_pairs={{0,2},{1,3},{2,0},{3,1},{4,6},{5,7},{6,4},{7,5},{8,10},{9,11},{10,... | collective-permute-start | bytes 129032 | tf_op jit(solution)/shard_map/ppermute | solution.py:248
  181.9 6.1 %collective-permute-start.35 = (f32[56,192]{1,0:T(8,128)S(1)}, f32[56,192]{1,0:T(8,128)S(1)}, u32[]{:S(2)}, u32[]{:S(2)}) collective-permute-start(f32[56,192]{1,0:T(8,128)S(1)} %bitcast.259), channel_id=1, source_target_pairs={{0,3},{1,2},{2,1},{3,0},{4,7},{5,6},{6,5},{7,4},{8,11},{9,10},{10,... | collective-permute-start | bytes 129032 | tf_op jit(solution)/shard_map/ppermute | solution.py:248
  188.7 6.9 %collective-permute-start.36 = (f32[197,192]{1,0:T(8,128)}, f32[197,192]{1,0:T(8,128)}, u32[]{:S(2)}, u32[]{:S(2)}) collective-permute-start(f32[197,192]{1,0:T(8,128)} %slice.289), channel_id=1, source_target_pairs={{0,0},{1,4},{2,8},{3,12},{4,1},{5,5},{6,9},{7,13},{8,2},{9,6},{10,... | collective-permute-start | bytes 453896 | tf_op jit(solution)/shard_map/ppermute | solution.py:242
  196.6 7.7 %collective-permute-start.37 = (bf16[56,768]{1,0:T(8,128)(2,1)S(1)}, bf16[56,768]{1,0:T(8,128)(2,1)S(1)}, u32[]{:S(2)}, u32[]{:S(2)}) collective-permute-start(bf16[56,768]{1,0:T(8,128)(2,1)S(1)} %convert_element_type.142.refs_0_), channel_id=1, source_target_pairs={{0,1},{1,0},{2,3},{3,2},{4,5},{5,4},{6,7},{7,6},{8,9},{9,8},{10,11... | collective-permute-start | bytes 258056 | tf_op jit(solution)/shard_map/ppermute | solution.py:248
  199.0 8.0 %collective-permute-start.38 = (bf16[56,768]{1,0:T(8,128)(2,1)S(1)}, bf16[56,768]{1,0:T(8,128)(2,1)S(1)}, u32[]{:S(2)}, u32[]{:S(2)}) collective-permute-start(bf16[56,768]{1,0:T(8,128)(2,1)S(1)} %convert_element_type.142.refs_0_), channel_id=1, source_target_pairs={{0,2},{1,3},{2,0},{3,1},{4,6},{5,7},{6,4},{7,5},{8,10},{9,11},{10,... | collective-permute-start | bytes 258056 | tf_op jit(solution)/shard_map/ppermute | solution.py:248
  204.0 6.7 %collective-permute-start.39 = (bf16[56,768]{1,0:T(8,128)(2,1)S(1)}, bf16[56,768]{1,0:T(8,128)(2,1)S(1)}, u32[]{:S(2)}, u32[]{:S(2)}) collective-permute-start(bf16[56,768]{1,0:T(8,128)(2,1)S(1)} %convert_element_type.142.refs_0_), channel_id=1, source_target_pairs={{0,3},{1,2},{2,1},{3,0},{4,7},{5,6},{6,5},{7,4},{8,11},{9,10},{10,... | collective-permute-start | bytes 258056 | tf_op jit(solution)/shard_map/ppermute | solution.py:248
  214.7 9.7 %collective-permute-start.41 = (bf16[56,768]{1,0:T(8,128)(2,1)S(1)}, bf16[56,768]{1,0:T(8,128)(2,1)S(1)}, u32[]{:S(2)}, u32[]{:S(2)}) collective-permute-start(bf16[56,768]{1,0:T(8,128)(2,1)S(1)} %get-tuple-element.149), channel_id=1, source_target_pairs={{0,2},{1,3},{2,0},{3,1},{4,6},{5,7},{6,4},{7,5},{8,10},{9,11},{10,... | collective-permute-start | bytes 258056 | tf_op jit(solution)/shard_map/ppermute | solution.py:248
  216.2 8.2 %collective-permute-start.42 = (bf16[56,768]{1,0:T(8,128)(2,1)S(1)}, bf16[56,768]{1,0:T(8,128)(2,1)S(1)}, u32[]{:S(2)}, u32[]{:S(2)}) collective-permute-start(bf16[56,768]{1,0:T(8,128)(2,1)S(1)} %get-tuple-element.150), channel_id=1, source_target_pairs={{0,3},{1,2},{2,1},{3,0},{4,7},{5,6},{6,5},{7,4},{8,11},{9,10},{10,... | collective-permute-start | bytes 258056 | tf_op jit(solution)/shard_map/ppermute | solution.py:248
  224.6 5.5 collective-permute-start.43
  226.4 9.1 %collective-permute-start.44 = (bf16[56,768]{1,0:T(8,128)(2,1)S(1)}, bf16[56,768]{1,0:T(8,128)(2,1)S(1)}, u32[]{:S(2)}, u32[]{:S(2)}) collective-permute-start(bf16[56,768]{1,0:T(8,128)(2,1)S(1)} %get-tuple-element.151.refs_0_), channel_id=1, source_target_pairs={{0,2},{1,3},{2,0},{3,1},{4,6},{5,7},{6,4},{7,5},{8,10},{9,11},{10,... | collective-permute-start | bytes 258056 | tf_op jit(solution)/shard_map/ppermute | solution.py:248
  227.6 7.9 %collective-permute-start.45 = (bf16[56,768]{1,0:T(8,128)(2,1)S(1)}, bf16[56,768]{1,0:T(8,128)(2,1)S(1)}, u32[]{:S(2)}, u32[]{:S(2)}) collective-permute-start(bf16[56,768]{1,0:T(8,128)(2,1)S(1)} %get-tuple-element.151.refs_0_), channel_id=1, source_target_pairs={{0,3},{1,2},{2,1},{3,0},{4,7},{5,6},{6,5},{7,4},{8,11},{9,10},{10,... | collective-permute-start | bytes 258056 | tf_op jit(solution)/shard_map/ppermute | solution.py:248
  237.9 5.3 collective-permute-start.46
  239.5 8.7 %collective-permute-start.47 = (bf16[56,768]{1,0:T(8,128)(2,1)S(1)}, bf16[56,768]{1,0:T(8,128)(2,1)S(1)}, u32[]{:S(2)}, u32[]{:S(2)}) collective-permute-start(bf16[56,768]{1,0:T(8,128)(2,1)S(1)} %get-tuple-element.155), channel_id=1, source_target_pairs={{0,2},{1,3},{2,0},{3,1},{4,6},{5,7},{6,4},{7,5},{8,10},{9,11},{10,... | collective-permute-start | bytes 258056 | tf_op jit(solution)/shard_map/ppermute | solution.py:248
  240.9 7.2 %collective-permute-start.48 = (bf16[56,768]{1,0:T(8,128)(2,1)S(1)}, bf16[56,768]{1,0:T(8,128)(2,1)S(1)}, u32[]{:S(2)}, u32[]{:S(2)}) collective-permute-start(bf16[56,768]{1,0:T(8,128)(2,1)S(1)} %get-tuple-element.156), channel_id=1, source_target_pairs={{0,3},{1,2},{2,1},{3,0},{4,7},{5,6},{6,5},{7,4},{8,11},{9,10},{10,... | collective-permute-start | bytes 258056 | tf_op jit(solution)/shard_map/ppermute | solution.py:248
  249.9 8.7 %collective-permute-start.50 = (bf16[56,768]{1,0:T(8,128)(2,1)S(1)}, bf16[56,768]{1,0:T(8,128)(2,1)S(1)}, u32[]{:S(2)}, u32[]{:S(2)}) collective-permute-start(bf16[56,768]{1,0:T(8,128)(2,1)S(1)} %get-tuple-element.158.refs_0_), channel_id=1, source_target_pairs={{0,2},{1,3},{2,0},{3,1},{4,6},{5,7},{6,4},{7,5},{8,10},{9,11},{10,... | collective-permute-start | bytes 258056 | tf_op jit(solution)/shard_map/ppermute | solution.py:248
  251.4 7.3 %collective-permute-start.51 = (bf16[56,768]{1,0:T(8,128)(2,1)S(1)}, bf16[56,768]{1,0:T(8,128)(2,1)S(1)}, u32[]{:S(2)}, u32[]{:S(2)}) collective-permute-start(bf16[56,768]{1,0:T(8,128)(2,1)S(1)} %get-tuple-element.158.refs_0_), channel_id=1, source_target_pairs={{0,3},{1,2},{2,1},{3,0},{4,7},{5,6},{6,5},{7,4},{8,11},{9,10},{10,... | collective-permute-start | bytes 258056 | tf_op jit(solution)/shard_map/ppermute | solution.py:248
  261.1 8.7 %collective-permute-start.53 = (bf16[56,768]{1,0:T(8,128)(2,1)S(1)}, bf16[56,768]{1,0:T(8,128)(2,1)S(1)}, u32[]{:S(2)}, u32[]{:S(2)}) collective-permute-start(bf16[56,768]{1,0:T(8,128)(2,1)S(1)} %get-tuple-element.162), channel_id=1, source_target_pairs={{0,2},{1,3},{2,0},{3,1},{4,6},{5,7},{6,4},{7,5},{8,10},{9,11},{10,... | collective-permute-start | bytes 258056 | tf_op jit(solution)/shard_map/ppermute | solution.py:248
  262.6 7.3 %collective-permute-start.54 = (bf16[56,768]{1,0:T(8,128)(2,1)S(1)}, bf16[56,768]{1,0:T(8,128)(2,1)S(1)}, u32[]{:S(2)}, u32[]{:S(2)}) collective-permute-start(bf16[56,768]{1,0:T(8,128)(2,1)S(1)} %get-tuple-element.163), channel_id=1, source_target_pairs={{0,3},{1,2},{2,1},{3,0},{4,7},{5,6},{6,5},{7,4},{8,11},{9,10},{10,... | collective-permute-start | bytes 258056 | tf_op jit(solution)/shard_map/ppermute | solution.py:248
  270.1 5.2 collective-permute-start.55
  271.6 8.7 %collective-permute-start.56 = (bf16[56,768]{1,0:T(8,128)(2,1)S(1)}, bf16[56,768]{1,0:T(8,128)(2,1)S(1)}, u32[]{:S(2)}, u32[]{:S(2)}) collective-permute-start(bf16[56,768]{1,0:T(8,128)(2,1)S(1)} %get-tuple-element.165.refs_0_), channel_id=1, source_target_pairs={{0,2},{1,3},{2,0},{3,1},{4,6},{5,7},{6,4},{7,5},{8,10},{9,11},{10,... | collective-permute-start | bytes 258056 | tf_op jit(solution)/shard_map/ppermute | solution.py:248
  273.1 7.3 %collective-permute-start.57 = (bf16[56,768]{1,0:T(8,128)(2,1)S(1)}, bf16[56,768]{1,0:T(8,128)(2,1)S(1)}, u32[]{:S(2)}, u32[]{:S(2)}) collective-permute-start(bf16[56,768]{1,0:T(8,128)(2,1)S(1)} %get-tuple-element.165.refs_0_), channel_id=1, source_target_pairs={{0,3},{1,2},{2,1},{3,0},{4,7},{5,6},{6,5},{7,4},{8,11},{9,10},{10,... | collective-permute-start | bytes 258056 | tf_op jit(solution)/shard_map/ppermute | solution.py:248
  288.9 35.1 %all-to-all-start.3 = ((bf16[8,208,768]{2,1,0:T(8,128)(2,1)}), bf16[8,208,768]{2,1,0:T(8,128)(2,1)}, u32[]{:S(2)}, u32[]{:S(2)}) async-start(bf16[8,208,768]{2,1,0:T(8,128)(2,1)} %bitcast_dynamic-update-slice_fusion.8), calls=%async_computation.3 | async-start | bytes 5111808 | tf_op jit(solution)/shard_map/all_to_all | solution.py:576
  324.0 49.0 %all-to-all-start.4 = ((bf16[8,208,768]{2,1,0:T(8,128)(2,1)}), bf16[8,208,768]{2,1,0:T(8,128)(2,1)}, u32[]{:S(2)}, u32[]{:S(2)}) async-start(bf16[8,208,768]{2,1,0:T(8,128)(2,1)} %bitcast_dynamic-update-slice_fusion), calls=%async_computation.4 | async-start | bytes 5111808 | tf_op jit(solution)/shard_map/all_to_all | solution.py:576
  330.2 9.8 %collective-permute-start.59 = (bf16[56,768]{1,0:T(8,128)(2,1)S(1)}, bf16[56,768]{1,0:T(8,128)(2,1)S(1)}, u32[]{:S(2)}, u32[]{:S(2)}) collective-permute-start(bf16[56,768]{1,0:T(8,128)(2,1)S(1)} %get-tuple-element.169), channel_id=1, source_target_pairs={{0,2},{1,3},{2,0},{3,1},{4,6},{5,7},{6,4},{7,5},{8,10},{9,11},{10,... | collective-permute-start | bytes 258056 | tf_op jit(solution)/shard_map/ppermute | solution.py:248
  331.6 8.3 %collective-permute-start.60 = (bf16[56,768]{1,0:T(8,128)(2,1)S(1)}, bf16[56,768]{1,0:T(8,128)(2,1)S(1)}, u32[]{:S(2)}, u32[]{:S(2)}) collective-permute-start(bf16[56,768]{1,0:T(8,128)(2,1)S(1)} %get-tuple-element.170), channel_id=1, source_target_pairs={{0,3},{1,2},{2,1},{3,0},{4,7},{5,6},{6,5},{7,4},{8,11},{9,10},{10,... | collective-permute-start | bytes 258056 | tf_op jit(solution)/shard_map/ppermute | solution.py:248
  342.2 17.5 %collective-permute-start.66 = (f32[2,4,768]{2,1,0:T(4,128)S(1)}, f32[2,4,768]{2,1,0:T(4,128)S(1)}, u32[]{:S(2)}, u32[]{:S(2)}) collective-permute-start(f32[2,4,768]{2,1,0:T(4,128)S(1)} %fusion.14), channel_id=1, source_target_pairs={{0,8},{4,12},{8,0},{12,4},{1,9},{5,13},{9,1},{13,5},{2,10},{6,14},... | collective-permute-start | bytes 73736 | tf_op jit(solution)/shard_map/ppermute | solution.py:248
  505.5 33.0 %all-to-all-start.8 = ((bf16[8,192,768]{2,1,0:T(8,128)(2,1)}), bf16[8,192,768]{2,1,0:T(8,128)(2,1)}, u32[]{:S(2)}, u32[]{:S(2)}) async-start(bf16[8,192,768]{2,1,0:T(8,128)(2,1)} %pad_maximum_fusion.2), calls=%async_computation.8 | async-start | bytes 4718592 | tf_op jit(solution)/shard_map/all_to_all | solution.py:649
  510.7 31.4 %collective-permute-start.62 = (f32[56,192]{1,0:T(8,128)S(1)}, f32[56,192]{1,0:T(8,128)S(1)}, u32[]{:S(2)}, u32[]{:S(2)}) collective-permute-start(f32[56,192]{1,0:T(8,128)S(1)} %bitcast.258), channel_id=1, source_target_pairs={{0,2},{1,3},{2,0},{3,1},{4,6},{5,7},{6,4},{7,5},{8,10},{9,11},{10,... | collective-permute-start | bytes 129032 | tf_op jit(solution)/shard_map/ppermute | solution.py:248
  512.5 29.7 %collective-permute-start.63 = (f32[56,192]{1,0:T(8,128)S(1)}, f32[56,192]{1,0:T(8,128)S(1)}, u32[]{:S(2)}, u32[]{:S(2)}) collective-permute-start(f32[56,192]{1,0:T(8,128)S(1)} %bitcast.257), channel_id=1, source_target_pairs={{0,3},{1,2},{2,1},{3,0},{4,7},{5,6},{6,5},{7,4},{8,11},{9,10},{10,... | collective-permute-start | bytes 129032 | tf_op jit(solution)/shard_map/ppermute | solution.py:248
  538.5 36.4 %all-to-all-start.7 = ((bf16[8,192,768]{2,1,0:T(8,128)(2,1)}), bf16[8,192,768]{2,1,0:T(8,128)(2,1)S(1)}, u32[]{:S(2)}, u32[]{:S(2)}) async-start(bf16[8,192,768]{2,1,0:T(8,128)(2,1)} %pad_maximum_fusion.1), calls=%async_computation.7 | async-start | bytes 4718592 | tf_op jit(solution)/shard_map/all_to_all | solution.py:649
  (87 other events, 946.2 us)

commit v5 on v4

--- a/solution.py
+++ b/solution.py
@@ -309,7 +309,7 @@
     ]
     packed = jnp.concatenate(strips, axis=1)
     blocks = lax.all_to_all(packed.reshape(size, third // size, -1), "col", 0, 0)
-    return to_all(jnp.sum(blocks, axis=0), "col").reshape(third, -1)
+    return jnp.sum(blocks, axis=0)
 
 
 def halves(values):
@@ -520,9 +520,6 @@
 
     own_groups = [[own_weights(i, which) for which in groups] for i in range(levels)]
     weight_sets = [weights_of(own_groups[0])] + [None] * (levels - 1)
-    chunks, own_groups[1:] = lax.optimization_barrier((chunks, own_groups[1:]))
-    for level_index in range(1, levels):
-        weight_sets[level_index] = weights_of(own_groups[level_index])
     saved = []
     early = [None] * levels
     for level_index in range(levels):
@@ -537,6 +534,12 @@
             position,
         )
         stream_two, normed = norm_step(swap_parts(parts), stream, level_index, 2)
+        if level_index == 0:
+            normed, own_groups[1:] = lax.optimization_barrier((normed, own_groups[1:]))
+            for later in range(1, levels):
+                weight_sets[later] = weights_of(own_groups[later])
+        if level_index == levels - 1:
+            normed, back_chunks = lax.optimization_barrier((normed, back_chunks))
         chunks = to_partners(normed)
         *parts, slope, normed_two, activated = kernel_call(
             functools.partial(mlp_kernel, tokens),
@@ -552,6 +555,10 @@
             stream, normed = norm_step(parts, stream_two, level_index + 1, 0)
             if level_index == 0:
                 normed, late_me, cotangent = lax.optimization_barrier((normed, me, cotangent))
+                cotangent_blocks = pad_rows(swap_row_col(cotangent), padded)
+                cotangent_blocks = cotangent_blocks.reshape(col_size, chunk, width_row)
+                upstream = features_first(lax.all_to_all(cotangent_blocks, "col", 0, 0))
+                back_chunks = to_partners(upstream.astype(jnp.bfloat16))
             chunks = to_partners(normed)
         else:
             stream = stream_two
@@ -587,24 +594,16 @@
     stacked_moment = jnp.stack(near_moments)
     own_moment = lax.all_to_all(stacked_moment, "row", 0, 0).reshape(model_width, widest)
 
-    cotangent_blocks = pad_rows(swap_row_col(cotangent), padded)
-    cotangent_blocks = cotangent_blocks.reshape(col_size, chunk, width_row)
-    upstream = features_first(lax.all_to_all(cotangent_blocks, "col", 0, 0))
-
-    block_output = placed(stream)
-    upstream, own_moment, block_output = lax.optimization_barrier(
-        (upstream, own_moment, block_output)
-    )
+    back_chunks, own_moment = lax.optimization_barrier((back_chunks, own_moment))
     early_all = spread(early)
     late = [None] * levels
     norm_sums = [None] * levels
-    back_low = upstream.astype(jnp.bfloat16)
     for level_index in reversed(range(levels)):
         weight_qkv, weight_proj, weight_up, weight_down = weight_sets[level_index]
         stream_one, stream_two, mixed, slope = saved[level_index]
         *parts, hidden_grad, back_two = kernel_call(
             mlp_back_kernel,
-            [*to_partners(back_low), slope, weight_up, weight_down],
+            [*back_chunks, slope, weight_up, weight_down],
             low_chunks + [sent, sent_model],
             [whole_scratch],
             perceptron_flops,
@@ -613,6 +612,8 @@
         upstream, back_low, sums_two = norm_back_step(
             swap_parts(parts), stream_two, upstream, level_index, 2
         )
+        if level_index == 0:
+            back_low, early_all = lax.optimization_barrier((back_low, early_all))
         *parts, mixed_grad, back_one = kernel_call(
             functools.partial(attend_back_kernel, tokens, heads),
             [*to_partners(back_low), mixed, weight_qkv, weight_proj],
@@ -629,13 +630,12 @@
         )
         norm_sums[level_index] = jnp.concatenate([sums_one, sums_two])
 
-    norm_whole = jnp.stack(norm_sums)
-    for axis in ("row", "col", "dp"):
-        norm_whole = sum_by_pairs(norm_whole, axis)
-    norm_grad = lax.dynamic_slice_in_dim(norm_whole, my_row * width_row, width_row, 2)
-    norm_moment_new = moment_decay * norm_moment + norm_grad
-    late_all, norm_grad, norm_moment_new = lax.optimization_barrier(
-        (late_all, norm_grad, norm_moment_new)
+        if level_index:
+            back_chunks = to_partners(back_low)
+
+    norm_whole = sum_by_pairs(jnp.stack(norm_sums), "col")
+    late_all, norm_whole, stream, upstream = lax.optimization_barrier(
+        (late_all, norm_whole, stream, upstream)
     )
 
     turned = (me // levels) % 2 == 1
@@ -647,12 +647,24 @@
         blocks = whole.astype(jnp.bfloat16).reshape(row_size, width_row, widest)
         blocks = jnp.concatenate([blocks] * dp_size)
         received = lax.all_to_all(blocks, ("dp", "row"), 0, 0)
-        return [received[j].astype(jnp.float32) for j in range(jobs)]
+        return [received[j] for j in range(jobs)]
 
     own_raw = moment_decay * own_moment + own_grad
-    gram, own_grad = lax.optimization_barrier((gram_strips(own_raw), own_grad))
+    for axis in ("row", "dp"):
+        norm_whole = sum_by_pairs(norm_whole, axis)
+    block_output = placed(stream)
+    own_strip, norm_whole, block_output = lax.optimization_barrier(
+        (gram_strips(own_raw), norm_whole, block_output)
+    )
+    norm_grad = lax.dynamic_slice_in_dim(norm_whole, my_row * width_row, width_row, 2)
+    norm_moment_new = moment_decay * norm_moment + norm_grad
+    input_grad = placed(upstream)
+    gram = to_all(own_strip, "col").reshape(-1, own_strip.shape[1])
+    gram, own_grad, input_grad = lax.optimization_barrier((gram, own_grad, input_grad))
     grads = returned(own_grad)
-    orths = returned(schulz(own_raw, gram))
+    orth_whole, grads = lax.optimization_barrier((schulz(own_raw, gram), grads))
+    orths = [block.astype(jnp.float32) for block in returned(orth_whole)]
+    grads = [block.astype(jnp.float32) for block in grads]
 
     grad_outs = []
     moment_outs = []
@@ -678,7 +690,7 @@
     norm_new = norm_params - norm_rate / math.sqrt(tokens_all) * norm_moment_new
     return (
         block_output,
-        placed(upstream),
+        input_grad,
         *grad_outs,
         norm_grad,
         *moment_outs,

time: 603 us -> 537 us (0.89)
  blocking collectives: 75 us -> 0 us
  local copies, waits for them, and re-layouts: 63.8 us -> 80 us
  waiting for transfers between devices: 200 us -> 185 us
  starting transfers between devices: 142 us -> 156 us
  other arithmetic: 47.5 us -> 37.6 us
    all_to_all x2 -> x0, blocking collectives: 75 us -> none  [the longest x1 37.9 us: to_all(): lax.all_to_all(jnp.broadcast_to(block[None], (size,) + block.shape), axis...]
    ppermute x66, waiting for transfers between devices: 123 us -> 153 us  [from_partner(): return lax.ppermute(values, axes, pairs)]
    all_to_all x2, waiting for transfers between devices: 43.6 us -> 14.7 us  [returned(): received = lax.all_to_all(blocks, ('dp', 'row'), 0, 0)]
    all_to_all x2, waiting for transfers between devices: 29.1 us -> 4.95 us  [spread(): return lax.all_to_all(stack, ('dp', 'row'), 0, 0).reshape(-1, widest)]
    unnamed x173 -> x197, local copies, waits for them, and re-layouts: 26.7 us -> 35.4 us
    all_to_all x2, starting transfers between devices: 8.12 us -> 16.2 us  [returned(): received = lax.all_to_all(blocks, ('dp', 'row'), 0, 0)]
    all_to_all x1, waiting for transfers between devices: 0.01 us -> 6.19 us  [on_device(): upstream = features_first(lax.all_to_all(cotangent_blocks, 'col', 0, 0))]
  transfers between devices with their start and end apart: 77 -> 79, of which waited for: 39 -> 36; matrix products, arithmetic and copies ran while one was open for 12% -> 14% of each run, Pallas kernels for 1% -> 10%
where the time goes in v5:
time: 537 us; the launch traced here: 528 us
  waiting for transfers between devices  185 us (34%)
  starting transfers between devices  156 us (29%)
  local copies, waits for them, and re-layouts  80 us (15%)
  Pallas kernels  57.5 us (11%)
  other arithmetic  37.6 us (7%)
  matrix products  9.3 us (2%)
    ppermute x66, waiting for transfers between devices, from_partner(): return lax.ppermute(values, axes, pairs)  153 us
    ppermute x66, starting transfers between devices, from_partner(): return lax.ppermute(values, axes, pairs)  94.5 us
    pallas_call x15, Pallas kernels, kernel_call(): pl.pallas_call(body, out_shape=list(outputs), in_specs=specs, out_specs=i...  57.5 us
    unnamed x197, local copies, waits for them, and re-layouts  35.4 us
    all_to_all x2, starting transfers between devices, returned(): received = lax.all_to_all(blocks, ('dp', 'row'), 0, 0)  16.2 us
    all_to_all x2, waiting for transfers between devices, returned(): received = lax.all_to_all(blocks, ('dp', 'row'), 0, 0)  14.7 us
  transfers between devices with their start and end apart: 79, of which 36 were waited for; matrix products, arithmetic and copies ran while one was open for 14% of the time, Pallas kernels for 10%

profile of v5, /device:TPU:0, one launch (start us, length us, event | category | flops | bytes accessed | tf_op | source)
XLA Modules:
  0.0 528.2 jit_solution(4065020046734958475)
XLA Ops:
  3.7 3.0 collective-permute-start.3
  8.6 5.7 %collective-permute-start.11 = (bf16[1,192,1536]{2,1,0:T(8,128)(2,1)}, bf16[1,192,1536]{2,1,0:T(8,128)(2,1)S(1)}, u32[]{:S(2)}, u32[]{:S(2)}) collective-permute-start(bf16[1,192,1536]{2,1,0:T(8,128)(2,1)} %maximum_bitcast_fusion), channel_id=1, source_target_pairs={{0,8},{4,12},{8,0},{12,4},{1,9},{5,13},{9,1},{13,5},{2,10},{6,14},... | collective-permute-start | bytes 1769480 | tf_op jit(solution)/shard_map/ppermute | solution.py:248
  20.5 3.8 all-to-all-start
  30.0 6.6 %all-to-all-done = bf16[4,197,192]{1,2,0:T(8,128)(2,1)S(1)} async-done(((bf16[4,197,192]{1,2,0:T(8,128)(2,1)}), bf16[4,197,192]{1,2,0:T(8,128)(2,1)S(1)}, u32[]{:S(2)}, u32[]{:S(2)}) %all-to-all-start) | async-done | bytes 302624 | tf_op jit(solution)/shard_map/all_to_all | solution.py:285
  41.9 2.0 collective-permute-start.6
  43.9 2.4 collective-permute-start.7
  46.6 4.6 collective-permute-done.6.refs_2_
  58.7 8.0 %collective-permute-done.31 = bf16[1,192,1536]{2,1,0:T(8,128)(2,1)S(1)} collective-permute-done((bf16[1,192,1536]{2,1,0:T(8,128)(2,1)S(1)}, bf16[1,192,1536]{2,1,0:T(8,128)(2,1)S(1)}, u32[]{:S(2)}, u32[]{:S(2)}) %collective-permute-start.31) | collective-permute-done | bytes 589856 | tf_op jit(solution)/shard_map/ppermute | solution.py:248
  67.1 2.7 collective-permute-done.19
  72.0 2.7 collective-permute-start.9
  81.7 2.2 collective-permute-start.14
  86.8 3.9 collective-permute-done.14.refs_2_
  94.0 3.4 collective-permute-start.24
  97.5 2.3 fusion.14
  101.5 9.6 %all-to-all-start.1 = ((f32[4,56,192]{2,1,0:T(8,128)}), f32[4,56,192]{2,1,0:T(8,128)}, u32[]{:S(2)}, u32[]{:S(2)}) async-start(f32[4,56,192]{2,1,0:T(8,128)} %bitcast.250), calls=%async_computation.1 | async-start | bytes 458752 | tf_op jit(solution)/shard_map/all_to_all | solution.py:560
  113.8 6.2 %all-to-all-done.1 = f32[4,56,192]{2,1,0:T(8,128)} async-done(((f32[4,56,192]{2,1,0:T(8,128)}), f32[4,56,192]{2,1,0:T(8,128)}, u32[]{:S(2)}, u32[]{:S(2)}) %all-to-all-start.1) | async-done | bytes 172064 | tf_op jit(solution)/shard_map/all_to_all | solution.py:560
  120.0 4.7 all-to-all-start.2
  127.4 2.6 collective-permute-start.18
  131.9 4.5 collective-permute-done.17
  136.4 3.1 shard_map.267
  141.2 2.7 collective-permute-start.23
  150.9 2.7 collective-permute-start.27
  160.8 2.7 collective-permute-start.30
  165.2 2.4 collective-permute-done.29
  171.2 4.4 all-to-all-start.3
  187.6 6.3 %collective-permute-done.34.refs_2_ = bf16[56,768]{1,0:T(8,128)(2,1)S(1)} collective-permute-done((bf16[56,768]{1,0:T(8,128)(2,1)S(1)}, bf16[56,768]{1,0:T(8,128)(2,1)S(1)}, u32[]{:S(2)}, u32[]{:S(2)}) %collective-permute-start.34) | collective-permute-done | bytes 86048 | tf_op jit(solution)/shard_map/ppermute | solution.py:248
  199.1 6.1 %collective-permute-done.37.refs_2_ = bf16[56,768]{1,0:T(8,128)(2,1)S(1)} collective-permute-done((bf16[56,768]{1,0:T(8,128)(2,1)S(1)}, bf16[56,768]{1,0:T(8,128)(2,1)S(1)}, u32[]{:S(2)}, u32[]{:S(2)}) %collective-permute-start.37) | collective-permute-done | bytes 86048 | tf_op jit(solution)/shard_map/ppermute | solution.py:248
  205.2 2.4 shard_map.259
  209.9 2.2 collective-permute-start.41
  212.2 5.9 %collective-permute-done.40.refs_2_ = bf16[56,768]{1,0:T(8,128)(2,1)S(1)} collective-permute-done((bf16[56,768]{1,0:T(8,128)(2,1)S(1)}, bf16[56,768]{1,0:T(8,128)(2,1)S(1)}, u32[]{:S(2)}, u32[]{:S(2)}) %collective-permute-start.40) | collective-permute-done | bytes 86048 | tf_op jit(solution)/shard_map/ppermute | solution.py:248
  220.4 2.3 collective-permute-start.44
  222.9 5.7 %collective-permute-done.43.refs_2_ = bf16[56,768]{1,0:T(8,128)(2,1)S(1)} collective-permute-done((bf16[56,768]{1,0:T(8,128)(2,1)S(1)}, bf16[56,768]{1,0:T(8,128)(2,1)S(1)}, u32[]{:S(2)}, u32[]{:S(2)}) %collective-permute-start.43) | collective-permute-done | bytes 86048 | tf_op jit(solution)/shard_map/ppermute | solution.py:248
  232.3 2.4 collective-permute-start.47
  234.9 5.6 %collective-permute-done.46.refs_2_ = bf16[56,768]{1,0:T(8,128)(2,1)S(1)} collective-permute-done((bf16[56,768]{1,0:T(8,128)(2,1)S(1)}, bf16[56,768]{1,0:T(8,128)(2,1)S(1)}, u32[]{:S(2)}, u32[]{:S(2)}) %collective-permute-start.46) | collective-permute-done | bytes 86048 | tf_op jit(solution)/shard_map/ppermute | solution.py:248
  242.8 2.3 collective-permute-start.50
  245.3 5.6 %collective-permute-done.49.refs_2_ = bf16[56,768]{1,0:T(8,128)(2,1)S(1)} collective-permute-done((bf16[56,768]{1,0:T(8,128)(2,1)S(1)}, bf16[56,768]{1,0:T(8,128)(2,1)S(1)}, u32[]{:S(2)}, u32[]{:S(2)}) %collective-permute-start.49) | collective-permute-done | bytes 86048 | tf_op jit(solution)/shard_map/ppermute | solution.py:248
  251.9 2.4 shard_map.263
  260.4 4.8 all-to-all-start.4
  267.3 2.3 collective-permute-start.53
  270.1 6.3 %collective-permute-done.52.refs_2_ = bf16[56,768]{1,0:T(8,128)(2,1)S(1)} collective-permute-done((bf16[56,768]{1,0:T(8,128)(2,1)S(1)}, bf16[56,768]{1,0:T(8,128)(2,1)S(1)}, u32[]{:S(2)}, u32[]{:S(2)}) %collective-permute-start.52) | collective-permute-done | bytes 86048 | tf_op jit(solution)/shard_map/ppermute | solution.py:248
  277.3 2.0 collective-permute-start.54
  281.3 2.4 collective-permute-start.58
  284.2 5.4 %collective-permute-done.57 = bf16[56,768]{1,0:T(8,128)(2,1)S(1)} collective-permute-done((bf16[56,768]{1,0:T(8,128)(2,1)S(1)}, bf16[56,768]{1,0:T(8,128)(2,1)S(1)}, u32[]{:S(2)}, u32[]{:S(2)}) %collective-permute-start.57) | collective-permute-done | bytes 86048 | tf_op jit(solution)/shard_map/ppermute | solution.py:248
  290.8 4.9 all-to-all-done.4
  295.8 6.7 %multiply_add_fusion = (f32[768,768]{1,0:T(8,128)S(1)}, bf16[768,768]{1,0:T(8,128)(2,1)}) fusion(f32[768,768]{1,0:T(8,128)} %bitcast.39, bf16[1664,768]{1,0:T(8,128)(2,1)} %bitcast.50, bf16[1664,768]{1,0:T(8,128)(2,1)} %bitcast.59, pred[]{:T(512)S(6)} %eq.11), kind=kOutput, calls=%fused_computation.7 | convolution fusion | flops 1967259648 | bytes 11010049 | tf_op jit(solution)/shard_map/dot_general | solution.py:24
  306.5 4.4 all-to-all-start.5
  313.3 2.4 collective-permute-start.63
  315.8 22.9 %collective-permute-done.62 = f32[56,192]{1,0:T(8,128)S(1)} collective-permute-done((f32[56,192]{1,0:T(8,128)S(1)}, f32[56,192]{1,0:T(8,128)S(1)}, u32[]{:S(2)}, u32[]{:S(2)}) %collective-permute-start.62) | collective-permute-done | bytes 43040 | tf_op jit(solution)/shard_map/ppermute | solution.py:248
  338.6 13.5 %collective-permute-done.63 = f32[56,192]{1,0:T(8,128)S(1)} collective-permute-done((f32[56,192]{1,0:T(8,128)S(1)}, f32[56,192]{1,0:T(8,128)S(1)}, u32[]{:S(2)}, u32[]{:S(2)}) %collective-permute-start.63) | collective-permute-done | bytes 43040 | tf_op jit(solution)/shard_map/ppermute | solution.py:248
  358.8 2.1 collective-permute-done.60
  361.5 3.2 collective-permute-done.61
  368.3 4.4 all-to-all-start.6
  376.2 2.1 collective-permute-start.66
  378.3 2.4 collective-permute-start.67
  380.9 18.2 %collective-permute-done.66 = f32[56,192]{1,0:T(8,128)S(1)} collective-permute-done((f32[56,192]{1,0:T(8,128)S(1)}, f32[56,192]{1,0:T(8,128)S(1)}, u32[]{:S(2)}, u32[]{:S(2)}) %collective-permute-start.66) | collective-permute-done | bytes 43040 | tf_op jit(solution)/shard_map/ppermute | solution.py:248
  399.1 13.7 %collective-permute-done.67 = f32[56,192]{1,0:T(8,128)S(1)} collective-permute-done((f32[56,192]{1,0:T(8,128)S(1)}, f32[56,192]{1,0:T(8,128)S(1)}, u32[]{:S(2)}, u32[]{:S(2)}) %collective-permute-start.67) | collective-permute-done | bytes 43040 | tf_op jit(solution)/shard_map/ppermute | solution.py:248
  413.6 3.4 collective-permute-start.69
  421.8 11.9 %all-to-all-start.7 = ((bf16[8,192,768]{2,1,0:T(8,128)(2,1)}), bf16[8,192,768]{2,1,0:T(8,128)(2,1)}, u32[]{:S(2)}, u32[]{:S(2)}) async-start(bf16[8,192,768]{2,1,0:T(8,128)(2,1)} %pad_maximum_fusion.1), calls=%async_computation.7 | async-start | bytes 4718592 | tf_op jit(solution)/shard_map/all_to_all | solution.py:649
  435.5 44.4 %shard_map.265 = bf16[768,768]{1,0:T(8,128)(2,1)S(1)} custom-call(f32[256,1536]{1,0:T(8,128)} %bitcast.71.packed, f32[768,768]{1,0:T(8,128)S(1)} %get-tuple-element.373.raw), custom_call_target="tpu_custom_call" | custom-call | flops 38050725888 | bytes 5111808 | tf_op jit(solution)/shard_map/pallas_call | solution.py:71
  479.9 3.0 slice_bitcast_fusion.8
  484.6 4.3 all-to-all-start.8
  495.4 2.0 multiply_add_fusion.4
  502.6 14.7 %all-to-all-done.8 = bf16[8,192,768]{2,1,0:T(8,128)(2,1)S(1)} async-done(((bf16[8,192,768]{2,1,0:T(8,128)(2,1)}), bf16[8,192,768]{2,1,0:T(8,128)(2,1)S(1)}, u32[]{:S(2)}, u32[]{:S(2)}) %all-to-all-start.8) | async-done | bytes 2359328 | tf_op jit(solution)/shard_map/all_to_all | solution.py:649
  523.3 2.3 convert_subtract_fusion
  (430 shorter events, 167.4 us)
Async XLA Ops:
  3.7 14.1 %collective-permute-start.3 = (bf16[1,192,768]{2,1,0:T(8,128)(2,1)S(1)}, bf16[1,192,768]{2,1,0:T(8,128)(2,1)S(1)}, u32[]{:S(2)}, u32[]{:S(2)}) collective-permute-start(bf16[1,192,768]{2,1,0:T(8,128)(2,1)S(1)} %get-tuple-element.328), channel_id=1, source_target_pairs={{0,8},{4,12},{8,0},{12,4},{1,9},{5,13},{9,1},{13,5},{2,10},{6,14},... | collective-permute-start | bytes 884744 | tf_op jit(solution)/shard_map/ppermute | solution.py:248
  6.8 12.9 %collective-permute-start.1 = (f32[1,2,4,192]{3,2,1,0:T(4,128)S(1)}, f32[1,2,4,192]{3,2,1,0:T(4,128)S(1)}, u32[]{:S(2)}, u32[]{:S(2)}) collective-permute-start(f32[1,2,4,192]{3,2,1,0:T(4,128)S(1)} %bitcast.256), channel_id=1, source_target_pairs={{0,8},{4,12},{8,0},{12,4},{1,9},{5,13},{9,1},{13,5},{2,10},{6,14},... | collective-permute-start | bytes 18440 | tf_op jit(solution)/shard_map/ppermute | solution.py:248
  6.9 12.9 %collective-permute-start = (bf16[197,192]{0,1:T(8,128)(2,1)S(1)}, bf16[197,192]{0,1:T(8,128)(2,1)S(1)}, u32[]{:S(2)}, u32[]{:S(2)}) collective-permute-start(bf16[197,192]{0,1:T(8,128)(2,1)S(1)} %copy-done.85), channel_id=1, source_target_pairs={{0,0},{1,4},{2,8},{3,12},{4,1},{5,5},{6,9},{7,13},{8,2},{9,6},{10,... | collective-permute-start | bytes 226952 | tf_op jit(solution)/shard_map/ppermute | solution.py:242
  8.6 43.5 %collective-permute-start.11 = (bf16[1,192,1536]{2,1,0:T(8,128)(2,1)}, bf16[1,192,1536]{2,1,0:T(8,128)(2,1)S(1)}, u32[]{:S(2)}, u32[]{:S(2)}) collective-permute-start(bf16[1,192,1536]{2,1,0:T(8,128)(2,1)} %maximum_bitcast_fusion), channel_id=1, source_target_pairs={{0,8},{4,12},{8,0},{12,4},{1,9},{5,13},{9,1},{13,5},{2,10},{6,14},... | collective-permute-start | bytes 1769480 | tf_op jit(solution)/shard_map/ppermute | solution.py:248
  18.8 18.4 %collective-permute-start.4 = (bf16[2,192,768]{2,1,0:T(8,128)(2,1)}, bf16[2,192,768]{2,1,0:T(8,128)(2,1)}, u32[]{:S(2)}, u32[]{:S(2)}) collective-permute-start(bf16[2,192,768]{2,1,0:T(8,128)(2,1)} %pad_maximum_fusion.6), channel_id=1, source_target_pairs={{0,4},{4,0},{8,12},{12,8},{1,5},{5,1},{9,13},{13,9},{2,6},{6,2},{1... | collective-permute-start | bytes 1769480 | tf_op jit(solution)/shard_map/ppermute | solution.py:248
  19.7 9.0 %collective-permute-start.2 = (f32[2,2,4,192]{3,2,1,0:T(4,128)S(1)}, f32[2,2,4,192]{3,2,1,0:T(4,128)S(1)}, u32[]{:S(2)}, u32[]{:S(2)}) collective-permute-start(f32[2,2,4,192]{3,2,1,0:T(4,128)S(1)} %pad_maximum_fusion.11), channel_id=1, source_target_pairs={{0,4},{4,0},{8,12},{12,8},{1,5},{5,1},{9,13},{13,9},{2,6},{6,2},{1... | collective-permute-start | bytes 36872 | tf_op jit(solution)/shard_map/ppermute | solution.py:248
  20.5 16.0 %all-to-all-start = ((bf16[4,197,192]{1,2,0:T(8,128)(2,1)}), bf16[4,197,192]{1,2,0:T(8,128)(2,1)S(1)}, u32[]{:S(2)}, u32[]{:S(2)}) async-start(bf16[4,197,192]{1,2,0:T(8,128)(2,1)} %broadcast_in_dim.74), calls=%async_computation | async-start | bytes 786432 | tf_op jit(solution)/shard_map/all_to_all | solution.py:285
  41.9 9.3 %collective-permute-start.6 = (bf16[56,768]{1,0:T(8,128)(2,1)S(1)}, bf16[56,768]{1,0:T(8,128)(2,1)S(1)}, u32[]{:S(2)}, u32[]{:S(2)}) collective-permute-start(bf16[56,768]{1,0:T(8,128)(2,1)S(1)} %get-tuple-element.134), channel_id=1, source_target_pairs={{0,2},{1,3},{2,0},{3,1},{4,6},{5,7},{6,4},{7,5},{8,10},{9,11},{10,... | collective-permute-start | bytes 258056 | tf_op jit(solution)/shard_map/ppermute | solution.py:248
  43.9 7.3 %collective-permute-start.7 = (bf16[56,768]{1,0:T(8,128)(2,1)S(1)}, bf16[56,768]{1,0:T(8,128)(2,1)S(1)}, u32[]{:S(2)}, u32[]{:S(2)}) collective-permute-start(bf16[56,768]{1,0:T(8,128)(2,1)S(1)} %get-tuple-element.135), channel_id=1, source_target_pairs={{0,3},{1,2},{2,1},{3,0},{4,7},{5,6},{6,5},{7,4},{8,11},{9,10},{10,... | collective-permute-start | bytes 258056 | tf_op jit(solution)/shard_map/ppermute | solution.py:248
  51.4 15.3 %collective-permute-start.31 = (bf16[1,192,1536]{2,1,0:T(8,128)(2,1)S(1)}, bf16[1,192,1536]{2,1,0:T(8,128)(2,1)S(1)}, u32[]{:S(2)}, u32[]{:S(2)}) collective-permute-start(bf16[1,192,1536]{2,1,0:T(8,128)(2,1)S(1)} %bitcast.241), channel_id=1, source_target_pairs={{0,8},{4,12},{8,0},{12,4},{1,9},{5,13},{9,1},{13,5},{2,10},{6,14},... | collective-permute-start | bytes 1769480 | tf_op jit(solution)/shard_map/ppermute | solution.py:248
  53.3 21.4 %collective-permute-start.12 = (bf16[2,192,1536]{2,1,0:T(8,128)(2,1)S(1)}, bf16[2,192,1536]{2,1,0:T(8,128)(2,1)S(1)}, u32[]{:S(2)}, u32[]{:S(2)}) collective-permute-start(bf16[2,192,1536]{2,1,0:T(8,128)(2,1)S(1)} %pad_maximum_fusion.4), channel_id=1, source_target_pairs={{0,4},{4,0},{8,12},{12,8},{1,5},{5,1},{9,13},{13,9},{2,6},{6,2},{1... | collective-permute-start | bytes 3538952 | tf_op jit(solution)/shard_map/ppermute | solution.py:248
  55.0 24.3 %collective-permute-start.10 = (bf16[56,768]{1,0:T(8,128)(2,1)S(1)}, bf16[56,768]{1,0:T(8,128)(2,1)S(1)}, u32[]{:S(2)}, u32[]{:S(2)}) collective-permute-start(bf16[56,768]{1,0:T(8,128)(2,1)S(1)} %get-tuple-element.138.refs_0_), channel_id=1, source_target_pairs={{0,3},{1,2},{2,1},{3,0},{4,7},{5,6},{6,5},{7,4},{8,11},{9,10},{10,... | collective-permute-start | bytes 258056 | tf_op jit(solution)/shard_map/ppermute | solution.py:248
  56.8 22.6 %collective-permute-start.8 = (bf16[56,768]{1,0:T(8,128)(2,1)S(1)}, bf16[56,768]{1,0:T(8,128)(2,1)S(1)}, u32[]{:S(2)}, u32[]{:S(2)}) collective-permute-start(bf16[56,768]{1,0:T(8,128)(2,1)S(1)} %get-tuple-element.138.refs_0_), channel_id=1, source_target_pairs={{0,1},{1,0},{2,3},{3,2},{4,5},{5,4},{6,7},{7,6},{8,9},{9,8},{10,11... | collective-permute-start | bytes 258056 | tf_op jit(solution)/shard_map/ppermute | solution.py:248
  57.3 12.5 %collective-permute-start.19 = (bf16[1,192,768]{2,1,0:T(8,128)(2,1)S(1)}, bf16[1,192,768]{2,1,0:T(8,128)(2,1)S(1)}, u32[]{:S(2)}, u32[]{:S(2)}) collective-permute-start(bf16[1,192,768]{2,1,0:T(8,128)(2,1)S(1)} %bitcast.243), channel_id=1, source_target_pairs={{0,8},{4,12},{8,0},{12,4},{1,9},{5,13},{9,1},{13,5},{2,10},{6,14},... | collective-permute-start | bytes 884744 | tf_op jit(solution)/shard_map/ppermute | solution.py:248
  66.8 7.9 %collective-permute-start.32 = (bf16[2,192,1536]{2,1,0:T(8,128)(2,1)S(1)}, bf16[2,192,1536]{2,1,0:T(8,128)(2,1)S(1)}, u32[]{:S(2)}, u32[]{:S(2)}) collective-permute-start(bf16[2,192,1536]{2,1,0:T(8,128)(2,1)S(1)} %pad_maximum_fusion.5), channel_id=1, source_target_pairs={{0,4},{4,0},{8,12},{12,8},{1,5},{5,1},{9,13},{13,9},{2,6},{6,2},{1... | collective-permute-start | bytes 3538952 | tf_op jit(solution)/shard_map/ppermute | solution.py:248
  72.0 7.3 %collective-permute-start.9 = (bf16[56,768]{1,0:T(8,128)(2,1)S(1)}, bf16[56,768]{1,0:T(8,128)(2,1)S(1)}, u32[]{:S(2)}, u32[]{:S(2)}) collective-permute-start(bf16[56,768]{1,0:T(8,128)(2,1)S(1)} %get-tuple-element.138.refs_0_), channel_id=1, source_target_pairs={{0,2},{1,3},{2,0},{3,1},{4,6},{5,7},{6,4},{7,5},{8,10},{9,11},{10,... | collective-permute-start | bytes 258056 | tf_op jit(solution)/shard_map/ppermute | solution.py:248
  80.4 6.4 %collective-permute-start.13 = (bf16[56,768]{1,0:T(8,128)(2,1)S(1)}, bf16[56,768]{1,0:T(8,128)(2,1)S(1)}, u32[]{:S(2)}, u32[]{:S(2)}) collective-permute-start(bf16[56,768]{1,0:T(8,128)(2,1)S(1)} %get-tuple-element.140), channel_id=1, source_target_pairs={{0,1},{1,0},{2,3},{3,2},{4,5},{5,4},{6,7},{7,6},{8,9},{9,8},{10,11... | collective-permute-start | bytes 258056 | tf_op jit(solution)/shard_map/ppermute | solution.py:248
  81.7 9.0 %collective-permute-start.14 = (bf16[56,768]{1,0:T(8,128)(2,1)S(1)}, bf16[56,768]{1,0:T(8,128)(2,1)S(1)}, u32[]{:S(2)}, u32[]{:S(2)}) collective-permute-start(bf16[56,768]{1,0:T(8,128)(2,1)S(1)} %get-tuple-element.141), channel_id=1, source_target_pairs={{0,2},{1,3},{2,0},{3,1},{4,6},{5,7},{6,4},{7,5},{8,10},{9,11},{10,... | collective-permute-start | bytes 258056 | tf_op jit(solution)/shard_map/ppermute | solution.py:248
  83.9 6.8 %collective-permute-start.15 = (bf16[56,768]{1,0:T(8,128)(2,1)S(1)}, bf16[56,768]{1,0:T(8,128)(2,1)S(1)}, u32[]{:S(2)}, u32[]{:S(2)}) collective-permute-start(bf16[56,768]{1,0:T(8,128)(2,1)S(1)} %get-tuple-element.142), channel_id=1, source_target_pairs={{0,3},{1,2},{2,1},{3,0},{4,7},{5,6},{6,5},{7,4},{8,11},{9,10},{10,... | collective-permute-start | bytes 258056 | tf_op jit(solution)/shard_map/ppermute | solution.py:248
  101.5 18.5 %all-to-all-start.1 = ((f32[4,56,192]{2,1,0:T(8,128)}), f32[4,56,192]{2,1,0:T(8,128)}, u32[]{:S(2)}, u32[]{:S(2)}) async-start(f32[4,56,192]{2,1,0:T(8,128)} %bitcast.250), calls=%async_computation.1 | async-start | bytes 458752 | tf_op jit(solution)/shard_map/all_to_all | solution.py:560
  120.0 51.2 %all-to-all-start.2 = ((f32[4,192,768]{2,1,0:T(8,128)}), f32[4,192,768]{2,1,0:T(8,128)}, u32[]{:S(2)}, u32[]{:S(2)}) async-start(f32[4,192,768]{2,1,0:T(8,128)} %pad_maximum_fusion), calls=%async_computation.2 | async-start | bytes 4718592 | tf_op jit(solution)/shard_map/all_to_all | solution.py:595
  125.6 6.3 %collective-permute-start.16 = (bf16[56,768]{1,0:T(8,128)(2,1)}, bf16[56,768]{1,0:T(8,128)(2,1)S(1)}, u32[]{:S(2)}, u32[]{:S(2)}) collective-permute-start(bf16[56,768]{1,0:T(8,128)(2,1)} %get-tuple-element.145), channel_id=1, source_target_pairs={{0,1},{1,0},{2,3},{3,2},{4,5},{5,4},{6,7},{7,6},{8,9},{9,8},{10,11... | collective-permute-start | bytes 258056 | tf_op jit(solution)/shard_map/ppermute | solution.py:248
  126.2 10.2 %collective-permute-start.17 = (bf16[56,768]{1,0:T(8,128)(2,1)}, bf16[56,768]{1,0:T(8,128)(2,1)S(1)}, u32[]{:S(2)}, u32[]{:S(2)}) collective-permute-start(bf16[56,768]{1,0:T(8,128)(2,1)} %get-tuple-element.145), channel_id=1, source_target_pairs={{0,2},{1,3},{2,0},{3,1},{4,6},{5,7},{6,4},{7,5},{8,10},{9,11},{10,... | collective-permute-start | bytes 258056 | tf_op jit(solution)/shard_map/ppermute | solution.py:248
  127.4 9.0 %collective-permute-start.18 = (bf16[56,768]{1,0:T(8,128)(2,1)}, bf16[56,768]{1,0:T(8,128)(2,1)S(1)}, u32[]{:S(2)}, u32[]{:S(2)}) collective-permute-start(bf16[56,768]{1,0:T(8,128)(2,1)} %get-tuple-element.145), channel_id=1, source_target_pairs={{0,3},{1,2},{2,1},{3,0},{4,7},{5,6},{6,5},{7,4},{8,11},{9,10},{10,... | collective-permute-start | bytes 258056 | tf_op jit(solution)/shard_map/ppermute | solution.py:248
  139.5 11.4 %collective-permute-start.21 = (bf16[56,768]{1,0:T(8,128)(2,1)}, bf16[56,768]{1,0:T(8,128)(2,1)}, u32[]{:S(2)}, u32[]{:S(2)}) collective-permute-start(bf16[56,768]{1,0:T(8,128)(2,1)} %get-tuple-element.308), channel_id=1, source_target_pairs={{0,1},{1,0},{2,3},{3,2},{4,5},{5,4},{6,7},{7,6},{8,9},{9,8},{10,11... | collective-permute-start | bytes 258056 | tf_op jit(solution)/shard_map/ppermute | solution.py:248
  141.2 14.0 %collective-permute-start.22 = (bf16[56,768]{1,0:T(8,128)(2,1)}, bf16[56,768]{1,0:T(8,128)(2,1)}, u32[]{:S(2)}, u32[]{:S(2)}) collective-permute-start(bf16[56,768]{1,0:T(8,128)(2,1)} %get-tuple-element.310), channel_id=1, source_target_pairs={{0,2},{1,3},{2,0},{3,1},{4,6},{5,7},{6,4},{7,5},{8,10},{9,11},{10,... | collective-permute-start | bytes 258056 | tf_op jit(solution)/shard_map/ppermute | solution.py:248
  141.2 14.0 %collective-permute-start.23 = (bf16[56,768]{1,0:T(8,128)(2,1)}, bf16[56,768]{1,0:T(8,128)(2,1)}, u32[]{:S(2)}, u32[]{:S(2)}) collective-permute-start(bf16[56,768]{1,0:T(8,128)(2,1)} %get-tuple-element.312), channel_id=1, source_target_pairs={{0,3},{1,2},{2,1},{3,0},{4,7},{5,6},{6,5},{7,4},{8,11},{9,10},{10,... | collective-permute-start | bytes 258056 | tf_op jit(solution)/shard_map/ppermute | solution.py:248
  149.1 9.9 %collective-permute-start.25 = (bf16[56,768]{1,0:T(8,128)(2,1)S(1)}, bf16[56,768]{1,0:T(8,128)(2,1)S(1)}, u32[]{:S(2)}, u32[]{:S(2)}) collective-permute-start(bf16[56,768]{1,0:T(8,128)(2,1)S(1)} %convert_element_type.118.refs_0_), channel_id=1, source_target_pairs={{0,1},{1,0},{2,3},{3,2},{4,5},{5,4},{6,7},{7,6},{8,9},{9,8},{10,11... | collective-permute-start | bytes 258056 | tf_op jit(solution)/shard_map/ppermute | solution.py:248
  149.9 9.0 %collective-permute-start.26 = (bf16[56,768]{1,0:T(8,128)(2,1)S(1)}, bf16[56,768]{1,0:T(8,128)(2,1)S(1)}, u32[]{:S(2)}, u32[]{:S(2)}) collective-permute-start(bf16[56,768]{1,0:T(8,128)(2,1)S(1)} %convert_element_type.118.refs_0_), channel_id=1, source_target_pairs={{0,2},{1,3},{2,0},{3,1},{4,6},{5,7},{6,4},{7,5},{8,10},{9,11},{10,... | collective-permute-start | bytes 258056 | tf_op jit(solution)/shard_map/ppermute | solution.py:248
  150.9 8.1 %collective-permute-start.27 = (bf16[56,768]{1,0:T(8,128)(2,1)S(1)}, bf16[56,768]{1,0:T(8,128)(2,1)S(1)}, u32[]{:S(2)}, u32[]{:S(2)}) collective-permute-start(bf16[56,768]{1,0:T(8,128)(2,1)S(1)} %convert_element_type.118.refs_0_), channel_id=1, source_target_pairs={{0,3},{1,2},{2,1},{3,0},{4,7},{5,6},{6,5},{7,4},{8,11},{9,10},{10,... | collective-permute-start | bytes 258056 | tf_op jit(solution)/shard_map/ppermute | solution.py:248
  159.8 7.9 %collective-permute-start.29 = (bf16[56,768]{1,0:T(8,128)(2,1)S(1)}, bf16[56,768]{1,0:T(8,128)(2,1)S(1)}, u32[]{:S(2)}, u32[]{:S(2)}) collective-permute-start(bf16[56,768]{1,0:T(8,128)(2,1)S(1)} %get-tuple-element.164), channel_id=1, source_target_pairs={{0,2},{1,3},{2,0},{3,1},{4,6},{5,7},{6,4},{7,5},{8,10},{9,11},{10,... | collective-permute-start | bytes 258056 | tf_op jit(solution)/shard_map/ppermute | solution.py:248
  160.8 6.9 %collective-permute-start.30 = (bf16[56,768]{1,0:T(8,128)(2,1)S(1)}, bf16[56,768]{1,0:T(8,128)(2,1)S(1)}, u32[]{:S(2)}, u32[]{:S(2)}) collective-permute-start(bf16[56,768]{1,0:T(8,128)(2,1)S(1)} %get-tuple-element.164), channel_id=1, source_target_pairs={{0,3},{1,2},{2,1},{3,0},{4,7},{5,6},{6,5},{7,4},{8,11},{9,10},{10,... | collective-permute-start | bytes 258056 | tf_op jit(solution)/shard_map/ppermute | solution.py:248
  171.2 69.5 %all-to-all-start.3 = ((bf16[8,208,768]{2,1,0:T(8,128)(2,1)}), bf16[8,208,768]{2,1,0:T(8,128)(2,1)}, u32[]{:S(2)}, u32[]{:S(2)}) async-start(bf16[8,208,768]{2,1,0:T(8,128)(2,1)} %bitcast_dynamic-update-slice_fusion.8), calls=%async_computation.3 | async-start | bytes 5111808 | tf_op jit(solution)/shard_map/all_to_all | solution.py:583
  184.3 9.6 %collective-permute-start.34 = (bf16[56,768]{1,0:T(8,128)(2,1)S(1)}, bf16[56,768]{1,0:T(8,128)(2,1)S(1)}, u32[]{:S(2)}, u32[]{:S(2)}) collective-permute-start(bf16[56,768]{1,0:T(8,128)(2,1)S(1)} %get-tuple-element.169), channel_id=1, source_target_pairs={{0,2},{1,3},{2,0},{3,1},{4,6},{5,7},{6,4},{7,5},{8,10},{9,11},{10,... | collective-permute-start | bytes 258056 | tf_op jit(solution)/shard_map/ppermute | solution.py:248
  185.5 8.3 %collective-permute-start.35 = (bf16[56,768]{1,0:T(8,128)(2,1)S(1)}, bf16[56,768]{1,0:T(8,128)(2,1)S(1)}, u32[]{:S(2)}, u32[]{:S(2)}) collective-permute-start(bf16[56,768]{1,0:T(8,128)(2,1)S(1)} %get-tuple-element.170), channel_id=1, source_target_pairs={{0,3},{1,2},{2,1},{3,0},{4,7},{5,6},{6,5},{7,4},{8,11},{9,10},{10,... | collective-permute-start | bytes 258056 | tf_op jit(solution)/shard_map/ppermute | solution.py:248
  196.1 9.0 %collective-permute-start.37 = (bf16[56,768]{1,0:T(8,128)(2,1)S(1)}, bf16[56,768]{1,0:T(8,128)(2,1)S(1)}, u32[]{:S(2)}, u32[]{:S(2)}) collective-permute-start(bf16[56,768]{1,0:T(8,128)(2,1)S(1)} %get-tuple-element.172.refs_0_), channel_id=1, source_target_pairs={{0,2},{1,3},{2,0},{3,1},{4,6},{5,7},{6,4},{7,5},{8,10},{9,11},{10,... | collective-permute-start | bytes 258056 | tf_op jit(solution)/shard_map/ppermute | solution.py:248
  196.5 8.6 %collective-permute-start.38 = (bf16[56,768]{1,0:T(8,128)(2,1)S(1)}, bf16[56,768]{1,0:T(8,128)(2,1)S(1)}, u32[]{:S(2)}, u32[]{:S(2)}) collective-permute-start(bf16[56,768]{1,0:T(8,128)(2,1)S(1)} %get-tuple-element.172.refs_0_), channel_id=1, source_target_pairs={{0,3},{1,2},{2,1},{3,0},{4,7},{5,6},{6,5},{7,4},{8,11},{9,10},{10,... | collective-permute-start | bytes 258056 | tf_op jit(solution)/shard_map/ppermute | solution.py:248
  209.3 8.8 %collective-permute-start.40 = (bf16[56,768]{1,0:T(8,128)(2,1)S(1)}, bf16[56,768]{1,0:T(8,128)(2,1)S(1)}, u32[]{:S(2)}, u32[]{:S(2)}) collective-permute-start(bf16[56,768]{1,0:T(8,128)(2,1)S(1)} %get-tuple-element.176), channel_id=1, source_target_pairs={{0,2},{1,3},{2,0},{3,1},{4,6},{5,7},{6,4},{7,5},{8,10},{9,11},{10,... | collective-permute-start | bytes 258056 | tf_op jit(solution)/shard_map/ppermute | solution.py:248
  209.9 8.2 %collective-permute-start.41 = (bf16[56,768]{1,0:T(8,128)(2,1)S(1)}, bf16[56,768]{1,0:T(8,128)(2,1)S(1)}, u32[]{:S(2)}, u32[]{:S(2)}) collective-permute-start(bf16[56,768]{1,0:T(8,128)(2,1)S(1)} %get-tuple-element.177), channel_id=1, source_target_pairs={{0,3},{1,2},{2,1},{3,0},{4,7},{5,6},{6,5},{7,4},{8,11},{9,10},{10,... | collective-permute-start | bytes 258056 | tf_op jit(solution)/shard_map/ppermute | solution.py:248
  220.0 8.7 %collective-permute-start.43 = (bf16[56,768]{1,0:T(8,128)(2,1)S(1)}, bf16[56,768]{1,0:T(8,128)(2,1)S(1)}, u32[]{:S(2)}, u32[]{:S(2)}) collective-permute-start(bf16[56,768]{1,0:T(8,128)(2,1)S(1)} %get-tuple-element.179.refs_0_), channel_id=1, source_target_pairs={{0,2},{1,3},{2,0},{3,1},{4,6},{5,7},{6,4},{7,5},{8,10},{9,11},{10,... | collective-permute-start | bytes 258056 | tf_op jit(solution)/shard_map/ppermute | solution.py:248
  220.4 8.2 %collective-permute-start.44 = (bf16[56,768]{1,0:T(8,128)(2,1)S(1)}, bf16[56,768]{1,0:T(8,128)(2,1)S(1)}, u32[]{:S(2)}, u32[]{:S(2)}) collective-permute-start(bf16[56,768]{1,0:T(8,128)(2,1)S(1)} %get-tuple-element.179.refs_0_), channel_id=1, source_target_pairs={{0,3},{1,2},{2,1},{3,0},{4,7},{5,6},{6,5},{7,4},{8,11},{9,10},{10,... | collective-permute-start | bytes 258056 | tf_op jit(solution)/shard_map/ppermute | solution.py:248
  231.9 8.6 %collective-permute-start.46 = (bf16[56,768]{1,0:T(8,128)(2,1)S(1)}, bf16[56,768]{1,0:T(8,128)(2,1)S(1)}, u32[]{:S(2)}, u32[]{:S(2)}) collective-permute-start(bf16[56,768]{1,0:T(8,128)(2,1)S(1)} %get-tuple-element.183), channel_id=1, source_target_pairs={{0,2},{1,3},{2,0},{3,1},{4,6},{5,7},{6,4},{7,5},{8,10},{9,11},{10,... | collective-permute-start | bytes 258056 | tf_op jit(solution)/shard_map/ppermute | solution.py:248
  232.3 8.1 %collective-permute-start.47 = (bf16[56,768]{1,0:T(8,128)(2,1)S(1)}, bf16[56,768]{1,0:T(8,128)(2,1)S(1)}, u32[]{:S(2)}, u32[]{:S(2)}) collective-permute-start(bf16[56,768]{1,0:T(8,128)(2,1)S(1)} %get-tuple-element.184), channel_id=1, source_target_pairs={{0,3},{1,2},{2,1},{3,0},{4,7},{5,6},{6,5},{7,4},{8,11},{9,10},{10,... | collective-permute-start | bytes 258056 | tf_op jit(solution)/shard_map/ppermute | solution.py:248
  242.3 8.6 %collective-permute-start.49 = (bf16[56,768]{1,0:T(8,128)(2,1)S(1)}, bf16[56,768]{1,0:T(8,128)(2,1)S(1)}, u32[]{:S(2)}, u32[]{:S(2)}) collective-permute-start(bf16[56,768]{1,0:T(8,128)(2,1)S(1)} %get-tuple-element.195.refs_0_), channel_id=1, source_target_pairs={{0,2},{1,3},{2,0},{3,1},{4,6},{5,7},{6,4},{7,5},{8,10},{9,11},{10,... | collective-permute-start | bytes 258056 | tf_op jit(solution)/shard_map/ppermute | solution.py:248
  242.8 8.1 %collective-permute-start.50 = (bf16[56,768]{1,0:T(8,128)(2,1)S(1)}, bf16[56,768]{1,0:T(8,128)(2,1)S(1)}, u32[]{:S(2)}, u32[]{:S(2)}) collective-permute-start(bf16[56,768]{1,0:T(8,128)(2,1)S(1)} %get-tuple-element.195.refs_0_), channel_id=1, source_target_pairs={{0,3},{1,2},{2,1},{3,0},{4,7},{5,6},{6,5},{7,4},{8,11},{9,10},{10,... | collective-permute-start | bytes 258056 | tf_op jit(solution)/shard_map/ppermute | solution.py:248
  260.4 35.4 %all-to-all-start.4 = ((bf16[8,208,768]{2,1,0:T(8,128)(2,1)}), bf16[8,208,768]{2,1,0:T(8,128)(2,1)}, u32[]{:S(2)}, u32[]{:S(2)}) async-start(bf16[8,208,768]{2,1,0:T(8,128)(2,1)} %bitcast_dynamic-update-slice_fusion), calls=%async_computation.4 | async-start | bytes 5111808 | tf_op jit(solution)/shard_map/all_to_all | solution.py:583
  266.8 9.6 %collective-permute-start.52 = (bf16[56,768]{1,0:T(8,128)(2,1)S(1)}, bf16[56,768]{1,0:T(8,128)(2,1)S(1)}, u32[]{:S(2)}, u32[]{:S(2)}) collective-permute-start(bf16[56,768]{1,0:T(8,128)(2,1)S(1)} %get-tuple-element.207), channel_id=1, source_target_pairs={{0,2},{1,3},{2,0},{3,1},{4,6},{5,7},{6,4},{7,5},{8,10},{9,11},{10,... | collective-permute-start | bytes 258056 | tf_op jit(solution)/shard_map/ppermute | solution.py:248
  267.3 9.1 %collective-permute-start.53 = (bf16[56,768]{1,0:T(8,128)(2,1)S(1)}, bf16[56,768]{1,0:T(8,128)(2,1)S(1)}, u32[]{:S(2)}, u32[]{:S(2)}) collective-permute-start(bf16[56,768]{1,0:T(8,128)(2,1)S(1)} %get-tuple-element.208), channel_id=1, source_target_pairs={{0,3},{1,2},{2,1},{3,0},{4,7},{5,6},{6,5},{7,4},{8,11},{9,10},{10,... | collective-permute-start | bytes 258056 | tf_op jit(solution)/shard_map/ppermute | solution.py:248
  277.3 6.4 %collective-permute-start.54 = (f32[2,4,768]{2,1,0:T(4,128)S(1)}, f32[2,4,768]{2,1,0:T(4,128)S(1)}, u32[]{:S(2)}, u32[]{:S(2)}) collective-permute-start(f32[2,4,768]{2,1,0:T(4,128)S(1)} %pad_maximum_fusion.10), channel_id=1, source_target_pairs={{0,1},{1,0},{2,3},{3,2},{4,5},{5,4},{6,7},{7,6},{8,9},{9,8},{10,11... | collective-permute-start | bytes 73736 | tf_op jit(solution)/shard_map/ppermute | solution.py:248
  279.5 10.1 %collective-permute-start.57 = (bf16[56,768]{1,0:T(8,128)(2,1)S(1)}, bf16[56,768]{1,0:T(8,128)(2,1)S(1)}, u32[]{:S(2)}, u32[]{:S(2)}) collective-permute-start(bf16[56,768]{1,0:T(8,128)(2,1)S(1)} %copy-done.81), channel_id=1, source_target_pairs={{0,2},{1,3},{2,0},{3,1},{4,6},{5,7},{6,4},{7,5},{8,10},{9,11},{10,... | collective-permute-start | bytes 258056 | tf_op jit(solution)/shard_map/ppermute | solution.py:248
  281.3 8.3 %collective-permute-start.58 = (bf16[56,768]{1,0:T(8,128)(2,1)S(1)}, bf16[56,768]{1,0:T(8,128)(2,1)S(1)}, u32[]{:S(2)}, u32[]{:S(2)}) collective-permute-start(bf16[56,768]{1,0:T(8,128)(2,1)S(1)} %copy-done.80), channel_id=1, source_target_pairs={{0,3},{1,2},{2,1},{3,0},{4,7},{5,6},{6,5},{7,4},{8,11},{9,10},{10,... | collective-permute-start | bytes 258056 | tf_op jit(solution)/shard_map/ppermute | solution.py:248
  283.8 7.0 %collective-permute-start.55 = (f32[2,4,768]{2,1,0:T(4,128)S(1)}, f32[2,4,768]{2,1,0:T(4,128)S(1)}, u32[]{:S(2)}, u32[]{:S(2)}) collective-permute-start(f32[2,4,768]{2,1,0:T(4,128)S(1)} %fusion.17), channel_id=1, source_target_pairs={{0,2},{1,3},{2,0},{3,1},{4,6},{5,7},{6,4},{7,5},{8,10},{9,11},{10,... | collective-permute-start | bytes 73736 | tf_op jit(solution)/shard_map/ppermute | solution.py:248
  306.5 58.9 %all-to-all-start.5 = ((f32[4,64,1536]{2,1,0:T(8,128)}), f32[4,64,1536]{2,1,0:T(8,128)}, u32[]{:S(2)}, u32[]{:S(2)}) async-start(f32[4,64,1536]{2,1,0:T(8,128)} %bitcast.236), calls=%async_computation.5 | async-start | bytes 3145728 | tf_op jit(solution)/shard_map/all_to_all | solution.py:311
  311.2 27.4 %collective-permute-start.62 = (f32[56,192]{1,0:T(8,128)S(1)}, f32[56,192]{1,0:T(8,128)S(1)}, u32[]{:S(2)}, u32[]{:S(2)}) collective-permute-start(f32[56,192]{1,0:T(8,128)S(1)} %bitcast.264), channel_id=1, source_target_pairs={{0,1},{1,0},{2,3},{3,2},{4,5},{5,4},{6,7},{7,6},{8,9},{9,8},{10,11... | collective-permute-start | bytes 129032 | tf_op jit(solution)/shard_map/ppermute | solution.py:248
  313.3 38.9 %collective-permute-start.63 = (f32[56,192]{1,0:T(8,128)S(1)}, f32[56,192]{1,0:T(8,128)S(1)}, u32[]{:S(2)}, u32[]{:S(2)}) collective-permute-start(f32[56,192]{1,0:T(8,128)S(1)} %bitcast.263), channel_id=1, source_target_pairs={{0,2},{1,3},{2,0},{3,1},{4,6},{5,7},{6,4},{7,5},{8,10},{9,11},{10,... | collective-permute-start | bytes 129032 | tf_op jit(solution)/shard_map/ppermute | solution.py:248
  315.6 36.5 %collective-permute-start.64 = (f32[56,192]{1,0:T(8,128)S(1)}, f32[56,192]{1,0:T(8,128)S(1)}, u32[]{:S(2)}, u32[]{:S(2)}) collective-permute-start(f32[56,192]{1,0:T(8,128)S(1)} %bitcast.261), channel_id=1, source_target_pairs={{0,3},{1,2},{2,1},{3,0},{4,7},{5,6},{6,5},{7,4},{8,11},{9,10},{10,... | collective-permute-start | bytes 129032 | tf_op jit(solution)/shard_map/ppermute | solution.py:248
  352.9 14.1 %collective-permute-start.65 = (f32[197,192]{1,0:T(8,128)}, f32[197,192]{1,0:T(8,128)S(1)}, u32[]{:S(2)}, u32[]{:S(2)}) collective-permute-start(f32[197,192]{1,0:T(8,128)} %slice.298), channel_id=1, source_target_pairs={{0,0},{1,4},{2,8},{3,12},{4,1},{5,5},{6,9},{7,13},{8,2},{9,6},{10,... | collective-permute-start | bytes 453896 | tf_op jit(solution)/shard_map/ppermute | solution.py:242
  368.3 51.8 %all-to-all-start.6 = ((f32[4,64,1536]{2,1,0:T(8,128)}), f32[4,64,1536]{2,1,0:T(8,128)}, u32[]{:S(2)}, u32[]{:S(2)}) async-start(f32[4,64,1536]{2,1,0:T(8,128)} %broadcast_in_dim.84), calls=%async_computation.6 | async-start | bytes 3145728 | tf_op jit(solution)/shard_map/all_to_all | solution.py:285
  376.2 22.9 %collective-permute-start.66 = (f32[56,192]{1,0:T(8,128)S(1)}, f32[56,192]{1,0:T(8,128)S(1)}, u32[]{:S(2)}, u32[]{:S(2)}) collective-permute-start(f32[56,192]{1,0:T(8,128)S(1)} %bitcast.262), channel_id=1, source_target_pairs={{0,1},{1,0},{2,3},{3,2},{4,5},{5,4},{6,7},{7,6},{8,9},{9,8},{10,11... | collective-permute-start | bytes 129032 | tf_op jit(solution)/shard_map/ppermute | solution.py:248
  378.3 34.6 %collective-permute-start.67 = (f32[56,192]{1,0:T(8,128)S(1)}, f32[56,192]{1,0:T(8,128)S(1)}, u32[]{:S(2)}, u32[]{:S(2)}) collective-permute-start(f32[56,192]{1,0:T(8,128)S(1)} %bitcast.260), channel_id=1, source_target_pairs={{0,2},{1,3},{2,0},{3,1},{4,6},{5,7},{6,4},{7,5},{8,10},{9,11},{10,... | collective-permute-start | bytes 129032 | tf_op jit(solution)/shard_map/ppermute | solution.py:248
  380.6 32.2 %collective-permute-start.68 = (f32[56,192]{1,0:T(8,128)S(1)}, f32[56,192]{1,0:T(8,128)S(1)}, u32[]{:S(2)}, u32[]{:S(2)}) collective-permute-start(f32[56,192]{1,0:T(8,128)S(1)} %bitcast.259), channel_id=1, source_target_pairs={{0,3},{1,2},{2,1},{3,0},{4,7},{5,6},{6,5},{7,4},{8,11},{9,10},{10,... | collective-permute-start | bytes 129032 | tf_op jit(solution)/shard_map/ppermute | solution.py:248
  413.6 6.5 %collective-permute-start.69 = (f32[197,192]{1,0:T(8,128)}, f32[197,192]{1,0:T(8,128)}, u32[]{:S(2)}, u32[]{:S(2)}) collective-permute-start(f32[197,192]{1,0:T(8,128)} %slice.299), channel_id=1, source_target_pairs={{0,0},{1,4},{2,8},{3,12},{4,1},{5,5},{6,9},{7,13},{8,2},{9,6},{10,... | collective-permute-start | bytes 453896 | tf_op jit(solution)/shard_map/ppermute | solution.py:242
  421.8 58.1 %all-to-all-start.7 = ((bf16[8,192,768]{2,1,0:T(8,128)(2,1)}), bf16[8,192,768]{2,1,0:T(8,128)(2,1)}, u32[]{:S(2)}, u32[]{:S(2)}) async-start(bf16[8,192,768]{2,1,0:T(8,128)(2,1)} %pad_maximum_fusion.1), calls=%async_computation.7 | async-start | bytes 4718592 | tf_op jit(solution)/shard_map/all_to_all | solution.py:649
  484.6 32.8 %all-to-all-start.8 = ((bf16[8,192,768]{2,1,0:T(8,128)(2,1)}), bf16[8,192,768]{2,1,0:T(8,128)(2,1)S(1)}, u32[]{:S(2)}, u32[]{:S(2)}) async-start(bf16[8,192,768]{2,1,0:T(8,128)(2,1)} %pad_maximum_fusion.2), calls=%async_computation.8 | async-start | bytes 4718592 | tf_op jit(solution)/shard_map/all_to_all | solution.py:649
  (101 other events, 1114.4 us)

commit v6 on v5

--- a/solution.py
+++ b/solution.py
@@ -175,26 +175,31 @@
 
 
 def norm_back_kernel(level_index, first_row, size, *refs):
-    parts, (stream_ref, upstream_ref, norms) = refs[:size], refs[size : size + 3]
-    upstream_out, low_out, sums_out = refs[size + 3 :]
+    parts, (stream_ref, change_ref, base_ref, norms) = refs[:size], refs[size : size + 4]
+    change_out, low_out, sums_out = refs[size + 4 :]
     grad = parts[0][...].astype(jnp.float32)
     for part in parts[1:]:
         grad = grad + part[...].astype(jnp.float32)
     plain, inverse = norm_parts_of(stream_ref[...])
     gain = norms[level_index, first_row : first_row + 1, :]
-    upstream = upstream_ref[...] + norm_backward(grad, plain, inverse, gain)
-    upstream_out[...] = upstream
-    low_out[...] = upstream.astype(jnp.bfloat16)
+    change = change_ref[...] + norm_backward(grad, plain, inverse, gain)
+    change_out[...] = change
+    low_out[...] = (base_ref[...].astype(jnp.float32) + change).astype(jnp.bfloat16)
     sums_out[0:1, :] = jnp.sum(grad * plain, axis=0, keepdims=True)
     sums_out[1:2, :] = jnp.sum(grad, axis=0, keepdims=True)
 
 
 def first_kernel(tokens, position, blocks, norms, *refs):
-    outs, stream_out, whole = refs[:-2], refs[-2], refs[-1]
+    count = (len(refs) - 2) // 2
+    outs, back_outs, stream_out, whole = refs[:count], refs[count:-2], refs[-2], refs[-1]
     size, _, width = blocks.shape
+    width = width // 2
     whole[...] = jnp.zeros_like(whole)
     for i in range(size):
-        whole[0:tokens, i * width : (i + 1) * width] = blocks[i].astype(jnp.float32)
+        whole[0:tokens, i * width : (i + 1) * width] = blocks[i, :, width:].astype(jnp.float32)
+    take_chunks(position, whole, back_outs)
+    for i in range(size):
+        whole[0:tokens, i * width : (i + 1) * width] = blocks[i, :, :width].astype(jnp.float32)
     chunk = stream_out.shape[0]
     start = pl.multiple_of(position[0] * chunk, 8)
     stream_out[...] = whole[pl.ds(start, chunk), :]
@@ -259,13 +264,14 @@
     return result
 
 
-def gather_by_pairs(values, axis):
+def gather_by_pairs(values, axis, first=None):
     step = lax.axis_size(axis) // 2
     me = lax.axis_index(axis)
     blocks, places = [values], [me]
     while step:
         sent = blocks[0][None] if len(blocks) == 1 else jnp.stack(blocks)
-        received = from_partner(sent, step, (axis,))
+        received = from_partner(sent, step, (axis,)) if first is None else first
+        first = None
         blocks = blocks + [received[i] for i in range(len(blocks))]
         places = places + [p ^ step for p in places]
         step //= 2
@@ -406,6 +412,21 @@
         whole + pairs,
         2 * 3 * 14 * height * height * width,
     )[0]
+
+
+def finish_kernel(levels, flipped, rates, blocks, *refs):
+    olds, outs = refs[: len(flipped)], refs[len(flipped) :]
+    for kind_index, turned in enumerate(flipped):
+        old, new = olds[kind_index], outs[kind_index]
+        width = old.shape[1] if turned else old.shape[2]
+        for level_index in range(levels):
+            block = blocks[kind_index * levels + level_index].astype(jnp.float32)[:, :width]
+            block = block.T if turned else block
+            if rates is None:
+                outs[len(flipped) + kind_index][level_index] = block
+                new[level_index] = moment_decay * old[level_index] + block
+            else:
+                new[level_index] = old[level_index] - rates[kind_index] * block
 
 
 def on_device(
@@ -453,8 +474,8 @@
         parts = [upright(weights[k], k, level_index).astype(jnp.bfloat16) for k in which]
         return jnp.concatenate(parts, axis=1)
 
-    def gathered_weights(own, which):
-        whole = gather_by_pairs(own, "row")
+    def gathered_weights(own, which, first):
+        whole = gather_by_pairs(own, "row", first)
         whole = whole.reshape(model_width, -1)
         result = []
         start = 0
@@ -468,7 +489,8 @@
 
     all_norms = gather_by_pairs(norm_params, "row")
     all_norms = all_norms.transpose(1, 2, 0, 3).reshape(levels, kinds, model_width)
-    image_blocks = to_all(swap_row_col(residual_in), "col")
+    both_inputs = jnp.concatenate([residual_in, cotangent.astype(residual_in.dtype)], axis=1)
+    image_blocks = to_all(swap_row_col(both_inputs), "col")
     position = lax.axis_index("col").astype(jnp.int32).reshape(1)
     heads = widths[0] // (3 * HD)
 
@@ -496,10 +518,10 @@
             chunk_flops,
         )
 
-    def norm_back_step(parts, stream, upstream, level_index, first_row):
+    def norm_back_step(parts, stream, change, level_index, first_row):
         return kernel_call(
             functools.partial(norm_back_kernel, level_index, first_row, len(parts)),
-            [*parts, stream, upstream, all_norms],
+            [*parts, stream, change, back_base, all_norms],
             [full_chunk, low_chunk, shaped(2, model_width, jnp.float32)],
             [],
             chunk_flops,
@@ -508,18 +530,24 @@
     *chunks, stream = kernel_call(
         functools.partial(first_kernel, tokens),
         [image_blocks, all_norms],
-        low_chunks + [full_chunk],
+        low_chunks + low_chunks + [full_chunk],
         [whole_scratch],
         20 * padded * model_width,
         position,
     )
+    chunks, back_chunks = chunks[:col_size], chunks[col_size:]
+    back_base = back_chunks[0]
     groups = ((0, 1), (2, 3))
 
-    def weights_of(own_groups):
-        return sum([gathered_weights(own, which) for own, which in zip(own_groups, groups)], [])
+    def first_steps(own_groups):
+        return [from_partner(own[None], row_size // 2, ("row",)) for own in own_groups]
+
+    def weights_of(own_groups, firsts):
+        parts = zip(own_groups, groups, firsts)
+        return sum([gathered_weights(own, which, first) for own, which, first in parts], [])
 
     own_groups = [[own_weights(i, which) for which in groups] for i in range(levels)]
-    weight_sets = [weights_of(own_groups[0])] + [None] * (levels - 1)
+    weight_sets = [weights_of(own_groups[0], first_steps(own_groups[0]))] + [None] * (levels - 1)
     saved = []
     early = [None] * levels
     for level_index in range(levels):
@@ -536,10 +564,7 @@
         stream_two, normed = norm_step(swap_parts(parts), stream, level_index, 2)
         if level_index == 0:
             normed, own_groups[1:] = lax.optimization_barrier((normed, own_groups[1:]))
-            for later in range(1, levels):
-                weight_sets[later] = weights_of(own_groups[later])
-        if level_index == levels - 1:
-            normed, back_chunks = lax.optimization_barrier((normed, back_chunks))
+            later_firsts = [first_steps(own) for own in own_groups[1:]]
         chunks = to_partners(normed)
         *parts, slope, normed_two, activated = kernel_call(
             functools.partial(mlp_kernel, tokens),
@@ -549,16 +574,16 @@
             perceptron_flops,
             position,
         )
+        if level_index == 0:
+            parts, later_firsts = lax.optimization_barrier((parts, later_firsts))
+            for later in range(1, levels):
+                weight_sets[later] = weights_of(own_groups[later], later_firsts[later - 1])
         parts = swap_parts(parts)
         early[level_index] = (normed_one, attended, normed_two, activated)
         if level_index < levels - 1:
             stream, normed = norm_step(parts, stream_two, level_index + 1, 0)
             if level_index == 0:
-                normed, late_me, cotangent = lax.optimization_barrier((normed, me, cotangent))
-                cotangent_blocks = pad_rows(swap_row_col(cotangent), padded)
-                cotangent_blocks = cotangent_blocks.reshape(col_size, chunk, width_row)
-                upstream = features_first(lax.all_to_all(cotangent_blocks, "col", 0, 0))
-                back_chunks = to_partners(upstream.astype(jnp.bfloat16))
+                normed, late_me = lax.optimization_barrier((normed, me))
             chunks = to_partners(normed)
         else:
             stream = stream_two
@@ -566,19 +591,26 @@
                 stream = stream + part.astype(jnp.float32)
         saved.append((stream_one, stream_two, mixed, slope))
 
-    def placed(chunk_values):
-        blocks = chunk_values.reshape(chunk, col_size, width_row).transpose(1, 0, 2)
+    def sent_to_owners(values):
+        blocks = jnp.stack(
+            [v.reshape(chunk, col_size, width_row).transpose(1, 0, 2) for v in values], axis=1
+        )
         col = lax.axis_index("col")
-        received = [pick(blocks, col)]
-        for k in range(1, col_size):
-            received.append(from_partner(pick(blocks, col ^ k), k, ("col",)))
-        whole = placed_blocks(received, [col ^ k for k in range(col_size)])
-        return swap_row_col(whole.reshape(padded, width_row)[:tokens])
+        return [pick(blocks, col)] + [
+            from_partner(pick(blocks, col ^ k), k, ("col",)) for k in range(1, col_size)
+        ]
+
+    def placed(received):
+        col = lax.axis_index("col")
+        whole = placed_blocks(received, [col ^ k for k in range(col_size)]).transpose(1, 0, 2, 3)
+        return swap_row_col(whole.reshape(whole.shape[0], padded, width_row)[:, :tokens])
 
     groups_of_jobs = dp_size * row_size // jobs
 
-    def spread(parts_of_levels):
-        stack = jnp.stack([parts_of_levels[j % levels][j // levels] for j in range(jobs)])
+    def spread(parts_of_levels, arrival, kind_arrival):
+        order = [(i, k) for i in arrival for k in kind_arrival]
+        blocks = [parts_of_levels[i][k] for i, k in order]
+        stack = placed_blocks(blocks, [k * levels + i for i, k in order])
         stack = jnp.concatenate([stack] * groups_of_jobs) if groups_of_jobs > 1 else stack
         return lax.all_to_all(stack, ("dp", "row"), 0, 0).reshape(-1, widest)
 
@@ -595,7 +627,8 @@
     own_moment = lax.all_to_all(stacked_moment, "row", 0, 0).reshape(model_width, widest)
 
     back_chunks, own_moment = lax.optimization_barrier((back_chunks, own_moment))
-    early_all = spread(early)
+    change = jnp.zeros((chunk, model_width), jnp.float32)
+    early_all = spread(early, range(levels), range(kinds))
     late = [None] * levels
     norm_sums = [None] * levels
     for level_index in reversed(range(levels)):
@@ -609,8 +642,8 @@
             perceptron_flops,
             position,
         )
-        upstream, back_low, sums_two = norm_back_step(
-            swap_parts(parts), stream_two, upstream, level_index, 2
+        change, back_low, sums_two = norm_back_step(
+            swap_parts(parts), stream_two, change, level_index, 2
         )
         if level_index == 0:
             back_low, early_all = lax.optimization_barrier((back_low, early_all))
@@ -624,9 +657,9 @@
         )
         late[level_index] = (mixed_grad, back_one, hidden_grad, back_two)
         if level_index == 0:
-            late_all = spread(late)
-        upstream, back_low, sums_one = norm_back_step(
-            swap_parts(parts), stream_one, upstream, level_index, 0
+            late_all = spread(late, reversed(range(levels)), (3, 2, 1, 0))
+        change, back_low, sums_one = norm_back_step(
+            swap_parts(parts), stream_one, change, level_index, 0
         )
         norm_sums[level_index] = jnp.concatenate([sums_one, sums_two])
 
@@ -634,8 +667,8 @@
             back_chunks = to_partners(back_low)
 
     norm_whole = sum_by_pairs(jnp.stack(norm_sums), "col")
-    late_all, norm_whole, stream, upstream = lax.optimization_barrier(
-        (late_all, norm_whole, stream, upstream)
+    late_all, norm_whole, stream, change = lax.optimization_barrier(
+        (late_all, norm_whole, stream, change)
     )
 
     turned = (me // levels) % 2 == 1
@@ -646,45 +679,38 @@
     def returned(whole):
         blocks = whole.astype(jnp.bfloat16).reshape(row_size, width_row, widest)
         blocks = jnp.concatenate([blocks] * dp_size)
-        received = lax.all_to_all(blocks, ("dp", "row"), 0, 0)
-        return [received[j] for j in range(jobs)]
+        return lax.all_to_all(blocks, ("dp", "row"), 0, 0)[:jobs]
 
     own_raw = moment_decay * own_moment + own_grad
     for axis in ("row", "dp"):
         norm_whole = sum_by_pairs(norm_whole, axis)
-    block_output = placed(stream)
-    own_strip, norm_whole, block_output = lax.optimization_barrier(
-        (gram_strips(own_raw), norm_whole, block_output)
-    )
+    own_strip, norm_whole = lax.optimization_barrier((gram_strips(own_raw), norm_whole))
     norm_grad = lax.dynamic_slice_in_dim(norm_whole, my_row * width_row, width_row, 2)
     norm_moment_new = moment_decay * norm_moment + norm_grad
-    input_grad = placed(upstream)
     gram = to_all(own_strip, "col").reshape(-1, own_strip.shape[1])
-    gram, own_grad, input_grad = lax.optimization_barrier((gram, own_grad, input_grad))
+    gram, own_grad, stream, change = lax.optimization_barrier((gram, own_grad, stream, change))
+    tokens_moved = sent_to_owners([stream, change])
     grads = returned(own_grad)
-    orth_whole, grads = lax.optimization_barrier((schulz(own_raw, gram), grads))
-    orths = [block.astype(jnp.float32) for block in returned(orth_whole)]
-    grads = [block.astype(jnp.float32) for block in grads]
-
-    grad_outs = []
-    moment_outs = []
-    new_outs = []
-    for kind_index in range(kinds):
-        grad_levels = []
-        orth_levels = []
-        for level_index in range(levels):
-            job = kind_index * levels + level_index
-            grad_here = grads[job][:, : widths[kind_index]]
-            orth_here = orths[job][:, : widths[kind_index]]
-            if flipped[kind_index]:
-                grad_here = grad_here.T
-                orth_here = orth_here.T
-            grad_levels.append(grad_here)
-            orth_levels.append(orth_here)
-        grad_out = jnp.stack(grad_levels)
-        grad_outs.append(grad_out)
-        moment_outs.append(moment_decay * moments[kind_index] + grad_out)
-        new_outs.append(weights[kind_index] - step_rates[kind_index] * jnp.stack(orth_levels))
+    orth_whole, grads, tokens_moved = lax.optimization_barrier(
+        (schulz(own_raw, gram), grads, tokens_moved)
+    )
+    block_output, change = placed(tokens_moved)
+    input_grad = cotangent + change
+    orths = returned(orth_whole)
+
+    def finished(blocks, olds, rates):
+        shapes = [jax.ShapeDtypeStruct(old.shape, jnp.float32) for old in olds]
+        return kernel_call(
+            functools.partial(finish_kernel, levels, flipped, rates),
+            [blocks, *olds],
+            shapes if rates else shapes + shapes,
+            [],
+            2 * sum(math.prod(old.shape) for old in olds),
+        )
+
+    moment_and_grad = finished(grads, moments, None)
+    moment_outs, grad_outs = moment_and_grad[:kinds], moment_and_grad[kinds:]
+    new_outs = finished(orths, weights, step_rates)
 
     tokens_all = tokens * col_size * dp_size
     norm_new = norm_params - norm_rate / math.sqrt(tokens_all) * norm_moment_new

time: 537 us -> 487 us (0.907)
  starting transfers between devices: 156 us -> 128 us
  waiting for transfers between devices: 185 us -> 163 us
    ppermute x66 -> x60, waiting for transfers between devices: 153 us -> 86.5 us  [from_partner(): return lax.ppermute(values, axes, pairs)]
    all_to_all x2, waiting for transfers between devices: 6.6 us -> 44.5 us  [to_all(): lax.all_to_all(jnp.broadcast_to(block[None], (size,) + block.shape), axis...]
    all_to_all x1, waiting for transfers between devices: 0.01 us -> 27.4 us  [gram_strips(): lax.all_to_all(packed.reshape(size, third // size, -1), 'col', 0, 0)]
    all_to_all x3 -> x2, waiting for transfers between devices: 20.9 us -> 0.01 us  [returned(): return lax.all_to_all(blocks, ('dp', 'row'), 0, 0)[:jobs]]
    all_to_all x3 -> x2, starting transfers between devices: 25.8 us -> 8.93 us  [returned(): return lax.all_to_all(blocks, ('dp', 'row'), 0, 0)[:jobs]]
    dynamic_update_slice x25 -> x33, local copies, waits for them, and re-layouts: 7.3 us -> 19.5 us  [placed_blocks(): result = lax.dynamic_update_index_in_dim(result, block, place, 0)]
    ppermute x66 -> x60, starting transfers between devices: 94.5 us -> 83.7 us  [from_partner(): return lax.ppermute(values, axes, pairs)]
    another operation x19 -> x5, local copies, waits for them, and re-layouts: 12.2 us -> 2.13 us  [the longest x1 1.62 us: on_device(): block_output, change = placed(tokens_moved)]
  transfers between devices with their start and end apart: 79 -> 70, of which waited for: 36 -> 31; matrix products, arithmetic and copies ran while one was open for 14% -> 15% of each run, Pallas kernels for 10% -> 12%
where the time goes in v6:
time: 487 us; the launch traced here: 477 us
  waiting for transfers between devices  163 us (33%)
  starting transfers between devices  128 us (26%)
  local copies, waits for them, and re-layouts  76.9 us (16%)
  Pallas kernels  57 us (12%)
  other arithmetic  40.4 us (8%)
  matrix products  9.3 us (2%)
    ppermute x60, waiting for transfers between devices, from_partner(): return lax.ppermute(values, axes, pairs)  86.5 us
    ppermute x60, starting transfers between devices, from_partner(): return lax.ppermute(values, axes, pairs)  83.7 us
    pallas_call x14, Pallas kernels, kernel_call(): pl.pallas_call(body, out_shape=list(outputs), in_specs=specs, out_specs=i...  57 us
    all_to_all x2, waiting for transfers between devices, to_all(): lax.all_to_all(jnp.broadcast_to(block[None], (size,) + block.shape), axis...  44.5 us
    unnamed x156, local copies, waits for them, and re-layouts  42.7 us
    all_to_all x1, waiting for transfers between devices, gram_strips(): lax.all_to_all(packed.reshape(size, third // size, -1), 'col', 0, 0)  27.4 us
    dynamic_update_slice x33, local copies, waits for them, and re-layouts, placed_blocks(): result = lax.dynamic_update_index_in_dim(result, block, place, 0)  19.5 us
    pallas_call x5, other arithmetic, kernel_call(): pl.pallas_call(body, out_shape=list(outputs), in_specs=specs, out_specs=i...  13.3 us
  transfers between devices with their start and end apart: 70, of which 31 were waited for; matrix products, arithmetic and copies ran while one was open for 15% of the time, Pallas kernels for 12%

profile of v6, /device:TPU:0, one launch (start us, length us, event | category | flops | bytes accessed | tf_op | source)
XLA Modules:
  0.0 477.2 jit_solution(16007962405676732707)
XLA Ops:
  3.1 3.0 collective-permute-start.3
  8.8 3.0 collective-permute-start
  12.9 3.4 collective-permute-start.11
  23.7 4.1 all-to-all-start
  33.4 2.2 pad_maximum_fusion.4
  37.0 8.0 %all-to-all-done.blocks = bf16[4,197,384]{2,1,0:T(8,128)(2,1)S(1)} async-done(((bf16[4,197,384]{2,1,0:T(8,128)(2,1)}), bf16[4,197,384]{2,1,0:T(8,128)(2,1)S(1)}, u32[]{:S(2)}, u32[]{:S(2)}) %all-to-all-start) | async-done | bytes 605216 | tf_op jit(solution)/shard_map/all_to_all | solution.py:291
  49.0 2.0 collective-permute-start.6
  51.0 2.4 collective-permute-start.7
  55.8 3.2 collective-permute-done.6.refs_2_
  61.8 1.9 collective-permute-start.9
  64.1 2.1 collective-permute-start.13
  72.1 11.5 %collective-permute-done.13 = bf16[1,192,768]{2,1,0:T(8,128)(2,1)S(1)} collective-permute-done((bf16[1,192,768]{2,1,0:T(8,128)(2,1)S(1)}, bf16[1,192,768]{2,1,0:T(8,128)(2,1)S(1)}, u32[]{:S(2)}, u32[]{:S(2)}) %collective-permute-start.13) | collective-permute-done | bytes 294944 | tf_op jit(solution)/shard_map/ppermute | solution.py:253
  88.0 2.6 collective-permute-start.17
  92.1 5.0 %collective-permute-done.16.refs_2_ = bf16[56,768]{1,0:T(8,128)(2,1)S(1)} collective-permute-done((bf16[56,768]{1,0:T(8,128)(2,1)S(1)}, bf16[56,768]{1,0:T(8,128)(2,1)S(1)}, u32[]{:S(2)}, u32[]{:S(2)}) %collective-permute-start.16) | collective-permute-done | bytes 86048 | tf_op jit(solution)/shard_map/ppermute | solution.py:253
  100.9 2.1 collective-permute-start.20
  103.0 1.9 fusion.12
  106.5 4.8 %all-to-all-start.1 = ((f32[4,192,768]{2,1,0:T(8,128)}), f32[4,192,768]{2,1,0:T(8,128)}, u32[]{:S(2)}, u32[]{:S(2)}) async-start(f32[4,192,768]{2,1,0:T(8,128)} %pad_maximum_fusion), calls=%async_computation.1 | async-start | bytes 4718592 | tf_op jit(solution)/shard_map/all_to_all | solution.py:627
  113.6 3.6 shard_map.267
  119.6 2.1 collective-permute-start.24
  122.9 5.1 %collective-permute-done.23.refs_2_ = bf16[56,768]{1,0:T(8,128)(2,1)S(1)} collective-permute-done((bf16[56,768]{1,0:T(8,128)(2,1)S(1)}, bf16[56,768]{1,0:T(8,128)(2,1)S(1)}, u32[]{:S(2)}, u32[]{:S(2)}) %collective-permute-start.23) | collective-permute-done | bytes 86048 | tf_op jit(solution)/shard_map/ppermute | solution.py:253
  130.4 2.3 collective-permute-start.27
  135.1 3.8 collective-permute-done.26
  138.9 1.9 shard_map.266
  142.6 4.4 all-to-all-start.2
  156.3 2.0 collective-permute-start.31
  158.8 6.5 %collective-permute-done.30.refs_2_ = bf16[56,768]{1,0:T(8,128)(2,1)S(1)} collective-permute-done((bf16[56,768]{1,0:T(8,128)(2,1)S(1)}, bf16[56,768]{1,0:T(8,128)(2,1)S(1)}, u32[]{:S(2)}, u32[]{:S(2)}) %collective-permute-start.30) | collective-permute-done | bytes 86048 | tf_op jit(solution)/shard_map/ppermute | solution.py:253
  168.1 1.9 collective-permute-start.34
  170.4 5.9 %collective-permute-done.33 = bf16[56,768]{1,0:T(8,128)(2,1)S(1)} collective-permute-done((bf16[56,768]{1,0:T(8,128)(2,1)S(1)}, bf16[56,768]{1,0:T(8,128)(2,1)S(1)}, u32[]{:S(2)}, u32[]{:S(2)}) %collective-permute-start.33) | collective-permute-done | bytes 86048 | tf_op jit(solution)/shard_map/ppermute | solution.py:253
  176.4 2.4 shard_map.269
  181.3 2.0 collective-permute-start.37
  183.5 5.8 %collective-permute-done.36.refs_2_ = bf16[56,768]{1,0:T(8,128)(2,1)S(1)} collective-permute-done((bf16[56,768]{1,0:T(8,128)(2,1)S(1)}, bf16[56,768]{1,0:T(8,128)(2,1)S(1)}, u32[]{:S(2)}, u32[]{:S(2)}) %collective-permute-start.36) | collective-permute-done | bytes 86048 | tf_op jit(solution)/shard_map/ppermute | solution.py:253
  191.8 2.1 collective-permute-start.40
  194.1 5.9 %collective-permute-done.39 = bf16[56,768]{1,0:T(8,128)(2,1)S(1)} collective-permute-done((bf16[56,768]{1,0:T(8,128)(2,1)S(1)}, bf16[56,768]{1,0:T(8,128)(2,1)S(1)}, u32[]{:S(2)}, u32[]{:S(2)}) %collective-permute-start.39) | collective-permute-done | bytes 86048 | tf_op jit(solution)/shard_map/ppermute | solution.py:253
  203.5 2.3 collective-permute-start.43
  205.9 5.7 %collective-permute-done.42.refs_2_ = bf16[56,768]{1,0:T(8,128)(2,1)S(1)} collective-permute-done((bf16[56,768]{1,0:T(8,128)(2,1)S(1)}, bf16[56,768]{1,0:T(8,128)(2,1)S(1)}, u32[]{:S(2)}, u32[]{:S(2)}) %collective-permute-start.42) | collective-permute-done | bytes 86048 | tf_op jit(solution)/shard_map/ppermute | solution.py:253
  214.0 2.3 collective-permute-start.46
  218.1 4.0 collective-permute-done.45
  222.1 4.0 shard_map.265
  226.9 4.7 all-to-all-start.3
  233.7 2.3 collective-permute-start.49
  236.6 6.3 %collective-permute-done.48.refs_2_ = bf16[56,768]{1,0:T(8,128)(2,1)S(1)} collective-permute-done((bf16[56,768]{1,0:T(8,128)(2,1)S(1)}, bf16[56,768]{1,0:T(8,128)(2,1)S(1)}, u32[]{:S(2)}, u32[]{:S(2)}) %collective-permute-start.48) | collective-permute-done | bytes 86048 | tf_op jit(solution)/shard_map/ppermute | solution.py:253
  243.8 2.0 collective-permute-start.50
  247.8 2.4 collective-permute-start.54
  250.7 5.4 %collective-permute-done.53 = bf16[56,768]{1,0:T(8,128)(2,1)S(1)} collective-permute-done((bf16[56,768]{1,0:T(8,128)(2,1)S(1)}, bf16[56,768]{1,0:T(8,128)(2,1)S(1)}, u32[]{:S(2)}, u32[]{:S(2)}) %collective-permute-start.53) | collective-permute-done | bytes 86048 | tf_op jit(solution)/shard_map/ppermute | solution.py:253
  257.3 4.9 %all-to-all-done.3 = bf16[8,208,768]{2,1,0:T(8,128)(2,1)} async-done(((bf16[8,208,768]{2,1,0:T(8,128)(2,1)}), bf16[8,208,768]{2,1,0:T(8,128)(2,1)}, u32[]{:S(2)}, u32[]{:S(2)}) %all-to-all-start.3) | async-done | bytes 2555936 | tf_op jit(solution)/shard_map/all_to_all | solution.py:615
  262.2 6.7 %multiply_add_fusion = (f32[768,768]{1,0:T(8,128)S(1)}, bf16[768,768]{1,0:T(8,128)(2,1)}) fusion(f32[768,768]{1,0:T(8,128)} %bitcast.37, bf16[1664,768]{1,0:T(8,128)(2,1)} %bitcast.54, bf16[1664,768]{1,0:T(8,128)(2,1)} %bitcast.57, pred[]{:T(512)S(6)} %eq.11), kind=kOutput, calls=%fused_computation.7 | convolution fusion | flops 1967259648 | bytes 11010049 | tf_op jit(solution)/shard_map/dot_general | solution.py:24
  272.9 4.4 all-to-all-start.4
  280.1 2.4 collective-permute-done.56
  284.0 2.3 collective-permute-done.57
  287.0 27.4 %all-to-all-done.4 = f32[4,64,1536]{2,1,0:T(8,128)} async-done(((f32[4,64,1536]{2,1,0:T(8,128)}), f32[4,64,1536]{2,1,0:T(8,128)}, u32[]{:S(2)}, u32[]{:S(2)}) %all-to-all-start.4) | async-done | bytes 1572896 | tf_op jit(solution)/shard_map/all_to_all | solution.py:317
  317.3 4.4 all-to-all-start.5
  321.7 36.5 %all-to-all-done.5 = f32[4,64,1536]{2,1,0:T(8,128)} async-done(((f32[4,64,1536]{2,1,0:T(8,128)}), f32[4,64,1536]{2,1,0:T(8,128)}, u32[]{:S(2)}, u32[]{:S(2)}) %all-to-all-start.5) | async-done | bytes 1572896 | tf_op jit(solution)/shard_map/all_to_all | solution.py:291
  365.3 2.0 collective-permute-start.59
  367.3 2.4 collective-permute-start.60
  371.4 4.6 all-to-all-start.6
  376.0 44.3 %shard_map.262 = bf16[768,768]{1,0:T(8,128)(2,1)S(1)} custom-call(f32[256,1536]{1,0:T(8,128)} %bitcast.61.packed, f32[768,768]{1,0:T(8,128)S(1)} %get-tuple-element.394.raw), custom_call_target="tpu_custom_call" | custom-call | flops 38050725888 | bytes 5111808 | tf_op jit(solution)/shard_map/pallas_call | solution.py:71
  422.0 4.3 all-to-all-start.7
  429.9 5.3 %collective-permute-start.61 = (f32[2,197,192]{2,1,0:T(8,128)}, f32[2,197,192]{2,1,0:T(8,128)}, u32[]{:S(2)}, u32[]{:S(2)}) collective-permute-start(f32[2,197,192]{2,1,0:T(8,128)} %slice.195), channel_id=1, source_target_pairs={{0,0},{1,4},{2,8},{3,12},{4,1},{5,5},{6,9},{7,13},{8,2},{9,6},{10,... | collective-permute-start | bytes 907784 | tf_op jit(solution)/shard_map/ppermute | solution.py:247
  435.3 2.9 copy.61.refs_3_
  438.1 3.0 copy.62.refs_3_
  447.9 4.3 shard_map.263
  454.6 2.9 copy.65
  457.4 3.0 copy.66
  473.8 2.9 copy.67
  (358 shorter events, 141.6 us)
Async XLA Ops:
  3.1 24.7 %collective-permute-start.3 = (bf16[1,192,768]{2,1,0:T(8,128)(2,1)S(1)}, bf16[1,192,768]{2,1,0:T(8,128)(2,1)}, u32[]{:S(2)}, u32[]{:S(2)}) collective-permute-start(bf16[1,192,768]{2,1,0:T(8,128)(2,1)S(1)} %get-tuple-element.367), channel_id=1, source_target_pairs={{0,8},{4,12},{8,0},{12,4},{1,9},{5,13},{9,1},{13,5},{2,10},{6,14},... | collective-permute-start | bytes 884744 | tf_op jit(solution)/shard_map/ppermute | solution.py:253
  6.1 12.5 %collective-permute-start.1 = (f32[1,2,4,192]{3,2,1,0:T(4,128)S(1)}, f32[1,2,4,192]{3,2,1,0:T(4,128)S(1)}, u32[]{:S(2)}, u32[]{:S(2)}) collective-permute-start(f32[1,2,4,192]{3,2,1,0:T(4,128)S(1)} %bitcast.186), channel_id=1, source_target_pairs={{0,8},{4,12},{8,0},{12,4},{1,9},{5,13},{9,1},{13,5},{2,10},{6,14},... | collective-permute-start | bytes 18440 | tf_op jit(solution)/shard_map/ppermute | solution.py:253
  8.8 13.0 %collective-permute-start = (bf16[197,384]{0,1:T(8,128)(2,1)}, bf16[197,384]{0,1:T(8,128)(2,1)}, u32[]{:S(2)}, u32[]{:S(2)}) collective-permute-start(bf16[197,384]{0,1:T(8,128)(2,1)} %pad_maximum_fusion.10), channel_id=1, source_target_pairs={{0,0},{1,4},{2,8},{3,12},{4,1},{5,5},{6,9},{7,13},{8,2},{9,6},{10,... | collective-permute-start | bytes 453896 | tf_op jit(solution)/shard_map/ppermute | solution.py:247
  12.9 20.5 %collective-permute-start.11 = (bf16[1,192,1536]{2,1,0:T(8,128)(2,1)}, bf16[1,192,1536]{2,1,0:T(8,128)(2,1)S(1)}, u32[]{:S(2)}, u32[]{:S(2)}) collective-permute-start(bf16[1,192,1536]{2,1,0:T(8,128)(2,1)} %maximum_bitcast_fusion), channel_id=1, source_target_pairs={{0,8},{4,12},{8,0},{12,4},{1,9},{5,13},{9,1},{13,5},{2,10},{6,14},... | collective-permute-start | bytes 1769480 | tf_op jit(solution)/shard_map/ppermute | solution.py:253
  23.7 21.3 %all-to-all-start = ((bf16[4,197,384]{2,1,0:T(8,128)(2,1)}), bf16[4,197,384]{2,1,0:T(8,128)(2,1)S(1)}, u32[]{:S(2)}, u32[]{:S(2)}) async-start(bf16[4,197,384]{2,1,0:T(8,128)(2,1)} %broadcast_in_dim.122), calls=%async_computation | async-start | bytes 1228800 | tf_op jit(solution)/shard_map/all_to_all | solution.py:291
  28.8 7.8 %collective-permute-start.4 = (bf16[2,192,768]{2,1,0:T(8,128)(2,1)S(1)}, bf16[2,192,768]{2,1,0:T(8,128)(2,1)S(1)}, u32[]{:S(2)}, u32[]{:S(2)}) collective-permute-start(bf16[2,192,768]{2,1,0:T(8,128)(2,1)S(1)} %pad_maximum_fusion.6), channel_id=1, source_target_pairs={{0,4},{4,0},{8,12},{12,8},{1,5},{5,1},{9,13},{13,9},{2,6},{6,2},{1... | collective-permute-start | bytes 1769480 | tf_op jit(solution)/shard_map/ppermute | solution.py:253
  35.6 28.5 %collective-permute-start.12 = (bf16[2,192,1536]{2,1,0:T(8,128)(2,1)}, bf16[2,192,1536]{2,1,0:T(8,128)(2,1)}, u32[]{:S(2)}, u32[]{:S(2)}) collective-permute-start(bf16[2,192,1536]{2,1,0:T(8,128)(2,1)} %pad_maximum_fusion.4), channel_id=1, source_target_pairs={{0,4},{4,0},{8,12},{12,8},{1,5},{5,1},{9,13},{13,9},{2,6},{6,2},{1... | collective-permute-start | bytes 3538952 | tf_op jit(solution)/shard_map/ppermute | solution.py:253
  48.9 6.9 %collective-permute-start.5 = (bf16[56,768]{1,0:T(8,128)(2,1)S(1)}, bf16[56,768]{1,0:T(8,128)(2,1)S(1)}, u32[]{:S(2)}, u32[]{:S(2)}) collective-permute-start(bf16[56,768]{1,0:T(8,128)(2,1)S(1)} %get-tuple-element.150), channel_id=1, source_target_pairs={{0,1},{1,0},{2,3},{3,2},{4,5},{5,4},{6,7},{7,6},{8,9},{9,8},{10,11... | collective-permute-start | bytes 258056 | tf_op jit(solution)/shard_map/ppermute | solution.py:253
  49.0 10.0 %collective-permute-start.6 = (bf16[56,768]{1,0:T(8,128)(2,1)S(1)}, bf16[56,768]{1,0:T(8,128)(2,1)S(1)}, u32[]{:S(2)}, u32[]{:S(2)}) collective-permute-start(bf16[56,768]{1,0:T(8,128)(2,1)S(1)} %get-tuple-element.151), channel_id=1, source_target_pairs={{0,2},{1,3},{2,0},{3,1},{4,6},{5,7},{6,4},{7,5},{8,10},{9,11},{10,... | collective-permute-start | bytes 258056 | tf_op jit(solution)/shard_map/ppermute | solution.py:253
  51.0 8.0 %collective-permute-start.7 = (bf16[56,768]{1,0:T(8,128)(2,1)S(1)}, bf16[56,768]{1,0:T(8,128)(2,1)S(1)}, u32[]{:S(2)}, u32[]{:S(2)}) collective-permute-start(bf16[56,768]{1,0:T(8,128)(2,1)S(1)} %get-tuple-element.152), channel_id=1, source_target_pairs={{0,3},{1,2},{2,1},{3,0},{4,7},{5,6},{6,5},{7,4},{8,11},{9,10},{10,... | collective-permute-start | bytes 258056 | tf_op jit(solution)/shard_map/ppermute | solution.py:253
  59.2 9.3 %collective-permute-start.10 = (bf16[56,768]{1,0:T(8,128)(2,1)S(1)}, bf16[56,768]{1,0:T(8,128)(2,1)S(1)}, u32[]{:S(2)}, u32[]{:S(2)}) collective-permute-start(bf16[56,768]{1,0:T(8,128)(2,1)S(1)} %get-tuple-element.155.refs_0_), channel_id=1, source_target_pairs={{0,3},{1,2},{2,1},{3,0},{4,7},{5,6},{6,5},{7,4},{8,11},{9,10},{10,... | collective-permute-start | bytes 258056 | tf_op jit(solution)/shard_map/ppermute | solution.py:253
  60.7 7.8 %collective-permute-start.8 = (bf16[56,768]{1,0:T(8,128)(2,1)S(1)}, bf16[56,768]{1,0:T(8,128)(2,1)S(1)}, u32[]{:S(2)}, u32[]{:S(2)}) collective-permute-start(bf16[56,768]{1,0:T(8,128)(2,1)S(1)} %get-tuple-element.155.refs_0_), channel_id=1, source_target_pairs={{0,1},{1,0},{2,3},{3,2},{4,5},{5,4},{6,7},{7,6},{8,9},{9,8},{10,11... | collective-permute-start | bytes 258056 | tf_op jit(solution)/shard_map/ppermute | solution.py:253
  61.8 8.4 %collective-permute-start.9 = (bf16[56,768]{1,0:T(8,128)(2,1)S(1)}, bf16[56,768]{1,0:T(8,128)(2,1)S(1)}, u32[]{:S(2)}, u32[]{:S(2)}) collective-permute-start(bf16[56,768]{1,0:T(8,128)(2,1)S(1)} %get-tuple-element.155.refs_0_), channel_id=1, source_target_pairs={{0,2},{1,3},{2,0},{3,1},{4,6},{5,7},{6,4},{7,5},{8,10},{9,11},{10,... | collective-permute-start | bytes 258056 | tf_op jit(solution)/shard_map/ppermute | solution.py:253
  63.7 19.9 %collective-permute-start.14 = (bf16[1,192,1536]{2,1,0:T(8,128)(2,1)S(1)}, bf16[1,192,1536]{2,1,0:T(8,128)(2,1)S(1)}, u32[]{:S(2)}, u32[]{:S(2)}) collective-permute-start(bf16[1,192,1536]{2,1,0:T(8,128)(2,1)S(1)} %bitcast.175), channel_id=1, source_target_pairs={{0,8},{4,12},{8,0},{12,4},{1,9},{5,13},{9,1},{13,5},{2,10},{6,14},... | collective-permute-start | bytes 1769480 | tf_op jit(solution)/shard_map/ppermute | solution.py:253
  64.1 19.5 %collective-permute-start.13 = (bf16[1,192,768]{2,1,0:T(8,128)(2,1)S(1)}, bf16[1,192,768]{2,1,0:T(8,128)(2,1)S(1)}, u32[]{:S(2)}, u32[]{:S(2)}) collective-permute-start(bf16[1,192,768]{2,1,0:T(8,128)(2,1)S(1)} %bitcast.177), channel_id=1, source_target_pairs={{0,8},{4,12},{8,0},{12,4},{1,9},{5,13},{9,1},{13,5},{2,10},{6,14},... | collective-permute-start | bytes 884744 | tf_op jit(solution)/shard_map/ppermute | solution.py:253
  84.7 47.9 %collective-permute-start.28 = (bf16[2,192,1536]{2,1,0:T(8,128)(2,1)}, bf16[2,192,1536]{2,1,0:T(8,128)(2,1)}, u32[]{:S(2)}, u32[]{:S(2)}) collective-permute-start(bf16[2,192,1536]{2,1,0:T(8,128)(2,1)} %pad_maximum_fusion.5), channel_id=1, source_target_pairs={{0,4},{4,0},{8,12},{12,8},{1,5},{5,1},{9,13},{13,9},{2,6},{6,2},{1... | collective-permute-start | bytes 3538952 | tf_op jit(solution)/shard_map/ppermute | solution.py:253
  85.7 25.6 %collective-permute-start.21 = (bf16[2,192,768]{2,1,0:T(8,128)(2,1)}, bf16[2,192,768]{2,1,0:T(8,128)(2,1)}, u32[]{:S(2)}, u32[]{:S(2)}) collective-permute-start(bf16[2,192,768]{2,1,0:T(8,128)(2,1)} %pad_maximum_fusion.8), channel_id=1, source_target_pairs={{0,4},{4,0},{8,12},{12,8},{1,5},{5,1},{9,13},{13,9},{2,6},{6,2},{1... | collective-permute-start | bytes 1769480 | tf_op jit(solution)/shard_map/ppermute | solution.py:253
  86.2 5.9 %collective-permute-start.15 = (bf16[56,768]{1,0:T(8,128)(2,1)S(1)}, bf16[56,768]{1,0:T(8,128)(2,1)S(1)}, u32[]{:S(2)}, u32[]{:S(2)}) collective-permute-start(bf16[56,768]{1,0:T(8,128)(2,1)S(1)} %get-tuple-element.163), channel_id=1, source_target_pairs={{0,1},{1,0},{2,3},{3,2},{4,5},{5,4},{6,7},{7,6},{8,9},{9,8},{10,11... | collective-permute-start | bytes 258056 | tf_op jit(solution)/shard_map/ppermute | solution.py:253
  87.7 9.4 %collective-permute-start.16 = (bf16[56,768]{1,0:T(8,128)(2,1)S(1)}, bf16[56,768]{1,0:T(8,128)(2,1)S(1)}, u32[]{:S(2)}, u32[]{:S(2)}) collective-permute-start(bf16[56,768]{1,0:T(8,128)(2,1)S(1)} %get-tuple-element.164), channel_id=1, source_target_pairs={{0,2},{1,3},{2,0},{3,1},{4,6},{5,7},{6,4},{7,5},{8,10},{9,11},{10,... | collective-permute-start | bytes 258056 | tf_op jit(solution)/shard_map/ppermute | solution.py:253
  88.0 9.1 %collective-permute-start.17 = (bf16[56,768]{1,0:T(8,128)(2,1)S(1)}, bf16[56,768]{1,0:T(8,128)(2,1)S(1)}, u32[]{:S(2)}, u32[]{:S(2)}) collective-permute-start(bf16[56,768]{1,0:T(8,128)(2,1)S(1)} %get-tuple-element.165), channel_id=1, source_target_pairs={{0,3},{1,2},{2,1},{3,0},{4,7},{5,6},{6,5},{7,4},{8,11},{9,10},{10,... | collective-permute-start | bytes 258056 | tf_op jit(solution)/shard_map/ppermute | solution.py:253
  98.6 15.1 %collective-permute-start.18 = (bf16[56,768]{1,0:T(8,128)(2,1)}, bf16[56,768]{1,0:T(8,128)(2,1)}, u32[]{:S(2)}, u32[]{:S(2)}) collective-permute-start(bf16[56,768]{1,0:T(8,128)(2,1)} %get-tuple-element.174), channel_id=1, source_target_pairs={{0,1},{1,0},{2,3},{3,2},{4,5},{5,4},{6,7},{7,6},{8,9},{9,8},{10,11... | collective-permute-start | bytes 258056 | tf_op jit(solution)/shard_map/ppermute | solution.py:253
  100.3 13.3 %collective-permute-start.19 = (bf16[56,768]{1,0:T(8,128)(2,1)}, bf16[56,768]{1,0:T(8,128)(2,1)}, u32[]{:S(2)}, u32[]{:S(2)}) collective-permute-start(bf16[56,768]{1,0:T(8,128)(2,1)} %get-tuple-element.174), channel_id=1, source_target_pairs={{0,2},{1,3},{2,0},{3,1},{4,6},{5,7},{6,4},{7,5},{8,10},{9,11},{10,... | collective-permute-start | bytes 258056 | tf_op jit(solution)/shard_map/ppermute | solution.py:253
  100.9 12.7 %collective-permute-start.20 = (bf16[56,768]{1,0:T(8,128)(2,1)}, bf16[56,768]{1,0:T(8,128)(2,1)}, u32[]{:S(2)}, u32[]{:S(2)}) collective-permute-start(bf16[56,768]{1,0:T(8,128)(2,1)} %get-tuple-element.174), channel_id=1, source_target_pairs={{0,3},{1,2},{2,1},{3,0},{4,7},{5,6},{6,5},{7,4},{8,11},{9,10},{10,... | collective-permute-start | bytes 258056 | tf_op jit(solution)/shard_map/ppermute | solution.py:253
  106.5 36.1 %all-to-all-start.1 = ((f32[4,192,768]{2,1,0:T(8,128)}), f32[4,192,768]{2,1,0:T(8,128)}, u32[]{:S(2)}, u32[]{:S(2)}) async-start(f32[4,192,768]{2,1,0:T(8,128)} %pad_maximum_fusion), calls=%async_computation.1 | async-start | bytes 4718592 | tf_op jit(solution)/shard_map/all_to_all | solution.py:627
  117.2 5.7 %collective-permute-start.22 = (bf16[56,768]{1,0:T(8,128)(2,1)S(1)}, bf16[56,768]{1,0:T(8,128)(2,1)S(1)}, u32[]{:S(2)}, u32[]{:S(2)}) collective-permute-start(bf16[56,768]{1,0:T(8,128)(2,1)S(1)} %get-tuple-element.315), channel_id=1, source_target_pairs={{0,1},{1,0},{2,3},{3,2},{4,5},{5,4},{6,7},{7,6},{8,9},{9,8},{10,11... | collective-permute-start | bytes 258056 | tf_op jit(solution)/shard_map/ppermute | solution.py:253
  118.1 9.9 %collective-permute-start.23 = (bf16[56,768]{1,0:T(8,128)(2,1)S(1)}, bf16[56,768]{1,0:T(8,128)(2,1)S(1)}, u32[]{:S(2)}, u32[]{:S(2)}) collective-permute-start(bf16[56,768]{1,0:T(8,128)(2,1)S(1)} %get-tuple-element.317), channel_id=1, source_target_pairs={{0,2},{1,3},{2,0},{3,1},{4,6},{5,7},{6,4},{7,5},{8,10},{9,11},{10,... | collective-permute-start | bytes 258056 | tf_op jit(solution)/shard_map/ppermute | solution.py:253
  119.6 8.4 %collective-permute-start.24 = (bf16[56,768]{1,0:T(8,128)(2,1)S(1)}, bf16[56,768]{1,0:T(8,128)(2,1)S(1)}, u32[]{:S(2)}, u32[]{:S(2)}) collective-permute-start(bf16[56,768]{1,0:T(8,128)(2,1)S(1)} %get-tuple-element.319), channel_id=1, source_target_pairs={{0,3},{1,2},{2,1},{3,0},{4,7},{5,6},{6,5},{7,4},{8,11},{9,10},{10,... | collective-permute-start | bytes 258056 | tf_op jit(solution)/shard_map/ppermute | solution.py:253
  128.2 6.9 %collective-permute-start.25 = (bf16[56,768]{1,0:T(8,128)(2,1)S(1)}, bf16[56,768]{1,0:T(8,128)(2,1)S(1)}, u32[]{:S(2)}, u32[]{:S(2)}) collective-permute-start(bf16[56,768]{1,0:T(8,128)(2,1)S(1)} %get-tuple-element.181), channel_id=1, source_target_pairs={{0,1},{1,0},{2,3},{3,2},{4,5},{5,4},{6,7},{7,6},{8,9},{9,8},{10,11... | collective-permute-start | bytes 258056 | tf_op jit(solution)/shard_map/ppermute | solution.py:253
  130.0 8.9 %collective-permute-start.26 = (bf16[56,768]{1,0:T(8,128)(2,1)S(1)}, bf16[56,768]{1,0:T(8,128)(2,1)S(1)}, u32[]{:S(2)}, u32[]{:S(2)}) collective-permute-start(bf16[56,768]{1,0:T(8,128)(2,1)S(1)} %get-tuple-element.181), channel_id=1, source_target_pairs={{0,2},{1,3},{2,0},{3,1},{4,6},{5,7},{6,4},{7,5},{8,10},{9,11},{10,... | collective-permute-start | bytes 258056 | tf_op jit(solution)/shard_map/ppermute | solution.py:253
  130.4 8.5 %collective-permute-start.27 = (bf16[56,768]{1,0:T(8,128)(2,1)S(1)}, bf16[56,768]{1,0:T(8,128)(2,1)S(1)}, u32[]{:S(2)}, u32[]{:S(2)}) collective-permute-start(bf16[56,768]{1,0:T(8,128)(2,1)S(1)} %get-tuple-element.181), channel_id=1, source_target_pairs={{0,3},{1,2},{2,1},{3,0},{4,7},{5,6},{6,5},{7,4},{8,11},{9,10},{10,... | collective-permute-start | bytes 258056 | tf_op jit(solution)/shard_map/ppermute | solution.py:253
  142.6 69.3 %all-to-all-start.2 = ((bf16[8,208,768]{2,1,0:T(8,128)(2,1)}), bf16[8,208,768]{2,1,0:T(8,128)(2,1)}, u32[]{:S(2)}, u32[]{:S(2)}) async-start(bf16[8,208,768]{2,1,0:T(8,128)(2,1)} %bitcast_dynamic-update-slice_fusion.2), calls=%async_computation.2 | async-start | bytes 5111808 | tf_op jit(solution)/shard_map/all_to_all | solution.py:615
  153.9 4.9 %collective-permute-start.29 = (bf16[56,768]{1,0:T(8,128)(2,1)S(1)}, bf16[56,768]{1,0:T(8,128)(2,1)S(1)}, u32[]{:S(2)}, u32[]{:S(2)}) collective-permute-start(bf16[56,768]{1,0:T(8,128)(2,1)S(1)} %get-tuple-element.187), channel_id=1, source_target_pairs={{0,1},{1,0},{2,3},{3,2},{4,5},{5,4},{6,7},{7,6},{8,9},{9,8},{10,11... | collective-permute-start | bytes 258056 | tf_op jit(solution)/shard_map/ppermute | solution.py:253
  155.6 9.7 %collective-permute-start.30 = (bf16[56,768]{1,0:T(8,128)(2,1)S(1)}, bf16[56,768]{1,0:T(8,128)(2,1)S(1)}, u32[]{:S(2)}, u32[]{:S(2)}) collective-permute-start(bf16[56,768]{1,0:T(8,128)(2,1)S(1)} %get-tuple-element.188), channel_id=1, source_target_pairs={{0,2},{1,3},{2,0},{3,1},{4,6},{5,7},{6,4},{7,5},{8,10},{9,11},{10,... | collective-permute-start | bytes 258056 | tf_op jit(solution)/shard_map/ppermute | solution.py:253
  156.3 8.9 %collective-permute-start.31 = (bf16[56,768]{1,0:T(8,128)(2,1)S(1)}, bf16[56,768]{1,0:T(8,128)(2,1)S(1)}, u32[]{:S(2)}, u32[]{:S(2)}) collective-permute-start(bf16[56,768]{1,0:T(8,128)(2,1)S(1)} %get-tuple-element.189), channel_id=1, source_target_pairs={{0,3},{1,2},{2,1},{3,0},{4,7},{5,6},{6,5},{7,4},{8,11},{9,10},{10,... | collective-permute-start | bytes 258056 | tf_op jit(solution)/shard_map/ppermute | solution.py:253
  165.6 4.8 %collective-permute-start.32 = (bf16[56,768]{1,0:T(8,128)(2,1)S(1)}, bf16[56,768]{1,0:T(8,128)(2,1)S(1)}, u32[]{:S(2)}, u32[]{:S(2)}) collective-permute-start(bf16[56,768]{1,0:T(8,128)(2,1)S(1)} %get-tuple-element.191), channel_id=1, source_target_pairs={{0,1},{1,0},{2,3},{3,2},{4,5},{5,4},{6,7},{7,6},{8,9},{9,8},{10,11... | collective-permute-start | bytes 258056 | tf_op jit(solution)/shard_map/ppermute | solution.py:253
  167.4 8.9 %collective-permute-start.33 = (bf16[56,768]{1,0:T(8,128)(2,1)S(1)}, bf16[56,768]{1,0:T(8,128)(2,1)S(1)}, u32[]{:S(2)}, u32[]{:S(2)}) collective-permute-start(bf16[56,768]{1,0:T(8,128)(2,1)S(1)} %get-tuple-element.191), channel_id=1, source_target_pairs={{0,2},{1,3},{2,0},{3,1},{4,6},{5,7},{6,4},{7,5},{8,10},{9,11},{10,... | collective-permute-start | bytes 258056 | tf_op jit(solution)/shard_map/ppermute | solution.py:253
  168.1 8.2 %collective-permute-start.34 = (bf16[56,768]{1,0:T(8,128)(2,1)S(1)}, bf16[56,768]{1,0:T(8,128)(2,1)S(1)}, u32[]{:S(2)}, u32[]{:S(2)}) collective-permute-start(bf16[56,768]{1,0:T(8,128)(2,1)S(1)} %get-tuple-element.191), channel_id=1, source_target_pairs={{0,3},{1,2},{2,1},{3,0},{4,7},{5,6},{6,5},{7,4},{8,11},{9,10},{10,... | collective-permute-start | bytes 258056 | tf_op jit(solution)/shard_map/ppermute | solution.py:253
  178.8 4.7 collective-permute-start.35
  180.5 8.8 %collective-permute-start.36 = (bf16[56,768]{1,0:T(8,128)(2,1)S(1)}, bf16[56,768]{1,0:T(8,128)(2,1)S(1)}, u32[]{:S(2)}, u32[]{:S(2)}) collective-permute-start(bf16[56,768]{1,0:T(8,128)(2,1)S(1)} %get-tuple-element.308), channel_id=1, source_target_pairs={{0,2},{1,3},{2,0},{3,1},{4,6},{5,7},{6,4},{7,5},{8,10},{9,11},{10,... | collective-permute-start | bytes 258056 | tf_op jit(solution)/shard_map/ppermute | solution.py:253
  181.3 8.0 %collective-permute-start.37 = (bf16[56,768]{1,0:T(8,128)(2,1)S(1)}, bf16[56,768]{1,0:T(8,128)(2,1)S(1)}, u32[]{:S(2)}, u32[]{:S(2)}) collective-permute-start(bf16[56,768]{1,0:T(8,128)(2,1)S(1)} %get-tuple-element.310), channel_id=1, source_target_pairs={{0,3},{1,2},{2,1},{3,0},{4,7},{5,6},{6,5},{7,4},{8,11},{9,10},{10,... | collective-permute-start | bytes 258056 | tf_op jit(solution)/shard_map/ppermute | solution.py:253
  191.3 8.7 %collective-permute-start.39 = (bf16[56,768]{1,0:T(8,128)(2,1)S(1)}, bf16[56,768]{1,0:T(8,128)(2,1)S(1)}, u32[]{:S(2)}, u32[]{:S(2)}) collective-permute-start(bf16[56,768]{1,0:T(8,128)(2,1)S(1)} %get-tuple-element.200), channel_id=1, source_target_pairs={{0,2},{1,3},{2,0},{3,1},{4,6},{5,7},{6,4},{7,5},{8,10},{9,11},{10,... | collective-permute-start | bytes 258056 | tf_op jit(solution)/shard_map/ppermute | solution.py:253
  191.8 8.2 %collective-permute-start.40 = (bf16[56,768]{1,0:T(8,128)(2,1)S(1)}, bf16[56,768]{1,0:T(8,128)(2,1)S(1)}, u32[]{:S(2)}, u32[]{:S(2)}) collective-permute-start(bf16[56,768]{1,0:T(8,128)(2,1)S(1)} %get-tuple-element.200), channel_id=1, source_target_pairs={{0,3},{1,2},{2,1},{3,0},{4,7},{5,6},{6,5},{7,4},{8,11},{9,10},{10,... | collective-permute-start | bytes 258056 | tf_op jit(solution)/shard_map/ppermute | solution.py:253
  203.0 8.6 %collective-permute-start.42 = (bf16[56,768]{1,0:T(8,128)(2,1)S(1)}, bf16[56,768]{1,0:T(8,128)(2,1)S(1)}, u32[]{:S(2)}, u32[]{:S(2)}) collective-permute-start(bf16[56,768]{1,0:T(8,128)(2,1)S(1)} %get-tuple-element.360), channel_id=1, source_target_pairs={{0,2},{1,3},{2,0},{3,1},{4,6},{5,7},{6,4},{7,5},{8,10},{9,11},{10,... | collective-permute-start | bytes 258056 | tf_op jit(solution)/shard_map/ppermute | solution.py:253
  203.5 8.2 %collective-permute-start.43 = (bf16[56,768]{1,0:T(8,128)(2,1)S(1)}, bf16[56,768]{1,0:T(8,128)(2,1)S(1)}, u32[]{:S(2)}, u32[]{:S(2)}) collective-permute-start(bf16[56,768]{1,0:T(8,128)(2,1)S(1)} %get-tuple-element.362), channel_id=1, source_target_pairs={{0,3},{1,2},{2,1},{3,0},{4,7},{5,6},{6,5},{7,4},{8,11},{9,10},{10,... | collective-permute-start | bytes 258056 | tf_op jit(solution)/shard_map/ppermute | solution.py:253
  211.9 6.2 %collective-permute-start.44 = (bf16[56,768]{1,0:T(8,128)(2,1)S(1)}, bf16[56,768]{1,0:T(8,128)(2,1)S(1)}, u32[]{:S(2)}, u32[]{:S(2)}) collective-permute-start(bf16[56,768]{1,0:T(8,128)(2,1)S(1)} %get-tuple-element.218), channel_id=1, source_target_pairs={{0,1},{1,0},{2,3},{3,2},{4,5},{5,4},{6,7},{7,6},{8,9},{9,8},{10,11... | collective-permute-start | bytes 258056 | tf_op jit(solution)/shard_map/ppermute | solution.py:253
  213.5 8.6 %collective-permute-start.45 = (bf16[56,768]{1,0:T(8,128)(2,1)S(1)}, bf16[56,768]{1,0:T(8,128)(2,1)S(1)}, u32[]{:S(2)}, u32[]{:S(2)}) collective-permute-start(bf16[56,768]{1,0:T(8,128)(2,1)S(1)} %get-tuple-element.218), channel_id=1, source_target_pairs={{0,2},{1,3},{2,0},{3,1},{4,6},{5,7},{6,4},{7,5},{8,10},{9,11},{10,... | collective-permute-start | bytes 258056 | tf_op jit(solution)/shard_map/ppermute | solution.py:253
  214.0 8.1 %collective-permute-start.46 = (bf16[56,768]{1,0:T(8,128)(2,1)S(1)}, bf16[56,768]{1,0:T(8,128)(2,1)S(1)}, u32[]{:S(2)}, u32[]{:S(2)}) collective-permute-start(bf16[56,768]{1,0:T(8,128)(2,1)S(1)} %get-tuple-element.218), channel_id=1, source_target_pairs={{0,3},{1,2},{2,1},{3,0},{4,7},{5,6},{6,5},{7,4},{8,11},{9,10},{10,... | collective-permute-start | bytes 258056 | tf_op jit(solution)/shard_map/ppermute | solution.py:253
  226.9 35.4 %all-to-all-start.3 = ((bf16[8,208,768]{2,1,0:T(8,128)(2,1)}), bf16[8,208,768]{2,1,0:T(8,128)(2,1)}, u32[]{:S(2)}, u32[]{:S(2)}) async-start(bf16[8,208,768]{2,1,0:T(8,128)(2,1)} %bitcast_dynamic-update-slice_fusion), calls=%async_computation.3 | async-start | bytes 5111808 | tf_op jit(solution)/shard_map/all_to_all | solution.py:615
  231.6 4.9 %collective-permute-start.47 = (bf16[56,768]{1,0:T(8,128)(2,1)S(1)}, bf16[56,768]{1,0:T(8,128)(2,1)S(1)}, u32[]{:S(2)}, u32[]{:S(2)}) collective-permute-start(bf16[56,768]{1,0:T(8,128)(2,1)S(1)} %get-tuple-element.346), channel_id=1, source_target_pairs={{0,1},{1,0},{2,3},{3,2},{4,5},{5,4},{6,7},{7,6},{8,9},{9,8},{10,11... | collective-permute-start | bytes 258056 | tf_op jit(solution)/shard_map/ppermute | solution.py:253
  233.3 9.6 %collective-permute-start.48 = (bf16[56,768]{1,0:T(8,128)(2,1)S(1)}, bf16[56,768]{1,0:T(8,128)(2,1)S(1)}, u32[]{:S(2)}, u32[]{:S(2)}) collective-permute-start(bf16[56,768]{1,0:T(8,128)(2,1)S(1)} %get-tuple-element.348), channel_id=1, source_target_pairs={{0,2},{1,3},{2,0},{3,1},{4,6},{5,7},{6,4},{7,5},{8,10},{9,11},{10,... | collective-permute-start | bytes 258056 | tf_op jit(solution)/shard_map/ppermute | solution.py:253
  233.7 9.1 %collective-permute-start.49 = (bf16[56,768]{1,0:T(8,128)(2,1)S(1)}, bf16[56,768]{1,0:T(8,128)(2,1)S(1)}, u32[]{:S(2)}, u32[]{:S(2)}) collective-permute-start(bf16[56,768]{1,0:T(8,128)(2,1)S(1)} %get-tuple-element.350), channel_id=1, source_target_pairs={{0,3},{1,2},{2,1},{3,0},{4,7},{5,6},{6,5},{7,4},{8,11},{9,10},{10,... | collective-permute-start | bytes 258056 | tf_op jit(solution)/shard_map/ppermute | solution.py:253
  243.8 6.4 %collective-permute-start.50 = (f32[2,4,768]{2,1,0:T(4,128)S(1)}, f32[2,4,768]{2,1,0:T(4,128)S(1)}, u32[]{:S(2)}, u32[]{:S(2)}) collective-permute-start(f32[2,4,768]{2,1,0:T(4,128)S(1)} %pad_maximum_fusion.11), channel_id=1, source_target_pairs={{0,1},{1,0},{2,3},{3,2},{4,5},{5,4},{6,7},{7,6},{8,9},{9,8},{10,11... | collective-permute-start | bytes 73736 | tf_op jit(solution)/shard_map/ppermute | solution.py:253
  245.8 4.9 %collective-permute-start.52 = (bf16[56,768]{1,0:T(8,128)(2,1)S(1)}, bf16[56,768]{1,0:T(8,128)(2,1)S(1)}, u32[]{:S(2)}, u32[]{:S(2)}) collective-permute-start(bf16[56,768]{1,0:T(8,128)(2,1)S(1)} %copy-done.70), channel_id=1, source_target_pairs={{0,1},{1,0},{2,3},{3,2},{4,5},{5,4},{6,7},{7,6},{8,9},{9,8},{10,11... | collective-permute-start | bytes 258056 | tf_op jit(solution)/shard_map/ppermute | solution.py:253
  245.9 10.1 %collective-permute-start.53 = (bf16[56,768]{1,0:T(8,128)(2,1)S(1)}, bf16[56,768]{1,0:T(8,128)(2,1)S(1)}, u32[]{:S(2)}, u32[]{:S(2)}) collective-permute-start(bf16[56,768]{1,0:T(8,128)(2,1)S(1)} %copy-done.69), channel_id=1, source_target_pairs={{0,2},{1,3},{2,0},{3,1},{4,6},{5,7},{6,4},{7,5},{8,10},{9,11},{10,... | collective-permute-start | bytes 258056 | tf_op jit(solution)/shard_map/ppermute | solution.py:253
  247.8 8.3 %collective-permute-start.54 = (bf16[56,768]{1,0:T(8,128)(2,1)S(1)}, bf16[56,768]{1,0:T(8,128)(2,1)S(1)}, u32[]{:S(2)}, u32[]{:S(2)}) collective-permute-start(bf16[56,768]{1,0:T(8,128)(2,1)S(1)} %copy-done.68), channel_id=1, source_target_pairs={{0,3},{1,2},{2,1},{3,0},{4,7},{5,6},{6,5},{7,4},{8,11},{9,10},{10,... | collective-permute-start | bytes 258056 | tf_op jit(solution)/shard_map/ppermute | solution.py:253
  250.2 7.0 %collective-permute-start.51 = (f32[2,4,768]{2,1,0:T(4,128)S(1)}, f32[2,4,768]{2,1,0:T(4,128)S(1)}, u32[]{:S(2)}, u32[]{:S(2)}) collective-permute-start(f32[2,4,768]{2,1,0:T(4,128)S(1)} %fusion.24), channel_id=1, source_target_pairs={{0,2},{1,3},{2,0},{3,1},{4,6},{5,7},{6,4},{7,5},{8,10},{9,11},{10,... | collective-permute-start | bytes 73736 | tf_op jit(solution)/shard_map/ppermute | solution.py:253
  272.9 41.5 %all-to-all-start.4 = ((f32[4,64,1536]{2,1,0:T(8,128)}), f32[4,64,1536]{2,1,0:T(8,128)}, u32[]{:S(2)}, u32[]{:S(2)}) async-start(f32[4,64,1536]{2,1,0:T(8,128)} %bitcast.170), calls=%async_computation.4 | async-start | bytes 3145728 | tf_op jit(solution)/shard_map/all_to_all | solution.py:317
  317.3 40.9 %all-to-all-start.5 = ((f32[4,64,1536]{2,1,0:T(8,128)}), f32[4,64,1536]{2,1,0:T(8,128)}, u32[]{:S(2)}, u32[]{:S(2)}) async-start(f32[4,64,1536]{2,1,0:T(8,128)} %broadcast_in_dim.146), calls=%async_computation.5 | async-start | bytes 3145728 | tf_op jit(solution)/shard_map/all_to_all | solution.py:291
  365.3 55.1 %collective-permute-start.58 = (f32[2,56,192]{2,1,0:T(8,128)}, f32[2,56,192]{2,1,0:T(8,128)}, u32[]{:S(2)}, u32[]{:S(2)}) collective-permute-start(f32[2,56,192]{2,1,0:T(8,128)} %get-tuple-element.386), channel_id=1, source_target_pairs={{0,1},{1,0},{2,3},{3,2},{4,5},{5,4},{6,7},{7,6},{8,9},{9,8},{10,11... | collective-permute-start | bytes 258056 | tf_op jit(solution)/shard_map/ppermute | solution.py:253
  365.3 55.1 %collective-permute-start.59 = (f32[2,56,192]{2,1,0:T(8,128)}, f32[2,56,192]{2,1,0:T(8,128)}, u32[]{:S(2)}, u32[]{:S(2)}) collective-permute-start(f32[2,56,192]{2,1,0:T(8,128)} %get-tuple-element.387), channel_id=1, source_target_pairs={{0,2},{1,3},{2,0},{3,1},{4,6},{5,7},{6,4},{7,5},{8,10},{9,11},{10,... | collective-permute-start | bytes 258056 | tf_op jit(solution)/shard_map/ppermute | solution.py:253
  367.3 53.0 %collective-permute-start.60 = (f32[2,56,192]{2,1,0:T(8,128)}, f32[2,56,192]{2,1,0:T(8,128)}, u32[]{:S(2)}, u32[]{:S(2)}) collective-permute-start(f32[2,56,192]{2,1,0:T(8,128)} %get-tuple-element.384), channel_id=1, source_target_pairs={{0,3},{1,2},{2,1},{3,0},{4,7},{5,6},{6,5},{7,4},{8,11},{9,10},{10,... | collective-permute-start | bytes 258056 | tf_op jit(solution)/shard_map/ppermute | solution.py:253
  371.4 49.0 %all-to-all-start.6 = ((bf16[8,192,768]{2,1,0:T(8,128)(2,1)}), bf16[8,192,768]{2,1,0:T(8,128)(2,1)}, u32[]{:S(2)}, u32[]{:S(2)}) async-start(bf16[8,192,768]{2,1,0:T(8,128)(2,1)} %pad_maximum_fusion.1), calls=%async_computation.6 | async-start | bytes 4718592 | tf_op jit(solution)/shard_map/all_to_all | solution.py:682
  422.0 45.2 %all-to-all-start.7 = ((bf16[8,192,768]{2,1,0:T(8,128)(2,1)}), bf16[8,192,768]{2,1,0:T(8,128)(2,1)S(1)}, u32[]{:S(2)}, u32[]{:S(2)}) async-start(bf16[8,192,768]{2,1,0:T(8,128)(2,1)} %pad_maximum_fusion.2), calls=%async_computation.7 | async-start | bytes 4718592 | tf_op jit(solution)/shard_map/all_to_all | solution.py:682
  429.9 30.5 %collective-permute-start.61 = (f32[2,197,192]{2,1,0:T(8,128)}, f32[2,197,192]{2,1,0:T(8,128)}, u32[]{:S(2)}, u32[]{:S(2)}) collective-permute-start(f32[2,197,192]{2,1,0:T(8,128)} %slice.195), channel_id=1, source_target_pairs={{0,0},{1,4},{2,8},{3,12},{4,1},{5,5},{6,9},{7,13},{8,2},{9,6},{10,... | collective-permute-start | bytes 907784 | tf_op jit(solution)/shard_map/ppermute | solution.py:247
  (79 other events, 812.8 us)
